TPU v7x, 32 devices: a whole 2x2x4 slice. The times are simulated.
32 devices in a mesh: space: 8 (over y, x, core), head: 4 (over z).
Axes of the slice: x: 2, y: 2, z: 4, core: 2. Of those that a mesh axis runs over, the one named last changes fastest.
Arguments:
- snapshot: bfloat16 [8192, 1536], P('space'), may hold values from -6 to 6
- norm_gain: float32 [1536], replicated, may hold values from 0.25 to 1.75
- w_query: bfloat16 [1536, 1536], P(None, 'head'), may hold values from -0.15625 to 0.15625
- w_key: bfloat16 [1536, 1536], P(None, 'head'), may hold values from -0.15625 to 0.15625
- w_value: bfloat16 [1536, 1536], P(None, 'head'), may hold values from -0.15625 to 0.15625
- w_out: bfloat16 [1536, 1536], P('head'), may hold values from -0.15625 to 0.15625
- cache_key: bfloat16 [8, 8192, 1536], P(None, 'space', 'head'), may hold values from -420 to 420
- cache_value: bfloat16 [8, 8192, 1536], P(None, 'space', 'head'), may hold values from -6 to 6
- pattern: int32 [64, 8], P('space'), may hold values from 0 to 63, as said below
- counts: int32 [64], P('space'), may hold values from 1 to 8, as said below
Outputs:
- rolled: bfloat16 [8192, 1536], P('space')
Inputs may be any that keep to these rules, and one draw needn't show every extreme that they name: `pattern`: each index is a block within 12 blocks of its query block, counted periodically over the 64 blocks; the 8 entries of one query block are distinct. `counts`: loads are uneven; some query block has all 8 slots live.
All inputs are finite; a program needn't handle non-finite values.
Results may differ from a plain program's by a relative error of at most 0.014.
Values may be sent and summed in bfloat16 or wider, within the bound.
No kernel may reach another device: no remote copies, remote signals or barrier semaphores. Data moves between devices by JAX's collectives and lax.ppermute only.
A program may use at most 192 MiB of HBM per device.

v0:
```python
import jax
import jax.numpy as jnp
from jax import lax
from jax.sharding import PartitionSpec as P

HD = 128
BLK = 128
MAXK = 8
FRAMES = 8
STEPS = 2


def shifted(value, axis, steps):
    count = lax.axis_size(axis)
    pairs = [(source, (source + steps) % count) for source in range(count)]
    return lax.ppermute(value, axis, pairs)


def on_device(
    snapshot, norm_gain, w_query, w_key, w_value, w_out, cache_key, cache_value, pattern, counts
):
    tok_rows = snapshot.shape[0]
    blocks = tok_rows // BLK
    reach_blocks = blocks + blocks // 2
    block_count_total = blocks * lax.axis_size("space")
    first_block = lax.axis_index("space") * blocks
    local_width = w_query.shape[1]
    heads_here = local_width // HD
    inv_scale = 1.0 / HD**0.5
    own_block = first_block + jnp.arange(blocks, dtype=jnp.int32)
    relative = (
        pattern - own_block[:, None] + block_count_total // 2
    ) % block_count_total - block_count_total // 2
    where_block = (jnp.arange(blocks, dtype=jnp.int32)[:, None] + reach_blocks + relative).reshape(
        blocks * MAXK
    )
    live_slot = jnp.arange(MAXK, dtype=jnp.int32)[None, :] < counts[:, None]
    live_keys = jnp.repeat(live_slot, BLK, axis=1)[:, None, :]
    state = snapshot
    key_frames = [cache_key[frame].reshape(blocks, BLK, local_width) for frame in range(FRAMES)]
    value_frames = [cache_value[frame].reshape(blocks, BLK, local_width) for frame in range(FRAMES)]
    for rollout in range(STEPS):
        state_wide = state.astype(jnp.float32)
        meansq = jnp.mean(state_wide * state_wide, axis=-1, keepdims=True)
        normed = (state_wide * lax.rsqrt(meansq + 1e-05) * norm_gain).astype(jnp.bfloat16)
        queries = jnp.dot(normed, w_query, preferred_element_type=jnp.float32).astype(jnp.bfloat16)
        key_new = jnp.dot(normed, w_key, preferred_element_type=jnp.float32).astype(jnp.bfloat16)
        value_new = jnp.dot(normed, w_value, preferred_element_type=jnp.float32).astype(
            jnp.bfloat16
        )
        key_value = jnp.stack([key_new, value_new])
        half_rows = tok_rows // 2
        distant = []
        for stride, portion in ((2, key_value[:, half_rows:]), (-2, key_value[:, :half_rows])):
            distant.append(shifted(portion, "space", stride))
        nearby = []
        for stride in (1, -1):
            nearby.append(shifted(key_value, "space", stride))
        window = jnp.concatenate([distant[0], nearby[0], key_value, nearby[1], distant[1]], axis=1)
        window = window.reshape(2, blocks + 2 * reach_blocks, BLK, local_width)
        taken = jnp.take(window, where_block, axis=1).reshape(2, blocks, MAXK * BLK, local_width)
        block_query = queries.reshape(blocks, BLK, local_width)
        head_outputs = []
        for head in range(heads_here):
            low = head * HD
            high = low + HD
            per_head_query = block_query[:, :, low:high]
            per_head_key = taken[0, :, :, low:high]
            per_head_value = taken[1, :, :, low:high]
            spatial = (
                jnp.einsum(
                    "hcj,hmj->hcm", per_head_query, per_head_key, preferred_element_type=jnp.float32
                )
                * inv_scale
            )
            spatial = jnp.where(live_keys, spatial, jnp.float32(-1e30))
            temporal = [
                jnp.einsum(
                    "urt,urt->ur",
                    per_head_query,
                    key_frames[frame][:, :, low:high],
                    preferred_element_type=jnp.float32,
                )
                * inv_scale
                for frame in range(FRAMES)
            ]
            top_score = spatial.max(axis=2)
            for frame in range(FRAMES):
                top_score = jnp.maximum(top_score, temporal[frame])
            spatial_exponent = jnp.exp(spatial - top_score[..., None])
            temporal_exp = [jnp.exp(temporal[frame] - top_score) for frame in range(FRAMES)]
            total = spatial_exponent.sum(axis=2)
            for frame in range(FRAMES):
                total = total + temporal_exp[frame]
            spatial_attention_weight = (spatial_exponent / total[..., None]).astype(jnp.bfloat16)
            mixed = jnp.einsum(
                "iwe,iea->iwa",
                spatial_attention_weight,
                per_head_value,
                preferred_element_type=jnp.float32,
            )
            for frame in range(FRAMES):
                temporal_weight = (temporal_exp[frame] / total).astype(jnp.bfloat16)
                mixed = mixed + temporal_weight.astype(jnp.float32)[..., None] * value_frames[
                    frame
                ][:, :, low:high].astype(jnp.float32)
            head_outputs.append(mixed.astype(jnp.bfloat16))
        attended_output = jnp.concatenate(head_outputs, axis=2).reshape(tok_rows, local_width)
        out_term = jnp.dot(attended_output, w_out, preferred_element_type=jnp.float32)
        update = lax.psum(out_term.astype(jnp.bfloat16), "head").astype(jnp.float32)
        state = (state_wide + update).astype(jnp.bfloat16)
        if rollout + 1 < STEPS:
            key_frames = key_frames[1:] + [key_new.reshape(blocks, BLK, local_width)]
            value_frames = value_frames[1:] + [value_new.reshape(blocks, BLK, local_width)]
    return state


def solution(mesh):
    placed = (
        P("space", None),
        P(),
        P(None, "head"),
        P(None, "head"),
        P(None, "head"),
        P("head", None),
        P(None, "space", "head"),
        P(None, "space", "head"),
        P("space", None),
        P("space"),
    )
    return jax.shard_map(
        on_device, mesh=mesh, in_specs=placed, out_specs=P("space", None), check_vma=False
    )
```

profile of v0, /device:TPU:0, one launch (start us, length us, event | category | flops | bytes accessed | tf_op | source)
XLA Modules:
  0.0 528.2 jit_solution(17118771061583152083)
XLA Ops:
  6.5 2.7 fusion
  9.3 4.2 convolution_convert_fusion.6
  13.5 1.9 convolution_convert_fusion.5
  17.2 2.9 collective-permute-start.2
  21.4 2.3 collective-permute-start.3
  25.5 4.2 convolution_convert_fusion.7
  29.7 2.5 fusion.218
  35.0 2.0 fusion.221
  37.0 1.8 copy.305
  38.8 1.8 copy.318
  40.6 1.8 copy.326
  42.5 2.2 fusion.225
  44.6 2.0 fusion.226
  46.6 2.0 fusion.227
  53.5 1.8 copy.321
  55.3 1.8 copy.309
  62.4 1.8 copy.316
  66.0 1.8 copy.307
  67.8 1.8 copy.315
  69.6 1.8 copy.323
  71.4 1.8 copy.306
  75.0 1.8 copy.322
  76.8 1.8 copy.312
  78.6 1.8 copy.320
  85.7 1.8 copy.327
  87.6 3.4 fusion.219
  91.8 1.9 fusion.98
  93.8 1.9 fusion.99
  97.2 2.1 constant_dynamic-update-slice_fusion.4
  99.3 2.7 constant_dynamic-update-slice_fusion.3
  103.4 2.8 constant_dynamic-update-slice_fusion.1
  106.1 2.1 constant_dynamic-update-slice_fusion
  108.2 10.8 %gather_fusion = bf16[64,2,128,384]{3,2,1,0:T(8,128)(2,1)} fusion(bf16[2,32,128,384]{3,2,1,0:T(8,128)(2,1)} %bitcast.4, s32[1024]{0:T(1024)} %pad_clamp_fusion), kind=kCustom, calls=%fused_computation.clone | custom fusion | bytes 25166080 | tf_op jit(solution)/shard_map/jit(_take)/gather | solution.py:61
  119.1 6.9 %select_bitcast_fusion.1 = bf16[2,64,128,384]{3,2,0,1:T(8,128)(2,1)S(1)} fusion(bf16[64,2,128,384]{3,2,1,0:T(8,128)(2,1)} %gather_fusion, pred[64]{0:T(512)(128)(4,1)} %compare_and_fusion), kind=kLoop, calls=%fused_computation.3 | loop fusion | flops 6291456 | bytes 25165888 | tf_op jit(solution)/shard_map/jit(_take)/select_n | solution.py:61
  126.0 3.3 copy.22
  131.3 2.7 fusion.14
  134.3 2.2 fusion.15
  136.8 2.1 fusion.93
  139.1 2.1 fusion.92
  141.2 2.1 fusion.91
  144.6 4.6 convolution_convert_fusion.1
  149.4 122.7 %all-reduce.3.cloned.1.call-done = bf16[1024,1536]{1,0:T(8,128)(2,1)} async-done(((bf16[1024,1536]{1,0:T(8,128)(2,1)}), bf16[1024,1536]{1,0:T(8,128)(2,1)}) %all-reduce.3.cloned.1.call-update) | async-done | bytes 3145744 | tf_op jit(solution)/shard_map/psum | solution.py:110
  272.1 4.1 fusion.4
  286.2 1.8 copy.330
  288.0 1.8 copy.331
  289.8 2.6 collective-permute-start.6
  294.4 4.3 convolution_convert_fusion.4
  298.8 2.1 collective-permute-start.7
  300.9 1.9 fusion.123
  302.8 1.9 fusion.122
  305.6 40.7 %collective-permute-done.4 = bf16[2,512,384]{2,1,0:T(8,128)(2,1)S(1)} collective-permute-done((bf16[2,512,384]{2,1,0:T(8,128)(2,1)S(1)}, bf16[2,512,384]{2,1,0:T(8,128)(2,1)S(1)}, u32[]{:S(2)}, u32[]{:S(2)}) %collective-permute-start.4) | collective-permute-done | bytes 786464 | tf_op jit(solution)/shard_map/ppermute | solution.py:16
  347.3 2.7 constant_dynamic-update-slice_fusion.8
  352.7 2.2 collective-permute-done.7
  355.9 10.9 %gather_fusion.1 = bf16[64,2,128,384]{3,2,1,0:T(8,128)(2,1)} fusion(bf16[2,32,128,384]{3,2,1,0:T(8,128)(2,1)} %bitcast.33, s32[1024]{0:T(1024)} %pad_clamp_fusion), kind=kCustom, calls=%fused_computation.1.clone | custom fusion | bytes 25166080 | tf_op jit(solution)/shard_map/jit(_take)/gather | solution.py:61
  366.8 7.0 %select_bitcast_fusion = bf16[2,64,128,384]{3,2,0,1:T(8,128)(2,1)S(1)} fusion(bf16[64,2,128,384]{3,2,1,0:T(8,128)(2,1)} %gather_fusion.1, pred[64]{0:T(512)(128)(4,1)S(1)} %copy-done.113), kind=kLoop, calls=%fused_computation.2 | loop fusion | flops 6291456 | bytes 25165888 | tf_op jit(solution)/shard_map/jit(_take)/select_n | solution.py:61
  373.8 3.3 copy.51
  379.0 2.7 fusion.17
  382.0 2.2 fusion.18
  384.5 2.1 fusion.90
  386.8 2.1 fusion.89
  388.9 2.1 fusion.88
  391.5 3.5 convolution_convert_fusion
  394.9 119.4 %all-reduce.5.cloned.1.call-done = bf16[1024,1536]{1,0:T(8,128)(2,1)} async-done(((bf16[1024,1536]{1,0:T(8,128)(2,1)}), bf16[1024,1536]{1,0:T(8,128)(2,1)}) %all-reduce.5.cloned.1.call-update) | async-done | bytes 3145744 | tf_op jit(solution)/shard_map/psum | solution.py:110
  514.3 6.7 %fusion.7 = bf16[1024,1536]{1,0:T(8,128)(2,1)} fusion(bf16[1024,1536]{1,0:T(8,128)(2,1)} %all-reduce.5.cloned.1.call-done, bf16[1024,1536]{1,0:T(8,128)(2,1)} %all-reduce.3.cloned.1.call-done, bf16[1024,1536]{1,0:T(8,128)(2,1)} %param.12), kind=kLoop, calls=%fused_computation.17 | loop fusion | flops 12582912 | bytes 12582912 | tf_op jit(solution)/shard_map/convert_element_type | solution.py:111
  (323 shorter events, 53.7 us)
Async XLA Ops:
  6.5 138.0 %copy-start = (bf16[384,1536]{1,0:T(8,128)(2,1)S(1)}, bf16[384,1536]{1,0:T(8,128)(2,1)}, u32[]{:S(2)}) copy-start(bf16[384,1536]{1,0:T(8,128)(2,1)} %param.17) | copy-start | bytes 3538948
  6.5 265.6 %all-reduce.3.cloned.1.call-start = ((), (), s32[]{:S(2)}) async-start(), calls=%async_computation | async-start | bytes 6291456 | tf_op jit(solution)/shard_map/psum | solution.py:110
  9.2 4.3 copy-start.1
  9.2 4.3 copy-start.110
  9.2 4.3 copy-start.115
  15.4 8.8 %copy-start.112 = (s32[8,8]{1,0:T(8,128)S(1)}, s32[8,8]{1,0:T(8,128)}, u32[]{:S(2)}) copy-start(s32[8,8]{1,0:T(8,128)} %param.20) | copy-start | bytes 772
  15.4 10.1 %copy-start.118 = (s32[8]{0:T(128)S(1)}, s32[8]{0:T(128)}, u32[]{:S(2)}) copy-start(s32[8]{0:T(128)} %param.21) | copy-start | bytes 100
  16.7 82.6 %collective-permute-start.1 = (bf16[2,1024,384]{2,1,0:T(8,128)(2,1)}, bf16[2,1024,384]{2,1,0:T(8,128)(2,1)}, u32[]{:S(2)}, u32[]{:S(2)}) collective-permute-start(bf16[2,1024,384]{2,1,0:T(8,128)(2,1)} %pad_maximum_fusion), channel_id=1, source_target_pairs={{0,4},{4,8},{8,12},{12,16},{16,20},{20,24},{24,28},{28,0},{1,5},{5... | collective-permute-start | bytes 4718600 | tf_op jit(solution)/shard_map/ppermute | solution.py:16
  17.2 86.2 %collective-permute-start.2 = (bf16[2,1024,384]{2,1,0:T(8,128)(2,1)}, bf16[2,1024,384]{2,1,0:T(8,128)(2,1)}, u32[]{:S(2)}, u32[]{:S(2)}) collective-permute-start(bf16[2,1024,384]{2,1,0:T(8,128)(2,1)} %pad_maximum_fusion), channel_id=1, source_target_pairs={{0,28},{4,0},{8,4},{12,8},{16,12},{20,16},{24,20},{28,24},{1,29},{... | collective-permute-start | bytes 4718600 | tf_op jit(solution)/shard_map/ppermute | solution.py:16
  21.4 84.7 %collective-permute-start.3 = (bf16[2,512,384]{2,1,0:T(8,128)(2,1)}, bf16[2,512,384]{2,1,0:T(8,128)(2,1)}, u32[]{:S(2)}, u32[]{:S(2)}) collective-permute-start(bf16[2,512,384]{2,1,0:T(8,128)(2,1)} %get-tuple-element.124), channel_id=1, source_target_pairs={{0,24},{4,28},{8,0},{12,4},{16,8},{20,12},{24,16},{28,20},{1,25},{... | collective-permute-start | bytes 2359304 | tf_op jit(solution)/shard_map/ppermute | solution.py:16
  23.7 73.5 %collective-permute-start = (bf16[2,512,384]{2,1,0:T(8,128)(2,1)}, bf16[2,512,384]{2,1,0:T(8,128)(2,1)}, u32[]{:S(2)}, u32[]{:S(2)}) collective-permute-start(bf16[2,512,384]{2,1,0:T(8,128)(2,1)} %get-tuple-element.125), channel_id=1, source_target_pairs={{0,8},{4,12},{8,16},{12,20},{16,24},{20,28},{24,0},{28,4},{1,9},{5... | collective-permute-start | bytes 2359304 | tf_op jit(solution)/shard_map/ppermute | solution.py:16
  25.5 4.2 slice-start
  25.5 4.2 slice-start.1
  42.4 6.2 %copy-start.23 = (bf16[1,1024,384]{2,1,0:T(8,128)(2,1)S(1)}, bf16[1,1024,384]{2,1,0:T(8,128)(2,1)}, u32[]{:S(2)}) copy-start(bf16[1,1024,384]{2,1,0:T(8,128)(2,1)} %get-tuple-element.111) | copy-start | bytes 2359300
  42.5 7.2 %copy-start.22 = (bf16[1,1024,384]{2,1,0:T(8,128)(2,1)S(1)}, bf16[1,1024,384]{2,1,0:T(8,128)(2,1)}, u32[]{:S(2)}) copy-start(bf16[1,1024,384]{2,1,0:T(8,128)(2,1)} %get-tuple-element.112) | copy-start | bytes 2359300
  42.5 8.2 %copy-start.21 = (bf16[1,1024,384]{2,1,0:T(8,128)(2,1)S(1)}, bf16[1,1024,384]{2,1,0:T(8,128)(2,1)}, u32[]{:S(2)}) copy-start(bf16[1,1024,384]{2,1,0:T(8,128)(2,1)} %get-tuple-element.113) | copy-start | bytes 2359300
  87.6 3.5 copy-start.114
  91.1 6.1 %copy-start.4 = (bf16[1,1024,384]{2,1,0:T(8,128)(2,1)}, bf16[1,1024,384]{2,1,0:T(8,128)(2,1)S(1)}, u32[]{:S(2)}) copy-start(bf16[1,1024,384]{2,1,0:T(8,128)(2,1)S(1)} %get-tuple-element.114) | copy-start | bytes 2359300
  91.1 6.1 %copy-start.6 = (bf16[1,1024,384]{2,1,0:T(8,128)(2,1)}, bf16[1,1024,384]{2,1,0:T(8,128)(2,1)S(1)}, u32[]{:S(2)}) copy-start(bf16[1,1024,384]{2,1,0:T(8,128)(2,1)S(1)} %get-tuple-element.116) | copy-start | bytes 2359300
  91.1 6.1 %copy-start.8 = (bf16[1,1024,384]{2,1,0:T(8,128)(2,1)}, bf16[1,1024,384]{2,1,0:T(8,128)(2,1)S(1)}, u32[]{:S(2)}) copy-start(bf16[1,1024,384]{2,1,0:T(8,128)(2,1)S(1)} %get-tuple-element.118) | copy-start | bytes 2359300
  91.1 6.1 %copy-start.10 = (bf16[1,1024,384]{2,1,0:T(8,128)(2,1)}, bf16[1,1024,384]{2,1,0:T(8,128)(2,1)S(1)}, u32[]{:S(2)}) copy-start(bf16[1,1024,384]{2,1,0:T(8,128)(2,1)S(1)} %get-tuple-element.120) | copy-start | bytes 2359300
  91.1 6.0 %copy-start.12 = (bf16[1,1024,384]{2,1,0:T(8,128)(2,1)}, bf16[1,1024,384]{2,1,0:T(8,128)(2,1)S(1)}, u32[]{:S(2)}) copy-start(bf16[1,1024,384]{2,1,0:T(8,128)(2,1)S(1)} %get-tuple-element.115) | copy-start | bytes 2359300
  91.1 6.0 %copy-start.14 = (bf16[1,1024,384]{2,1,0:T(8,128)(2,1)}, bf16[1,1024,384]{2,1,0:T(8,128)(2,1)S(1)}, u32[]{:S(2)}) copy-start(bf16[1,1024,384]{2,1,0:T(8,128)(2,1)S(1)} %get-tuple-element.117) | copy-start | bytes 2359300
  91.1 6.0 %copy-start.16 = (bf16[1,1024,384]{2,1,0:T(8,128)(2,1)}, bf16[1,1024,384]{2,1,0:T(8,128)(2,1)S(1)}, u32[]{:S(2)}) copy-start(bf16[1,1024,384]{2,1,0:T(8,128)(2,1)S(1)} %get-tuple-element.121) | copy-start | bytes 2359300
  131.1 2.9 copy-start.83
  131.1 2.9 copy-start.84
  131.1 2.9 copy-start.87
  131.2 2.9 copy-start.88
  131.2 2.9 copy-start.89
  131.2 2.9 copy-start.90
  131.2 2.9 copy-start.91
  131.2 2.9 copy-start.106
  131.2 2.9 copy-start.78
  131.2 2.9 copy-start.79
  131.2 2.9 copy-start.80
  131.2 2.9 copy-start.81
  131.2 2.9 copy-start.82
  131.3 2.9 copy-start.104
  149.2 127.1 %copy-start.111 = (f32[1536]{0:T(1024)S(1)}, f32[1536]{0:T(1024)}, u32[]{:S(2)}) copy-start(f32[1536]{0:T(1024)} %param.13) | copy-start | bytes 18436
  149.2 365.1 %all-reduce.5.cloned.1.call-start = ((), (), s32[]{:S(2)}) async-start(), calls=%async_computation.1 | async-start | bytes 6291456 | tf_op jit(solution)/shard_map/psum | solution.py:110
  272.1 4.1 copy-start.2
  272.1 4.7 copy-start.3
  278.1 3.9 copy-start.20
  283.4 63.9 %collective-permute-start.5 = (bf16[2,1024,384]{2,1,0:T(8,128)(2,1)}, bf16[2,1024,384]{2,1,0:T(8,128)(2,1)}, u32[]{:S(2)}, u32[]{:S(2)}) collective-permute-start(bf16[2,1024,384]{2,1,0:T(8,128)(2,1)} %pad_maximum_fusion.1), channel_id=1, source_target_pairs={{0,4},{4,8},{8,12},{12,16},{16,20},{20,24},{24,28},{28,0},{1,5},{5... | collective-permute-start | bytes 4718600 | tf_op jit(solution)/shard_map/ppermute | solution.py:16
  289.8 61.6 %collective-permute-start.6 = (bf16[2,1024,384]{2,1,0:T(8,128)(2,1)}, bf16[2,1024,384]{2,1,0:T(8,128)(2,1)S(1)}, u32[]{:S(2)}, u32[]{:S(2)}) collective-permute-start(bf16[2,1024,384]{2,1,0:T(8,128)(2,1)} %pad_maximum_fusion.1), channel_id=1, source_target_pairs={{0,28},{4,0},{8,4},{12,8},{16,12},{20,16},{24,20},{28,24},{1,29},{... | collective-permute-start | bytes 4718600 | tf_op jit(solution)/shard_map/ppermute | solution.py:16
  293.7 7.1 %copy-start.13 = (bf16[1,1024,384]{2,1,0:T(8,128)(2,1)S(1)}, bf16[1,1024,384]{2,1,0:T(8,128)(2,1)}, u32[]{:S(2)}) copy-start(bf16[1,1024,384]{2,1,0:T(8,128)(2,1)} %copy-done.12) | copy-start | bytes 2359300
  293.8 7.1 %copy-start.15 = (bf16[1,1024,384]{2,1,0:T(8,128)(2,1)S(1)}, bf16[1,1024,384]{2,1,0:T(8,128)(2,1)}, u32[]{:S(2)}) copy-start(bf16[1,1024,384]{2,1,0:T(8,128)(2,1)} %copy-done.14) | copy-start | bytes 2359300
  293.8 7.1 %copy-start.17 = (bf16[1,1024,384]{2,1,0:T(8,128)(2,1)S(1)}, bf16[1,1024,384]{2,1,0:T(8,128)(2,1)}, u32[]{:S(2)}) copy-start(bf16[1,1024,384]{2,1,0:T(8,128)(2,1)} %copy-done.16) | copy-start | bytes 2359300
  293.8 9.0 %copy-start.9 = (bf16[1,1024,384]{2,1,0:T(8,128)(2,1)S(1)}, bf16[1,1024,384]{2,1,0:T(8,128)(2,1)}, u32[]{:S(2)}) copy-start(bf16[1,1024,384]{2,1,0:T(8,128)(2,1)} %copy-done.8) | copy-start | bytes 2359300
  293.8 9.0 %copy-start.11 = (bf16[1,1024,384]{2,1,0:T(8,128)(2,1)S(1)}, bf16[1,1024,384]{2,1,0:T(8,128)(2,1)}, u32[]{:S(2)}) copy-start(bf16[1,1024,384]{2,1,0:T(8,128)(2,1)} %copy-done.10) | copy-start | bytes 2359300
  293.8 52.5 %collective-permute-start.4 = (bf16[2,512,384]{2,1,0:T(8,128)(2,1)S(1)}, bf16[2,512,384]{2,1,0:T(8,128)(2,1)S(1)}, u32[]{:S(2)}, u32[]{:S(2)}) collective-permute-start(bf16[2,512,384]{2,1,0:T(8,128)(2,1)S(1)} %get-tuple-element.123), channel_id=1, source_target_pairs={{0,8},{4,12},{8,16},{12,20},{16,24},{20,28},{24,0},{28,4},{1,9},{5... | collective-permute-start | bytes 2359304 | tf_op jit(solution)/shard_map/ppermute | solution.py:16
  298.7 6.0 %copy-start.5 = (bf16[1,1024,384]{2,1,0:T(8,128)(2,1)S(1)}, bf16[1,1024,384]{2,1,0:T(8,128)(2,1)}, u32[]{:S(2)}) copy-start(bf16[1,1024,384]{2,1,0:T(8,128)(2,1)} %copy-done.4) | copy-start | bytes 2359300
  298.8 5.9 %copy-start.7 = (bf16[1,1024,384]{2,1,0:T(8,128)(2,1)S(1)}, bf16[1,1024,384]{2,1,0:T(8,128)(2,1)}, u32[]{:S(2)}) copy-start(bf16[1,1024,384]{2,1,0:T(8,128)(2,1)} %copy-done.6) | copy-start | bytes 2359300
  298.8 56.2 %collective-permute-start.7 = (bf16[2,512,384]{2,1,0:T(8,128)(2,1)S(1)}, bf16[2,512,384]{2,1,0:T(8,128)(2,1)S(1)}, u32[]{:S(2)}, u32[]{:S(2)}) collective-permute-start(bf16[2,512,384]{2,1,0:T(8,128)(2,1)S(1)} %get-tuple-element.122), channel_id=1, source_target_pairs={{0,24},{4,28},{8,0},{12,4},{16,8},{20,12},{24,16},{28,20},{1,25},{... | collective-permute-start | bytes 2359304 | tf_op jit(solution)/shard_map/ppermute | solution.py:16
  304.7 45.3 %copy-start.19 = (bf16[1,1024,384]{2,1,0:T(8,128)(2,1)S(1)}, bf16[1,1024,384]{2,1,0:T(8,128)(2,1)}, u32[]{:S(2)}) copy-start(bf16[1,1024,384]{2,1,0:T(8,128)(2,1)} %copy-done.18) | copy-start | bytes 2359300
  355.9 10.9 %copy-start.113 = (pred[64]{0:T(512)(128)(4,1)S(1)}, pred[64]{0:T(512)(128)(4,1)}, u32[]{:S(2)}) copy-start(pred[64]{0:T(512)(128)(4,1)} %compare_and_fusion) | copy-start | bytes 196
  378.9 2.9 copy-start.75
  378.9 2.9 copy-start.76
  378.9 2.9 copy-start.77
  378.9 2.9 copy-start.85
  379.0 2.9 copy-start.72
  379.0 2.9 copy-start.73
  379.0 2.9 copy-start.74
  379.0 2.9 copy-start.105
  (67 other events, 133.7 us)
Sparse Core Ops, SparseCore 0:
  149.3 122.7 all-reduce.2
  395.1 119.1 all-reduce.4
where the time goes:
time: 533 us; the launch traced here: 528 us
  waiting for transfers between devices  285 us (53%)
  local copies, waits for them, and re-layouts  115 us (22%)
  other arithmetic  53.4 us (10%)
  matrix products  47.3 us (9%)
  between operations  15.9 us (3%)
  starting transfers between devices  11.7 us (2%)
    psum x2, waiting for transfers between devices, on_device(): update = lax.psum(out_term.astype(jnp.bfloat16), 'head').astype(jnp.float32)  242 us
    unnamed x275, local copies, waits for them, and re-layouts  62.6 us
    ppermute x8, waiting for transfers between devices, shifted(): return lax.ppermute(value, axis, pairs)  42.9 us
    gather x2, local copies, waits for them, and re-layouts, on_device(): jnp.take(window, where_block, axis=1)  21.8 us
    select_n x3, other arithmetic, on_device(): jnp.take(window, where_block, axis=1)  14.4 us
    slice x9, local copies, waits for them, and re-layouts, on_device(): value_frames[frame][:, :, low:high].astype(jnp.float32)  13.2 us
    dot_general x6, matrix products, on_device(): jnp.einsum('iwe,iea->iwa', spatial_attention_weight, per_head_value, pref...  12.6 us
    ppermute x8, starting transfers between devices, shifted(): return lax.ppermute(value, axis, pairs)  11.4 us
  transfers between devices with their start and end apart: 10, of which 4 were waited for; matrix products, arithmetic and copies ran while one was open for 20% of the time, Pallas kernels for 0%

commit v1 on v0

v1 whole, which is shorter than its diff:
```python
import functools
import math

import jax
import jax.numpy as jnp
from jax import lax
from jax.experimental import pallas as pl
from jax.experimental.pallas import tpu as pltpu
from jax.sharding import PartitionSpec as P

HD = 128
BLK = 128
STEPS = 2
TILE = 256
VMEM_LIMIT = 48 * 1024 * 1024
NT = (((1,), (1,)), ((), ()))


def shifted(value, axis, steps):
    count = lax.axis_size(axis)
    pairs = [(source, (source + steps) % count) for source in range(count)]
    return lax.ppermute(value, axis, pairs)


def around(value, axis):
    count = lax.axis_size(axis)
    order = list(range(0, count, 2)) + list(range(1, count, 2))[::-1]
    pairs = [(order[i], order[(i + 1) % count]) for i in range(count)]
    return lax.ppermute(value, axis, pairs)


def call(body, grid, in_specs, out_specs, out_shape, scratch=(), prefetch=0, flops=0, moved=0, exps=0):
    return pl.pallas_call(
        body,
        grid_spec=pltpu.PrefetchScalarGridSpec(
            num_scalar_prefetch=prefetch,
            grid=grid,
            in_specs=in_specs,
            out_specs=out_specs,
            scratch_shapes=list(scratch),
        ),
        out_shape=out_shape,
        compiler_params=pltpu.CompilerParams(
            dimension_semantics=("arbitrary",) * len(grid), vmem_limit_bytes=VMEM_LIMIT
        ),
        cost_estimate=pl.CostEstimate(flops=flops, bytes_accessed=moved, transcendentals=exps),
    )


def dot(a, b):
    return jnp.dot(a, b, preferred_element_type=jnp.float32)


def normalize(state, gain):
    meansq = jnp.mean(state * state, axis=-1, keepdims=True)
    return (state * lax.rsqrt(meansq + 1e-05) * gain).astype(jnp.bfloat16)


def store_blocks(kv_ref, key, value):
    for block in range(key.shape[0] // BLK):
        rows = slice(block * BLK, (block + 1) * BLK)
        kv_ref[block, 0] = key[rows].astype(jnp.bfloat16)
        kv_ref[block, 1] = value[rows].T.astype(jnp.bfloat16)


def first_body(state_ref, gain_ref, wk_ref, wv_ref, normed_ref, kv_ref, w_scr):
    @pl.when(pl.program_id(0) == 0)
    def _():
        w_scr[:, :HD] = wk_ref[...]
        w_scr[:, HD:] = wv_ref[...]

    normed = normalize(state_ref[...].astype(jnp.float32), gain_ref[...])
    normed_ref[...] = normed
    both = dot(normed, w_scr[...])
    store_blocks(kv_ref, both[:, :HD], both[:, HD:])


def first_projection(state, gain, w_key, w_value):
    rows, width = state.shape
    per_tile = TILE // BLK
    return call(
        first_body,
        (rows // TILE,),
        [
            pl.BlockSpec((TILE, width), lambda i: (i, 0)),
            pl.BlockSpec((1, width), lambda i: (0, 0)),
            pl.BlockSpec((width, HD), lambda i: (0, 0)),
            pl.BlockSpec((width, HD), lambda i: (0, 0)),
        ],
        [
            pl.BlockSpec((TILE, width), lambda i: (i, 0)),
            pl.BlockSpec((per_tile, 2, BLK, HD), lambda i: (i, 0, 0, 0)),
        ],
        [
            jax.ShapeDtypeStruct((rows, width), jnp.bfloat16),
            jax.ShapeDtypeStruct((rows // BLK, 2, BLK, HD), jnp.bfloat16),
        ],
        scratch=[pltpu.VMEM((width, 2 * HD), jnp.bfloat16)],
        flops=2 * rows * width * 2 * HD,
        moved=4 * rows * width,
    )(state, gain, w_key, w_value)


def rest_body(heads, normed_ref, wq_ref, wk_ref, wv_ref, *outs):
    normed = normed_ref[...]
    key = dot(normed, wk_ref[:, HD:])
    value = dot(normed, wv_ref[:, HD:])
    for head in range(1, heads):
        cols = slice((head - 1) * HD, head * HD)
        store_blocks(outs[head - 1], key[:, cols], value[:, cols])
    outs[heads - 1][...] = dot(normed, wq_ref[...]).astype(jnp.bfloat16)


def rest_projection(normed, w_query, w_key, w_value):
    rows, width = normed.shape
    local = w_query.shape[1]
    heads = local // HD
    per_tile = TILE // BLK
    full = pl.BlockSpec((width, local), lambda i: (0, 0))
    blocks = pl.BlockSpec((per_tile, 2, BLK, HD), lambda i: (i, 0, 0, 0))
    return call(
        functools.partial(rest_body, heads),
        (rows // TILE,),
        [pl.BlockSpec((TILE, width), lambda i: (i, 0)), full, full, full],
        [blocks] * (heads - 1) + [pl.BlockSpec((TILE, local), lambda i: (i, 0))],
        [jax.ShapeDtypeStruct((rows // BLK, 2, BLK, HD), jnp.bfloat16)] * (heads - 1)
        + [jax.ShapeDtypeStruct((rows, local), jnp.bfloat16)],
        flops=2 * rows * width * (3 * local - 2 * HD),
        moved=2 * rows * width + 6 * width * local,
    )(normed, w_query, w_key, w_value)


def attend_body(blocks, slots, frames, newer, where_ref, counts_ref, q_ref, ck_ref, cv_ref, *rest):
    rest = list(rest)
    last_ref = rest.pop(0) if newer else None
    own, left, right, far_left, far_right, out_ref, window, sem = rest
    index = pl.program_id(0)
    half = blocks // 2

    @pl.when(index == 0)
    def _():
        place = 0
        copies = []
        for piece, length in ((far_left, half), (left, blocks), (own, blocks), (right, blocks), (far_right, half)):
            copies.append(pltpu.make_async_copy(piece, window.at[pl.ds(place, length)], sem.at[len(copies)]))
            place += length
        for copy in copies:
            copy.start()
        for copy in copies:
            copy.wait()

    scale = math.log2(math.e) / math.sqrt(HD)
    live = counts_ref[index]
    query = q_ref[...]
    eye = lax.broadcasted_iota(jnp.int32, (BLK, BLK), 0) == lax.broadcasted_iota(jnp.int32, (BLK, BLK), 1)
    places = [where_ref[index * slots + slot] for slot in range(slots)]
    scores = []
    for slot in range(slots):
        score = lax.dot_general(window[places[slot], 0], query, NT, preferred_element_type=jnp.float32)
        scores.append(jnp.where(slot < live, score, jnp.float32(-1e30)))
    temporal = []
    for frame in range(frames):
        key = last_ref[0, 0] if newer and frame == 0 else ck_ref[frame]
        pairs = lax.dot_general(key, query, NT, preferred_element_type=jnp.float32)
        temporal.append(jnp.sum(jnp.where(eye, pairs, 0.0), axis=0, keepdims=True))
    top = functools.reduce(jnp.maximum, scores).max(axis=0, keepdims=True)
    top = functools.reduce(jnp.maximum, temporal, top)
    weights = [jnp.exp2((score - top) * scale) for score in scores]
    temporal = [jnp.exp2((score - top) * scale) for score in temporal]
    total = functools.reduce(jnp.add, weights).sum(axis=0, keepdims=True)
    total = functools.reduce(jnp.add, temporal, total)
    share = 1.0 / total
    values = jnp.concatenate([window[place, 1] for place in places], axis=1)
    mixed = dot(values, jnp.concatenate([weight.astype(jnp.bfloat16) for weight in weights], axis=0)) * share
    if newer:
        mixed = mixed + last_ref[0, 1].astype(jnp.float32) * (temporal[0] * share)
    skip = 1 if newer else 0
    spread = jnp.concatenate(
        [jnp.where(eye, weight * share, 0.0).astype(jnp.bfloat16) for weight in temporal[skip:]], axis=1
    )
    past = dot(spread, cv_ref[skip:].reshape((frames - skip) * BLK, HD))
    out_ref[...] = (mixed.T + past).astype(jnp.bfloat16)


def attend(head, where_block, counts, queries, cache_key, cache_value, last, pieces):
    rows = queries.shape[0]
    blocks = rows // BLK
    slots = where_block.shape[0] // blocks
    frames = cache_key.shape[0]
    newer = last is not None
    cached = pl.BlockSpec((frames, BLK, HD), lambda i, *_: (0, i, head))
    anywhere = pl.BlockSpec(memory_space=pl.ANY)
    total_blocks = sum(piece.shape[0] for piece in pieces)
    return call(
        functools.partial(attend_body, blocks, slots, frames, newer),
        (blocks,),
        [pl.BlockSpec((BLK, HD), lambda i, *_: (i, head)), cached, cached]
        + ([pl.BlockSpec((1, 2, BLK, HD), lambda i, *_: (i, 0, 0, 0))] if newer else [])
        + [anywhere] * len(pieces),
        pl.BlockSpec((BLK, HD), lambda i, *_: (i, 0)),
        jax.ShapeDtypeStruct((rows, HD), jnp.bfloat16),
        scratch=[
            pltpu.VMEM((total_blocks, 2, BLK, HD), jnp.bfloat16),
            pltpu.SemaphoreType.DMA((len(pieces),)),
        ],
        prefetch=2,
        flops=4 * rows * (slots + frames) * BLK * HD,
        moved=4 * frames * rows * HD + total_blocks * 4 * BLK * HD,
        exps=rows * slots * BLK,
    )(where_block, counts, queries, cache_key, cache_value, *([last] if newer else []), *pieces)


def gather_rows(w_scr, own_ref, others_ref, heads):
    groups = others_ref.shape[1] + 1
    for group in range(groups):
        for at, head in enumerate(heads):
            start = (group * len(heads) + at) * HD
            if group == 0:
                w_scr[start : start + HD] = own_ref[head * HD : (head + 1) * HD]
            else:
                w_scr[start : start + HD] = others_ref[:, group - 1, head].reshape(HD, w_scr.shape[1])


def part_body(heads, count, state_ref, own_ref, others_ref, *rest):
    pieces, (out_ref, w_scr) = rest[:count], rest[count:]

    @pl.when(pl.program_id(0) == 0)
    def _():
        gather_rows(w_scr, own_ref, others_ref, heads)

    attended = jnp.concatenate([piece[...] for piece in pieces], axis=1)
    out_ref[...] = (state_ref[...].astype(jnp.float32) + dot(attended, w_scr[...])).astype(out_ref.dtype)


def add_heads(heads, state, w_own, w_others, pieces, out_dtype):
    rows, width = state.shape
    depth = len(pieces) * HD
    return call(
        functools.partial(part_body, heads, len(pieces)),
        (rows // TILE,),
        [
            pl.BlockSpec((TILE, width), lambda i: (i, 0)),
            pl.BlockSpec(w_own.shape, lambda i: (0, 0)),
            pl.BlockSpec(w_others.shape, lambda i: (0, 0, 0, 0, 0)),
        ]
        + [pl.BlockSpec((TILE, HD), lambda i: (i, 0))] * len(pieces),
        pl.BlockSpec((TILE, width), lambda i: (i, 0)),
        jax.ShapeDtypeStruct((rows, width), out_dtype),
        scratch=[pltpu.VMEM((depth, width), jnp.bfloat16)],
        flops=2 * rows * width * depth,
        moved=6 * rows * width + 2 * depth * width,
    )(state, w_own, w_others, *pieces)


def turn_body(heads, count, part_ref, own_ref, others_ref, gain_ref, wk_ref, wv_ref, *rest):
    pieces, (state_ref, normed_ref, kv_ref, w_scr, kv_scr) = rest[:count], rest[count:]

    @pl.when(pl.program_id(0) == 0)
    def _():
        gather_rows(w_scr, own_ref, others_ref, heads)
        kv_scr[:, :HD] = wk_ref[...]
        kv_scr[:, HD:] = wv_ref[...]

    attended = jnp.concatenate([piece[...] for piece in pieces], axis=1)
    state = (part_ref[...] + dot(attended, w_scr[...])).astype(jnp.bfloat16)
    state_ref[...] = state
    normed = normalize(state.astype(jnp.float32), gain_ref[...])
    normed_ref[...] = normed
    both = dot(normed, kv_scr[...])
    store_blocks(kv_ref, both[:, :HD], both[:, HD:])


def turn(heads, part, w_own, w_others, pieces, gain, w_key, w_value):
    rows, width = part.shape
    depth = len(pieces) * HD
    per_tile = TILE // BLK
    tile = pl.BlockSpec((TILE, width), lambda i: (i, 0))
    return call(
        functools.partial(turn_body, heads, len(pieces)),
        (rows // TILE,),
        [
            tile,
            pl.BlockSpec(w_own.shape, lambda i: (0, 0)),
            pl.BlockSpec(w_others.shape, lambda i: (0, 0, 0, 0, 0)),
            pl.BlockSpec((1, width), lambda i: (0, 0)),
            pl.BlockSpec((width, HD), lambda i: (0, 0)),
            pl.BlockSpec((width, HD), lambda i: (0, 0)),
        ]
        + [pl.BlockSpec((TILE, HD), lambda i: (i, 0))] * len(pieces),
        [tile, tile, pl.BlockSpec((per_tile, 2, BLK, HD), lambda i: (i, 0, 0, 0))],
        [
            jax.ShapeDtypeStruct((rows, width), jnp.bfloat16),
            jax.ShapeDtypeStruct((rows, width), jnp.bfloat16),
            jax.ShapeDtypeStruct((rows // BLK, 2, BLK, HD), jnp.bfloat16),
        ],
        scratch=[pltpu.VMEM((depth, width), jnp.bfloat16), pltpu.VMEM((width, 2 * HD), jnp.bfloat16)],
        flops=2 * rows * width * (depth + 2 * HD),
        moved=8 * rows * width + 2 * depth * width,
    )(part, w_own, w_others, gain, w_key, w_value, *pieces)


def other_groups(w_out):
    count = lax.axis_size("space")
    half = count // 2
    local, width = w_out.shape
    heads = local // HD
    slice_rows = HD // 4
    me = lax.axis_index("space")
    quarter = me % 2 + 2 * (me // half)
    mine = lax.dynamic_index_in_dim(w_out.reshape(heads, 4, slice_rows, width), quarter, 1, keepdims=False)
    fetched = []
    for _ in range(lax.axis_size("head") - 1):
        mine = around(mine, "head")
        fetched.append(mine)
    fours = [[2 * m, 2 * m + 1, half + 2 * m, half + 2 * m + 1] for m in range(half // 2)]
    return lax.all_gather(jnp.stack(fetched), "space", axis_index_groups=fours)


def halo(kv):
    half = kv.shape[0] // 2
    left = shifted(kv, "space", 1)
    right = shifted(kv, "space", -1)
    far_left = shifted(left[half:], "space", 1)
    far_right = shifted(right[:half], "space", -1)
    return kv, left, right, far_left, far_right


def on_device(snapshot, norm_gain, w_query, w_key, w_value, w_out, cache_key, cache_value, pattern, counts):
    tok_rows, width = snapshot.shape
    blocks = tok_rows // BLK
    reach_blocks = blocks + blocks // 2
    block_count_total = blocks * lax.axis_size("space")
    first_block = lax.axis_index("space") * blocks
    heads = w_query.shape[1] // HD
    own_block = jnp.arange(blocks, dtype=jnp.int32)[:, None]
    relative = (pattern - own_block - first_block + block_count_total // 2) % block_count_total
    where_block = (own_block + reach_blocks + relative - block_count_total // 2).reshape(-1)
    gain = norm_gain.reshape(1, width)
    others = other_groups(w_out)
    state = snapshot
    normed, kv_first = first_projection(state, gain, w_key, w_value)
    last_kv = None
    for rollout in range(STEPS):
        kv = [kv_first]
        *kv_rest, queries = rest_projection(normed, w_query, w_key, w_value)
        kv = kv + list(kv_rest)
        came = []
        for head in range(heads):
            pieces = halo(kv[head])
            order = (pieces[0], pieces[1], pieces[2], pieces[3], pieces[4])
            attended = attend(
                head, where_block, counts, queries, cache_key, cache_value, last_kv[head] if last_kv else None, order
            )
            rounds = [attended]
            for _ in range(lax.axis_size("head") - 1):
                rounds.append(around(rounds[-1], "head"))
            came.append(rounds)
        early = list(range(heads - 1))
        groups = lax.axis_size("head")
        part = add_heads(
            early, state, w_out, others, [came[head][group] for group in range(groups) for head in early], jnp.float32
        )
        if rollout + 1 < STEPS:
            state, normed, kv_first = turn([heads - 1], part, w_out, others, came[-1], gain, w_key, w_value)
            last_kv = kv
        else:
            state = add_heads([heads - 1], part, w_out, others, came[-1], jnp.bfloat16)
    return state


def solution(mesh):
    placed = (
        P("space", None),
        P(),
        P(None, "head"),
        P(None, "head"),
        P(None, "head"),
        P("head", None),
        P(None, "space", "head"),
        P(None, "space", "head"),
        P("space", None),
        P("space"),
    )
    return jax.shard_map(
        on_device, mesh=mesh, in_specs=placed, out_specs=P("space", None), check_vma=False
    )
```

time: 533 us -> 327 us (0.61)
  waiting for transfers between devices: 285 us -> 104 us
  Pallas kernels: 0 us -> 109 us
  local copies, waits for them, and re-layouts: 115 us -> 26.5 us
  starting transfers between devices: 11.7 us -> 70.7 us
  other arithmetic: 53.4 us -> 1.1 us
  matrix products: 47.3 us -> 0 us
    psum x2 -> x0, waiting for transfers between devices: 242 us -> none  [on_device(): update = lax.psum(out_term.astype(jnp.bfloat16), 'head').astype(jnp.float32)]
    pallas_call x0 -> x13, Pallas kernels: none -> 109 us  [the longest x6 59.4 us: attend(): call(functools.partial(attend_body, blocks, slots, frames, newer), (block...]
    ppermute x0 -> x21, starting transfers between devices: none -> 51.5 us  [around(): return lax.ppermute(value, axis, pairs)]
    ppermute x0 -> x21, waiting for transfers between devices: none -> 50.7 us  [around(): return lax.ppermute(value, axis, pairs)]
    dot_general x20 -> x0, matrix products: 47.3 us -> none  [the longest x6 12.6 us: on_device(): jnp.einsum('iwe,iea->iwa', spatial_attention_weight, per_head_value, pref...]
    unnamed x275 -> x80, local copies, waits for them, and re-layouts: 62.6 us -> 19.4 us
    gather x2 -> x0, local copies, waits for them, and re-layouts: 21.8 us -> none  [on_device(): jnp.take(window, where_block, axis=1)]
    select_n x3 -> x0, other arithmetic: 14.4 us -> none  [on_device(): jnp.take(window, where_block, axis=1)]
  transfers between devices with their start and end apart: 10 -> 46, of which waited for: 4 -> 31; matrix products, arithmetic and copies ran while one was open for 20% -> 2% of each run, Pallas kernels for 0% -> 29%
where the time goes in v1:
time: 327 us; the launch traced here: 325 us
  Pallas kernels  109 us (33%)
  waiting for transfers between devices  104 us (32%)
  starting transfers between devices  70.7 us (22%)
  local copies, waits for them, and re-layouts  26.5 us (8%)
  between operations  13.7 us (4%)
    pallas_call x6, Pallas kernels, attend(): call(functools.partial(attend_body, blocks, slots, frames, newer), (block...  59.4 us
    ppermute x24, waiting for transfers between devices, shifted(): return lax.ppermute(value, axis, pairs)  53.6 us
    ppermute x21, starting transfers between devices, around(): return lax.ppermute(value, axis, pairs)  51.5 us
    ppermute x21, waiting for transfers between devices, around(): return lax.ppermute(value, axis, pairs)  50.7 us
    pallas_call x3, Pallas kernels, add_heads(): call(functools.partial(part_body, heads, len(pieces)), (rows // TILE,), [...  23.1 us
    unnamed x80, local copies, waits for them, and re-layouts  19.4 us
    ppermute x24, starting transfers between devices, shifted(): return lax.ppermute(value, axis, pairs)  19.2 us
    pallas_call x2, Pallas kernels, rest_projection(): call(functools.partial(rest_body, heads), (rows // TILE,), [pl.BlockSpec(...  11.4 us
  transfers between devices with their start and end apart: 46, of which 31 were waited for; matrix products, arithmetic and copies ran while one was open for 2% of the time, Pallas kernels for 29%

profile of v1, /device:TPU:0, one launch (start us, length us, event | category | flops | bytes accessed | tf_op | source)
XLA Modules:
  0.0 324.9 jit_solution(3156564568163300573)
XLA Ops:
  7.7 4.1 %collective-permute-start = (bf16[3,32,1536]{2,1,0:T(8,128)(2,1)S(1)}, bf16[3,32,1536]{2,1,0:T(8,128)(2,1)S(1)}, u32[]{:S(2)}, u32[]{:S(2)}) collective-permute-start(bf16[3,32,1536]{2,1,0:T(8,128)(2,1)S(1)} %dynamic-slice_bitcast_fusion), channel_id=1, source_target_pairs={{0,2},{2,3},{3,1},{1,0},{4,6},{6,7},{7,5},{5,4},{8,10},{10,11},{11... | collective-permute-start | bytes 884744 | tf_op jit(solution)/shard_map/ppermute | solution.py:29
  11.8 6.3 %collective-permute-done = bf16[3,32,1536]{2,1,0:T(8,128)(2,1)S(1)} collective-permute-done((bf16[3,32,1536]{2,1,0:T(8,128)(2,1)S(1)}, bf16[3,32,1536]{2,1,0:T(8,128)(2,1)S(1)}, u32[]{:S(2)}, u32[]{:S(2)}) %collective-permute-start) | collective-permute-done | bytes 294944 | tf_op jit(solution)/shard_map/ppermute | solution.py:29
  18.0 3.4 %collective-permute-start.1 = (bf16[3,32,1536]{2,1,0:T(8,128)(2,1)S(1)}, bf16[3,32,1536]{2,1,0:T(8,128)(2,1)S(1)}, u32[]{:S(2)}, u32[]{:S(2)}) collective-permute-start(bf16[3,32,1536]{2,1,0:T(8,128)(2,1)S(1)} %collective-permute-done), channel_id=1, source_target_pairs={{0,2},{2,3},{3,1},{1,0},{4,6},{6,7},{7,5},{5,4},{8,10},{10,11},{11... | collective-permute-start | bytes 884744 | tf_op jit(solution)/shard_map/ppermute | solution.py:29
  21.4 5.4 %collective-permute-done.1 = bf16[3,32,1536]{2,1,0:T(8,128)(2,1)S(1)} collective-permute-done((bf16[3,32,1536]{2,1,0:T(8,128)(2,1)S(1)}, bf16[3,32,1536]{2,1,0:T(8,128)(2,1)S(1)}, u32[]{:S(2)}, u32[]{:S(2)}) %collective-permute-start.1) | collective-permute-done | bytes 294944 | tf_op jit(solution)/shard_map/ppermute | solution.py:29
  26.8 3.4 %collective-permute-start.2 = (bf16[3,32,1536]{2,1,0:T(8,128)(2,1)S(1)}, bf16[3,32,1536]{2,1,0:T(8,128)(2,1)S(1)}, u32[]{:S(2)}, u32[]{:S(2)}) collective-permute-start(bf16[3,32,1536]{2,1,0:T(8,128)(2,1)S(1)} %collective-permute-done.1), channel_id=1, source_target_pairs={{0,2},{2,3},{3,1},{1,0},{4,6},{6,7},{7,5},{5,4},{8,10},{10,11},{11... | collective-permute-start | bytes 884744 | tf_op jit(solution)/shard_map/ppermute | solution.py:29
  30.2 4.5 %collective-permute-done.2 = bf16[3,32,1536]{2,1,0:T(8,128)(2,1)S(1)} collective-permute-done((bf16[3,32,1536]{2,1,0:T(8,128)(2,1)S(1)}, bf16[3,32,1536]{2,1,0:T(8,128)(2,1)S(1)}, u32[]{:S(2)}, u32[]{:S(2)}) %collective-permute-start.2) | collective-permute-done | bytes 294944 | tf_op jit(solution)/shard_map/ppermute | solution.py:29
  35.8 5.1 %shard_map.100 = (bf16[1024,1536]{1,0:T(8,128)(2,1)S(1)}, bf16[8,2,128,128]{3,2,1,0:T(8,128)(2,1)}) custom-call(bf16[1024,1536]{1,0:T(8,128)(2,1)} %state_ref.3, f32[1,1536]{1,0:T(1,128)S(1)} %reshape.16.gain_ref, bf16[1536,384]{1,0:T(8,128)(2,1)S(1)} %copy-done.2, bf16[1536,384]{1,0:T(8,128)(2,1)S(1)} %copy-done.3), custom_call_target="tpu_custom_call" | custom-call | flops 805306368 | bytes 6291456 | tf_op jit(solution)/shard_map/pallas_call | solution.py:81
  42.6 6.1 %shard_map.101 = (bf16[8,2,128,128]{3,2,1,0:T(8,128)(2,1)S(1)}, bf16[8,2,128,128]{3,2,1,0:T(8,128)(2,1)}, bf16[1024,384]{1,0:T(8,128)(2,1)S(1)}) custom-call(bf16[1024,1536]{1,0:T(8,128)(2,1)} %copy-done.35, bf16[1536,384]{1,0:T(8,128)(2,1)S(1)} %copy-done.36, bf16[1536,384]{1,0:T(8,128)(2,1)S(1)} %copy-done.2, bf16[1536,384]{1,0:T(8,128)(2,1)S(1)} %copy-done.3), custom_call_target="tpu_custom_call" | custom-call | flops 2818572288 | bytes 6684672 | tf_op jit(solution)/shard_map/pallas_call | solution.py:121
  50.1 2.1 collective-permute-start.4
  52.2 2.6 collective-permute-start.18
  54.8 5.4 %collective-permute-done.8.rest_2_ = bf16[8,2,128,128]{3,2,1,0:T(8,128)(2,1)S(1)} collective-permute-done((bf16[8,2,128,128]{3,2,1,0:T(8,128)(2,1)S(1)}, bf16[8,2,128,128]{3,2,1,0:T(8,128)(2,1)S(1)}, u32[]{:S(2)}, u32[]{:S(2)}) %collective-permute-start.8) | collective-permute-done | bytes 524320 | tf_op jit(solution)/shard_map/ppermute | solution.py:22
  60.3 1.9 collective-permute-start.17
  65.5 6.1 %collective-permute-done.4.rest_2_ = bf16[8,2,128,128]{3,2,1,0:T(8,128)(2,1)} collective-permute-done((bf16[8,2,128,128]{3,2,1,0:T(8,128)(2,1)}, bf16[8,2,128,128]{3,2,1,0:T(8,128)(2,1)}, u32[]{:S(2)}, u32[]{:S(2)}) %collective-permute-start.4) | collective-permute-done | bytes 524320 | tf_op jit(solution)/shard_map/ppermute | solution.py:22
  71.6 1.8 collective-permute-start.9
  76.1 1.7 slice.48
  77.8 5.0 %collective-permute-done.18.rest_2_ = bf16[8,2,128,128]{3,2,1,0:T(8,128)(2,1)S(1)} collective-permute-done((bf16[8,2,128,128]{3,2,1,0:T(8,128)(2,1)}, bf16[8,2,128,128]{3,2,1,0:T(8,128)(2,1)S(1)}, u32[]{:S(2)}, u32[]{:S(2)}) %collective-permute-start.18) | collective-permute-done | bytes 524320 | tf_op jit(solution)/shard_map/ppermute | solution.py:22
  82.9 1.8 collective-permute-start.5
  89.2 1.8 collective-permute-start.19
  95.1 10.2 %shard_map.103.rest_1_ = bf16[1024,128]{1,0:T(8,128)(2,1)S(1)} custom-call(s32[64]{0:T(128)S(1)} %reshape.15.where_ref, s32[8]{0:T(128)S(1)} %copy-done.34, bf16[1024,384]{1,0:T(8,128)(2,1)S(1)} %get-tuple-element.17.q_ref, bf16[8,1024,384]{2,1,0:T(8,128)(2,1)} %ck_ref.11, bf16[8,1024,384]{2,1,0:T(8,128)(2,1)} %cv_ref.11, ...), custom_call_target="tpu_custom_call" | custom-call | flops 1073741824 | bytes 6291456 | tf_op jit(solution)/shard_map/pallas_call | solution.py:194
  105.3 3.2 collective-permute-start.12
  108.5 10.7 %shard_map.102.rest_0_ = bf16[1024,128]{1,0:T(8,128)(2,1)S(1)} custom-call(s32[64]{0:T(128)S(1)} %reshape.15.where_ref, s32[8]{0:T(128)S(1)} %copy-done.34, bf16[1024,384]{1,0:T(8,128)(2,1)S(1)} %get-tuple-element.17.q_ref, bf16[8,1024,384]{2,1,0:T(8,128)(2,1)} %ck_ref.11, bf16[8,1024,384]{2,1,0:T(8,128)(2,1)} %cv_ref.11, ...), custom_call_target="tpu_custom_call" | custom-call | flops 1073741824 | bytes 6291456 | tf_op jit(solution)/shard_map/pallas_call | solution.py:194
  119.3 10.4 %shard_map.105.rest_0_ = bf16[1024,128]{1,0:T(8,128)(2,1)S(1)} custom-call(s32[64]{0:T(128)S(1)} %reshape.15.where_ref, s32[8]{0:T(128)S(1)} %copy-done.34, bf16[1024,384]{1,0:T(8,128)(2,1)S(1)} %get-tuple-element.17.q_ref, bf16[8,1024,384]{2,1,0:T(8,128)(2,1)} %ck_ref.11, bf16[8,1024,384]{2,1,0:T(8,128)(2,1)} %cv_ref.11, ...), custom_call_target="tpu_custom_call" | custom-call | flops 1073741824 | bytes 6291456 | tf_op jit(solution)/shard_map/pallas_call | solution.py:194
  129.8 1.9 collective-permute-start.21
  133.1 3.0 collective-permute-start.13
  136.8 2.2 collective-permute-done.21.rest_1_
  139.1 2.8 collective-permute-start.22
  142.5 2.2 collective-permute-done.14.rest_5_
  144.7 2.8 collective-permute-start.16
  148.1 2.2 collective-permute-done.13.rest_4_
  150.3 2.8 collective-permute-start.15
  153.7 2.3 collective-permute-done.22.rest_2_
  156.0 2.8 collective-permute-start.23
  158.8 2.8 collective-permute-done.16.rest_7_
  162.3 4.9 %collective-permute-done.15.rest_6_ = bf16[1024,128]{1,0:T(8,128)(2,1)S(1)} collective-permute-done((bf16[1024,128]{1,0:T(8,128)(2,1)S(1)}, bf16[1024,128]{1,0:T(8,128)(2,1)S(1)}, u32[]{:S(2)}, u32[]{:S(2)}) %collective-permute-start.15) | collective-permute-done | bytes 262176 | tf_op jit(solution)/shard_map/ppermute | solution.py:29
  174.5 8.5 %shard_map.104.part_ref = f32[1024,1536]{1,0:T(8,128)} custom-call(bf16[1024,1536]{1,0:T(8,128)(2,1)} %state_ref.3, bf16[384,1536]{1,0:T(8,128)(2,1)S(1)} %copy-done.1, bf16[4,3,3,32,1536]{4,3,2,1,0:T(8,128)(2,1)} %bitcast.9, bf16[1024,128]{1,0:T(8,128)(2,1)S(1)} %copy-done.15, bf16[1024,128]{1,0:T(8,128)(2,1)S(1)} %shard_map.103.rest_1_, ...), custom_call_target="tpu_custom_call" | custom-call | flops 3221225472 | bytes 12582912 | tf_op jit(solution)/shard_map/pallas_call | solution.py:238
  183.0 9.6 %shard_map.106 = (bf16[1024,1536]{1,0:T(8,128)(2,1)}, bf16[1024,1536]{1,0:T(8,128)(2,1)}, bf16[8,2,128,128]{3,2,1,0:T(8,128)(2,1)S(1)}) custom-call(f32[1024,1536]{1,0:T(8,128)} %shard_map.104.part_ref, bf16[384,1536]{1,0:T(8,128)(2,1)S(1)} %copy-done.1, bf16[4,3,3,32,1536]{4,3,2,1,0:T(8,128)(2,1)} %bitcast.10, f32[1,1536]{1,0:T(1,128)S(1)} %reshape.16.gain_ref, ...), custom_call_target="tpu_custom_call" | custom-call | flops 2415919104 | bytes 14155776 | tf_op jit(solution)/shard_map/pallas_call | solution.py:278
  193.2 5.3 %shard_map.107 = (bf16[8,2,128,128]{3,2,1,0:T(8,128)(2,1)S(1)}, bf16[8,2,128,128]{3,2,1,0:T(8,128)(2,1)S(1)}, bf16[1024,384]{1,0:T(8,128)(2,1)S(1)}) custom-call(bf16[1024,1536]{1,0:T(8,128)(2,1)} %get-tuple-element.22.normed_ref, bf16[1536,384]{1,0:T(8,128)(2,1)S(1)} %copy-done.37, bf16[1536,384]{1,0:T(8,128)(2,1)S(1)} %copy-done.2, ...), custom_call_target="tpu_custom_call" | custom-call | flops 2818572288 | bytes 6684672 | tf_op jit(solution)/shard_map/pallas_call | solution.py:121
  198.5 2.2 collective-permute-start.29
  200.7 2.6 collective-permute-start.39
  204.9 2.8 collective-permute-done.24.rest_2_
  207.8 8.3 %collective-permute-done.29.rest_3_ = bf16[8,2,128,128]{3,2,1,0:T(8,128)(2,1)S(1)} collective-permute-done((bf16[8,2,128,128]{3,2,1,0:T(8,128)(2,1)S(1)}, bf16[8,2,128,128]{3,2,1,0:T(8,128)(2,1)S(1)}, u32[]{:S(2)}, u32[]{:S(2)}) %collective-permute-start.29) | collective-permute-done | bytes 524320 | tf_op jit(solution)/shard_map/ppermute | solution.py:22
  216.1 2.8 collective-permute-done.28.rest_2_
  219.0 8.3 %collective-permute-done.39.rest_3_ = bf16[8,2,128,128]{3,2,1,0:T(8,128)(2,1)S(1)} collective-permute-done((bf16[8,2,128,128]{3,2,1,0:T(8,128)(2,1)S(1)}, bf16[8,2,128,128]{3,2,1,0:T(8,128)(2,1)S(1)}, u32[]{:S(2)}, u32[]{:S(2)}) %collective-permute-start.39) | collective-permute-done | bytes 524320 | tf_op jit(solution)/shard_map/ppermute | solution.py:22
  227.4 2.8 collective-permute-done.38.rest_2_
  230.3 2.7 collective-permute-done.27.rest_5_
  233.0 2.9 collective-permute-done.26.rest_4_
  235.8 9.3 %shard_map.108.rest_0_ = bf16[1024,128]{1,0:T(8,128)(2,1)S(1)} custom-call(s32[64]{0:T(128)S(1)} %reshape.15.where_ref, s32[8]{0:T(128)S(1)} %copy-done.34, bf16[1024,384]{1,0:T(8,128)(2,1)S(1)} %get-tuple-element.23.q_ref, bf16[8,1024,384]{2,1,0:T(8,128)(2,1)} %ck_ref.11, bf16[8,1024,384]{2,1,0:T(8,128)(2,1)} %cv_ref.11, ...), custom_call_target="tpu_custom_call" | custom-call | flops 1073741824 | bytes 6291456 | tf_op jit(solution)/shard_map/pallas_call | solution.py:194
  245.2 2.8 collective-permute-start.32
  248.0 9.3 %shard_map.109.rest_1_ = bf16[1024,128]{1,0:T(8,128)(2,1)S(1)} custom-call(s32[64]{0:T(128)S(1)} %reshape.15.where_ref, s32[8]{0:T(128)S(1)} %copy-done.34, bf16[1024,384]{1,0:T(8,128)(2,1)S(1)} %get-tuple-element.23.q_ref, bf16[8,1024,384]{2,1,0:T(8,128)(2,1)} %ck_ref.11, bf16[8,1024,384]{2,1,0:T(8,128)(2,1)} %cv_ref.11, ...), custom_call_target="tpu_custom_call" | custom-call | flops 1073741824 | bytes 6291456 | tf_op jit(solution)/shard_map/pallas_call | solution.py:194
  257.5 9.4 %shard_map.111.rest_0_ = bf16[1024,128]{1,0:T(8,128)(2,1)S(1)} custom-call(s32[64]{0:T(128)S(1)} %reshape.15.where_ref, s32[8]{0:T(128)S(1)} %copy-done.34, bf16[1024,384]{1,0:T(8,128)(2,1)S(1)} %get-tuple-element.23.q_ref, bf16[8,1024,384]{2,1,0:T(8,128)(2,1)} %ck_ref.11, bf16[8,1024,384]{2,1,0:T(8,128)(2,1)} %cv_ref.11, ...), custom_call_target="tpu_custom_call" | custom-call | flops 1073741824 | bytes 6291456 | tf_op jit(solution)/shard_map/pallas_call | solution.py:194
  266.8 3.1 collective-permute-start.42
  270.0 1.8 collective-permute-start.35
  271.8 4.9 %collective-permute-done.42.rest_1_ = bf16[1024,128]{1,0:T(8,128)(2,1)S(1)} collective-permute-done((bf16[1024,128]{1,0:T(8,128)(2,1)S(1)}, bf16[1024,128]{1,0:T(8,128)(2,1)S(1)}, u32[]{:S(2)}, u32[]{:S(2)}) %collective-permute-start.42) | collective-permute-done | bytes 262176 | tf_op jit(solution)/shard_map/ppermute | solution.py:29
  276.7 3.4 %collective-permute-start.43 = (bf16[1024,128]{1,0:T(8,128)(2,1)S(1)}, bf16[1024,128]{1,0:T(8,128)(2,1)S(1)}, u32[]{:S(2)}, u32[]{:S(2)}) collective-permute-start(bf16[1024,128]{1,0:T(8,128)(2,1)S(1)} %collective-permute-done.42.rest_1_), channel_id=1, source_target_pairs={{0,2},{2,3},{3,1},{1,0},{4,6},{6,7},{7,5},{5,4},{8,10},{10,11},{11... | collective-permute-start | bytes 786440 | tf_op jit(solution)/shard_map/ppermute | solution.py:29
  280.0 2.2 collective-permute-done.34.rest_4_
  282.3 3.4 %collective-permute-start.36 = (bf16[1024,128]{1,0:T(8,128)(2,1)S(1)}, bf16[1024,128]{1,0:T(8,128)(2,1)S(1)}, u32[]{:S(2)}, u32[]{:S(2)}) collective-permute-start(bf16[1024,128]{1,0:T(8,128)(2,1)S(1)} %collective-permute-done.34.rest_4_), channel_id=1, source_target_pairs={{0,2},{2,3},{3,1},{1,0},{4,6},{6,7},{7,5},{5,4},{8,10},{10,11},{11... | collective-permute-start | bytes 786440 | tf_op jit(solution)/shard_map/ppermute | solution.py:29
  285.7 2.2 collective-permute-done.35.rest_5_
  287.9 3.4 %collective-permute-start.37 = (bf16[1024,128]{1,0:T(8,128)(2,1)S(1)}, bf16[1024,128]{1,0:T(8,128)(2,1)S(1)}, u32[]{:S(2)}, u32[]{:S(2)}) collective-permute-start(bf16[1024,128]{1,0:T(8,128)(2,1)S(1)} %collective-permute-done.35.rest_5_), channel_id=1, source_target_pairs={{0,2},{2,3},{3,1},{1,0},{4,6},{6,7},{7,5},{5,4},{8,10},{10,11},{11... | collective-permute-start | bytes 786440 | tf_op jit(solution)/shard_map/ppermute | solution.py:29
  291.3 2.2 collective-permute-done.43.rest_2_
  293.5 3.4 %collective-permute-start.44 = (bf16[1024,128]{1,0:T(8,128)(2,1)S(1)}, bf16[1024,128]{1,0:T(8,128)(2,1)S(1)}, u32[]{:S(2)}, u32[]{:S(2)}) collective-permute-start(bf16[1024,128]{1,0:T(8,128)(2,1)S(1)} %collective-permute-done.43.rest_2_), channel_id=1, source_target_pairs={{0,2},{2,3},{3,1},{1,0},{4,6},{6,7},{7,5},{5,4},{8,10},{10,11},{11... | collective-permute-start | bytes 786440 | tf_op jit(solution)/shard_map/ppermute | solution.py:29
  296.9 2.2 collective-permute-done.36.rest_6_
  299.1 4.2 %collective-permute-done.37.rest_7_ = bf16[1024,128]{1,0:T(8,128)(2,1)S(1)} collective-permute-done((bf16[1024,128]{1,0:T(8,128)(2,1)S(1)}, bf16[1024,128]{1,0:T(8,128)(2,1)S(1)}, u32[]{:S(2)}, u32[]{:S(2)}) %collective-permute-start.37) | collective-permute-done | bytes 262176 | tf_op jit(solution)/shard_map/ppermute | solution.py:29
  303.4 8.5 %shard_map.110.state_ref = f32[1024,1536]{1,0:T(8,128)} custom-call(bf16[1024,1536]{1,0:T(8,128)(2,1)} %get-tuple-element.21.state_ref, bf16[384,1536]{1,0:T(8,128)(2,1)S(1)} %copy-done.1, bf16[4,3,3,32,1536]{4,3,2,1,0:T(8,128)(2,1)} %bitcast.11, bf16[1024,128]{1,0:T(8,128)(2,1)S(1)} %shard_map.108.rest_0_, bf16[1024,128]{1,0:T(8,128)(2,1)S(1)} %shard_map.109.rest_1_, ...), custom_call_target="tpu_custom_call" | custom-call | flops 3221225472 | bytes 12582912 | tf_op jit(solution)/shard_map/pallas_call | solution.py:238
  311.9 6.1 %shard_map.112 = bf16[1024,1536]{1,0:T(8,128)(2,1)} custom-call(f32[1024,1536]{1,0:T(8,128)} %shard_map.110.state_ref, bf16[384,1536]{1,0:T(8,128)(2,1)S(1)} %copy-done.1, bf16[4,3,3,32,1536]{4,3,2,1,0:T(8,128)(2,1)S(1)} %bitcast.12, bf16[1024,128]{1,0:T(8,128)(2,1)S(1)} %shard_map.111.rest_0_, bf16[1024,128]{1,0:T(8,128)(2,1)S(1)} %collective-permute-done.42.rest_1_, ...), custom_call_target="tpu_custom_call" | custom-call | flops 1610612736 | bytes 11010048 | tf_op jit(solution)/shard_map/pallas_call | solution.py:238
  (140 shorter events, 34.7 us)
Async XLA Ops:
  6.5 29.2 %copy-start.38 = (f32[1536]{0:T(1024)S(1)}, f32[1536]{0:T(1024)}, u32[]{:S(2)}) copy-start(f32[1536]{0:T(1024)} %param.11) | copy-start | bytes 18436
  6.5 29.2 %copy-start.3 = (bf16[1536,384]{1,0:T(8,128)(2,1)S(1)}, bf16[1536,384]{1,0:T(8,128)(2,1)}, u32[]{:S(2)}) copy-start(bf16[1536,384]{1,0:T(8,128)(2,1)} %wv_ref.7) | copy-start | bytes 3538948
  6.5 29.2 %copy-start.2 = (bf16[1536,384]{1,0:T(8,128)(2,1)S(1)}, bf16[1536,384]{1,0:T(8,128)(2,1)}, u32[]{:S(2)}) copy-start(bf16[1536,384]{1,0:T(8,128)(2,1)} %wk_ref.7) | copy-start | bytes 3538948
  6.5 161.3 %all-gather.3.cloned.1.call-start = ((), (), s32[]{:S(2)}) async-start(), calls=%async_computation | async-start | bytes 4423680 | tf_op jit(solution)/shard_map/all_gather | solution.py:316
  7.7 10.4 %collective-permute-start = (bf16[3,32,1536]{2,1,0:T(8,128)(2,1)S(1)}, bf16[3,32,1536]{2,1,0:T(8,128)(2,1)S(1)}, u32[]{:S(2)}, u32[]{:S(2)}) collective-permute-start(bf16[3,32,1536]{2,1,0:T(8,128)(2,1)S(1)} %dynamic-slice_bitcast_fusion), channel_id=1, source_target_pairs={{0,2},{2,3},{3,1},{1,0},{4,6},{6,7},{7,5},{5,4},{8,10},{10,11},{11... | collective-permute-start | bytes 884744 | tf_op jit(solution)/shard_map/ppermute | solution.py:29
  18.0 8.8 %collective-permute-start.1 = (bf16[3,32,1536]{2,1,0:T(8,128)(2,1)S(1)}, bf16[3,32,1536]{2,1,0:T(8,128)(2,1)S(1)}, u32[]{:S(2)}, u32[]{:S(2)}) collective-permute-start(bf16[3,32,1536]{2,1,0:T(8,128)(2,1)S(1)} %collective-permute-done), channel_id=1, source_target_pairs={{0,2},{2,3},{3,1},{1,0},{4,6},{6,7},{7,5},{5,4},{8,10},{10,11},{11... | collective-permute-start | bytes 884744 | tf_op jit(solution)/shard_map/ppermute | solution.py:29
  26.8 7.9 %collective-permute-start.2 = (bf16[3,32,1536]{2,1,0:T(8,128)(2,1)S(1)}, bf16[3,32,1536]{2,1,0:T(8,128)(2,1)S(1)}, u32[]{:S(2)}, u32[]{:S(2)}) collective-permute-start(bf16[3,32,1536]{2,1,0:T(8,128)(2,1)S(1)} %collective-permute-done.1), channel_id=1, source_target_pairs={{0,2},{2,3},{3,1},{1,0},{4,6},{6,7},{7,5},{5,4},{8,10},{10,11},{11... | collective-permute-start | bytes 884744 | tf_op jit(solution)/shard_map/ppermute | solution.py:29
  35.7 6.8 %copy-start.36 = (bf16[1536,384]{1,0:T(8,128)(2,1)S(1)}, bf16[1536,384]{1,0:T(8,128)(2,1)}, u32[]{:S(2)}) copy-start(bf16[1536,384]{1,0:T(8,128)(2,1)} %wq_ref.3) | copy-start | bytes 3538948
  42.6 42.1 %copy-start.39 = (s32[8,8]{1,0:T(8,128)S(1)}, s32[8,8]{1,0:T(8,128)}, u32[]{:S(2)}) copy-start(s32[8,8]{1,0:T(8,128)} %param.18) | copy-start | bytes 772
  48.7 43.3 %copy-start.34 = (s32[8]{0:T(128)S(1)}, s32[8]{0:T(128)}, u32[]{:S(2)}) copy-start(s32[8]{0:T(128)} %counts_ref.11) | copy-start | bytes 100
  48.7 11.6 %collective-permute-start.8 = (bf16[8,2,128,128]{3,2,1,0:T(8,128)(2,1)S(1)}, bf16[8,2,128,128]{3,2,1,0:T(8,128)(2,1)S(1)}, u32[]{:S(2)}, u32[]{:S(2)}) collective-permute-start(bf16[8,2,128,128]{3,2,1,0:T(8,128)(2,1)S(1)} %get-tuple-element.19.rest_0_), channel_id=1, source_target_pairs={{0,28},{4,0},{8,4},{12,8},{16,12},{20,16},{24,20},{28,24},{1,29},{... | collective-permute-start | bytes 1572872 | tf_op jit(solution)/shard_map/ppermute | solution.py:22
  48.7 15.1 %collective-permute-start.7 = (bf16[8,2,128,128]{3,2,1,0:T(8,128)(2,1)S(1)}, bf16[8,2,128,128]{3,2,1,0:T(8,128)(2,1)S(1)}, u32[]{:S(2)}, u32[]{:S(2)}) collective-permute-start(bf16[8,2,128,128]{3,2,1,0:T(8,128)(2,1)S(1)} %get-tuple-element.19.rest_0_), channel_id=1, source_target_pairs={{0,4},{4,8},{8,12},{12,16},{16,20},{20,24},{24,28},{28,0},{1,5},{5... | collective-permute-start | bytes 1572872 | tf_op jit(solution)/shard_map/ppermute | solution.py:22
  50.1 42.0 %copy-start.6 = (bf16[8,2,128,128]{3,2,1,0:T(8,128)(2,1)S(1)}, bf16[8,2,128,128]{3,2,1,0:T(8,128)(2,1)}, u32[]{:S(2)}) copy-start(bf16[8,2,128,128]{3,2,1,0:T(8,128)(2,1)} %copy-done.5) | copy-start | bytes 1572868
  50.1 21.6 %collective-permute-start.4 = (bf16[8,2,128,128]{3,2,1,0:T(8,128)(2,1)}, bf16[8,2,128,128]{3,2,1,0:T(8,128)(2,1)}, u32[]{:S(2)}, u32[]{:S(2)}) collective-permute-start(bf16[8,2,128,128]{3,2,1,0:T(8,128)(2,1)} %get-tuple-element.18.rest_0_), channel_id=1, source_target_pairs={{0,28},{4,0},{8,4},{12,8},{16,12},{20,16},{24,20},{28,24},{1,29},{... | collective-permute-start | bytes 1572872 | tf_op jit(solution)/shard_map/ppermute | solution.py:22
  52.2 23.0 %collective-permute-start.3 = (bf16[8,2,128,128]{3,2,1,0:T(8,128)(2,1)}, bf16[8,2,128,128]{3,2,1,0:T(8,128)(2,1)}, u32[]{:S(2)}, u32[]{:S(2)}) collective-permute-start(bf16[8,2,128,128]{3,2,1,0:T(8,128)(2,1)} %get-tuple-element.18.rest_0_), channel_id=1, source_target_pairs={{0,4},{4,8},{8,12},{12,16},{16,20},{20,24},{24,28},{28,0},{1,5},{5... | collective-permute-start | bytes 1572872 | tf_op jit(solution)/shard_map/ppermute | solution.py:22
  52.2 30.7 %collective-permute-start.18 = (bf16[8,2,128,128]{3,2,1,0:T(8,128)(2,1)}, bf16[8,2,128,128]{3,2,1,0:T(8,128)(2,1)S(1)}, u32[]{:S(2)}, u32[]{:S(2)}) collective-permute-start(bf16[8,2,128,128]{3,2,1,0:T(8,128)(2,1)} %get-tuple-element.20.rest_0_), channel_id=1, source_target_pairs={{0,28},{4,0},{8,4},{12,8},{16,12},{20,16},{24,20},{28,24},{1,29},{... | collective-permute-start | bytes 1572872 | tf_op jit(solution)/shard_map/ppermute | solution.py:22
  60.3 3.6 %copy-start.10 = (bf16[8,2,128,128]{3,2,1,0:T(8,128)(2,1)}, bf16[8,2,128,128]{3,2,1,0:T(8,128)(2,1)S(1)}, u32[]{:S(2)}) copy-start(bf16[8,2,128,128]{3,2,1,0:T(8,128)(2,1)S(1)} %collective-permute-done.8.rest_2_) | copy-start | bytes 1572868
  60.3 26.1 %collective-permute-start.17 = (bf16[8,2,128,128]{3,2,1,0:T(8,128)(2,1)}, bf16[8,2,128,128]{3,2,1,0:T(8,128)(2,1)}, u32[]{:S(2)}, u32[]{:S(2)}) collective-permute-start(bf16[8,2,128,128]{3,2,1,0:T(8,128)(2,1)} %get-tuple-element.20.rest_0_), channel_id=1, source_target_pairs={{0,4},{4,8},{8,12},{12,16},{16,20},{20,24},{24,28},{28,0},{1,5},{5... | collective-permute-start | bytes 1572872 | tf_op jit(solution)/shard_map/ppermute | solution.py:22
  63.9 24.6 %collective-permute-start.10 = (bf16[4,2,128,128]{3,2,1,0:T(8,128)(2,1)}, bf16[4,2,128,128]{3,2,1,0:T(8,128)(2,1)S(1)}, u32[]{:S(2)}, u32[]{:S(2)}) collective-permute-start(bf16[4,2,128,128]{3,2,1,0:T(8,128)(2,1)} %slice.51), channel_id=1, source_target_pairs={{0,28},{4,0},{8,4},{12,8},{16,12},{20,16},{24,20},{28,24},{1,29},{... | collective-permute-start | bytes 786440 | tf_op jit(solution)/shard_map/ppermute | solution.py:22
  71.6 20.4 %collective-permute-start.9 = (bf16[4,2,128,128]{3,2,1,0:T(8,128)(2,1)}, bf16[4,2,128,128]{3,2,1,0:T(8,128)(2,1)}, u32[]{:S(2)}, u32[]{:S(2)}) collective-permute-start(bf16[4,2,128,128]{3,2,1,0:T(8,128)(2,1)} %slice.50), channel_id=1, source_target_pairs={{0,4},{4,8},{8,12},{12,16},{16,20},{20,24},{24,28},{28,0},{1,5},{5... | collective-permute-start | bytes 786440 | tf_op jit(solution)/shard_map/ppermute | solution.py:22
  75.2 33.3 %collective-permute-start.6 = (bf16[4,2,128,128]{3,2,1,0:T(8,128)(2,1)}, bf16[4,2,128,128]{3,2,1,0:T(8,128)(2,1)}, u32[]{:S(2)}, u32[]{:S(2)}) collective-permute-start(bf16[4,2,128,128]{3,2,1,0:T(8,128)(2,1)} %slice.49), channel_id=1, source_target_pairs={{0,28},{4,0},{8,4},{12,8},{16,12},{20,16},{24,20},{28,24},{1,29},{... | collective-permute-start | bytes 786440 | tf_op jit(solution)/shard_map/ppermute | solution.py:22
  82.9 22.4 %copy-start.8 = (bf16[8,2,128,128]{3,2,1,0:T(8,128)(2,1)}, bf16[8,2,128,128]{3,2,1,0:T(8,128)(2,1)S(1)}, u32[]{:S(2)}) copy-start(bf16[8,2,128,128]{3,2,1,0:T(8,128)(2,1)S(1)} %collective-permute-done.18.rest_2_) | copy-start | bytes 1572868
  82.9 25.6 %collective-permute-start.5 = (bf16[4,2,128,128]{3,2,1,0:T(8,128)(2,1)}, bf16[4,2,128,128]{3,2,1,0:T(8,128)(2,1)}, u32[]{:S(2)}, u32[]{:S(2)}) collective-permute-start(bf16[4,2,128,128]{3,2,1,0:T(8,128)(2,1)} %slice.48), channel_id=1, source_target_pairs={{0,4},{4,8},{8,12},{12,16},{16,20},{20,24},{24,28},{28,0},{1,5},{5... | collective-permute-start | bytes 786440 | tf_op jit(solution)/shard_map/ppermute | solution.py:22
  86.4 32.9 %collective-permute-start.20 = (bf16[4,2,128,128]{3,2,1,0:T(8,128)(2,1)S(1)}, bf16[4,2,128,128]{3,2,1,0:T(8,128)(2,1)S(1)}, u32[]{:S(2)}, u32[]{:S(2)}) collective-permute-start(bf16[4,2,128,128]{3,2,1,0:T(8,128)(2,1)S(1)} %slice.53), channel_id=1, source_target_pairs={{0,28},{4,0},{8,4},{12,8},{16,12},{20,16},{24,20},{28,24},{1,29},{... | collective-permute-start | bytes 786440 | tf_op jit(solution)/shard_map/ppermute | solution.py:22
  89.2 30.1 %collective-permute-start.19 = (bf16[4,2,128,128]{3,2,1,0:T(8,128)(2,1)S(1)}, bf16[4,2,128,128]{3,2,1,0:T(8,128)(2,1)S(1)}, u32[]{:S(2)}, u32[]{:S(2)}) collective-permute-start(bf16[4,2,128,128]{3,2,1,0:T(8,128)(2,1)S(1)} %slice.52), channel_id=1, source_target_pairs={{0,4},{4,8},{8,12},{12,16},{16,20},{20,24},{24,28},{28,0},{1,5},{5... | collective-permute-start | bytes 786440 | tf_op jit(solution)/shard_map/ppermute | solution.py:22
  105.3 27.1 %collective-permute-start.12 = (bf16[1024,128]{1,0:T(8,128)(2,1)S(1)}, bf16[1024,128]{1,0:T(8,128)(2,1)S(1)}, u32[]{:S(2)}, u32[]{:S(2)}) collective-permute-start(bf16[1024,128]{1,0:T(8,128)(2,1)S(1)} %shard_map.103.rest_1_), channel_id=1, source_target_pairs={{0,2},{2,3},{3,1},{1,0},{4,6},{6,7},{7,5},{5,4},{8,10},{10,11},{11... | collective-permute-start | bytes 786440 | tf_op jit(solution)/shard_map/ppermute | solution.py:29
  108.5 10.9 %copy-start.9 = (bf16[8,2,128,128]{3,2,1,0:T(8,128)(2,1)S(1)}, bf16[8,2,128,128]{3,2,1,0:T(8,128)(2,1)}, u32[]{:S(2)}) copy-start(bf16[8,2,128,128]{3,2,1,0:T(8,128)(2,1)} %copy-done.8) | copy-start | bytes 1572868
  119.2 10.6 %copy-start.14 = (bf16[1024,128]{1,0:T(8,128)(2,1)}, bf16[1024,128]{1,0:T(8,128)(2,1)S(1)}, u32[]{:S(2)}) copy-start(bf16[1024,128]{1,0:T(8,128)(2,1)S(1)} %shard_map.102.rest_0_) | copy-start | bytes 786436
  119.2 48.7 %copy-start.1 = (bf16[384,1536]{1,0:T(8,128)(2,1)S(1)}, bf16[384,1536]{1,0:T(8,128)(2,1)}, u32[]{:S(2)}) copy-start(bf16[384,1536]{1,0:T(8,128)(2,1)} %own_ref.7) | copy-start | bytes 3538948
  119.2 13.9 %collective-permute-start.11 = (bf16[1024,128]{1,0:T(8,128)(2,1)S(1)}, bf16[1024,128]{1,0:T(8,128)(2,1)S(1)}, u32[]{:S(2)}, u32[]{:S(2)}) collective-permute-start(bf16[1024,128]{1,0:T(8,128)(2,1)S(1)} %shard_map.102.rest_0_), channel_id=1, source_target_pairs={{0,2},{2,3},{3,1},{1,0},{4,6},{6,7},{7,5},{5,4},{8,10},{10,11},{11... | collective-permute-start | bytes 786440 | tf_op jit(solution)/shard_map/ppermute | solution.py:29
  129.8 9.3 %collective-permute-start.21 = (bf16[1024,128]{1,0:T(8,128)(2,1)S(1)}, bf16[1024,128]{1,0:T(8,128)(2,1)S(1)}, u32[]{:S(2)}, u32[]{:S(2)}) collective-permute-start(bf16[1024,128]{1,0:T(8,128)(2,1)S(1)} %shard_map.105.rest_0_), channel_id=1, source_target_pairs={{0,2},{2,3},{3,1},{1,0},{4,6},{6,7},{7,5},{5,4},{8,10},{10,11},{11... | collective-permute-start | bytes 786440 | tf_op jit(solution)/shard_map/ppermute | solution.py:29
  132.4 12.3 %collective-permute-start.14 = (bf16[1024,128]{1,0:T(8,128)(2,1)S(1)}, bf16[1024,128]{1,0:T(8,128)(2,1)S(1)}, u32[]{:S(2)}, u32[]{:S(2)}) collective-permute-start(bf16[1024,128]{1,0:T(8,128)(2,1)S(1)} %collective-permute-done.12.rest_3_), channel_id=1, source_target_pairs={{0,2},{2,3},{3,1},{1,0},{4,6},{6,7},{7,5},{5,4},{8,10},{10,11},{11... | collective-permute-start | bytes 786440 | tf_op jit(solution)/shard_map/ppermute | solution.py:29
  133.1 17.2 %collective-permute-start.13 = (bf16[1024,128]{1,0:T(8,128)(2,1)S(1)}, bf16[1024,128]{1,0:T(8,128)(2,1)S(1)}, u32[]{:S(2)}, u32[]{:S(2)}) collective-permute-start(bf16[1024,128]{1,0:T(8,128)(2,1)S(1)} %collective-permute-done.11.rest_2_), channel_id=1, source_target_pairs={{0,2},{2,3},{3,1},{1,0},{4,6},{6,7},{7,5},{5,4},{8,10},{10,11},{11... | collective-permute-start | bytes 786440 | tf_op jit(solution)/shard_map/ppermute | solution.py:29
  139.1 17.0 %collective-permute-start.22 = (bf16[1024,128]{1,0:T(8,128)(2,1)S(1)}, bf16[1024,128]{1,0:T(8,128)(2,1)}, u32[]{:S(2)}, u32[]{:S(2)}) collective-permute-start(bf16[1024,128]{1,0:T(8,128)(2,1)S(1)} %collective-permute-done.21.rest_1_), channel_id=1, source_target_pairs={{0,2},{2,3},{3,1},{1,0},{4,6},{6,7},{7,5},{5,4},{8,10},{10,11},{11... | collective-permute-start | bytes 786440 | tf_op jit(solution)/shard_map/ppermute | solution.py:29
  144.7 16.9 %collective-permute-start.16 = (bf16[1024,128]{1,0:T(8,128)(2,1)S(1)}, bf16[1024,128]{1,0:T(8,128)(2,1)S(1)}, u32[]{:S(2)}, u32[]{:S(2)}) collective-permute-start(bf16[1024,128]{1,0:T(8,128)(2,1)S(1)} %collective-permute-done.14.rest_5_), channel_id=1, source_target_pairs={{0,2},{2,3},{3,1},{1,0},{4,6},{6,7},{7,5},{5,4},{8,10},{10,11},{11... | collective-permute-start | bytes 786440 | tf_op jit(solution)/shard_map/ppermute | solution.py:29
  150.3 16.9 %collective-permute-start.15 = (bf16[1024,128]{1,0:T(8,128)(2,1)S(1)}, bf16[1024,128]{1,0:T(8,128)(2,1)S(1)}, u32[]{:S(2)}, u32[]{:S(2)}) collective-permute-start(bf16[1024,128]{1,0:T(8,128)(2,1)S(1)} %collective-permute-done.13.rest_4_), channel_id=1, source_target_pairs={{0,2},{2,3},{3,1},{1,0},{4,6},{6,7},{7,5},{5,4},{8,10},{10,11},{11... | collective-permute-start | bytes 786440 | tf_op jit(solution)/shard_map/ppermute | solution.py:29
  156.0 27.0 %collective-permute-start.23 = (bf16[1024,128]{1,0:T(8,128)(2,1)}, bf16[1024,128]{1,0:T(8,128)(2,1)}, u32[]{:S(2)}, u32[]{:S(2)}) collective-permute-start(bf16[1024,128]{1,0:T(8,128)(2,1)} %collective-permute-done.22.rest_2_), channel_id=1, source_target_pairs={{0,2},{2,3},{3,1},{1,0},{4,6},{6,7},{7,5},{5,4},{8,10},{10,11},{11... | collective-permute-start | bytes 786440 | tf_op jit(solution)/shard_map/ppermute | solution.py:29
  174.5 8.5 %copy-start.4 = (bf16[1536,384]{1,0:T(8,128)(2,1)S(1)}, bf16[1536,384]{1,0:T(8,128)(2,1)}, u32[]{:S(2)}) copy-start(bf16[1536,384]{1,0:T(8,128)(2,1)} %wv_ref.7) | copy-start | bytes 3538948
  174.5 8.5 %copy-start.17 = (bf16[1024,128]{1,0:T(8,128)(2,1)S(1)}, bf16[1024,128]{1,0:T(8,128)(2,1)}, u32[]{:S(2)}) copy-start(bf16[1024,128]{1,0:T(8,128)(2,1)} %copy-done.16) | copy-start | bytes 786436
  174.5 8.5 %copy-start.23 = (bf16[1024,128]{1,0:T(8,128)(2,1)S(1)}, bf16[1024,128]{1,0:T(8,128)(2,1)}, u32[]{:S(2)}) copy-start(bf16[1024,128]{1,0:T(8,128)(2,1)} %copy-done.22) | copy-start | bytes 786436
  183.0 10.2 %copy-start.37 = (bf16[1536,384]{1,0:T(8,128)(2,1)S(1)}, bf16[1536,384]{1,0:T(8,128)(2,1)}, u32[]{:S(2)}) copy-start(bf16[1536,384]{1,0:T(8,128)(2,1)} %wq_ref.3) | copy-start | bytes 3538948
  192.7 12.2 %collective-permute-start.25 = (bf16[8,2,128,128]{3,2,1,0:T(8,128)(2,1)S(1)}, bf16[8,2,128,128]{3,2,1,0:T(8,128)(2,1)S(1)}, u32[]{:S(2)}, u32[]{:S(2)}) collective-permute-start(bf16[8,2,128,128]{3,2,1,0:T(8,128)(2,1)S(1)} %get-tuple-element.24.rest_1_), channel_id=1, source_target_pairs={{0,28},{4,0},{8,4},{12,8},{16,12},{20,16},{24,20},{28,24},{1,29},{... | collective-permute-start | bytes 1572872 | tf_op jit(solution)/shard_map/ppermute | solution.py:22
  192.7 15.1 %collective-permute-start.24 = (bf16[8,2,128,128]{3,2,1,0:T(8,128)(2,1)S(1)}, bf16[8,2,128,128]{3,2,1,0:T(8,128)(2,1)S(1)}, u32[]{:S(2)}, u32[]{:S(2)}) collective-permute-start(bf16[8,2,128,128]{3,2,1,0:T(8,128)(2,1)S(1)} %get-tuple-element.24.rest_1_), channel_id=1, source_target_pairs={{0,4},{4,8},{8,12},{12,16},{16,20},{20,24},{24,28},{28,0},{1,5},{5... | collective-permute-start | bytes 1572872 | tf_op jit(solution)/shard_map/ppermute | solution.py:22
  198.5 17.6 %collective-permute-start.29 = (bf16[8,2,128,128]{3,2,1,0:T(8,128)(2,1)S(1)}, bf16[8,2,128,128]{3,2,1,0:T(8,128)(2,1)S(1)}, u32[]{:S(2)}, u32[]{:S(2)}) collective-permute-start(bf16[8,2,128,128]{3,2,1,0:T(8,128)(2,1)S(1)} %get-tuple-element.25.rest_1_), channel_id=1, source_target_pairs={{0,28},{4,0},{8,4},{12,8},{16,12},{20,16},{24,20},{28,24},{1,29},{... | collective-permute-start | bytes 1572872 | tf_op jit(solution)/shard_map/ppermute | solution.py:22
  200.7 18.3 %collective-permute-start.28 = (bf16[8,2,128,128]{3,2,1,0:T(8,128)(2,1)S(1)}, bf16[8,2,128,128]{3,2,1,0:T(8,128)(2,1)S(1)}, u32[]{:S(2)}, u32[]{:S(2)}) collective-permute-start(bf16[8,2,128,128]{3,2,1,0:T(8,128)(2,1)S(1)} %get-tuple-element.25.rest_1_), channel_id=1, source_target_pairs={{0,4},{4,8},{8,12},{12,16},{16,20},{20,24},{24,28},{28,0},{1,5},{5... | collective-permute-start | bytes 1572872 | tf_op jit(solution)/shard_map/ppermute | solution.py:22
  200.7 26.7 %collective-permute-start.39 = (bf16[8,2,128,128]{3,2,1,0:T(8,128)(2,1)S(1)}, bf16[8,2,128,128]{3,2,1,0:T(8,128)(2,1)S(1)}, u32[]{:S(2)}, u32[]{:S(2)}) collective-permute-start(bf16[8,2,128,128]{3,2,1,0:T(8,128)(2,1)S(1)} %get-tuple-element.26.rest_1_), channel_id=1, source_target_pairs={{0,28},{4,0},{8,4},{12,8},{16,12},{20,16},{24,20},{28,24},{1,29},{... | collective-permute-start | bytes 1572872 | tf_op jit(solution)/shard_map/ppermute | solution.py:22
  204.9 25.3 %collective-permute-start.38 = (bf16[8,2,128,128]{3,2,1,0:T(8,128)(2,1)S(1)}, bf16[8,2,128,128]{3,2,1,0:T(8,128)(2,1)S(1)}, u32[]{:S(2)}, u32[]{:S(2)}) collective-permute-start(bf16[8,2,128,128]{3,2,1,0:T(8,128)(2,1)S(1)} %get-tuple-element.26.rest_1_), channel_id=1, source_target_pairs={{0,4},{4,8},{8,12},{12,16},{16,20},{20,24},{24,28},{28,0},{1,5},{5... | collective-permute-start | bytes 1572872 | tf_op jit(solution)/shard_map/ppermute | solution.py:22
  207.7 25.2 %collective-permute-start.27 = (bf16[4,2,128,128]{3,2,1,0:T(8,128)(2,1)S(1)}, bf16[4,2,128,128]{3,2,1,0:T(8,128)(2,1)S(1)}, u32[]{:S(2)}, u32[]{:S(2)}) collective-permute-start(bf16[4,2,128,128]{3,2,1,0:T(8,128)(2,1)S(1)} %slice.55), channel_id=1, source_target_pairs={{0,28},{4,0},{8,4},{12,8},{16,12},{20,16},{24,20},{28,24},{1,29},{... | collective-permute-start | bytes 786440 | tf_op jit(solution)/shard_map/ppermute | solution.py:22
  216.1 19.7 %collective-permute-start.26 = (bf16[4,2,128,128]{3,2,1,0:T(8,128)(2,1)S(1)}, bf16[4,2,128,128]{3,2,1,0:T(8,128)(2,1)S(1)}, u32[]{:S(2)}, u32[]{:S(2)}) collective-permute-start(bf16[4,2,128,128]{3,2,1,0:T(8,128)(2,1)S(1)} %slice.54), channel_id=1, source_target_pairs={{0,4},{4,8},{8,12},{12,16},{16,20},{20,24},{24,28},{28,0},{1,5},{5... | collective-permute-start | bytes 786440 | tf_op jit(solution)/shard_map/ppermute | solution.py:22
  219.0 29.1 %collective-permute-start.31 = (bf16[4,2,128,128]{3,2,1,0:T(8,128)(2,1)S(1)}, bf16[4,2,128,128]{3,2,1,0:T(8,128)(2,1)S(1)}, u32[]{:S(2)}, u32[]{:S(2)}) collective-permute-start(bf16[4,2,128,128]{3,2,1,0:T(8,128)(2,1)S(1)} %slice.57), channel_id=1, source_target_pairs={{0,28},{4,0},{8,4},{12,8},{16,12},{20,16},{24,20},{28,24},{1,29},{... | collective-permute-start | bytes 786440 | tf_op jit(solution)/shard_map/ppermute | solution.py:22
  227.3 20.7 %collective-permute-start.30 = (bf16[4,2,128,128]{3,2,1,0:T(8,128)(2,1)S(1)}, bf16[4,2,128,128]{3,2,1,0:T(8,128)(2,1)S(1)}, u32[]{:S(2)}, u32[]{:S(2)}) collective-permute-start(bf16[4,2,128,128]{3,2,1,0:T(8,128)(2,1)S(1)} %slice.56), channel_id=1, source_target_pairs={{0,4},{4,8},{8,12},{12,16},{16,20},{20,24},{24,28},{28,0},{1,5},{5... | collective-permute-start | bytes 786440 | tf_op jit(solution)/shard_map/ppermute | solution.py:22
  230.2 27.3 %collective-permute-start.41 = (bf16[4,2,128,128]{3,2,1,0:T(8,128)(2,1)S(1)}, bf16[4,2,128,128]{3,2,1,0:T(8,128)(2,1)S(1)}, u32[]{:S(2)}, u32[]{:S(2)}) collective-permute-start(bf16[4,2,128,128]{3,2,1,0:T(8,128)(2,1)S(1)} %slice.59), channel_id=1, source_target_pairs={{0,28},{4,0},{8,4},{12,8},{16,12},{20,16},{24,20},{28,24},{1,29},{... | collective-permute-start | bytes 786440 | tf_op jit(solution)/shard_map/ppermute | solution.py:22
  233.0 24.5 %collective-permute-start.40 = (bf16[4,2,128,128]{3,2,1,0:T(8,128)(2,1)S(1)}, bf16[4,2,128,128]{3,2,1,0:T(8,128)(2,1)S(1)}, u32[]{:S(2)}, u32[]{:S(2)}) collective-permute-start(bf16[4,2,128,128]{3,2,1,0:T(8,128)(2,1)S(1)} %slice.58), channel_id=1, source_target_pairs={{0,4},{4,8},{8,12},{12,16},{16,20},{20,24},{24,28},{28,0},{1,5},{5... | collective-permute-start | bytes 786440 | tf_op jit(solution)/shard_map/ppermute | solution.py:22
  235.8 12.2 %copy-start.7 = (bf16[8,2,128,128]{3,2,1,0:T(8,128)(2,1)S(1)}, bf16[8,2,128,128]{3,2,1,0:T(8,128)(2,1)}, u32[]{:S(2)}) copy-start(bf16[8,2,128,128]{3,2,1,0:T(8,128)(2,1)} %copy-done.5) | copy-start | bytes 1572868
  245.2 24.7 %collective-permute-start.32 = (bf16[1024,128]{1,0:T(8,128)(2,1)S(1)}, bf16[1024,128]{1,0:T(8,128)(2,1)S(1)}, u32[]{:S(2)}, u32[]{:S(2)}) collective-permute-start(bf16[1024,128]{1,0:T(8,128)(2,1)S(1)} %shard_map.108.rest_0_), channel_id=1, source_target_pairs={{0,2},{2,3},{3,1},{1,0},{4,6},{6,7},{7,5},{5,4},{8,10},{10,11},{11... | collective-permute-start | bytes 786440 | tf_op jit(solution)/shard_map/ppermute | solution.py:29
  257.4 12.6 %collective-permute-start.33 = (bf16[1024,128]{1,0:T(8,128)(2,1)S(1)}, bf16[1024,128]{1,0:T(8,128)(2,1)S(1)}, u32[]{:S(2)}, u32[]{:S(2)}) collective-permute-start(bf16[1024,128]{1,0:T(8,128)(2,1)S(1)} %shard_map.109.rest_1_), channel_id=1, source_target_pairs={{0,2},{2,3},{3,1},{1,0},{4,6},{6,7},{7,5},{5,4},{8,10},{10,11},{11... | collective-permute-start | bytes 786440 | tf_op jit(solution)/shard_map/ppermute | solution.py:29
  266.8 9.8 %collective-permute-start.42 = (bf16[1024,128]{1,0:T(8,128)(2,1)S(1)}, bf16[1024,128]{1,0:T(8,128)(2,1)S(1)}, u32[]{:S(2)}, u32[]{:S(2)}) collective-permute-start(bf16[1024,128]{1,0:T(8,128)(2,1)S(1)} %shard_map.111.rest_0_), channel_id=1, source_target_pairs={{0,2},{2,3},{3,1},{1,0},{4,6},{6,7},{7,5},{5,4},{8,10},{10,11},{11... | collective-permute-start | bytes 786440 | tf_op jit(solution)/shard_map/ppermute | solution.py:29
  269.9 12.4 %collective-permute-start.34 = (bf16[1024,128]{1,0:T(8,128)(2,1)S(1)}, bf16[1024,128]{1,0:T(8,128)(2,1)S(1)}, u32[]{:S(2)}, u32[]{:S(2)}) collective-permute-start(bf16[1024,128]{1,0:T(8,128)(2,1)S(1)} %collective-permute-done.32.rest_2_), channel_id=1, source_target_pairs={{0,2},{2,3},{3,1},{1,0},{4,6},{6,7},{7,5},{5,4},{8,10},{10,11},{11... | collective-permute-start | bytes 786440 | tf_op jit(solution)/shard_map/ppermute | solution.py:29
  270.0 17.9 %collective-permute-start.35 = (bf16[1024,128]{1,0:T(8,128)(2,1)S(1)}, bf16[1024,128]{1,0:T(8,128)(2,1)S(1)}, u32[]{:S(2)}, u32[]{:S(2)}) collective-permute-start(bf16[1024,128]{1,0:T(8,128)(2,1)S(1)} %collective-permute-done.33.rest_3_), channel_id=1, source_target_pairs={{0,2},{2,3},{3,1},{1,0},{4,6},{6,7},{7,5},{5,4},{8,10},{10,11},{11... | collective-permute-start | bytes 786440 | tf_op jit(solution)/shard_map/ppermute | solution.py:29
  276.7 16.9 %collective-permute-start.43 = (bf16[1024,128]{1,0:T(8,128)(2,1)S(1)}, bf16[1024,128]{1,0:T(8,128)(2,1)S(1)}, u32[]{:S(2)}, u32[]{:S(2)}) collective-permute-start(bf16[1024,128]{1,0:T(8,128)(2,1)S(1)} %collective-permute-done.42.rest_1_), channel_id=1, source_target_pairs={{0,2},{2,3},{3,1},{1,0},{4,6},{6,7},{7,5},{5,4},{8,10},{10,11},{11... | collective-permute-start | bytes 786440 | tf_op jit(solution)/shard_map/ppermute | solution.py:29
  282.3 16.9 %collective-permute-start.36 = (bf16[1024,128]{1,0:T(8,128)(2,1)S(1)}, bf16[1024,128]{1,0:T(8,128)(2,1)S(1)}, u32[]{:S(2)}, u32[]{:S(2)}) collective-permute-start(bf16[1024,128]{1,0:T(8,128)(2,1)S(1)} %collective-permute-done.34.rest_4_), channel_id=1, source_target_pairs={{0,2},{2,3},{3,1},{1,0},{4,6},{6,7},{7,5},{5,4},{8,10},{10,11},{11... | collective-permute-start | bytes 786440 | tf_op jit(solution)/shard_map/ppermute | solution.py:29
  287.9 15.5 %collective-permute-start.37 = (bf16[1024,128]{1,0:T(8,128)(2,1)S(1)}, bf16[1024,128]{1,0:T(8,128)(2,1)S(1)}, u32[]{:S(2)}, u32[]{:S(2)}) collective-permute-start(bf16[1024,128]{1,0:T(8,128)(2,1)S(1)} %collective-permute-done.35.rest_5_), channel_id=1, source_target_pairs={{0,2},{2,3},{3,1},{1,0},{4,6},{6,7},{7,5},{5,4},{8,10},{10,11},{11... | collective-permute-start | bytes 786440 | tf_op jit(solution)/shard_map/ppermute | solution.py:29
  293.5 18.3 %collective-permute-start.44 = (bf16[1024,128]{1,0:T(8,128)(2,1)S(1)}, bf16[1024,128]{1,0:T(8,128)(2,1)S(1)}, u32[]{:S(2)}, u32[]{:S(2)}) collective-permute-start(bf16[1024,128]{1,0:T(8,128)(2,1)S(1)} %collective-permute-done.43.rest_2_), channel_id=1, source_target_pairs={{0,2},{2,3},{3,1},{1,0},{4,6},{6,7},{7,5},{5,4},{8,10},{10,11},{11... | collective-permute-start | bytes 786440 | tf_op jit(solution)/shard_map/ppermute | solution.py:29
  303.4 8.5 %copy-start = (bf16[12,3,32,1536]{3,2,1,0:T(8,128)(2,1)S(1)}, bf16[12,3,32,1536]{3,2,1,0:T(8,128)(2,1)}, u32[]{:S(2)}) copy-start(bf16[12,3,32,1536]{3,2,1,0:T(8,128)(2,1)} %all-gather.3.cloned.1.call-done) | copy-start | bytes 10616836
  (22 other events, 19.3 us)
Sparse Core Ops, SparseCore 0:
  35.8 45.2 all-gather.2

commit v2 on v1

v2 whole, which is shorter than its diff:
```python
import functools
import math

import jax
import jax.numpy as jnp
from jax import lax
from jax.experimental import pallas as pl
from jax.experimental.pallas import tpu as pltpu
from jax.sharding import PartitionSpec as P

HD = 128
BLK = 128
STEPS = 2
TILE = 256
MIB = 1024 * 1024
SCALE = math.log2(math.e) / math.sqrt(HD)


def shifted(value, axis, steps):
    count = lax.axis_size(axis)
    pairs = [(source, (source + steps) % count) for source in range(count)]
    return lax.ppermute(value, axis, pairs)


def around(value, axis):
    count = lax.axis_size(axis)
    order = list(range(0, count, 2)) + list(range(1, count, 2))[::-1]
    onward = [(order[i], order[(i + 1) % count]) for i in range(count)]
    back = [(target, source) for source, target in onward]
    came, ahead, behind = [value], value, value
    for hop in range(count - 1):
        if hop % 2 == 0:
            ahead = lax.ppermute(ahead, axis, onward)
            came.append(ahead)
        else:
            behind = lax.ppermute(behind, axis, back)
            came.append(behind)
    return came


def after(value, *others):
    return lax.optimization_barrier((value,) + others)[0]


def call(body, grid, in_specs, out_specs, out_shape, vmem, scratch=(), prefetch=0, flops=0, moved=0, exps=0):
    return pl.pallas_call(
        body,
        grid_spec=pltpu.PrefetchScalarGridSpec(
            num_scalar_prefetch=prefetch,
            grid=grid,
            in_specs=in_specs,
            out_specs=out_specs,
            scratch_shapes=list(scratch),
        ),
        out_shape=out_shape,
        compiler_params=pltpu.CompilerParams(
            dimension_semantics=("arbitrary",) * len(grid), vmem_limit_bytes=vmem * MIB
        ),
        cost_estimate=pl.CostEstimate(flops=flops, bytes_accessed=moved, transcendentals=exps),
    )


def dot(a, b):
    return jnp.dot(a, b, preferred_element_type=jnp.float32)


def normalize(state, gain):
    meansq = jnp.mean(state * state, axis=-1, keepdims=True)
    return (state * lax.rsqrt(meansq + 1e-05) * gain).astype(jnp.bfloat16)


def store_blocks(kv_ref, key, value):
    for block in range(key.shape[0] // BLK):
        rows = slice(block * BLK, (block + 1) * BLK)
        kv_ref[block, 0] = key[rows].astype(jnp.bfloat16)
        kv_ref[block, 1] = value[rows].T.astype(jnp.bfloat16)


def first_body(state_ref, gain_ref, wk_ref, wv_ref, kv_ref, w_scr):
    @pl.when(pl.program_id(0) == 0)
    def _():
        w_scr[:, :HD] = wk_ref[...]
        w_scr[:, HD:] = wv_ref[...]

    both = dot(normalize(state_ref[...].astype(jnp.float32), gain_ref[...]), w_scr[...])
    store_blocks(kv_ref, both[:, :HD], both[:, HD:])


def first_projection(state, gain, w_key, w_value):
    rows, width = state.shape
    per_tile = TILE // BLK
    return call(
        first_body,
        (rows // TILE,),
        [
            pl.BlockSpec((TILE, width), lambda i: (i, 0)),
            pl.BlockSpec((1, width), lambda i: (0, 0)),
            pl.BlockSpec((width, HD), lambda i: (0, 0)),
            pl.BlockSpec((width, HD), lambda i: (0, 0)),
        ],
        pl.BlockSpec((per_tile, 2, BLK, HD), lambda i: (i, 0, 0, 0)),
        jax.ShapeDtypeStruct((rows // BLK, 2, BLK, HD), jnp.bfloat16),
        12,
        scratch=[pltpu.VMEM((width, 2 * HD), jnp.bfloat16)],
        flops=2 * rows * width * 2 * HD,
        moved=2 * rows * width,
    )(state, gain, w_key, w_value)


def rest_body(heads, state_ref, gain_ref, wq_ref, wk_ref, wv_ref, *outs):
    normed = normalize(state_ref[...].astype(jnp.float32), gain_ref[...])
    key = dot(normed, wk_ref[:, HD:])
    value = dot(normed, wv_ref[:, HD:])
    for head in range(1, heads):
        cols = slice((head - 1) * HD, head * HD)
        store_blocks(outs[head - 1], key[:, cols], value[:, cols])
    query = dot(normed, wq_ref[...])
    for block in range(TILE // BLK):
        for head in range(heads):
            part = query[block * BLK : (block + 1) * BLK, head * HD : (head + 1) * HD]
            outs[heads - 1][block, head] = part.T.astype(jnp.bfloat16)


def rest_projection(state, gain, w_query, w_key, w_value):
    rows, width = state.shape
    local = w_query.shape[1]
    heads = local // HD
    per_tile = TILE // BLK
    full = pl.BlockSpec((width, local), lambda i: (0, 0))
    blocks = pl.BlockSpec((per_tile, 2, BLK, HD), lambda i: (i, 0, 0, 0))
    return call(
        functools.partial(rest_body, heads),
        (rows // TILE,),
        [
            pl.BlockSpec((TILE, width), lambda i: (i, 0)),
            pl.BlockSpec((1, width), lambda i: (0, 0)),
            full,
            full,
            full,
        ],
        [blocks] * (heads - 1) + [pl.BlockSpec((per_tile, heads, HD, BLK), lambda i: (i, 0, 0, 0))],
        [jax.ShapeDtypeStruct((rows // BLK, 2, BLK, HD), jnp.bfloat16)] * (heads - 1)
        + [jax.ShapeDtypeStruct((rows // BLK, heads, HD, BLK), jnp.bfloat16)],
        16,
        flops=2 * rows * width * (3 * local - 2 * HD),
        moved=2 * rows * width + 6 * width * local,
    )(state, gain, w_query, w_key, w_value)


def same_token():
    return lax.broadcasted_iota(jnp.int32, (BLK, BLK), 0) == lax.broadcasted_iota(jnp.int32, (BLK, BLK), 1)


def past_body(frames, heads, newer, qt_ref, ck_ref, cv_ref, *rest):
    last, (acc_ref, stat_ref) = rest[:-2], rest[-2:]
    eye = same_token()
    skip = 1 if newer else 0
    for head in range(heads):
        cols = slice(head * HD, (head + 1) * HD)
        keys = [ck_ref[frame, :, cols] for frame in range(skip, frames)]
        if newer:
            keys = [last[head][0, 0]] + keys
        pairs = dot(jnp.concatenate(keys, axis=0), qt_ref[0, head])
        scores = [
            jnp.sum(jnp.where(eye, pairs[frame * BLK : (frame + 1) * BLK], 0.0), axis=0, keepdims=True)
            for frame in range(frames)
        ]
        top = functools.reduce(jnp.maximum, scores)
        weights = [jnp.exp2((score - top) * SCALE) for score in scores]
        stat_ref[0, head, 0:1] = top
        stat_ref[0, head, 1:2] = functools.reduce(jnp.add, weights)
        spread = jnp.concatenate([jnp.where(eye, weight, 0.0).astype(jnp.bfloat16) for weight in weights[skip:]], axis=1)
        mixed = dot(spread, jnp.concatenate([cv_ref[frame, :, cols] for frame in range(skip, frames)], axis=0)).T
        if newer:
            mixed = mixed + last[head][0, 1].astype(jnp.float32) * weights[0]
        acc_ref[0, head] = mixed


def attend_past(queries, cache_key, cache_value, last):
    blocks, heads = queries.shape[:2]
    frames, rows, local = cache_key.shape
    cached = pl.BlockSpec((frames, BLK, local), lambda i: (0, i, 0))
    return call(
        functools.partial(past_body, frames, heads, len(last) > 0),
        (blocks,),
        [pl.BlockSpec((1, heads, HD, BLK), lambda i: (i, 0, 0, 0)), cached, cached]
        + [pl.BlockSpec((1, 2, BLK, HD), lambda i: (i, 0, 0, 0))] * len(last),
        [
            pl.BlockSpec((1, heads, HD, BLK), lambda i: (i, 0, 0, 0)),
            pl.BlockSpec((1, heads, 2, BLK), lambda i: (i, 0, 0, 0)),
        ],
        [
            jax.ShapeDtypeStruct((blocks, heads, HD, BLK), jnp.float32),
            jax.ShapeDtypeStruct((blocks, heads, 2, BLK), jnp.float32),
        ],
        14,
        flops=4 * rows * frames * BLK * local,
        moved=4 * frames * rows * local,
    )(queries, cache_key, cache_value, *last)


def attend_body(blocks, slots, where_ref, counts_ref, qt_ref, acc_ref, stat_ref, *rest):
    own, left, right, far_left, far_right, out_ref, window, sem = rest
    half = blocks // 2
    place = 0
    copies = []
    for piece, length in ((far_left, half), (left, blocks), (own, blocks), (right, blocks), (far_right, half)):
        copies.append(pltpu.make_async_copy(piece, window.at[pl.ds(place, length)], sem.at[len(copies)]))
        place += length
    for copy in copies:
        copy.start()
    for copy in copies:
        copy.wait()
    for block in range(blocks):
        live = counts_ref[block]
        places = [where_ref[block * slots + slot] for slot in range(slots)]
        pairs = dot(jnp.concatenate([window[at, 0] for at in places], axis=0), qt_ref[block, 0])
        scores = [pairs[:BLK]]
        for slot in range(1, slots):
            score = pairs[slot * BLK : (slot + 1) * BLK]
            scores.append(jnp.where(slot < live, score, jnp.float32(-1e30)))
        past_top = stat_ref[block, 0, 0:1]
        top = jnp.maximum(functools.reduce(jnp.maximum, scores).max(axis=0, keepdims=True), past_top)
        weights = [jnp.exp2((score - top) * SCALE) for score in scores]
        fade = jnp.exp2((past_top - top) * SCALE)
        total = functools.reduce(jnp.add, weights).sum(axis=0, keepdims=True) + stat_ref[block, 0, 1:2] * fade
        share = 1.0 / total
        values = jnp.concatenate([window[at, 1] for at in places], axis=1)
        mixed = dot(values, jnp.concatenate([weight.astype(jnp.bfloat16) for weight in weights], axis=0))
        mixed = mixed * share + acc_ref[block, 0] * (fade * share)
        out_ref[block * BLK : (block + 1) * BLK] = mixed.T.astype(jnp.bfloat16)


def attend(head, where_block, counts, queries, past, stats, pieces):
    blocks = queries.shape[0]
    rows = blocks * BLK
    slots = where_block.shape[0] // blocks
    total_blocks = sum(piece.shape[0] for piece in pieces)
    return call(
        functools.partial(attend_body, blocks, slots),
        (1,),
        [
            pl.BlockSpec((blocks, 1, HD, BLK), lambda i, *_: (0, head, 0, 0)),
            pl.BlockSpec((blocks, 1, HD, BLK), lambda i, *_: (0, head, 0, 0)),
            pl.BlockSpec((blocks, 1, 2, BLK), lambda i, *_: (0, head, 0, 0)),
        ]
        + [pl.BlockSpec(memory_space=pl.ANY)] * len(pieces),
        pl.BlockSpec((rows, HD), lambda i, *_: (0, 0)),
        jax.ShapeDtypeStruct((rows, HD), jnp.bfloat16),
        12,
        scratch=[
            pltpu.VMEM((total_blocks, 2, BLK, HD), jnp.bfloat16),
            pltpu.SemaphoreType.DMA((len(pieces),)),
        ],
        prefetch=2,
        flops=4 * rows * slots * BLK * HD,
        moved=total_blocks * 4 * BLK * HD,
        exps=rows * slots * BLK,
    )(where_block, counts, queries, past, stats, *pieces)


def part_body(count, state_ref, w_ref, *rest):
    pieces, out_ref = rest[:count], rest[count]
    attended = jnp.concatenate([piece[...] for piece in pieces], axis=1)
    out_ref[...] = (state_ref[...].astype(jnp.float32) + dot(attended, w_ref[...])).astype(out_ref.dtype)


def add_heads(state, w_rows, pieces, out_dtype):
    rows, width = state.shape
    return call(
        functools.partial(part_body, len(pieces)),
        (rows // TILE,),
        [pl.BlockSpec((TILE, width), lambda i: (i, 0)), pl.BlockSpec(w_rows.shape, lambda i: (0, 0))]
        + [pl.BlockSpec((TILE, HD), lambda i: (i, 0))] * len(pieces),
        pl.BlockSpec((TILE, width), lambda i: (i, 0)),
        jax.ShapeDtypeStruct((rows, width), out_dtype),
        18,
        flops=2 * rows * width * w_rows.shape[0],
        moved=6 * rows * width + 2 * w_rows.size,
    )(state, w_rows, *pieces)


def turn_body(count, part_ref, w_ref, gain_ref, wk_ref, wv_ref, *rest):
    pieces, (state_ref, kv_ref, kv_scr) = rest[:count], rest[count:]

    @pl.when(pl.program_id(0) == 0)
    def _():
        kv_scr[:, :HD] = wk_ref[...]
        kv_scr[:, HD:] = wv_ref[...]

    attended = jnp.concatenate([piece[...] for piece in pieces], axis=1)
    state = (part_ref[...] + dot(attended, w_ref[...])).astype(jnp.bfloat16)
    state_ref[...] = state
    both = dot(normalize(state.astype(jnp.float32), gain_ref[...]), kv_scr[...])
    store_blocks(kv_ref, both[:, :HD], both[:, HD:])


def turn(part, w_rows, pieces, gain, w_key, w_value):
    rows, width = part.shape
    per_tile = TILE // BLK
    tile = pl.BlockSpec((TILE, width), lambda i: (i, 0))
    return call(
        functools.partial(turn_body, len(pieces)),
        (rows // TILE,),
        [
            tile,
            pl.BlockSpec(w_rows.shape, lambda i: (0, 0)),
            pl.BlockSpec((1, width), lambda i: (0, 0)),
            pl.BlockSpec((width, HD), lambda i: (0, 0)),
            pl.BlockSpec((width, HD), lambda i: (0, 0)),
        ]
        + [pl.BlockSpec((TILE, HD), lambda i: (i, 0))] * len(pieces),
        [tile, pl.BlockSpec((per_tile, 2, BLK, HD), lambda i: (i, 0, 0, 0))],
        [
            jax.ShapeDtypeStruct((rows, width), jnp.bfloat16),
            jax.ShapeDtypeStruct((rows // BLK, 2, BLK, HD), jnp.bfloat16),
        ],
        18,
        scratch=[pltpu.VMEM((width, 2 * HD), jnp.bfloat16)],
        flops=2 * rows * width * (w_rows.shape[0] + 2 * HD),
        moved=6 * rows * width + 2 * w_rows.size,
    )(part, w_rows, gain, w_key, w_value, *pieces)


def all_rows(w_out, start):
    count = lax.axis_size("space")
    half = count // 2
    local, width = w_out.shape
    heads = local // HD
    me = lax.axis_index("space")
    quarter = me % 2 + 2 * (me // half)
    own = w_out.reshape(heads, 4, HD // 4, width)
    mine = lax.dynamic_index_in_dim(own, quarter, 1, keepdims=False)
    fetched = jnp.stack(around(after(mine, start), "head")[1:])
    fours = [[2 * m, 2 * m + 1, half + 2 * m, half + 2 * m + 1] for m in range(half // 2)]
    others = lax.all_gather(fetched, "space", axis_index_groups=fours)
    others = others.transpose(1, 2, 0, 3, 4).reshape(-1, heads, HD, width)
    return jnp.concatenate([w_out.reshape(1, heads, HD, width), others])


def on_device(snapshot, norm_gain, w_query, w_key, w_value, w_out, cache_key, cache_value, pattern, counts):
    tok_rows, width = snapshot.shape
    blocks = tok_rows // BLK
    half = blocks // 2
    reach_blocks = blocks + half
    block_count_total = blocks * lax.axis_size("space")
    first_block = lax.axis_index("space") * blocks
    heads = w_query.shape[1] // HD
    own_block = jnp.arange(blocks, dtype=jnp.int32)[:, None]
    relative = (pattern - own_block - first_block + block_count_total // 2) % block_count_total
    where_block = (own_block + reach_blocks + relative - block_count_total // 2).reshape(-1)
    gain = norm_gain.reshape(1, width)
    state = snapshot
    kv_first = first_projection(state, gain, w_key, w_value)
    rows_of = all_rows(w_out, kv_first)
    w_early = rows_of[:, : heads - 1].reshape(-1, width)
    w_last = rows_of[:, heads - 1].reshape(-1, width)
    last = []
    for rollout in range(STEPS):
        *kv_rest, queries = rest_projection(state, gain, w_query, w_key, w_value)
        kv = [kv_first] + list(kv_rest)
        past, stats = attend_past(queries, cache_key, cache_value, last)
        near = []
        for head in range(heads):
            sent = kv[head] if head < 2 else after(kv[head], *near[head - 2])
            near.append((shifted(sent, "space", 1), shifted(sent, "space", -1)))
        came = []
        for head in range(heads):
            left, right = near[head]
            pieces = (kv[head], left, right, shifted(left[half:], "space", 1), shifted(right[:half], "space", -1))
            came.append(around(attend(head, where_block, counts, queries, past, stats, pieces), "head"))
        early = [piece for group in zip(*came[:-1], strict=True) for piece in group]
        part = add_heads(state, w_early, early, jnp.float32)
        if rollout + 1 < STEPS:
            state, kv_first = turn(part, w_last, came[-1], gain, w_key, w_value)
            last = kv
        else:
            state = add_heads(part, w_last, came[-1], jnp.bfloat16)
    return state


def solution(mesh):
    placed = (
        P("space", None),
        P(),
        P(None, "head"),
        P(None, "head"),
        P(None, "head"),
        P("head", None),
        P(None, "space", "head"),
        P(None, "space", "head"),
        P("space", None),
        P("space"),
    )
    return jax.shard_map(
        on_device, mesh=mesh, in_specs=placed, out_specs=P("space", None), check_vma=False
    )
```

time: 327 us -> 284 us (0.87)
  Pallas kernels: 109 us -> 78.3 us
  waiting for transfers between devices: 104 us -> 94 us
  starting transfers between devices: 70.7 us -> 65 us
  local copies, waits for them, and re-layouts: 26.5 us -> 30.5 us
    pallas_call x10 -> x12, Pallas kernels: 92.1 us -> 65.2 us  [the longest x6 23.6 us: attend(): call(functools.partial(attend_body, blocks, slots), (1,), [pl.BlockSpec((...]
    ppermute x24, waiting for transfers between devices: 53.6 us -> 37.9 us  [shifted(): return lax.ppermute(value, axis, pairs)]
    ppermute x21, starting transfers between devices: 51.5 us -> 42.9 us  [the longest x14 38.5 us: around(): ahead = lax.ppermute(ahead, axis, onward)]
    ppermute x21, waiting for transfers between devices: 50.7 us -> 56 us  [the longest x14 45.3 us: around(): ahead = lax.ppermute(ahead, axis, onward)]
    unnamed x80 -> x58, local copies, waits for them, and re-layouts: 19.4 us -> 18.5 us
  transfers between devices with their start and end apart: 46 -> 46, of which waited for: 31 -> 21; matrix products, arithmetic and copies ran while one was open for 2% -> 4% of each run, Pallas kernels for 29% -> 23%
where the time goes in v2:
time: 284 us; the launch traced here: 283 us
  waiting for transfers between devices  94 us (33%)
  Pallas kernels  78.3 us (28%)
  starting transfers between devices  65 us (23%)
  local copies, waits for them, and re-layouts  30.5 us (11%)
  between operations  13.9 us (5%)
    ppermute x14, waiting for transfers between devices, around(): ahead = lax.ppermute(ahead, axis, onward)  45.3 us
    ppermute x14, starting transfers between devices, around(): ahead = lax.ppermute(ahead, axis, onward)  38.5 us
    ppermute x24, waiting for transfers between devices, shifted(): return lax.ppermute(value, axis, pairs)  37.9 us
    pallas_call x6, Pallas kernels, attend(): call(functools.partial(attend_body, blocks, slots), (1,), [pl.BlockSpec((...  23.6 us
    ppermute x24, starting transfers between devices, shifted(): return lax.ppermute(value, axis, pairs)  22 us
    pallas_call x2, Pallas kernels, attend_past(): call(functools.partial(past_body, frames, heads, len(last) > 0), (blocks,...  21.7 us
    unnamed x58, local copies, waits for them, and re-layouts  18.5 us
    pallas_call x3, Pallas kernels, add_heads(): call(functools.partial(part_body, len(pieces)), (rows // TILE,), [pl.Bloc...  12.6 us
  transfers between devices with their start and end apart: 46, of which 21 were waited for; matrix products, arithmetic and copies ran while one was open for 4% of the time, Pallas kernels for 23%

profile of v2, /device:TPU:0, one launch (start us, length us, event | category | flops | bytes accessed | tf_op | source)
XLA Modules:
  0.0 283.2 jit_solution(5238510503497449342)
XLA Ops:
  8.2 1.9 copy-done.2
  10.1 1.3 copy-done.10
  12.7 2.7 shard_map.100.rest_0_
  16.2 4.0 %collective-permute-start = (bf16[3,32,1536]{2,1,0:T(8,128)(2,1)S(1)}, bf16[3,32,1536]{2,1,0:T(8,128)(2,1)S(1)}, u32[]{:S(2)}, u32[]{:S(2)}) collective-permute-start(bf16[3,32,1536]{2,1,0:T(8,128)(2,1)S(1)} %dynamic-slice_bitcast_fusion), channel_id=1, source_target_pairs={{0,2},{2,3},{3,1},{1,0},{4,6},{6,7},{7,5},{5,4},{8,10},{10,11},{11... | collective-permute-start | bytes 884744 | tf_op jit(solution)/shard_map/ppermute | solution.py:33
  20.2 7.5 %collective-permute-done = bf16[3,32,1536]{2,1,0:T(8,128)(2,1)S(1)} collective-permute-done((bf16[3,32,1536]{2,1,0:T(8,128)(2,1)S(1)}, bf16[3,32,1536]{2,1,0:T(8,128)(2,1)S(1)}, u32[]{:S(2)}, u32[]{:S(2)}) %collective-permute-start) | collective-permute-done | bytes 294944 | tf_op jit(solution)/shard_map/ppermute | solution.py:33
  27.7 3.4 %collective-permute-start.2 = (bf16[3,32,1536]{2,1,0:T(8,128)(2,1)S(1)}, bf16[3,32,1536]{2,1,0:T(8,128)(2,1)S(1)}, u32[]{:S(2)}, u32[]{:S(2)}) collective-permute-start(bf16[3,32,1536]{2,1,0:T(8,128)(2,1)S(1)} %collective-permute-done), channel_id=1, source_target_pairs={{0,2},{2,3},{3,1},{1,0},{4,6},{6,7},{7,5},{5,4},{8,10},{10,11},{11... | collective-permute-start | bytes 884744 | tf_op jit(solution)/shard_map/ppermute | solution.py:33
  31.1 4.7 %collective-permute-done.1 = bf16[3,32,1536]{2,1,0:T(8,128)(2,1)S(1)} collective-permute-done((bf16[3,32,1536]{2,1,0:T(8,128)(2,1)S(1)}, bf16[3,32,1536]{2,1,0:T(8,128)(2,1)S(1)}, u32[]{:S(2)}, u32[]{:S(2)}) %collective-permute-start.1) | collective-permute-done | bytes 294944 | tf_op jit(solution)/shard_map/ppermute | solution.py:36
  35.8 4.8 %collective-permute-done.2 = bf16[3,32,1536]{2,1,0:T(8,128)(2,1)S(1)} collective-permute-done((bf16[3,32,1536]{2,1,0:T(8,128)(2,1)S(1)}, bf16[3,32,1536]{2,1,0:T(8,128)(2,1)S(1)}, u32[]{:S(2)}, u32[]{:S(2)}) %collective-permute-start.2) | collective-permute-done | bytes 294944 | tf_op jit(solution)/shard_map/ppermute | solution.py:33
  41.6 1.6 collective-permute-start.4
  43.2 1.3 copy-done.11
  44.5 1.3 copy-done.14
  47.0 5.5 %shard_map.101 = (bf16[8,2,128,128]{3,2,1,0:T(8,128)(2,1)}, bf16[8,2,128,128]{3,2,1,0:T(8,128)(2,1)}, bf16[8,3,128,128]{3,2,1,0:T(8,128)(2,1)S(1)}) custom-call(bf16[1024,1536]{1,0:T(8,128)(2,1)S(1)} %copy-done.3, f32[1,1536]{1,0:T(1,128)S(1)} %reshape.25.gain_ref, bf16[1536,384]{1,0:T(8,128)(2,1)S(1)} %copy-done.21, bf16[1536,384]{1,0:T(8,128)(2,1)S(1)} %copy-done.11, ...), custom_call_target="tpu_custom_call" | custom-call | flops 2818572288 | bytes 6684672 | tf_op jit(solution)/shard_map/pallas_call | solution.py:131
  53.4 2.6 collective-permute-start.8
  57.6 2.6 collective-permute-start.6
  60.7 1.7 slice.58
  62.4 6.3 %collective-permute-done.8.rest_2_ = bf16[8,2,128,128]{3,2,1,0:T(8,128)(2,1)} collective-permute-done((bf16[8,2,128,128]{3,2,1,0:T(8,128)(2,1)}, bf16[8,2,128,128]{3,2,1,0:T(8,128)(2,1)}, u32[]{:S(2)}, u32[]{:S(2)}) %collective-permute-start.8) | collective-permute-done | bytes 524320 | tf_op jit(solution)/shard_map/ppermute | solution.py:22
  68.8 1.7 slice.61
  71.6 1.7 collective-permute-start.10
  73.2 1.7 slice.60
  75.1 2.8 copy-done
  77.9 2.8 copy-done.1
  81.8 8.5 %shard_map.102 = (f32[8,3,128,128]{3,2,1,0:T(8,128)S(1)}, f32[8,3,2,128]{3,2,1,0:T(2,128)S(1)}) custom-call(bf16[8,3,128,128]{3,2,1,0:T(8,128)(2,1)S(1)} %copy-done.5, bf16[8,1024,384]{2,1,0:T(8,128)(2,1)S(1)} %copy-done, bf16[8,1024,384]{2,1,0:T(8,128)(2,1)S(1)} %copy-done.1), custom_call_target="tpu_custom_call" | custom-call | flops 1610612736 | bytes 12582912 | tf_op jit(solution)/shard_map/pallas_call | solution.py:183
  91.3 4.1 %shard_map.103.rest_0_ = bf16[1024,128]{1,0:T(8,128)(2,1)S(1)} custom-call(s32[64]{0:T(128)S(1)} %reshape.28.where_ref, s32[8]{0:T(128)S(1)} %copy-done.20, bf16[8,3,128,128]{3,2,1,0:T(8,128)(2,1)S(1)} %copy-done.6, f32[8,3,128,128]{3,2,1,0:T(8,128)S(1)} %get-tuple-element.22.acc_ref, f32[8,3,2,128]{3,2,1,0:T(2,128)S(1)} %get-tuple-element.23.stat_ref, ...), custom_call_target="tpu_custom_call" | custom-call | flops 536870912 | bytes 2097152 | tf_op jit(solution)/shard_map/pallas_call | solution.py:239
  95.4 1.4 collective-permute-start.11
  96.8 5.1 %shard_map.104.rest_1_ = bf16[1024,128]{1,0:T(8,128)(2,1)} custom-call(s32[64]{0:T(128)S(1)} %reshape.28.where_ref, s32[8]{0:T(128)S(1)} %copy-done.20, bf16[8,3,128,128]{3,2,1,0:T(8,128)(2,1)S(1)} %copy-done.6, f32[8,3,128,128]{3,2,1,0:T(8,128)S(1)} %get-tuple-element.22.acc_ref, f32[8,3,2,128]{3,2,1,0:T(2,128)S(1)} %get-tuple-element.23.stat_ref, ...), custom_call_target="tpu_custom_call" | custom-call | flops 536870912 | bytes 2097152 | tf_op jit(solution)/shard_map/pallas_call | solution.py:239
  101.9 2.3 collective-permute-start.12
  105.2 2.1 collective-permute-start.20
  108.4 1.3 collective-permute-start.14
  110.4 3.4 %collective-permute-start.15 = (bf16[1024,128]{1,0:T(8,128)(2,1)}, bf16[1024,128]{1,0:T(8,128)(2,1)}, u32[]{:S(2)}, u32[]{:S(2)}) collective-permute-start(bf16[1024,128]{1,0:T(8,128)(2,1)} %collective-permute-done.11.rest_2_), channel_id=1, source_target_pairs={{0,2},{2,3},{3,1},{1,0},{4,6},{6,7},{7,5},{5,4},{8,10},{10,11},{11... | collective-permute-start | bytes 786440 | tf_op jit(solution)/shard_map/ppermute | solution.py:33
  115.0 5.1 %shard_map.106.rest_0_ = bf16[1024,128]{1,0:T(8,128)(2,1)} custom-call(s32[64]{0:T(128)S(1)} %reshape.28.where_ref, s32[8]{0:T(128)S(1)} %copy-done.20, bf16[8,3,128,128]{3,2,1,0:T(8,128)(2,1)S(1)} %copy-done.6, f32[8,3,128,128]{3,2,1,0:T(8,128)S(1)} %get-tuple-element.22.acc_ref, f32[8,3,2,128]{3,2,1,0:T(2,128)S(1)} %get-tuple-element.23.stat_ref, ...), custom_call_target="tpu_custom_call" | custom-call | flops 536870912 | bytes 2097152 | tf_op jit(solution)/shard_map/pallas_call | solution.py:239
  120.5 2.5 copy.19
  123.3 1.8 collective-permute-start.22
  125.1 14.8 %collective-permute-done.21.rest_1_ = bf16[1024,128]{1,0:T(8,128)(2,1)} collective-permute-done((bf16[1024,128]{1,0:T(8,128)(2,1)}, bf16[1024,128]{1,0:T(8,128)(2,1)}, u32[]{:S(2)}, u32[]{:S(2)}) %collective-permute-start.21) | collective-permute-done | bytes 262176 | tf_op jit(solution)/shard_map/ppermute | solution.py:33
  139.9 2.0 collective-permute-start.23
  141.9 5.2 %shard_map.105.part_ref = f32[1024,1536]{1,0:T(8,128)S(1)} custom-call(bf16[1024,1536]{1,0:T(8,128)(2,1)S(1)} %copy-done.3, bf16[1024,1536]{1,0:T(8,128)(2,1)S(1)} %bitcast.15, bf16[1024,128]{1,0:T(8,128)(2,1)S(1)} %shard_map.103.rest_0_, bf16[1024,128]{1,0:T(8,128)(2,1)} %shard_map.104.rest_1_, bf16[1024,128]{1,0:T(8,128)(2,1)} %collective-permute-done.11.rest_2_, ...), custom_call_target="tpu_custom_call" | custom-call | flops 3221225472 | bytes 12582912 | tf_op jit(solution)/shard_map/pallas_call | solution.py:270
  147.3 3.5 %collective-permute-done.22.rest_2_ = bf16[1024,128]{1,0:T(8,128)(2,1)S(1)} collective-permute-done((bf16[1024,128]{1,0:T(8,128)(2,1)}, bf16[1024,128]{1,0:T(8,128)(2,1)S(1)}, u32[]{:S(2)}, u32[]{:S(2)}) %collective-permute-start.22) | collective-permute-done | bytes 262176 | tf_op jit(solution)/shard_map/ppermute | solution.py:36
  150.8 7.2 %shard_map.107 = (bf16[1024,1536]{1,0:T(8,128)(2,1)S(1)}, bf16[8,2,128,128]{3,2,1,0:T(8,128)(2,1)S(1)}) custom-call(f32[1024,1536]{1,0:T(8,128)S(1)} %shard_map.105.part_ref, bf16[512,1536]{1,0:T(8,128)(2,1)S(1)} %bitcast.21, f32[1,1536]{1,0:T(1,128)S(1)} %reshape.25.gain_ref, bf16[1536,384]{1,0:T(8,128)(2,1)S(1)} %copy-done.12, ...), custom_call_target="tpu_custom_call" | custom-call | flops 2415919104 | bytes 11010048 | tf_op jit(solution)/shard_map/pallas_call | solution.py:302
  158.0 2.4 collective-permute-start.25
  160.4 4.9 %shard_map.108 = (bf16[8,2,128,128]{3,2,1,0:T(8,128)(2,1)S(1)}, bf16[8,2,128,128]{3,2,1,0:T(8,128)(2,1)S(1)}, bf16[8,3,128,128]{3,2,1,0:T(8,128)(2,1)S(1)}) custom-call(bf16[1024,1536]{1,0:T(8,128)(2,1)S(1)} %get-tuple-element.27.state_ref, f32[1,1536]{1,0:T(1,128)S(1)} %reshape.25.gain_ref, bf16[1536,384]{1,0:T(8,128)(2,1)S(1)} %copy-done.22, ...), custom_call_target="tpu_custom_call" | custom-call | flops 2818572288 | bytes 6684672 | tf_op jit(solution)/shard_map/pallas_call | solution.py:131
  165.3 2.7 collective-permute-start.29
  168.0 4.7 %collective-permute-done.25.rest_2_ = bf16[8,2,128,128]{3,2,1,0:T(8,128)(2,1)S(1)} collective-permute-done((bf16[8,2,128,128]{3,2,1,0:T(8,128)(2,1)S(1)}, bf16[8,2,128,128]{3,2,1,0:T(8,128)(2,1)S(1)}, u32[]{:S(2)}, u32[]{:S(2)}) %collective-permute-start.25) | collective-permute-done | bytes 524320 | tf_op jit(solution)/shard_map/ppermute | solution.py:22
  172.7 2.8 %collective-permute-done.24.rest_1_ = bf16[8,2,128,128]{3,2,1,0:T(8,128)(2,1)S(1)} collective-permute-done((bf16[8,2,128,128]{3,2,1,0:T(8,128)(2,1)S(1)}, bf16[8,2,128,128]{3,2,1,0:T(8,128)(2,1)S(1)}, u32[]{:S(2)}, u32[]{:S(2)}) %collective-permute-start.24) | collective-permute-done | bytes 524320 | tf_op jit(solution)/shard_map/ppermute | solution.py:22
  176.1 2.2 collective-permute-start.27
  178.3 5.6 %collective-permute-done.29.rest_2_ = bf16[8,2,128,128]{3,2,1,0:T(8,128)(2,1)S(1)} collective-permute-done((bf16[8,2,128,128]{3,2,1,0:T(8,128)(2,1)S(1)}, bf16[8,2,128,128]{3,2,1,0:T(8,128)(2,1)S(1)}, u32[]{:S(2)}, u32[]{:S(2)}) %collective-permute-start.29) | collective-permute-done | bytes 524320 | tf_op jit(solution)/shard_map/ppermute | solution.py:22
  184.0 2.8 collective-permute-done.28.rest_1_
  186.9 13.2 %collective-permute-done.27.rest_4_ = bf16[4,2,128,128]{3,2,1,0:T(8,128)(2,1)S(1)} collective-permute-done((bf16[4,2,128,128]{3,2,1,0:T(8,128)(2,1)S(1)}, bf16[4,2,128,128]{3,2,1,0:T(8,128)(2,1)S(1)}, u32[]{:S(2)}, u32[]{:S(2)}) %collective-permute-start.27) | collective-permute-done | bytes 262176 | tf_op jit(solution)/shard_map/ppermute | solution.py:22
  200.1 13.3 %shard_map.109 = (f32[8,3,128,128]{3,2,1,0:T(8,128)S(1)}, f32[8,3,2,128]{3,2,1,0:T(2,128)S(1)}) custom-call(bf16[8,3,128,128]{3,2,1,0:T(8,128)(2,1)S(1)} %get-tuple-element.28.qt_ref, bf16[8,1024,384]{2,1,0:T(8,128)(2,1)S(1)} %bitcast.18, bf16[8,1024,384]{2,1,0:T(8,128)(2,1)S(1)} %bitcast.20, bf16[8,2,128,128]{3,2,1,0:T(8,128)(2,1)S(1)} %copy-done.9, ...), custom_call_target="tpu_custom_call" | custom-call | flops 1610612736 | bytes 12582912 | tf_op jit(solution)/shard_map/pallas_call | solution.py:183
  213.4 3.1 %shard_map.110.rest_0_ = bf16[1024,128]{1,0:T(8,128)(2,1)S(1)} custom-call(s32[64]{0:T(128)S(1)} %reshape.28.where_ref, s32[8]{0:T(128)S(1)} %copy-done.20, bf16[8,3,128,128]{3,2,1,0:T(8,128)(2,1)S(1)} %get-tuple-element.28.qt_ref, f32[8,3,128,128]{3,2,1,0:T(8,128)S(1)} %get-tuple-element.29.acc_ref, f32[8,3,2,128]{3,2,1,0:T(2,128)S(1)} %get-tuple-element.30.stat_ref, ...), custom_call_target="tpu_custom_call" | custom-call | flops 536870912 | bytes 2097152 | tf_op jit(solution)/shard_map/pallas_call | solution.py:239
  216.6 2.9 %collective-permute-start.41 = (bf16[4,2,128,128]{3,2,1,0:T(8,128)(2,1)S(1)}, bf16[4,2,128,128]{3,2,1,0:T(8,128)(2,1)S(1)}, u32[]{:S(2)}, u32[]{:S(2)}) collective-permute-start(bf16[4,2,128,128]{3,2,1,0:T(8,128)(2,1)S(1)} %slice.69), channel_id=1, source_target_pairs={{0,28},{4,0},{8,4},{12,8},{16,12},{20,16},{24,20},{28,24},{1,29},{... | collective-permute-start | bytes 786440 | tf_op jit(solution)/shard_map/ppermute | solution.py:22
  219.6 2.0 collective-permute-start.32
  221.6 3.1 %shard_map.111.rest_1_ = bf16[1024,128]{1,0:T(8,128)(2,1)S(1)} custom-call(s32[64]{0:T(128)S(1)} %reshape.28.where_ref, s32[8]{0:T(128)S(1)} %copy-done.20, bf16[8,3,128,128]{3,2,1,0:T(8,128)(2,1)S(1)} %get-tuple-element.28.qt_ref, f32[8,3,128,128]{3,2,1,0:T(8,128)S(1)} %get-tuple-element.29.acc_ref, f32[8,3,2,128]{3,2,1,0:T(2,128)S(1)} %get-tuple-element.30.stat_ref, ...), custom_call_target="tpu_custom_call" | custom-call | flops 536870912 | bytes 2097152 | tf_op jit(solution)/shard_map/pallas_call | solution.py:239
  224.7 2.0 collective-permute-start.33
  228.0 3.1 %shard_map.113.rest_0_ = bf16[1024,128]{1,0:T(8,128)(2,1)S(1)} custom-call(s32[64]{0:T(128)S(1)} %reshape.28.where_ref, s32[8]{0:T(128)S(1)} %copy-done.20, bf16[8,3,128,128]{3,2,1,0:T(8,128)(2,1)S(1)} %get-tuple-element.28.qt_ref, f32[8,3,128,128]{3,2,1,0:T(8,128)S(1)} %get-tuple-element.29.acc_ref, f32[8,3,2,128]{3,2,1,0:T(2,128)S(1)} %get-tuple-element.30.stat_ref, ...), custom_call_target="tpu_custom_call" | custom-call | flops 536870912 | bytes 2097152 | tf_op jit(solution)/shard_map/pallas_call | solution.py:239
  231.1 1.8 collective-permute-start.42
  232.9 1.9 collective-permute-start.36
  235.0 11.6 %collective-permute-start.37 = (bf16[1024,128]{1,0:T(8,128)(2,1)S(1)}, bf16[1024,128]{1,0:T(8,128)(2,1)S(1)}, u32[]{:S(2)}, u32[]{:S(2)}) collective-permute-start(bf16[1024,128]{1,0:T(8,128)(2,1)S(1)} %collective-permute-done.33.rest_3_), channel_id=1, source_target_pairs={{0,2},{2,3},{3,1},{1,0},{4,6},{6,7},{7,5},{5,4},{8,10},{10,11},{11... | collective-permute-start | bytes 786440 | tf_op jit(solution)/shard_map/ppermute | solution.py:33
  246.6 4.9 %collective-permute-done.42.rest_1_ = bf16[1024,128]{1,0:T(8,128)(2,1)S(1)} collective-permute-done((bf16[1024,128]{1,0:T(8,128)(2,1)S(1)}, bf16[1024,128]{1,0:T(8,128)(2,1)S(1)}, u32[]{:S(2)}, u32[]{:S(2)}) %collective-permute-start.42) | collective-permute-done | bytes 262176 | tf_op jit(solution)/shard_map/ppermute | solution.py:33
  251.5 2.3 collective-permute-start.44
  253.8 3.3 %collective-permute-done.36.rest_6_ = bf16[1024,128]{1,0:T(8,128)(2,1)S(1)} collective-permute-done((bf16[1024,128]{1,0:T(8,128)(2,1)S(1)}, bf16[1024,128]{1,0:T(8,128)(2,1)S(1)}, u32[]{:S(2)}, u32[]{:S(2)}) %collective-permute-start.36) | collective-permute-done | bytes 262176 | tf_op jit(solution)/shard_map/ppermute | solution.py:33
  257.1 5.9 %collective-permute-done.37.rest_7_ = bf16[1024,128]{1,0:T(8,128)(2,1)S(1)} collective-permute-done((bf16[1024,128]{1,0:T(8,128)(2,1)S(1)}, bf16[1024,128]{1,0:T(8,128)(2,1)S(1)}, u32[]{:S(2)}, u32[]{:S(2)}) %collective-permute-start.37) | collective-permute-done | bytes 262176 | tf_op jit(solution)/shard_map/ppermute | solution.py:33
  263.0 3.9 %shard_map.112.state_ref = f32[1024,1536]{1,0:T(8,128)S(1)} custom-call(bf16[1024,1536]{1,0:T(8,128)(2,1)S(1)} %get-tuple-element.27.state_ref, bf16[1024,1536]{1,0:T(8,128)(2,1)S(1)} %bitcast.16, bf16[1024,128]{1,0:T(8,128)(2,1)S(1)} %shard_map.110.rest_0_, bf16[1024,128]{1,0:T(8,128)(2,1)S(1)} %shard_map.111.rest_1_, ...), custom_call_target="tpu_custom_call" | custom-call | flops 3221225472 | bytes 12582912 | tf_op jit(solution)/shard_map/pallas_call | solution.py:270
  267.0 2.5 collective-permute-done.43.rest_2_
  269.5 3.3 %collective-permute-done.44.rest_3_ = bf16[1024,128]{1,0:T(8,128)(2,1)S(1)} collective-permute-done((bf16[1024,128]{1,0:T(8,128)(2,1)S(1)}, bf16[1024,128]{1,0:T(8,128)(2,1)S(1)}, u32[]{:S(2)}, u32[]{:S(2)}) %collective-permute-start.44) | collective-permute-done | bytes 262176 | tf_op jit(solution)/shard_map/ppermute | solution.py:33
  272.8 3.5 %shard_map.114 = bf16[1024,1536]{1,0:T(8,128)(2,1)} custom-call(f32[1024,1536]{1,0:T(8,128)S(1)} %shard_map.112.state_ref, bf16[512,1536]{1,0:T(8,128)(2,1)S(1)} %bitcast.22, bf16[1024,128]{1,0:T(8,128)(2,1)S(1)} %shard_map.113.rest_0_, bf16[1024,128]{1,0:T(8,128)(2,1)S(1)} %collective-permute-done.42.rest_1_, ...), custom_call_target="tpu_custom_call" | custom-call | flops 1610612736 | bytes 11010048 | tf_op jit(solution)/shard_map/pallas_call | solution.py:270
  (125 shorter events, 19.5 us)
Async XLA Ops:
  6.5 113.9 %all-gather.3.cloned.1.call-start = ((), (), s32[]{:S(2)}) async-start(), calls=%async_computation | async-start | bytes 4423680 | tf_op jit(solution)/shard_map/all_gather | solution.py:336
  12.7 30.6 %copy-start.3 = (bf16[1024,1536]{1,0:T(8,128)(2,1)S(1)}, bf16[1024,1536]{1,0:T(8,128)(2,1)}, u32[]{:S(2)}) copy-start(bf16[1024,1536]{1,0:T(8,128)(2,1)} %state_ref.5) | copy-start | bytes 9437188
  16.2 11.5 %collective-permute-start = (bf16[3,32,1536]{2,1,0:T(8,128)(2,1)S(1)}, bf16[3,32,1536]{2,1,0:T(8,128)(2,1)S(1)}, u32[]{:S(2)}, u32[]{:S(2)}) collective-permute-start(bf16[3,32,1536]{2,1,0:T(8,128)(2,1)S(1)} %dynamic-slice_bitcast_fusion), channel_id=1, source_target_pairs={{0,2},{2,3},{3,1},{1,0},{4,6},{6,7},{7,5},{5,4},{8,10},{10,11},{11... | collective-permute-start | bytes 884744 | tf_op jit(solution)/shard_map/ppermute | solution.py:33
  20.2 15.6 %collective-permute-start.1 = (bf16[3,32,1536]{2,1,0:T(8,128)(2,1)S(1)}, bf16[3,32,1536]{2,1,0:T(8,128)(2,1)S(1)}, u32[]{:S(2)}, u32[]{:S(2)}) collective-permute-start(bf16[3,32,1536]{2,1,0:T(8,128)(2,1)S(1)} %dynamic-slice_bitcast_fusion), channel_id=1, source_target_pairs={{2,0},{3,2},{1,3},{0,1},{6,4},{7,6},{5,7},{4,5},{10,8},{11,10},{9,... | collective-permute-start | bytes 884744 | tf_op jit(solution)/shard_map/ppermute | solution.py:36
  27.7 12.9 %collective-permute-start.2 = (bf16[3,32,1536]{2,1,0:T(8,128)(2,1)S(1)}, bf16[3,32,1536]{2,1,0:T(8,128)(2,1)S(1)}, u32[]{:S(2)}, u32[]{:S(2)}) collective-permute-start(bf16[3,32,1536]{2,1,0:T(8,128)(2,1)S(1)} %collective-permute-done), channel_id=1, source_target_pairs={{0,2},{2,3},{3,1},{1,0},{4,6},{6,7},{7,5},{5,4},{8,10},{10,11},{11... | collective-permute-start | bytes 884744 | tf_op jit(solution)/shard_map/ppermute | solution.py:33
  41.6 33.4 %copy-start.24 = (s32[8,8]{1,0:T(8,128)S(1)}, s32[8,8]{1,0:T(8,128)}, u32[]{:S(2)}) copy-start(s32[8,8]{1,0:T(8,128)} %param.18) | copy-start | bytes 772
  41.6 14.5 %collective-permute-start.4 = (bf16[8,2,128,128]{3,2,1,0:T(8,128)(2,1)}, bf16[8,2,128,128]{3,2,1,0:T(8,128)(2,1)S(1)}, u32[]{:S(2)}, u32[]{:S(2)}) collective-permute-start(bf16[8,2,128,128]{3,2,1,0:T(8,128)(2,1)} %copy-done.7), channel_id=1, source_target_pairs={{0,28},{4,0},{8,4},{12,8},{16,12},{20,16},{24,20},{28,24},{1,29},{... | collective-permute-start | bytes 1572872 | tf_op jit(solution)/shard_map/ppermute | solution.py:22
  43.2 17.0 %collective-permute-start.3 = (bf16[8,2,128,128]{3,2,1,0:T(8,128)(2,1)}, bf16[8,2,128,128]{3,2,1,0:T(8,128)(2,1)}, u32[]{:S(2)}, u32[]{:S(2)}) collective-permute-start(bf16[8,2,128,128]{3,2,1,0:T(8,128)(2,1)} %copy-done.7), channel_id=1, source_target_pairs={{0,4},{4,8},{8,12},{12,16},{16,20},{20,24},{24,28},{28,0},{1,5},{5... | collective-permute-start | bytes 1572872 | tf_op jit(solution)/shard_map/ppermute | solution.py:22
  53.4 15.3 %collective-permute-start.8 = (bf16[8,2,128,128]{3,2,1,0:T(8,128)(2,1)}, bf16[8,2,128,128]{3,2,1,0:T(8,128)(2,1)}, u32[]{:S(2)}, u32[]{:S(2)}) collective-permute-start(bf16[8,2,128,128]{3,2,1,0:T(8,128)(2,1)} %get-tuple-element.24.rest_0_.rest_1_), channel_id=1, source_target_pairs={{0,28},{4,0},{8,4},{12,8},{16,12},{20,16},{24,20},{28,24},{1,29},{... | collective-permute-start | bytes 1572872 | tf_op jit(solution)/shard_map/ppermute | solution.py:22
  56.1 15.5 %collective-permute-start.7 = (bf16[8,2,128,128]{3,2,1,0:T(8,128)(2,1)}, bf16[8,2,128,128]{3,2,1,0:T(8,128)(2,1)}, u32[]{:S(2)}, u32[]{:S(2)}) collective-permute-start(bf16[8,2,128,128]{3,2,1,0:T(8,128)(2,1)} %get-tuple-element.24.rest_0_.rest_1_), channel_id=1, source_target_pairs={{0,4},{4,8},{8,12},{12,16},{16,20},{20,24},{24,28},{28,0},{1,5},{5... | collective-permute-start | bytes 1572872 | tf_op jit(solution)/shard_map/ppermute | solution.py:22
  57.6 17.3 %collective-permute-start.6 = (bf16[4,2,128,128]{3,2,1,0:T(8,128)(2,1)}, bf16[4,2,128,128]{3,2,1,0:T(8,128)(2,1)S(1)}, u32[]{:S(2)}, u32[]{:S(2)}) collective-permute-start(bf16[4,2,128,128]{3,2,1,0:T(8,128)(2,1)} %slice.59), channel_id=1, source_target_pairs={{0,28},{4,0},{8,4},{12,8},{16,12},{20,16},{24,20},{28,24},{1,29},{... | collective-permute-start | bytes 786440 | tf_op jit(solution)/shard_map/ppermute | solution.py:22
  60.2 44.0 %collective-permute-start.18 = (bf16[8,2,128,128]{3,2,1,0:T(8,128)(2,1)}, bf16[8,2,128,128]{3,2,1,0:T(8,128)(2,1)}, u32[]{:S(2)}, u32[]{:S(2)}) collective-permute-start(bf16[8,2,128,128]{3,2,1,0:T(8,128)(2,1)} %get-tuple-element.26.rest_0_.rest_2_), channel_id=1, source_target_pairs={{0,28},{4,0},{8,4},{12,8},{16,12},{20,16},{24,20},{28,24},{1,29},{... | collective-permute-start | bytes 1572872 | tf_op jit(solution)/shard_map/ppermute | solution.py:22
  60.3 47.0 %collective-permute-start.17 = (bf16[8,2,128,128]{3,2,1,0:T(8,128)(2,1)}, bf16[8,2,128,128]{3,2,1,0:T(8,128)(2,1)}, u32[]{:S(2)}, u32[]{:S(2)}) collective-permute-start(bf16[8,2,128,128]{3,2,1,0:T(8,128)(2,1)} %get-tuple-element.26.rest_0_.rest_2_), channel_id=1, source_target_pairs={{0,4},{4,8},{8,12},{12,16},{16,20},{20,24},{24,28},{28,0},{1,5},{5... | collective-permute-start | bytes 1572872 | tf_op jit(solution)/shard_map/ppermute | solution.py:22
  68.7 21.6 %collective-permute-start.5 = (bf16[4,2,128,128]{3,2,1,0:T(8,128)(2,1)}, bf16[4,2,128,128]{3,2,1,0:T(8,128)(2,1)}, u32[]{:S(2)}, u32[]{:S(2)}) collective-permute-start(bf16[4,2,128,128]{3,2,1,0:T(8,128)(2,1)} %slice.58), channel_id=1, source_target_pairs={{0,4},{4,8},{8,12},{12,16},{16,20},{20,24},{24,28},{28,0},{1,5},{5... | collective-permute-start | bytes 786440 | tf_op jit(solution)/shard_map/ppermute | solution.py:22
  71.6 25.2 %collective-permute-start.10 = (bf16[4,2,128,128]{3,2,1,0:T(8,128)(2,1)}, bf16[4,2,128,128]{3,2,1,0:T(8,128)(2,1)}, u32[]{:S(2)}, u32[]{:S(2)}) collective-permute-start(bf16[4,2,128,128]{3,2,1,0:T(8,128)(2,1)} %slice.61), channel_id=1, source_target_pairs={{0,28},{4,0},{8,4},{12,8},{16,12},{20,16},{24,20},{28,24},{1,29},{... | collective-permute-start | bytes 786440 | tf_op jit(solution)/shard_map/ppermute | solution.py:22
  74.9 15.4 %copy-start.18 = (bf16[4,2,128,128]{3,2,1,0:T(8,128)(2,1)}, bf16[4,2,128,128]{3,2,1,0:T(8,128)(2,1)S(1)}, u32[]{:S(2)}) copy-start(bf16[4,2,128,128]{3,2,1,0:T(8,128)(2,1)S(1)} %collective-permute-done.6.rest_4_) | copy-start | bytes 786436
  74.9 21.9 %collective-permute-start.9 = (bf16[4,2,128,128]{3,2,1,0:T(8,128)(2,1)}, bf16[4,2,128,128]{3,2,1,0:T(8,128)(2,1)}, u32[]{:S(2)}, u32[]{:S(2)}) collective-permute-start(bf16[4,2,128,128]{3,2,1,0:T(8,128)(2,1)} %slice.60), channel_id=1, source_target_pairs={{0,4},{4,8},{8,12},{12,16},{16,20},{20,24},{24,28},{28,0},{1,5},{5... | collective-permute-start | bytes 786440 | tf_op jit(solution)/shard_map/ppermute | solution.py:22
  75.1 2.8 copy-start
  77.9 2.8 copy-start.1
  81.8 8.5 %copy-start.6 = (bf16[8,3,128,128]{3,2,1,0:T(8,128)(2,1)S(1)}, bf16[8,3,128,128]{3,2,1,0:T(8,128)(2,1)}, u32[]{:S(2)}) copy-start(bf16[8,3,128,128]{3,2,1,0:T(8,128)(2,1)} %copy-done.4) | copy-start | bytes 2359300
  81.8 8.5 %copy-start.8 = (bf16[8,2,128,128]{3,2,1,0:T(8,128)(2,1)S(1)}, bf16[8,2,128,128]{3,2,1,0:T(8,128)(2,1)}, u32[]{:S(2)}) copy-start(bf16[8,2,128,128]{3,2,1,0:T(8,128)(2,1)} %copy-done.7) | copy-start | bytes 1572868
  81.8 8.5 %copy-start.17 = (bf16[8,2,128,128]{3,2,1,0:T(8,128)(2,1)S(1)}, bf16[8,2,128,128]{3,2,1,0:T(8,128)(2,1)}, u32[]{:S(2)}) copy-start(bf16[8,2,128,128]{3,2,1,0:T(8,128)(2,1)} %copy-done.16) | copy-start | bytes 1572868
  81.8 8.5 %copy-start.20 = (s32[8]{0:T(128)S(1)}, s32[8]{0:T(128)}, u32[]{:S(2)}) copy-start(s32[8]{0:T(128)} %counts_ref.11) | copy-start | bytes 100
  95.4 13.0 %collective-permute-start.11 = (bf16[1024,128]{1,0:T(8,128)(2,1)S(1)}, bf16[1024,128]{1,0:T(8,128)(2,1)}, u32[]{:S(2)}, u32[]{:S(2)}) collective-permute-start(bf16[1024,128]{1,0:T(8,128)(2,1)S(1)} %shard_map.103.rest_0_), channel_id=1, source_target_pairs={{0,2},{2,3},{3,1},{1,0},{4,6},{6,7},{7,5},{5,4},{8,10},{10,11},{11... | collective-permute-start | bytes 786440 | tf_op jit(solution)/shard_map/ppermute | solution.py:33
  101.9 8.5 %collective-permute-start.12 = (bf16[1024,128]{1,0:T(8,128)(2,1)}, bf16[1024,128]{1,0:T(8,128)(2,1)}, u32[]{:S(2)}, u32[]{:S(2)}) collective-permute-start(bf16[1024,128]{1,0:T(8,128)(2,1)} %shard_map.104.rest_1_), channel_id=1, source_target_pairs={{0,2},{2,3},{3,1},{1,0},{4,6},{6,7},{7,5},{5,4},{8,10},{10,11},{11... | collective-permute-start | bytes 786440 | tf_op jit(solution)/shard_map/ppermute | solution.py:33
  105.2 8.7 %collective-permute-start.20 = (bf16[4,2,128,128]{3,2,1,0:T(8,128)(2,1)S(1)}, bf16[4,2,128,128]{3,2,1,0:T(8,128)(2,1)S(1)}, u32[]{:S(2)}, u32[]{:S(2)}) collective-permute-start(bf16[4,2,128,128]{3,2,1,0:T(8,128)(2,1)S(1)} %slice.63), channel_id=1, source_target_pairs={{0,28},{4,0},{8,4},{12,8},{16,12},{20,16},{24,20},{28,24},{1,29},{... | collective-permute-start | bytes 786440 | tf_op jit(solution)/shard_map/ppermute | solution.py:22
  108.3 6.7 %collective-permute-start.19 = (bf16[4,2,128,128]{3,2,1,0:T(8,128)(2,1)S(1)}, bf16[4,2,128,128]{3,2,1,0:T(8,128)(2,1)S(1)}, u32[]{:S(2)}, u32[]{:S(2)}) collective-permute-start(bf16[4,2,128,128]{3,2,1,0:T(8,128)(2,1)S(1)} %slice.62), channel_id=1, source_target_pairs={{0,4},{4,8},{8,12},{12,16},{16,20},{20,24},{24,28},{28,0},{1,5},{5... | collective-permute-start | bytes 786440 | tf_op jit(solution)/shard_map/ppermute | solution.py:22
  108.3 15.0 %collective-permute-start.13 = (bf16[1024,128]{1,0:T(8,128)(2,1)S(1)}, bf16[1024,128]{1,0:T(8,128)(2,1)}, u32[]{:S(2)}, u32[]{:S(2)}) collective-permute-start(bf16[1024,128]{1,0:T(8,128)(2,1)S(1)} %shard_map.103.rest_0_), channel_id=1, source_target_pairs={{2,0},{3,2},{1,3},{0,1},{6,4},{7,6},{5,7},{4,5},{10,8},{11,10},{9,... | collective-permute-start | bytes 786440 | tf_op jit(solution)/shard_map/ppermute | solution.py:36
  108.4 33.5 %collective-permute-start.14 = (bf16[1024,128]{1,0:T(8,128)(2,1)}, bf16[1024,128]{1,0:T(8,128)(2,1)}, u32[]{:S(2)}, u32[]{:S(2)}) collective-permute-start(bf16[1024,128]{1,0:T(8,128)(2,1)} %shard_map.104.rest_1_), channel_id=1, source_target_pairs={{2,0},{3,2},{1,3},{0,1},{6,4},{7,6},{5,7},{4,5},{10,8},{11,10},{9,... | collective-permute-start | bytes 786440 | tf_op jit(solution)/shard_map/ppermute | solution.py:36
  110.4 31.5 %collective-permute-start.15 = (bf16[1024,128]{1,0:T(8,128)(2,1)}, bf16[1024,128]{1,0:T(8,128)(2,1)}, u32[]{:S(2)}, u32[]{:S(2)}) collective-permute-start(bf16[1024,128]{1,0:T(8,128)(2,1)} %collective-permute-done.11.rest_2_), channel_id=1, source_target_pairs={{0,2},{2,3},{3,1},{1,0},{4,6},{6,7},{7,5},{5,4},{8,10},{10,11},{11... | collective-permute-start | bytes 786440 | tf_op jit(solution)/shard_map/ppermute | solution.py:33
  113.9 28.0 %collective-permute-start.16 = (bf16[1024,128]{1,0:T(8,128)(2,1)}, bf16[1024,128]{1,0:T(8,128)(2,1)}, u32[]{:S(2)}, u32[]{:S(2)}) collective-permute-start(bf16[1024,128]{1,0:T(8,128)(2,1)} %collective-permute-done.12.rest_3_), channel_id=1, source_target_pairs={{0,2},{2,3},{3,1},{1,0},{4,6},{6,7},{7,5},{5,4},{8,10},{10,11},{11... | collective-permute-start | bytes 786440 | tf_op jit(solution)/shard_map/ppermute | solution.py:33
  120.1 19.8 %collective-permute-start.21 = (bf16[1024,128]{1,0:T(8,128)(2,1)}, bf16[1024,128]{1,0:T(8,128)(2,1)}, u32[]{:S(2)}, u32[]{:S(2)}) collective-permute-start(bf16[1024,128]{1,0:T(8,128)(2,1)} %shard_map.106.rest_0_), channel_id=1, source_target_pairs={{0,2},{2,3},{3,1},{1,0},{4,6},{6,7},{7,5},{5,4},{8,10},{10,11},{11... | collective-permute-start | bytes 786440 | tf_op jit(solution)/shard_map/ppermute | solution.py:33
  120.5 2.5 copy-start.23
  123.3 27.4 %collective-permute-start.22 = (bf16[1024,128]{1,0:T(8,128)(2,1)}, bf16[1024,128]{1,0:T(8,128)(2,1)S(1)}, u32[]{:S(2)}, u32[]{:S(2)}) collective-permute-start(bf16[1024,128]{1,0:T(8,128)(2,1)} %shard_map.106.rest_0_), channel_id=1, source_target_pairs={{2,0},{3,2},{1,3},{0,1},{6,4},{7,6},{5,7},{4,5},{10,8},{11,10},{9,... | collective-permute-start | bytes 786440 | tf_op jit(solution)/shard_map/ppermute | solution.py:36
  139.9 10.8 %collective-permute-start.23 = (bf16[1024,128]{1,0:T(8,128)(2,1)}, bf16[1024,128]{1,0:T(8,128)(2,1)S(1)}, u32[]{:S(2)}, u32[]{:S(2)}) collective-permute-start(bf16[1024,128]{1,0:T(8,128)(2,1)} %collective-permute-done.21.rest_1_), channel_id=1, source_target_pairs={{0,2},{2,3},{3,1},{1,0},{4,6},{6,7},{7,5},{5,4},{8,10},{10,11},{11... | collective-permute-start | bytes 786440 | tf_op jit(solution)/shard_map/ppermute | solution.py:33
  141.9 8.9 %copy-start.15 = (bf16[1536,384]{1,0:T(8,128)(2,1)S(1)}, bf16[1536,384]{1,0:T(8,128)(2,1)}, u32[]{:S(2)}) copy-start(bf16[1536,384]{1,0:T(8,128)(2,1)} %wv_ref.7) | copy-start | bytes 3538948
  147.1 3.7 %copy-start.12 = (bf16[1536,384]{1,0:T(8,128)(2,1)S(1)}, bf16[1536,384]{1,0:T(8,128)(2,1)}, u32[]{:S(2)}) copy-start(bf16[1536,384]{1,0:T(8,128)(2,1)} %wk_ref.7) | copy-start | bytes 3538948
  147.1 53.0 %slice-start.2 = ((s8[6291456]{0:T(1024)(128)(4,1)}), s8[4194304]{0:T(1024)(128)(4,1)S(1)}, s32[]{:S(2)}) async-start(s8[6291456]{0:T(1024)(128)(4,1)} %bitcast.19), calls=%async_computation.3 | async-start | bytes 8388608
  150.8 9.6 %copy-start.22 = (bf16[1536,384]{1,0:T(8,128)(2,1)S(1)}, bf16[1536,384]{1,0:T(8,128)(2,1)}, u32[]{:S(2)}) copy-start(bf16[1536,384]{1,0:T(8,128)(2,1)} %wq_ref.3) | copy-start | bytes 3538948
  150.8 49.3 %slice-start.3 = ((s8[6291456]{0:T(1024)(128)(4,1)}), s8[2097152]{0:T(1024)(128)(4,1)S(1)}, s32[]{:S(2)}) async-start(s8[6291456]{0:T(1024)(128)(4,1)} %bitcast.19), calls=%async_computation.4 | async-start | bytes 4194304
  158.0 14.7 %collective-permute-start.25 = (bf16[8,2,128,128]{3,2,1,0:T(8,128)(2,1)S(1)}, bf16[8,2,128,128]{3,2,1,0:T(8,128)(2,1)S(1)}, u32[]{:S(2)}, u32[]{:S(2)}) collective-permute-start(bf16[8,2,128,128]{3,2,1,0:T(8,128)(2,1)S(1)} %get-tuple-element.31.rest_0_), channel_id=1, source_target_pairs={{0,28},{4,0},{8,4},{12,8},{16,12},{20,16},{24,20},{28,24},{1,29},{... | collective-permute-start | bytes 1572872 | tf_op jit(solution)/shard_map/ppermute | solution.py:22
  160.4 15.2 %collective-permute-start.24 = (bf16[8,2,128,128]{3,2,1,0:T(8,128)(2,1)S(1)}, bf16[8,2,128,128]{3,2,1,0:T(8,128)(2,1)S(1)}, u32[]{:S(2)}, u32[]{:S(2)}) collective-permute-start(bf16[8,2,128,128]{3,2,1,0:T(8,128)(2,1)S(1)} %get-tuple-element.31.rest_0_), channel_id=1, source_target_pairs={{0,4},{4,8},{8,12},{12,16},{16,20},{20,24},{24,28},{28,0},{1,5},{5... | collective-permute-start | bytes 1572872 | tf_op jit(solution)/shard_map/ppermute | solution.py:22
  160.4 39.7 %slice-start = ((s8[6291456]{0:T(1024)(128)(4,1)}), s8[4194304]{0:T(1024)(128)(4,1)S(1)}, s32[]{:S(2)}) async-start(s8[6291456]{0:T(1024)(128)(4,1)} %bitcast.17), calls=%async_computation.1 | async-start | bytes 8388608
  160.4 39.7 %slice-start.1 = ((s8[6291456]{0:T(1024)(128)(4,1)}), s8[2097152]{0:T(1024)(128)(4,1)S(1)}, s32[]{:S(2)}) async-start(s8[6291456]{0:T(1024)(128)(4,1)} %bitcast.17), calls=%async_computation.2 | async-start | bytes 4194304
  160.4 39.7 %copy-start.9 = (bf16[8,2,128,128]{3,2,1,0:T(8,128)(2,1)S(1)}, bf16[8,2,128,128]{3,2,1,0:T(8,128)(2,1)}, u32[]{:S(2)}) copy-start(bf16[8,2,128,128]{3,2,1,0:T(8,128)(2,1)} %copy-done.7) | copy-start | bytes 1572868
  165.3 18.6 %collective-permute-start.29 = (bf16[8,2,128,128]{3,2,1,0:T(8,128)(2,1)S(1)}, bf16[8,2,128,128]{3,2,1,0:T(8,128)(2,1)S(1)}, u32[]{:S(2)}, u32[]{:S(2)}) collective-permute-start(bf16[8,2,128,128]{3,2,1,0:T(8,128)(2,1)S(1)} %get-tuple-element.32.rest_0_), channel_id=1, source_target_pairs={{0,28},{4,0},{8,4},{12,8},{16,12},{20,16},{24,20},{28,24},{1,29},{... | collective-permute-start | bytes 1572872 | tf_op jit(solution)/shard_map/ppermute | solution.py:22
  168.0 18.8 %collective-permute-start.28 = (bf16[8,2,128,128]{3,2,1,0:T(8,128)(2,1)S(1)}, bf16[8,2,128,128]{3,2,1,0:T(8,128)(2,1)S(1)}, u32[]{:S(2)}, u32[]{:S(2)}) collective-permute-start(bf16[8,2,128,128]{3,2,1,0:T(8,128)(2,1)S(1)} %get-tuple-element.32.rest_0_), channel_id=1, source_target_pairs={{0,4},{4,8},{8,12},{12,16},{16,20},{20,24},{24,28},{28,0},{1,5},{5... | collective-permute-start | bytes 1572872 | tf_op jit(solution)/shard_map/ppermute | solution.py:22
  175.6 41.0 %collective-permute-start.39 = (bf16[8,2,128,128]{3,2,1,0:T(8,128)(2,1)S(1)}, bf16[8,2,128,128]{3,2,1,0:T(8,128)(2,1)S(1)}, u32[]{:S(2)}, u32[]{:S(2)}) collective-permute-start(bf16[8,2,128,128]{3,2,1,0:T(8,128)(2,1)S(1)} %get-tuple-element.34.rest_0_), channel_id=1, source_target_pairs={{0,28},{4,0},{8,4},{12,8},{16,12},{20,16},{24,20},{28,24},{1,29},{... | collective-permute-start | bytes 1572872 | tf_op jit(solution)/shard_map/ppermute | solution.py:22
  175.6 43.9 %collective-permute-start.38 = (bf16[8,2,128,128]{3,2,1,0:T(8,128)(2,1)S(1)}, bf16[8,2,128,128]{3,2,1,0:T(8,128)(2,1)S(1)}, u32[]{:S(2)}, u32[]{:S(2)}) collective-permute-start(bf16[8,2,128,128]{3,2,1,0:T(8,128)(2,1)S(1)} %get-tuple-element.34.rest_0_), channel_id=1, source_target_pairs={{0,4},{4,8},{8,12},{12,16},{16,20},{20,24},{24,28},{28,0},{1,5},{5... | collective-permute-start | bytes 1572872 | tf_op jit(solution)/shard_map/ppermute | solution.py:22
  176.1 23.9 %collective-permute-start.27 = (bf16[4,2,128,128]{3,2,1,0:T(8,128)(2,1)S(1)}, bf16[4,2,128,128]{3,2,1,0:T(8,128)(2,1)S(1)}, u32[]{:S(2)}, u32[]{:S(2)}) collective-permute-start(bf16[4,2,128,128]{3,2,1,0:T(8,128)(2,1)S(1)} %slice.65), channel_id=1, source_target_pairs={{0,28},{4,0},{8,4},{12,8},{16,12},{20,16},{24,20},{28,24},{1,29},{... | collective-permute-start | bytes 786440 | tf_op jit(solution)/shard_map/ppermute | solution.py:22
  184.0 29.4 %collective-permute-start.26 = (bf16[4,2,128,128]{3,2,1,0:T(8,128)(2,1)S(1)}, bf16[4,2,128,128]{3,2,1,0:T(8,128)(2,1)S(1)}, u32[]{:S(2)}, u32[]{:S(2)}) collective-permute-start(bf16[4,2,128,128]{3,2,1,0:T(8,128)(2,1)S(1)} %slice.64), channel_id=1, source_target_pairs={{0,4},{4,8},{8,12},{12,16},{16,20},{20,24},{24,28},{28,0},{1,5},{5... | collective-permute-start | bytes 786440 | tf_op jit(solution)/shard_map/ppermute | solution.py:22
  186.8 34.8 %collective-permute-start.31 = (bf16[4,2,128,128]{3,2,1,0:T(8,128)(2,1)S(1)}, bf16[4,2,128,128]{3,2,1,0:T(8,128)(2,1)S(1)}, u32[]{:S(2)}, u32[]{:S(2)}) collective-permute-start(bf16[4,2,128,128]{3,2,1,0:T(8,128)(2,1)S(1)} %slice.67), channel_id=1, source_target_pairs={{0,28},{4,0},{8,4},{12,8},{16,12},{20,16},{24,20},{28,24},{1,29},{... | collective-permute-start | bytes 786440 | tf_op jit(solution)/shard_map/ppermute | solution.py:22
  200.1 21.5 %collective-permute-start.30 = (bf16[4,2,128,128]{3,2,1,0:T(8,128)(2,1)S(1)}, bf16[4,2,128,128]{3,2,1,0:T(8,128)(2,1)S(1)}, u32[]{:S(2)}, u32[]{:S(2)}) collective-permute-start(bf16[4,2,128,128]{3,2,1,0:T(8,128)(2,1)S(1)} %slice.66), channel_id=1, source_target_pairs={{0,4},{4,8},{8,12},{12,16},{16,20},{20,24},{24,28},{28,0},{1,5},{5... | collective-permute-start | bytes 786440 | tf_op jit(solution)/shard_map/ppermute | solution.py:22
  216.6 10.2 %collective-permute-start.41 = (bf16[4,2,128,128]{3,2,1,0:T(8,128)(2,1)S(1)}, bf16[4,2,128,128]{3,2,1,0:T(8,128)(2,1)S(1)}, u32[]{:S(2)}, u32[]{:S(2)}) collective-permute-start(bf16[4,2,128,128]{3,2,1,0:T(8,128)(2,1)S(1)} %slice.69), channel_id=1, source_target_pairs={{0,28},{4,0},{8,4},{12,8},{16,12},{20,16},{24,20},{28,24},{1,29},{... | collective-permute-start | bytes 786440 | tf_op jit(solution)/shard_map/ppermute | solution.py:22
  219.5 8.5 %collective-permute-start.40 = (bf16[4,2,128,128]{3,2,1,0:T(8,128)(2,1)S(1)}, bf16[4,2,128,128]{3,2,1,0:T(8,128)(2,1)S(1)}, u32[]{:S(2)}, u32[]{:S(2)}) collective-permute-start(bf16[4,2,128,128]{3,2,1,0:T(8,128)(2,1)S(1)} %slice.68), channel_id=1, source_target_pairs={{0,4},{4,8},{8,12},{12,16},{16,20},{20,24},{24,28},{28,0},{1,5},{5... | collective-permute-start | bytes 786440 | tf_op jit(solution)/shard_map/ppermute | solution.py:22
  219.6 13.4 %collective-permute-start.32 = (bf16[1024,128]{1,0:T(8,128)(2,1)S(1)}, bf16[1024,128]{1,0:T(8,128)(2,1)S(1)}, u32[]{:S(2)}, u32[]{:S(2)}) collective-permute-start(bf16[1024,128]{1,0:T(8,128)(2,1)S(1)} %shard_map.110.rest_0_), channel_id=1, source_target_pairs={{0,2},{2,3},{3,1},{1,0},{4,6},{6,7},{7,5},{5,4},{8,10},{10,11},{11... | collective-permute-start | bytes 786440 | tf_op jit(solution)/shard_map/ppermute | solution.py:33
  224.7 10.2 %collective-permute-start.33 = (bf16[1024,128]{1,0:T(8,128)(2,1)S(1)}, bf16[1024,128]{1,0:T(8,128)(2,1)S(1)}, u32[]{:S(2)}, u32[]{:S(2)}) collective-permute-start(bf16[1024,128]{1,0:T(8,128)(2,1)S(1)} %shard_map.111.rest_1_), channel_id=1, source_target_pairs={{0,2},{2,3},{3,1},{1,0},{4,6},{6,7},{7,5},{5,4},{8,10},{10,11},{11... | collective-permute-start | bytes 786440 | tf_op jit(solution)/shard_map/ppermute | solution.py:33
  226.7 19.9 %collective-permute-start.34 = (bf16[1024,128]{1,0:T(8,128)(2,1)S(1)}, bf16[1024,128]{1,0:T(8,128)(2,1)S(1)}, u32[]{:S(2)}, u32[]{:S(2)}) collective-permute-start(bf16[1024,128]{1,0:T(8,128)(2,1)S(1)} %shard_map.110.rest_0_), channel_id=1, source_target_pairs={{2,0},{3,2},{1,3},{0,1},{6,4},{7,6},{5,7},{4,5},{10,8},{11,10},{9,... | collective-permute-start | bytes 786440 | tf_op jit(solution)/shard_map/ppermute | solution.py:36
  226.8 27.0 %collective-permute-start.35 = (bf16[1024,128]{1,0:T(8,128)(2,1)S(1)}, bf16[1024,128]{1,0:T(8,128)(2,1)S(1)}, u32[]{:S(2)}, u32[]{:S(2)}) collective-permute-start(bf16[1024,128]{1,0:T(8,128)(2,1)S(1)} %shard_map.111.rest_1_), channel_id=1, source_target_pairs={{2,0},{3,2},{1,3},{0,1},{6,4},{7,6},{5,7},{4,5},{10,8},{11,10},{9,... | collective-permute-start | bytes 786440 | tf_op jit(solution)/shard_map/ppermute | solution.py:36
  231.1 20.3 %collective-permute-start.42 = (bf16[1024,128]{1,0:T(8,128)(2,1)S(1)}, bf16[1024,128]{1,0:T(8,128)(2,1)S(1)}, u32[]{:S(2)}, u32[]{:S(2)}) collective-permute-start(bf16[1024,128]{1,0:T(8,128)(2,1)S(1)} %shard_map.113.rest_0_), channel_id=1, source_target_pairs={{0,2},{2,3},{3,1},{1,0},{4,6},{6,7},{7,5},{5,4},{8,10},{10,11},{11... | collective-permute-start | bytes 786440 | tf_op jit(solution)/shard_map/ppermute | solution.py:33
  232.9 24.2 %collective-permute-start.36 = (bf16[1024,128]{1,0:T(8,128)(2,1)S(1)}, bf16[1024,128]{1,0:T(8,128)(2,1)S(1)}, u32[]{:S(2)}, u32[]{:S(2)}) collective-permute-start(bf16[1024,128]{1,0:T(8,128)(2,1)S(1)} %collective-permute-done.32.rest_2_), channel_id=1, source_target_pairs={{0,2},{2,3},{3,1},{1,0},{4,6},{6,7},{7,5},{5,4},{8,10},{10,11},{11... | collective-permute-start | bytes 786440 | tf_op jit(solution)/shard_map/ppermute | solution.py:33
  235.0 28.0 %collective-permute-start.37 = (bf16[1024,128]{1,0:T(8,128)(2,1)S(1)}, bf16[1024,128]{1,0:T(8,128)(2,1)S(1)}, u32[]{:S(2)}, u32[]{:S(2)}) collective-permute-start(bf16[1024,128]{1,0:T(8,128)(2,1)S(1)} %collective-permute-done.33.rest_3_), channel_id=1, source_target_pairs={{0,2},{2,3},{3,1},{1,0},{4,6},{6,7},{7,5},{5,4},{8,10},{10,11},{11... | collective-permute-start | bytes 786440 | tf_op jit(solution)/shard_map/ppermute | solution.py:33
  246.6 22.9 %collective-permute-start.43 = (bf16[1024,128]{1,0:T(8,128)(2,1)S(1)}, bf16[1024,128]{1,0:T(8,128)(2,1)S(1)}, u32[]{:S(2)}, u32[]{:S(2)}) collective-permute-start(bf16[1024,128]{1,0:T(8,128)(2,1)S(1)} %shard_map.113.rest_0_), channel_id=1, source_target_pairs={{2,0},{3,2},{1,3},{0,1},{6,4},{7,6},{5,7},{4,5},{10,8},{11,10},{9,... | collective-permute-start | bytes 786440 | tf_op jit(solution)/shard_map/ppermute | solution.py:36
  251.5 21.3 %collective-permute-start.44 = (bf16[1024,128]{1,0:T(8,128)(2,1)S(1)}, bf16[1024,128]{1,0:T(8,128)(2,1)S(1)}, u32[]{:S(2)}, u32[]{:S(2)}) collective-permute-start(bf16[1024,128]{1,0:T(8,128)(2,1)S(1)} %collective-permute-done.42.rest_1_), channel_id=1, source_target_pairs={{0,2},{2,3},{3,1},{1,0},{4,6},{6,7},{7,5},{5,4},{8,10},{10,11},{11... | collective-permute-start | bytes 786440 | tf_op jit(solution)/shard_map/ppermute | solution.py:33
  (11 other events, 12.8 us)
Sparse Core Ops, SparseCore 0:
  41.7 48.4 all-gather.2

commit v3 on v2

--- a/solution.py
+++ b/solution.py
@@ -22,13 +22,15 @@
     return lax.ppermute(value, axis, pairs)
 
 
-def around(value, axis):
+def around(value, axis, then=()):
     count = lax.axis_size(axis)
     order = list(range(0, count, 2)) + list(range(1, count, 2))[::-1]
     onward = [(order[i], order[(i + 1) % count]) for i in range(count)]
     back = [(target, source) for source, target in onward]
     came, ahead, behind = [value], value, value
     for hop in range(count - 1):
+        if hop == 2 and then:
+            ahead = after(ahead, *then)
         if hop % 2 == 0:
             ahead = lax.ppermute(ahead, axis, onward)
             came.append(ahead)
@@ -100,7 +102,7 @@
         ],
         pl.BlockSpec((per_tile, 2, BLK, HD), lambda i: (i, 0, 0, 0)),
         jax.ShapeDtypeStruct((rows // BLK, 2, BLK, HD), jnp.bfloat16),
-        12,
+        60,
         scratch=[pltpu.VMEM((width, 2 * HD), jnp.bfloat16)],
         flops=2 * rows * width * 2 * HD,
         moved=2 * rows * width,
@@ -154,46 +156,52 @@
 def past_body(frames, heads, newer, qt_ref, ck_ref, cv_ref, *rest):
     last, (acc_ref, stat_ref) = rest[:-2], rest[-2:]
     eye = same_token()
-    skip = 1 if newer else 0
-    for head in range(heads):
-        cols = slice(head * HD, (head + 1) * HD)
-        keys = [ck_ref[frame, :, cols] for frame in range(skip, frames)]
-        if newer:
-            keys = [last[head][0, 0]] + keys
-        pairs = dot(jnp.concatenate(keys, axis=0), qt_ref[0, head])
-        scores = [
-            jnp.sum(jnp.where(eye, pairs[frame * BLK : (frame + 1) * BLK], 0.0), axis=0, keepdims=True)
-            for frame in range(frames)
-        ]
-        top = functools.reduce(jnp.maximum, scores)
-        weights = [jnp.exp2((score - top) * SCALE) for score in scores]
-        stat_ref[0, head, 0:1] = top
-        stat_ref[0, head, 1:2] = functools.reduce(jnp.add, weights)
-        spread = jnp.concatenate([jnp.where(eye, weight, 0.0).astype(jnp.bfloat16) for weight in weights[skip:]], axis=1)
-        mixed = dot(spread, jnp.concatenate([cv_ref[frame, :, cols] for frame in range(skip, frames)], axis=0)).T
-        if newer:
-            mixed = mixed + last[head][0, 1].astype(jnp.float32) * weights[0]
-        acc_ref[0, head] = mixed
+    none = jnp.zeros((BLK, BLK), jnp.bfloat16)
+    for block in range(qt_ref.shape[0]):
+        rows = slice(block * BLK, (block + 1) * BLK)
+        for head in range(heads):
+            cols = slice(head * HD, (head + 1) * HD)
+            keys = [ck_ref[frame, rows, cols] for frame in range(frames)]
+            if newer:
+                keys[0] = last[head][block, 0]
+            pairs = dot(jnp.concatenate(keys, axis=0), qt_ref[block, head])
+            scores = [
+                jnp.sum(jnp.where(eye, pairs[frame * BLK : (frame + 1) * BLK], 0.0), axis=0, keepdims=True)
+                for frame in range(frames)
+            ]
+            top = functools.reduce(jnp.maximum, scores)
+            weights = [jnp.exp2((score - top) * SCALE) for score in scores]
+            stat_ref[block, head, 0:1] = top
+            stat_ref[block, head, 1:2] = functools.reduce(jnp.add, weights)
+            spread = [jnp.where(eye, weight, 0.0).astype(jnp.bfloat16) for weight in weights]
+            if newer:
+                spread[0] = none
+            values = jnp.concatenate([cv_ref[frame, rows, cols] for frame in range(frames)], axis=0)
+            mixed = dot(jnp.concatenate(spread, axis=1), values).T
+            if newer:
+                mixed = mixed + last[head][block, 1].astype(jnp.float32) * weights[0]
+            acc_ref[block, head] = mixed
 
 
 def attend_past(queries, cache_key, cache_value, last):
     blocks, heads = queries.shape[:2]
     frames, rows, local = cache_key.shape
-    cached = pl.BlockSpec((frames, BLK, local), lambda i: (0, i, 0))
+    per_tile = TILE // BLK
+    cached = pl.BlockSpec((frames, TILE, local), lambda i: (0, i, 0))
     return call(
         functools.partial(past_body, frames, heads, len(last) > 0),
-        (blocks,),
-        [pl.BlockSpec((1, heads, HD, BLK), lambda i: (i, 0, 0, 0)), cached, cached]
-        + [pl.BlockSpec((1, 2, BLK, HD), lambda i: (i, 0, 0, 0))] * len(last),
-        [
-            pl.BlockSpec((1, heads, HD, BLK), lambda i: (i, 0, 0, 0)),
-            pl.BlockSpec((1, heads, 2, BLK), lambda i: (i, 0, 0, 0)),
+        (blocks // per_tile,),
+        [pl.BlockSpec((per_tile, heads, HD, BLK), lambda i: (i, 0, 0, 0)), cached, cached]
+        + [pl.BlockSpec((per_tile, 2, BLK, HD), lambda i: (i, 0, 0, 0))] * len(last),
+        [
+            pl.BlockSpec((per_tile, heads, HD, BLK), lambda i: (i, 0, 0, 0)),
+            pl.BlockSpec((per_tile, heads, 2, BLK), lambda i: (i, 0, 0, 0)),
         ],
         [
             jax.ShapeDtypeStruct((blocks, heads, HD, BLK), jnp.float32),
             jax.ShapeDtypeStruct((blocks, heads, 2, BLK), jnp.float32),
         ],
-        14,
+        20,
         flops=4 * rows * frames * BLK * local,
         moved=4 * frames * rows * local,
     )(queries, cache_key, cache_value, *last)
@@ -322,7 +330,7 @@
     )(part, w_rows, gain, w_key, w_value, *pieces)
 
 
-def all_rows(w_out, start):
+def all_rows(w_out, start, then):
     count = lax.axis_size("space")
     half = count // 2
     local, width = w_out.shape
@@ -331,7 +339,7 @@
     quarter = me % 2 + 2 * (me // half)
     own = w_out.reshape(heads, 4, HD // 4, width)
     mine = lax.dynamic_index_in_dim(own, quarter, 1, keepdims=False)
-    fetched = jnp.stack(around(after(mine, start), "head")[1:])
+    fetched = jnp.stack(around(after(mine, start), "head", then)[1:])
     fours = [[2 * m, 2 * m + 1, half + 2 * m, half + 2 * m + 1] for m in range(half // 2)]
     others = lax.all_gather(fetched, "space", axis_index_groups=fours)
     others = others.transpose(1, 2, 0, 3, 4).reshape(-1, heads, HD, width)
@@ -352,23 +360,30 @@
     gain = norm_gain.reshape(1, width)
     state = snapshot
     kv_first = first_projection(state, gain, w_key, w_value)
-    rows_of = all_rows(w_out, kv_first)
-    w_early = rows_of[:, : heads - 1].reshape(-1, width)
-    w_last = rows_of[:, heads - 1].reshape(-1, width)
+    rows_of = None
     last = []
     for rollout in range(STEPS):
+        near = [(shifted(kv_first, "space", 1), shifted(kv_first, "space", -1))]
         *kv_rest, queries = rest_projection(state, gain, w_query, w_key, w_value)
         kv = [kv_first] + list(kv_rest)
         past, stats = attend_past(queries, cache_key, cache_value, last)
-        near = []
-        for head in range(heads):
-            sent = kv[head] if head < 2 else after(kv[head], *near[head - 2])
-            near.append((shifted(sent, "space", 1), shifted(sent, "space", -1)))
         came = []
         for head in range(heads):
             left, right = near[head]
-            pieces = (kv[head], left, right, shifted(left[half:], "space", 1), shifted(right[:half], "space", -1))
-            came.append(around(attend(head, where_block, counts, queries, past, stats, pieces), "head"))
+            if head == 0:
+                left, right = after(left, past), after(right, past)
+            if rows_of is None:
+                rows_of = all_rows(w_out, kv_rest[-1], (left, right))
+            far = (shifted(left[half:], "space", 1), shifted(right[:half], "space", -1))
+            if head + 1 < heads:
+                ready = near[0] if head == 0 else (*near[head], *came[head - 1][:1])
+                sent = after(kv[head + 1], *ready)
+                near.append((shifted(sent, "space", 1), shifted(sent, "space", -1)))
+            attended = attend(head, where_block, counts, queries, past, stats, (kv[head], left, right, *far))
+            came.append(around(attended, "head"))
+        if rollout == 0:
+            w_early = rows_of[:, : heads - 1].reshape(-1, width)
+            w_last = rows_of[:, heads - 1].reshape(-1, width)
         early = [piece for group in zip(*came[:-1], strict=True) for piece in group]
         part = add_heads(state, w_early, early, jnp.float32)
         if rollout + 1 < STEPS:

time: 284 us -> 282 us (level)
  waiting for transfers between devices: 94 us -> 105 us
  local copies, waits for them, and re-layouts: 30.5 us -> 23.3 us
  Pallas kernels: 78.3 us -> 72 us
    ppermute x24, waiting for transfers between devices: 37.9 us -> 51.4 us  [shifted(): return lax.ppermute(value, axis, pairs)]
    ppermute x14, waiting for transfers between devices: 45.3 us -> 34.9 us  [around(): ahead = lax.ppermute(ahead, axis, onward)]
    pallas_call x2, Pallas kernels: 21.7 us -> 13.1 us  [attend_past(): call(functools.partial(past_body, frames, heads, len(last) > 0), (blocks...]
    ppermute x7, waiting for transfers between devices: 10.7 us -> 18.3 us  [around(): behind = lax.ppermute(behind, axis, back)]
    ppermute x24, starting transfers between devices: 22 us -> 28.8 us  [shifted(): return lax.ppermute(value, axis, pairs)]
    ppermute x14, starting transfers between devices: 38.5 us -> 33 us  [around(): ahead = lax.ppermute(ahead, axis, onward)]
    unnamed x58 -> x54, local copies, waits for them, and re-layouts: 18.5 us -> 13.1 us
  transfers between devices with their start and end apart: 46 -> 46, of which waited for: 21 -> 19; matrix products, arithmetic and copies ran while one was open for 4% -> 3% of each run, Pallas kernels for 23% -> 20%
where the time goes in v3:
time: 282 us
  waiting for transfers between devices  105 us (37%)
  Pallas kernels  72 us (26%)
  starting transfers between devices  66.1 us (23%)
  local copies, waits for them, and re-layouts  23.3 us (8%)
  between operations  13.9 us (5%)
    ppermute x24, waiting for transfers between devices, shifted(): return lax.ppermute(value, axis, pairs)  51.4 us
    ppermute x14, waiting for transfers between devices, around(): ahead = lax.ppermute(ahead, axis, onward)  34.9 us
    ppermute x14, starting transfers between devices, around(): ahead = lax.ppermute(ahead, axis, onward)  33 us
    ppermute x24, starting transfers between devices, shifted(): return lax.ppermute(value, axis, pairs)  28.8 us
    pallas_call x6, Pallas kernels, attend(): call(functools.partial(attend_body, blocks, slots), (1,), [pl.BlockSpec((...  23.7 us
    ppermute x7, waiting for transfers between devices, around(): behind = lax.ppermute(behind, axis, back)  18.3 us
    unnamed x54, local copies, waits for them, and re-layouts  13.1 us
    pallas_call x2, Pallas kernels, attend_past(): call(functools.partial(past_body, frames, heads, len(last) > 0), (blocks...  13.1 us
  transfers between devices with their start and end apart: 46, of which 19 were waited for; matrix products, arithmetic and copies ran while one was open for 3% of the time, Pallas kernels for 20%

profile of v3, /device:TPU:0, one launch (start us, length us, event | category | flops | bytes accessed | tf_op | source)
XLA Modules:
  0.0 281.7 jit_solution(7900240987719076747)
XLA Ops:
  6.5 1.4 reshape.25.gain_ref
  8.0 5.2 %shard_map.101.rest_0_ = bf16[8,2,128,128]{3,2,1,0:T(8,128)(2,1)} custom-call(bf16[1024,1536]{1,0:T(8,128)(2,1)} %state_ref.5, f32[1,1536]{1,0:T(1,128)} %reshape.25.gain_ref, bf16[1536,384]{1,0:T(8,128)(2,1)} %wk_ref.7, bf16[1536,384]{1,0:T(8,128)(2,1)} %wv_ref.7), custom_call_target="tpu_custom_call" | custom-call | flops 805306368 | bytes 3145728 | tf_op jit(solution)/shard_map/pallas_call | solution.py:94
  13.7 2.9 %collective-permute-start.3 = (bf16[8,2,128,128]{3,2,1,0:T(8,128)(2,1)}, bf16[8,2,128,128]{3,2,1,0:T(8,128)(2,1)}, u32[]{:S(2)}, u32[]{:S(2)}) collective-permute-start(bf16[8,2,128,128]{3,2,1,0:T(8,128)(2,1)} %shard_map.101.rest_0_), channel_id=1, source_target_pairs={{0,28},{4,0},{8,4},{12,8},{16,12},{20,16},{24,20},{28,24},{1,29},{... | collective-permute-start | bytes 1572872 | tf_op jit(solution)/shard_map/ppermute | solution.py:22
  16.6 1.3 copy-done.8
  17.8 1.3 copy-done.10
  19.1 1.3 copy-done.19
  20.4 5.0 %shard_map.100 = (bf16[8,2,128,128]{3,2,1,0:T(8,128)(2,1)S(1)}, bf16[8,2,128,128]{3,2,1,0:T(8,128)(2,1)S(1)}, bf16[8,3,128,128]{3,2,1,0:T(8,128)(2,1)S(1)}) custom-call(bf16[1024,1536]{1,0:T(8,128)(2,1)S(1)} %copy-done.2, f32[1,1536]{1,0:T(1,128)S(1)} %copy-done.17, bf16[1536,384]{1,0:T(8,128)(2,1)S(1)} %copy-done.19, bf16[1536,384]{1,0:T(8,128)(2,1)S(1)} %copy-done.8, ...), custom_call_target="tpu_custom_call" | custom-call | flops 2818572288 | bytes 6684672 | tf_op jit(solution)/shard_map/pallas_call | solution.py:133
  28.9 3.4 %collective-permute-start = (bf16[3,32,1536]{2,1,0:T(8,128)(2,1)S(1)}, bf16[3,32,1536]{2,1,0:T(8,128)(2,1)S(1)}, u32[]{:S(2)}, u32[]{:S(2)}) collective-permute-start(bf16[3,32,1536]{2,1,0:T(8,128)(2,1)S(1)} %dynamic-slice_bitcast_fusion), channel_id=1, source_target_pairs={{0,2},{2,3},{3,1},{1,0},{4,6},{6,7},{7,5},{5,4},{8,10},{10,11},{11... | collective-permute-start | bytes 884744 | tf_op jit(solution)/shard_map/ppermute | solution.py:35
  32.3 2.8 copy-done
  35.1 2.8 copy-done.1
  37.9 1.1 copy-done.5
  39.0 6.5 %shard_map.102 = (f32[8,3,128,128]{3,2,1,0:T(8,128)S(1)}, f32[8,3,2,128]{3,2,1,0:T(2,128)S(1)}) custom-call(bf16[8,3,128,128]{3,2,1,0:T(8,128)(2,1)S(1)} %copy-done.5, bf16[8,1024,384]{2,1,0:T(8,128)(2,1)S(1)} %copy-done, bf16[8,1024,384]{2,1,0:T(8,128)(2,1)S(1)} %copy-done.1), custom_call_target="tpu_custom_call" | custom-call | flops 1610612736 | bytes 12582912 | tf_op jit(solution)/shard_map/pallas_call | solution.py:191
  45.6 3.0 %collective-permute-start.4 = (bf16[3,32,1536]{2,1,0:T(8,128)(2,1)S(1)}, bf16[3,32,1536]{2,1,0:T(8,128)(2,1)S(1)}, u32[]{:S(2)}, u32[]{:S(2)}) collective-permute-start(bf16[3,32,1536]{2,1,0:T(8,128)(2,1)S(1)} %collective-permute-done), channel_id=1, source_target_pairs={{0,2},{2,3},{3,1},{1,0},{4,6},{6,7},{7,5},{5,4},{8,10},{10,11},{11... | collective-permute-start | bytes 884744 | tf_op jit(solution)/shard_map/ppermute | solution.py:35
  48.6 4.9 %collective-permute-done.4 = bf16[3,32,1536]{2,1,0:T(8,128)(2,1)S(1)} collective-permute-done((bf16[3,32,1536]{2,1,0:T(8,128)(2,1)S(1)}, bf16[3,32,1536]{2,1,0:T(8,128)(2,1)S(1)}, u32[]{:S(2)}, u32[]{:S(2)}) %collective-permute-start.4) | collective-permute-done | bytes 294944 | tf_op jit(solution)/shard_map/ppermute | solution.py:35
  54.5 2.6 collective-permute-start.8
  57.2 1.7 slice.43
  58.9 1.7 slice.44
  60.5 2.6 collective-permute-start.6
  63.3 11.3 %collective-permute-done.5.rest_3_ = bf16[4,2,128,128]{3,2,1,0:T(8,128)(2,1)} collective-permute-done((bf16[4,2,128,128]{3,2,1,0:T(8,128)(2,1)}, bf16[4,2,128,128]{3,2,1,0:T(8,128)(2,1)}, u32[]{:S(2)}, u32[]{:S(2)}) %collective-permute-start.5) | collective-permute-done | bytes 262176 | tf_op jit(solution)/shard_map/ppermute | solution.py:22
  74.6 5.1 %shard_map.103.rest_0_ = bf16[1024,128]{1,0:T(8,128)(2,1)} custom-call(s32[64]{0:T(128)S(1)} %reshape.28.where_ref, s32[8]{0:T(128)S(1)} %copy-done.18, bf16[8,3,128,128]{3,2,1,0:T(8,128)(2,1)S(1)} %copy-done.6, f32[8,3,128,128]{3,2,1,0:T(8,128)S(1)} %get-tuple-element.30.acc_ref, f32[8,3,2,128]{3,2,1,0:T(2,128)S(1)} %get-tuple-element.34.stat_ref, ...), custom_call_target="tpu_custom_call" | custom-call | flops 536870912 | bytes 2097152 | tf_op jit(solution)/shard_map/pallas_call | solution.py:247
  80.7 1.7 collective-permute-start.18
  85.0 3.4 %collective-permute-start.11 = (bf16[1024,128]{1,0:T(8,128)(2,1)}, bf16[1024,128]{1,0:T(8,128)(2,1)}, u32[]{:S(2)}, u32[]{:S(2)}) collective-permute-start(bf16[1024,128]{1,0:T(8,128)(2,1)} %shard_map.103.rest_0_), channel_id=1, source_target_pairs={{0,2},{2,3},{3,1},{1,0},{4,6},{6,7},{7,5},{5,4},{8,10},{10,11},{11... | collective-permute-start | bytes 786440 | tf_op jit(solution)/shard_map/ppermute | solution.py:35
  88.4 9.6 %collective-permute-done.10.rest_4_ = bf16[4,2,128,128]{3,2,1,0:T(8,128)(2,1)S(1)} collective-permute-done((bf16[4,2,128,128]{3,2,1,0:T(8,128)(2,1)S(1)}, bf16[4,2,128,128]{3,2,1,0:T(8,128)(2,1)S(1)}, u32[]{:S(2)}, u32[]{:S(2)}) %collective-permute-start.10) | collective-permute-done | bytes 262176 | tf_op jit(solution)/shard_map/ppermute | solution.py:22
  98.0 2.3 collective-permute-done.9.rest_3_
  100.3 5.0 %shard_map.104.rest_1_ = bf16[1024,128]{1,0:T(8,128)(2,1)} custom-call(s32[64]{0:T(128)S(1)} %reshape.28.where_ref, s32[8]{0:T(128)S(1)} %copy-done.18, bf16[8,3,128,128]{3,2,1,0:T(8,128)(2,1)S(1)} %copy-done.6, f32[8,3,128,128]{3,2,1,0:T(8,128)S(1)} %get-tuple-element.30.acc_ref, f32[8,3,2,128]{3,2,1,0:T(2,128)S(1)} %get-tuple-element.34.stat_ref, ...), custom_call_target="tpu_custom_call" | custom-call | flops 536870912 | bytes 2097152 | tf_op jit(solution)/shard_map/pallas_call | solution.py:247
  105.3 3.4 %collective-permute-start.12 = (bf16[1024,128]{1,0:T(8,128)(2,1)}, bf16[1024,128]{1,0:T(8,128)(2,1)}, u32[]{:S(2)}, u32[]{:S(2)}) collective-permute-start(bf16[1024,128]{1,0:T(8,128)(2,1)} %shard_map.104.rest_1_), channel_id=1, source_target_pairs={{0,2},{2,3},{3,1},{1,0},{4,6},{6,7},{7,5},{5,4},{8,10},{10,11},{11... | collective-permute-start | bytes 786440 | tf_op jit(solution)/shard_map/ppermute | solution.py:35
  108.9 2.7 collective-permute-start.20
  111.5 2.9 %collective-permute-start.15 = (bf16[1024,128]{1,0:T(8,128)(2,1)}, bf16[1024,128]{1,0:T(8,128)(2,1)}, u32[]{:S(2)}, u32[]{:S(2)}) collective-permute-start(bf16[1024,128]{1,0:T(8,128)(2,1)} %collective-permute-done.11.rest_2_), channel_id=1, source_target_pairs={{0,2},{2,3},{3,1},{1,0},{4,6},{6,7},{7,5},{5,4},{8,10},{10,11},{11... | collective-permute-start | bytes 786440 | tf_op jit(solution)/shard_map/ppermute | solution.py:35
  114.5 1.3 collective-permute-done.12.rest_3_
  115.8 2.3 collective-permute-start.14
  119.2 3.9 %shard_map.106.rest_0_ = bf16[1024,128]{1,0:T(8,128)(2,1)} custom-call(s32[64]{0:T(128)S(1)} %reshape.28.where_ref, s32[8]{0:T(128)S(1)} %copy-done.18, bf16[8,3,128,128]{3,2,1,0:T(8,128)(2,1)S(1)} %copy-done.6, f32[8,3,128,128]{3,2,1,0:T(8,128)S(1)} %get-tuple-element.30.acc_ref, f32[8,3,2,128]{3,2,1,0:T(2,128)S(1)} %get-tuple-element.34.stat_ref, ...), custom_call_target="tpu_custom_call" | custom-call | flops 536870912 | bytes 2097152 | tf_op jit(solution)/shard_map/pallas_call | solution.py:247
  123.1 2.1 collective-permute-start.21
  125.2 2.3 copy.19
  127.9 16.0 %collective-permute-done.21.rest_1_ = bf16[1024,128]{1,0:T(8,128)(2,1)S(1)} collective-permute-done((bf16[1024,128]{1,0:T(8,128)(2,1)}, bf16[1024,128]{1,0:T(8,128)(2,1)S(1)}, u32[]{:S(2)}, u32[]{:S(2)}) %collective-permute-start.21) | collective-permute-done | bytes 262176 | tf_op jit(solution)/shard_map/ppermute | solution.py:35
  144.0 3.3 %collective-permute-start.23 = (bf16[1024,128]{1,0:T(8,128)(2,1)S(1)}, bf16[1024,128]{1,0:T(8,128)(2,1)S(1)}, u32[]{:S(2)}, u32[]{:S(2)}) collective-permute-start(bf16[1024,128]{1,0:T(8,128)(2,1)S(1)} %collective-permute-done.21.rest_1_), channel_id=1, source_target_pairs={{0,2},{2,3},{3,1},{1,0},{4,6},{6,7},{7,5},{5,4},{8,10},{10,11},{11... | collective-permute-start | bytes 786440 | tf_op jit(solution)/shard_map/ppermute | solution.py:35
  147.3 5.2 %shard_map.105.part_ref = f32[1024,1536]{1,0:T(8,128)S(1)} custom-call(bf16[1024,1536]{1,0:T(8,128)(2,1)S(1)} %copy-done.3, bf16[1024,1536]{1,0:T(8,128)(2,1)S(1)} %bitcast.15, bf16[1024,128]{1,0:T(8,128)(2,1)} %shard_map.103.rest_0_, bf16[1024,128]{1,0:T(8,128)(2,1)} %shard_map.104.rest_1_, bf16[1024,128]{1,0:T(8,128)(2,1)} %collective-permute-done.11.rest_2_, ...), custom_call_target="tpu_custom_call" | custom-call | flops 3221225472 | bytes 12582912 | tf_op jit(solution)/shard_map/pallas_call | solution.py:278
  152.7 3.3 %collective-permute-done.23.rest_3_ = bf16[1024,128]{1,0:T(8,128)(2,1)S(1)} collective-permute-done((bf16[1024,128]{1,0:T(8,128)(2,1)S(1)}, bf16[1024,128]{1,0:T(8,128)(2,1)S(1)}, u32[]{:S(2)}, u32[]{:S(2)}) %collective-permute-start.23) | collective-permute-done | bytes 262176 | tf_op jit(solution)/shard_map/ppermute | solution.py:35
  156.0 7.3 %shard_map.107 = (bf16[1024,1536]{1,0:T(8,128)(2,1)S(1)}, bf16[8,2,128,128]{3,2,1,0:T(8,128)(2,1)S(1)}) custom-call(f32[1024,1536]{1,0:T(8,128)S(1)} %shard_map.105.part_ref, bf16[512,1536]{1,0:T(8,128)(2,1)S(1)} %bitcast.21, f32[1,1536]{1,0:T(1,128)S(1)} %copy-done.17, bf16[1536,384]{1,0:T(8,128)(2,1)S(1)} %copy-done.9, bf16[1536,384]{1,0:T(8,128)(2,1)S(1)} %copy-done.11, ...), custom_call_target="tpu_custom_call" | custom-call | flops 2415919104 | bytes 11010048 | tf_op jit(solution)/shard_map/pallas_call | solution.py:310
  163.4 2.6 collective-permute-start.25
  166.0 5.0 %shard_map.108 = (bf16[8,2,128,128]{3,2,1,0:T(8,128)(2,1)S(1)}, bf16[8,2,128,128]{3,2,1,0:T(8,128)(2,1)S(1)}, bf16[8,3,128,128]{3,2,1,0:T(8,128)(2,1)S(1)}) custom-call(bf16[1024,1536]{1,0:T(8,128)(2,1)S(1)} %get-tuple-element.38.state_ref, f32[1,1536]{1,0:T(1,128)S(1)} %copy-done.17, bf16[1536,384]{1,0:T(8,128)(2,1)S(1)} %copy-done.20, ...), custom_call_target="tpu_custom_call" | custom-call | flops 2818572288 | bytes 6684672 | tf_op jit(solution)/shard_map/pallas_call | solution.py:133
  171.1 7.4 %collective-permute-done.24.rest_1_ = bf16[8,2,128,128]{3,2,1,0:T(8,128)(2,1)S(1)} collective-permute-done((bf16[8,2,128,128]{3,2,1,0:T(8,128)(2,1)S(1)}, bf16[8,2,128,128]{3,2,1,0:T(8,128)(2,1)S(1)}, u32[]{:S(2)}, u32[]{:S(2)}) %collective-permute-start.24) | collective-permute-done | bytes 524320 | tf_op jit(solution)/shard_map/ppermute | solution.py:22
  178.4 2.6 collective-permute-start.29
  181.1 6.5 %shard_map.109 = (f32[8,3,128,128]{3,2,1,0:T(8,128)S(1)}, f32[8,3,2,128]{3,2,1,0:T(2,128)S(1)}) custom-call(bf16[8,3,128,128]{3,2,1,0:T(8,128)(2,1)S(1)} %get-tuple-element.39.qt_ref, bf16[8,1024,384]{2,1,0:T(8,128)(2,1)S(1)} %bitcast.18, bf16[8,1024,384]{2,1,0:T(8,128)(2,1)S(1)} %bitcast.20, bf16[8,2,128,128]{3,2,1,0:T(8,128)(2,1)S(1)} %copy-done.7, ...), custom_call_target="tpu_custom_call" | custom-call | flops 1610612736 | bytes 12582912 | tf_op jit(solution)/shard_map/pallas_call | solution.py:191
  188.4 6.0 %collective-permute-done.27.rest_4_ = bf16[4,2,128,128]{3,2,1,0:T(8,128)(2,1)S(1)} collective-permute-done((bf16[4,2,128,128]{3,2,1,0:T(8,128)(2,1)S(1)}, bf16[4,2,128,128]{3,2,1,0:T(8,128)(2,1)S(1)}, u32[]{:S(2)}, u32[]{:S(2)}) %collective-permute-start.27) | collective-permute-done | bytes 262176 | tf_op jit(solution)/shard_map/ppermute | solution.py:22
  194.4 4.0 %collective-permute-done.26.rest_3_ = bf16[4,2,128,128]{3,2,1,0:T(8,128)(2,1)S(1)} collective-permute-done((bf16[4,2,128,128]{3,2,1,0:T(8,128)(2,1)S(1)}, bf16[4,2,128,128]{3,2,1,0:T(8,128)(2,1)S(1)}, u32[]{:S(2)}, u32[]{:S(2)}) %collective-permute-start.26) | collective-permute-done | bytes 262176 | tf_op jit(solution)/shard_map/ppermute | solution.py:22
  198.3 3.2 %shard_map.110.rest_0_ = bf16[1024,128]{1,0:T(8,128)(2,1)S(1)} custom-call(s32[64]{0:T(128)S(1)} %reshape.28.where_ref, s32[8]{0:T(128)S(1)} %copy-done.18, bf16[8,3,128,128]{3,2,1,0:T(8,128)(2,1)S(1)} %get-tuple-element.39.qt_ref, f32[8,3,128,128]{3,2,1,0:T(8,128)S(1)} %get-tuple-element.40.acc_ref, f32[8,3,2,128]{3,2,1,0:T(2,128)S(1)} %get-tuple-element.41.stat_ref, ...), custom_call_target="tpu_custom_call" | custom-call | flops 536870912 | bytes 2097152 | tf_op jit(solution)/shard_map/pallas_call | solution.py:247
  201.7 2.6 collective-permute-start.39
  204.4 2.7 collective-permute-start.31
  207.1 9.7 %collective-permute-done.38.rest_1_ = bf16[8,2,128,128]{3,2,1,0:T(8,128)(2,1)S(1)} collective-permute-done((bf16[8,2,128,128]{3,2,1,0:T(8,128)(2,1)S(1)}, bf16[8,2,128,128]{3,2,1,0:T(8,128)(2,1)S(1)}, u32[]{:S(2)}, u32[]{:S(2)}) %collective-permute-start.38) | collective-permute-done | bytes 524320 | tf_op jit(solution)/shard_map/ppermute | solution.py:22
  216.9 2.7 collective-permute-start.41
  219.6 1.7 collective-permute-start.32
  222.4 3.2 %shard_map.111.rest_1_ = bf16[1024,128]{1,0:T(8,128)(2,1)S(1)} custom-call(s32[64]{0:T(128)S(1)} %reshape.28.where_ref, s32[8]{0:T(128)S(1)} %copy-done.18, bf16[8,3,128,128]{3,2,1,0:T(8,128)(2,1)S(1)} %get-tuple-element.39.qt_ref, f32[8,3,128,128]{3,2,1,0:T(8,128)S(1)} %get-tuple-element.40.acc_ref, f32[8,3,2,128]{3,2,1,0:T(2,128)S(1)} %get-tuple-element.41.stat_ref, ...), custom_call_target="tpu_custom_call" | custom-call | flops 536870912 | bytes 2097152 | tf_op jit(solution)/shard_map/pallas_call | solution.py:247
  225.7 1.8 collective-permute-start.33
  227.8 3.2 %shard_map.113.rest_0_ = bf16[1024,128]{1,0:T(8,128)(2,1)S(1)} custom-call(s32[64]{0:T(128)S(1)} %reshape.28.where_ref, s32[8]{0:T(128)S(1)} %copy-done.18, bf16[8,3,128,128]{3,2,1,0:T(8,128)(2,1)S(1)} %get-tuple-element.39.qt_ref, f32[8,3,128,128]{3,2,1,0:T(8,128)S(1)} %get-tuple-element.40.acc_ref, f32[8,3,2,128]{3,2,1,0:T(2,128)S(1)} %get-tuple-element.41.stat_ref, ...), custom_call_target="tpu_custom_call" | custom-call | flops 536870912 | bytes 2097152 | tf_op jit(solution)/shard_map/pallas_call | solution.py:247
  231.0 2.7 collective-permute-start.42
  234.1 1.6 collective-permute-start.35
  237.7 11.2 %collective-permute-done.34.rest_4_ = bf16[1024,128]{1,0:T(8,128)(2,1)S(1)} collective-permute-done((bf16[1024,128]{1,0:T(8,128)(2,1)S(1)}, bf16[1024,128]{1,0:T(8,128)(2,1)S(1)}, u32[]{:S(2)}, u32[]{:S(2)}) %collective-permute-start.34) | collective-permute-done | bytes 262176 | tf_op jit(solution)/shard_map/ppermute | solution.py:38
  248.9 2.9 %collective-permute-start.44 = (bf16[1024,128]{1,0:T(8,128)(2,1)S(1)}, bf16[1024,128]{1,0:T(8,128)(2,1)S(1)}, u32[]{:S(2)}, u32[]{:S(2)}) collective-permute-start(bf16[1024,128]{1,0:T(8,128)(2,1)S(1)} %collective-permute-done.42.rest_1_), channel_id=1, source_target_pairs={{0,2},{2,3},{3,1},{1,0},{4,6},{6,7},{7,5},{5,4},{8,10},{10,11},{11... | collective-permute-start | bytes 786440 | tf_op jit(solution)/shard_map/ppermute | solution.py:35
  251.8 1.7 collective-permute-done.36.rest_6_
  253.5 6.6 %collective-permute-done.35.rest_5_ = bf16[1024,128]{1,0:T(8,128)(2,1)S(1)} collective-permute-done((bf16[1024,128]{1,0:T(8,128)(2,1)S(1)}, bf16[1024,128]{1,0:T(8,128)(2,1)S(1)}, u32[]{:S(2)}, u32[]{:S(2)}) %collective-permute-start.35) | collective-permute-done | bytes 262176 | tf_op jit(solution)/shard_map/ppermute | solution.py:38
  260.1 4.6 %collective-permute-done.37.rest_7_ = bf16[1024,128]{1,0:T(8,128)(2,1)S(1)} collective-permute-done((bf16[1024,128]{1,0:T(8,128)(2,1)S(1)}, bf16[1024,128]{1,0:T(8,128)(2,1)S(1)}, u32[]{:S(2)}, u32[]{:S(2)}) %collective-permute-start.37) | collective-permute-done | bytes 262176 | tf_op jit(solution)/shard_map/ppermute | solution.py:35
  264.7 3.9 %shard_map.112.state_ref = f32[1024,1536]{1,0:T(8,128)S(1)} custom-call(bf16[1024,1536]{1,0:T(8,128)(2,1)S(1)} %get-tuple-element.38.state_ref, bf16[1024,1536]{1,0:T(8,128)(2,1)S(1)} %bitcast.16, bf16[1024,128]{1,0:T(8,128)(2,1)S(1)} %shard_map.110.rest_0_, bf16[1024,128]{1,0:T(8,128)(2,1)S(1)} %shard_map.111.rest_1_, ...), custom_call_target="tpu_custom_call" | custom-call | flops 3221225472 | bytes 12582912 | tf_op jit(solution)/shard_map/pallas_call | solution.py:278
  269.2 2.1 collective-permute-done.44.rest_3_
  271.3 3.5 %shard_map.114 = bf16[1024,1536]{1,0:T(8,128)(2,1)} custom-call(f32[1024,1536]{1,0:T(8,128)S(1)} %shard_map.112.state_ref, bf16[512,1536]{1,0:T(8,128)(2,1)S(1)} %bitcast.22, bf16[1024,128]{1,0:T(8,128)(2,1)S(1)} %shard_map.113.rest_0_, bf16[1024,128]{1,0:T(8,128)(2,1)S(1)} %collective-permute-done.42.rest_1_, ...), custom_call_target="tpu_custom_call" | custom-call | flops 1610612736 | bytes 11010048 | tf_op jit(solution)/shard_map/pallas_call | solution.py:278
  (121 shorter events, 15.9 us)
Async XLA Ops:
  6.5 10.0 %copy-start.2 = (bf16[1024,1536]{1,0:T(8,128)(2,1)S(1)}, bf16[1024,1536]{1,0:T(8,128)(2,1)}, u32[]{:S(2)}) copy-start(bf16[1024,1536]{1,0:T(8,128)(2,1)} %state_ref.5) | copy-start | bytes 9437188
  6.5 118.6 %all-gather.3.cloned.1.call-start = ((), (), s32[]{:S(2)}) async-start(), calls=%async_computation | async-start | bytes 4423680 | tf_op jit(solution)/shard_map/all_gather | solution.py:344
  8.0 8.6 %copy-start.17 = (f32[1,1536]{1,0:T(1,128)S(1)}, f32[1,1536]{1,0:T(1,128)}, u32[]{:S(2)}) copy-start(f32[1,1536]{1,0:T(1,128)} %reshape.25.gain_ref) | copy-start | bytes 18436
  13.2 32.3 %collective-permute-start.2 = (bf16[8,2,128,128]{3,2,1,0:T(8,128)(2,1)}, bf16[8,2,128,128]{3,2,1,0:T(8,128)(2,1)}, u32[]{:S(2)}, u32[]{:S(2)}) collective-permute-start(bf16[8,2,128,128]{3,2,1,0:T(8,128)(2,1)} %shard_map.101.rest_0_), channel_id=1, source_target_pairs={{0,4},{4,8},{8,12},{12,16},{16,20},{20,24},{24,28},{28,0},{1,5},{5... | collective-permute-start | bytes 1572872 | tf_op jit(solution)/shard_map/ppermute | solution.py:22
  13.7 31.9 %collective-permute-start.3 = (bf16[8,2,128,128]{3,2,1,0:T(8,128)(2,1)}, bf16[8,2,128,128]{3,2,1,0:T(8,128)(2,1)}, u32[]{:S(2)}, u32[]{:S(2)}) collective-permute-start(bf16[8,2,128,128]{3,2,1,0:T(8,128)(2,1)} %shard_map.101.rest_0_), channel_id=1, source_target_pairs={{0,28},{4,0},{8,4},{12,8},{16,12},{20,16},{24,20},{28,24},{1,29},{... | collective-permute-start | bytes 1572872 | tf_op jit(solution)/shard_map/ppermute | solution.py:22
  28.9 16.7 %collective-permute-start = (bf16[3,32,1536]{2,1,0:T(8,128)(2,1)S(1)}, bf16[3,32,1536]{2,1,0:T(8,128)(2,1)S(1)}, u32[]{:S(2)}, u32[]{:S(2)}) collective-permute-start(bf16[3,32,1536]{2,1,0:T(8,128)(2,1)S(1)} %dynamic-slice_bitcast_fusion), channel_id=1, source_target_pairs={{0,2},{2,3},{3,1},{1,0},{4,6},{6,7},{7,5},{5,4},{8,10},{10,11},{11... | collective-permute-start | bytes 884744 | tf_op jit(solution)/shard_map/ppermute | solution.py:35
  32.3 16.3 %collective-permute-start.1 = (bf16[3,32,1536]{2,1,0:T(8,128)(2,1)S(1)}, bf16[3,32,1536]{2,1,0:T(8,128)(2,1)S(1)}, u32[]{:S(2)}, u32[]{:S(2)}) collective-permute-start(bf16[3,32,1536]{2,1,0:T(8,128)(2,1)S(1)} %dynamic-slice_bitcast_fusion), channel_id=1, source_target_pairs={{2,0},{3,2},{1,3},{0,1},{6,4},{7,6},{5,7},{4,5},{10,8},{11,10},{9,... | collective-permute-start | bytes 884744 | tf_op jit(solution)/shard_map/ppermute | solution.py:38
  32.3 2.8 copy-start
  39.0 15.5 %copy-start.13 = (bf16[8,2,128,128]{3,2,1,0:T(8,128)(2,1)S(1)}, bf16[8,2,128,128]{3,2,1,0:T(8,128)(2,1)}, u32[]{:S(2)}) copy-start(bf16[8,2,128,128]{3,2,1,0:T(8,128)(2,1)} %copy-done.12) | copy-start | bytes 1572868
  45.5 17.6 %copy-start.22 = (s32[8,8]{1,0:T(8,128)S(1)}, s32[8,8]{1,0:T(8,128)}, u32[]{:S(2)}) copy-start(s32[8,8]{1,0:T(8,128)} %param.18) | copy-start | bytes 772
  45.5 29.1 %copy-start.6 = (bf16[8,3,128,128]{3,2,1,0:T(8,128)(2,1)S(1)}, bf16[8,3,128,128]{3,2,1,0:T(8,128)(2,1)}, u32[]{:S(2)}) copy-start(bf16[8,3,128,128]{3,2,1,0:T(8,128)(2,1)} %copy-done.4) | copy-start | bytes 2359300
  45.5 29.0 %copy-start.7 = (bf16[8,2,128,128]{3,2,1,0:T(8,128)(2,1)S(1)}, bf16[8,2,128,128]{3,2,1,0:T(8,128)(2,1)}, u32[]{:S(2)}) copy-start(bf16[8,2,128,128]{3,2,1,0:T(8,128)(2,1)} %shard_map.101.rest_0_) | copy-start | bytes 1572868
  45.6 29.0 %copy-start.18 = (s32[8]{0:T(128)S(1)}, s32[8]{0:T(128)}, u32[]{:S(2)}) copy-start(s32[8]{0:T(128)} %counts_ref.11) | copy-start | bytes 100
  45.6 7.8 %collective-permute-start.4 = (bf16[3,32,1536]{2,1,0:T(8,128)(2,1)S(1)}, bf16[3,32,1536]{2,1,0:T(8,128)(2,1)S(1)}, u32[]{:S(2)}, u32[]{:S(2)}) collective-permute-start(bf16[3,32,1536]{2,1,0:T(8,128)(2,1)S(1)} %collective-permute-done), channel_id=1, source_target_pairs={{0,2},{2,3},{3,1},{1,0},{4,6},{6,7},{7,5},{5,4},{8,10},{10,11},{11... | collective-permute-start | bytes 884744 | tf_op jit(solution)/shard_map/ppermute | solution.py:35
  54.5 25.2 %collective-permute-start.7 = (bf16[8,2,128,128]{3,2,1,0:T(8,128)(2,1)S(1)}, bf16[8,2,128,128]{3,2,1,0:T(8,128)(2,1)}, u32[]{:S(2)}, u32[]{:S(2)}) collective-permute-start(bf16[8,2,128,128]{3,2,1,0:T(8,128)(2,1)S(1)} %copy-done.13), channel_id=1, source_target_pairs={{0,4},{4,8},{8,12},{12,16},{16,20},{20,24},{24,28},{28,0},{1,5},{5... | collective-permute-start | bytes 1572872 | tf_op jit(solution)/shard_map/ppermute | solution.py:22
  54.5 25.2 %collective-permute-start.8 = (bf16[8,2,128,128]{3,2,1,0:T(8,128)(2,1)S(1)}, bf16[8,2,128,128]{3,2,1,0:T(8,128)(2,1)}, u32[]{:S(2)}, u32[]{:S(2)}) collective-permute-start(bf16[8,2,128,128]{3,2,1,0:T(8,128)(2,1)S(1)} %copy-done.13), channel_id=1, source_target_pairs={{0,28},{4,0},{8,4},{12,8},{16,12},{20,16},{24,20},{28,24},{1,29},{... | collective-permute-start | bytes 1572872 | tf_op jit(solution)/shard_map/ppermute | solution.py:22
  60.5 14.1 %collective-permute-start.5 = (bf16[4,2,128,128]{3,2,1,0:T(8,128)(2,1)}, bf16[4,2,128,128]{3,2,1,0:T(8,128)(2,1)}, u32[]{:S(2)}, u32[]{:S(2)}) collective-permute-start(bf16[4,2,128,128]{3,2,1,0:T(8,128)(2,1)} %slice.43), channel_id=1, source_target_pairs={{0,4},{4,8},{8,12},{12,16},{16,20},{20,24},{24,28},{28,0},{1,5},{5... | collective-permute-start | bytes 786440 | tf_op jit(solution)/shard_map/ppermute | solution.py:22
  60.5 14.1 %collective-permute-start.6 = (bf16[4,2,128,128]{3,2,1,0:T(8,128)(2,1)}, bf16[4,2,128,128]{3,2,1,0:T(8,128)(2,1)}, u32[]{:S(2)}, u32[]{:S(2)}) collective-permute-start(bf16[4,2,128,128]{3,2,1,0:T(8,128)(2,1)} %slice.44), channel_id=1, source_target_pairs={{0,28},{4,0},{8,4},{12,8},{16,12},{20,16},{24,20},{28,24},{1,29},{... | collective-permute-start | bytes 786440 | tf_op jit(solution)/shard_map/ppermute | solution.py:22
  63.3 16.4 %copy-start.15 = (bf16[8,2,128,128]{3,2,1,0:T(8,128)(2,1)S(1)}, bf16[8,2,128,128]{3,2,1,0:T(8,128)(2,1)}, u32[]{:S(2)}) copy-start(bf16[8,2,128,128]{3,2,1,0:T(8,128)(2,1)} %copy-done.14) | copy-start | bytes 1572868
  79.8 29.0 %collective-permute-start.17 = (bf16[8,2,128,128]{3,2,1,0:T(8,128)(2,1)S(1)}, bf16[8,2,128,128]{3,2,1,0:T(8,128)(2,1)S(1)}, u32[]{:S(2)}, u32[]{:S(2)}) collective-permute-start(bf16[8,2,128,128]{3,2,1,0:T(8,128)(2,1)S(1)} %copy-done.15), channel_id=1, source_target_pairs={{0,4},{4,8},{8,12},{12,16},{16,20},{20,24},{24,28},{28,0},{1,5},{5... | collective-permute-start | bytes 1572872 | tf_op jit(solution)/shard_map/ppermute | solution.py:22
  80.7 28.1 %collective-permute-start.18 = (bf16[8,2,128,128]{3,2,1,0:T(8,128)(2,1)S(1)}, bf16[8,2,128,128]{3,2,1,0:T(8,128)(2,1)S(1)}, u32[]{:S(2)}, u32[]{:S(2)}) collective-permute-start(bf16[8,2,128,128]{3,2,1,0:T(8,128)(2,1)S(1)} %copy-done.15), channel_id=1, source_target_pairs={{0,28},{4,0},{8,4},{12,8},{16,12},{20,16},{24,20},{28,24},{1,29},{... | collective-permute-start | bytes 1572872 | tf_op jit(solution)/shard_map/ppermute | solution.py:22
  83.4 14.6 %collective-permute-start.10 = (bf16[4,2,128,128]{3,2,1,0:T(8,128)(2,1)S(1)}, bf16[4,2,128,128]{3,2,1,0:T(8,128)(2,1)S(1)}, u32[]{:S(2)}, u32[]{:S(2)}) collective-permute-start(bf16[4,2,128,128]{3,2,1,0:T(8,128)(2,1)S(1)} %slice.59), channel_id=1, source_target_pairs={{0,28},{4,0},{8,4},{12,8},{16,12},{20,16},{24,20},{28,24},{1,29},{... | collective-permute-start | bytes 786440 | tf_op jit(solution)/shard_map/ppermute | solution.py:22
  84.5 15.8 %collective-permute-start.9 = (bf16[4,2,128,128]{3,2,1,0:T(8,128)(2,1)S(1)}, bf16[4,2,128,128]{3,2,1,0:T(8,128)(2,1)S(1)}, u32[]{:S(2)}, u32[]{:S(2)}) collective-permute-start(bf16[4,2,128,128]{3,2,1,0:T(8,128)(2,1)S(1)} %slice.58), channel_id=1, source_target_pairs={{0,4},{4,8},{8,12},{12,16},{16,20},{20,24},{24,28},{28,0},{1,5},{5... | collective-permute-start | bytes 786440 | tf_op jit(solution)/shard_map/ppermute | solution.py:22
  85.0 26.5 %collective-permute-start.11 = (bf16[1024,128]{1,0:T(8,128)(2,1)}, bf16[1024,128]{1,0:T(8,128)(2,1)}, u32[]{:S(2)}, u32[]{:S(2)}) collective-permute-start(bf16[1024,128]{1,0:T(8,128)(2,1)} %shard_map.103.rest_0_), channel_id=1, source_target_pairs={{0,2},{2,3},{3,1},{1,0},{4,6},{6,7},{7,5},{5,4},{8,10},{10,11},{11... | collective-permute-start | bytes 786440 | tf_op jit(solution)/shard_map/ppermute | solution.py:35
  105.3 10.5 %collective-permute-start.12 = (bf16[1024,128]{1,0:T(8,128)(2,1)}, bf16[1024,128]{1,0:T(8,128)(2,1)}, u32[]{:S(2)}, u32[]{:S(2)}) collective-permute-start(bf16[1024,128]{1,0:T(8,128)(2,1)} %shard_map.104.rest_1_), channel_id=1, source_target_pairs={{0,2},{2,3},{3,1},{1,0},{4,6},{6,7},{7,5},{5,4},{8,10},{10,11},{11... | collective-permute-start | bytes 786440 | tf_op jit(solution)/shard_map/ppermute | solution.py:35
  108.8 9.3 %collective-permute-start.19 = (bf16[4,2,128,128]{3,2,1,0:T(8,128)(2,1)S(1)}, bf16[4,2,128,128]{3,2,1,0:T(8,128)(2,1)S(1)}, u32[]{:S(2)}, u32[]{:S(2)}) collective-permute-start(bf16[4,2,128,128]{3,2,1,0:T(8,128)(2,1)S(1)} %slice.60), channel_id=1, source_target_pairs={{0,4},{4,8},{8,12},{12,16},{16,20},{20,24},{24,28},{28,0},{1,5},{5... | collective-permute-start | bytes 786440 | tf_op jit(solution)/shard_map/ppermute | solution.py:22
  108.9 10.3 %collective-permute-start.20 = (bf16[4,2,128,128]{3,2,1,0:T(8,128)(2,1)S(1)}, bf16[4,2,128,128]{3,2,1,0:T(8,128)(2,1)S(1)}, u32[]{:S(2)}, u32[]{:S(2)}) collective-permute-start(bf16[4,2,128,128]{3,2,1,0:T(8,128)(2,1)S(1)} %slice.61), channel_id=1, source_target_pairs={{0,28},{4,0},{8,4},{12,8},{16,12},{20,16},{24,20},{28,24},{1,29},{... | collective-permute-start | bytes 786440 | tf_op jit(solution)/shard_map/ppermute | solution.py:22
  111.5 16.3 %collective-permute-start.13 = (bf16[1024,128]{1,0:T(8,128)(2,1)}, bf16[1024,128]{1,0:T(8,128)(2,1)}, u32[]{:S(2)}, u32[]{:S(2)}) collective-permute-start(bf16[1024,128]{1,0:T(8,128)(2,1)} %shard_map.103.rest_0_), channel_id=1, source_target_pairs={{2,0},{3,2},{1,3},{0,1},{6,4},{7,6},{5,7},{4,5},{10,8},{11,10},{9,... | collective-permute-start | bytes 786440 | tf_op jit(solution)/shard_map/ppermute | solution.py:38
  111.5 35.7 %collective-permute-start.15 = (bf16[1024,128]{1,0:T(8,128)(2,1)}, bf16[1024,128]{1,0:T(8,128)(2,1)}, u32[]{:S(2)}, u32[]{:S(2)}) collective-permute-start(bf16[1024,128]{1,0:T(8,128)(2,1)} %collective-permute-done.11.rest_2_), channel_id=1, source_target_pairs={{0,2},{2,3},{3,1},{1,0},{4,6},{6,7},{7,5},{5,4},{8,10},{10,11},{11... | collective-permute-start | bytes 786440 | tf_op jit(solution)/shard_map/ppermute | solution.py:35
  115.8 31.5 %collective-permute-start.14 = (bf16[1024,128]{1,0:T(8,128)(2,1)}, bf16[1024,128]{1,0:T(8,128)(2,1)}, u32[]{:S(2)}, u32[]{:S(2)}) collective-permute-start(bf16[1024,128]{1,0:T(8,128)(2,1)} %shard_map.104.rest_1_), channel_id=1, source_target_pairs={{2,0},{3,2},{1,3},{0,1},{6,4},{7,6},{5,7},{4,5},{10,8},{11,10},{9,... | collective-permute-start | bytes 786440 | tf_op jit(solution)/shard_map/ppermute | solution.py:38
  118.1 29.1 %collective-permute-start.16 = (bf16[1024,128]{1,0:T(8,128)(2,1)}, bf16[1024,128]{1,0:T(8,128)(2,1)}, u32[]{:S(2)}, u32[]{:S(2)}) collective-permute-start(bf16[1024,128]{1,0:T(8,128)(2,1)} %collective-permute-done.12.rest_3_), channel_id=1, source_target_pairs={{0,2},{2,3},{3,1},{1,0},{4,6},{6,7},{7,5},{5,4},{8,10},{10,11},{11... | collective-permute-start | bytes 786440 | tf_op jit(solution)/shard_map/ppermute | solution.py:35
  123.1 20.9 %collective-permute-start.21 = (bf16[1024,128]{1,0:T(8,128)(2,1)}, bf16[1024,128]{1,0:T(8,128)(2,1)S(1)}, u32[]{:S(2)}, u32[]{:S(2)}) collective-permute-start(bf16[1024,128]{1,0:T(8,128)(2,1)} %shard_map.106.rest_0_), channel_id=1, source_target_pairs={{0,2},{2,3},{3,1},{1,0},{4,6},{6,7},{7,5},{5,4},{8,10},{10,11},{11... | collective-permute-start | bytes 786440 | tf_op jit(solution)/shard_map/ppermute | solution.py:35
  127.5 19.7 %copy-start.3 = (bf16[1024,1536]{1,0:T(8,128)(2,1)S(1)}, bf16[1024,1536]{1,0:T(8,128)(2,1)}, u32[]{:S(2)}) copy-start(bf16[1024,1536]{1,0:T(8,128)(2,1)} %state_ref.5) | copy-start | bytes 9437188
  127.9 24.8 %collective-permute-start.22 = (bf16[1024,128]{1,0:T(8,128)(2,1)}, bf16[1024,128]{1,0:T(8,128)(2,1)S(1)}, u32[]{:S(2)}, u32[]{:S(2)}) collective-permute-start(bf16[1024,128]{1,0:T(8,128)(2,1)} %shard_map.106.rest_0_), channel_id=1, source_target_pairs={{2,0},{3,2},{1,3},{0,1},{6,4},{7,6},{5,7},{4,5},{10,8},{11,10},{9,... | collective-permute-start | bytes 786440 | tf_op jit(solution)/shard_map/ppermute | solution.py:38
  144.0 12.0 %collective-permute-start.23 = (bf16[1024,128]{1,0:T(8,128)(2,1)S(1)}, bf16[1024,128]{1,0:T(8,128)(2,1)S(1)}, u32[]{:S(2)}, u32[]{:S(2)}) collective-permute-start(bf16[1024,128]{1,0:T(8,128)(2,1)S(1)} %collective-permute-done.21.rest_1_), channel_id=1, source_target_pairs={{0,2},{2,3},{3,1},{1,0},{4,6},{6,7},{7,5},{5,4},{8,10},{10,11},{11... | collective-permute-start | bytes 786440 | tf_op jit(solution)/shard_map/ppermute | solution.py:35
  152.5 3.5 %copy-start.9 = (bf16[1536,384]{1,0:T(8,128)(2,1)S(1)}, bf16[1536,384]{1,0:T(8,128)(2,1)}, u32[]{:S(2)}) copy-start(bf16[1536,384]{1,0:T(8,128)(2,1)} %wk_ref.7) | copy-start | bytes 3538948
  152.5 3.5 %copy-start.11 = (bf16[1536,384]{1,0:T(8,128)(2,1)S(1)}, bf16[1536,384]{1,0:T(8,128)(2,1)}, u32[]{:S(2)}) copy-start(bf16[1536,384]{1,0:T(8,128)(2,1)} %wv_ref.7) | copy-start | bytes 3538948
  152.5 13.5 %copy-start.20 = (bf16[1536,384]{1,0:T(8,128)(2,1)S(1)}, bf16[1536,384]{1,0:T(8,128)(2,1)}, u32[]{:S(2)}) copy-start(bf16[1536,384]{1,0:T(8,128)(2,1)} %wq_ref.3) | copy-start | bytes 3538948
  156.0 25.1 %slice-start = ((s8[6291456]{0:T(1024)(128)(4,1)}), s8[4194304]{0:T(1024)(128)(4,1)S(1)}, s32[]{:S(2)}) async-start(s8[6291456]{0:T(1024)(128)(4,1)} %bitcast.17), calls=%async_computation.1 | async-start | bytes 8388608
  156.0 25.1 %slice-start.2 = ((s8[6291456]{0:T(1024)(128)(4,1)}), s8[4194304]{0:T(1024)(128)(4,1)S(1)}, s32[]{:S(2)}) async-start(s8[6291456]{0:T(1024)(128)(4,1)} %bitcast.19), calls=%async_computation.3 | async-start | bytes 8388608
  156.0 25.1 %slice-start.1 = ((s8[6291456]{0:T(1024)(128)(4,1)}), s8[2097152]{0:T(1024)(128)(4,1)S(1)}, s32[]{:S(2)}) async-start(s8[6291456]{0:T(1024)(128)(4,1)} %bitcast.17), calls=%async_computation.2 | async-start | bytes 4194304
  156.0 25.1 %slice-start.3 = ((s8[6291456]{0:T(1024)(128)(4,1)}), s8[2097152]{0:T(1024)(128)(4,1)S(1)}, s32[]{:S(2)}) async-start(s8[6291456]{0:T(1024)(128)(4,1)} %bitcast.19), calls=%async_computation.4 | async-start | bytes 4194304
  163.3 15.1 %collective-permute-start.24 = (bf16[8,2,128,128]{3,2,1,0:T(8,128)(2,1)S(1)}, bf16[8,2,128,128]{3,2,1,0:T(8,128)(2,1)S(1)}, u32[]{:S(2)}, u32[]{:S(2)}) collective-permute-start(bf16[8,2,128,128]{3,2,1,0:T(8,128)(2,1)S(1)} %get-tuple-element.42.rest_0_), channel_id=1, source_target_pairs={{0,4},{4,8},{8,12},{12,16},{16,20},{20,24},{24,28},{28,0},{1,5},{5... | collective-permute-start | bytes 1572872 | tf_op jit(solution)/shard_map/ppermute | solution.py:22
  163.4 15.1 %collective-permute-start.25 = (bf16[8,2,128,128]{3,2,1,0:T(8,128)(2,1)S(1)}, bf16[8,2,128,128]{3,2,1,0:T(8,128)(2,1)S(1)}, u32[]{:S(2)}, u32[]{:S(2)}) collective-permute-start(bf16[8,2,128,128]{3,2,1,0:T(8,128)(2,1)S(1)} %get-tuple-element.42.rest_0_), channel_id=1, source_target_pairs={{0,28},{4,0},{8,4},{12,8},{16,12},{20,16},{24,20},{28,24},{1,29},{... | collective-permute-start | bytes 1572872 | tf_op jit(solution)/shard_map/ppermute | solution.py:22
  166.0 15.1 %copy-start.16 = (bf16[8,2,128,128]{3,2,1,0:T(8,128)(2,1)S(1)}, bf16[8,2,128,128]{3,2,1,0:T(8,128)(2,1)}, u32[]{:S(2)}) copy-start(bf16[8,2,128,128]{3,2,1,0:T(8,128)(2,1)} %copy-done.14) | copy-start | bytes 1572868
  178.4 23.1 %collective-permute-start.28 = (bf16[8,2,128,128]{3,2,1,0:T(8,128)(2,1)S(1)}, bf16[8,2,128,128]{3,2,1,0:T(8,128)(2,1)S(1)}, u32[]{:S(2)}, u32[]{:S(2)}) collective-permute-start(bf16[8,2,128,128]{3,2,1,0:T(8,128)(2,1)S(1)} %get-tuple-element.46.rest_0_), channel_id=1, source_target_pairs={{0,4},{4,8},{8,12},{12,16},{16,20},{20,24},{24,28},{28,0},{1,5},{5... | collective-permute-start | bytes 1572872 | tf_op jit(solution)/shard_map/ppermute | solution.py:22
  178.4 23.1 %collective-permute-start.29 = (bf16[8,2,128,128]{3,2,1,0:T(8,128)(2,1)S(1)}, bf16[8,2,128,128]{3,2,1,0:T(8,128)(2,1)S(1)}, u32[]{:S(2)}, u32[]{:S(2)}) collective-permute-start(bf16[8,2,128,128]{3,2,1,0:T(8,128)(2,1)S(1)} %get-tuple-element.46.rest_0_), channel_id=1, source_target_pairs={{0,28},{4,0},{8,4},{12,8},{16,12},{20,16},{24,20},{28,24},{1,29},{... | collective-permute-start | bytes 1572872 | tf_op jit(solution)/shard_map/ppermute | solution.py:22
  187.7 6.7 %collective-permute-start.27 = (bf16[4,2,128,128]{3,2,1,0:T(8,128)(2,1)S(1)}, bf16[4,2,128,128]{3,2,1,0:T(8,128)(2,1)S(1)}, u32[]{:S(2)}, u32[]{:S(2)}) collective-permute-start(bf16[4,2,128,128]{3,2,1,0:T(8,128)(2,1)S(1)} %slice.51), channel_id=1, source_target_pairs={{0,28},{4,0},{8,4},{12,8},{16,12},{20,16},{24,20},{28,24},{1,29},{... | collective-permute-start | bytes 786440 | tf_op jit(solution)/shard_map/ppermute | solution.py:22
  187.8 10.5 %collective-permute-start.26 = (bf16[4,2,128,128]{3,2,1,0:T(8,128)(2,1)S(1)}, bf16[4,2,128,128]{3,2,1,0:T(8,128)(2,1)S(1)}, u32[]{:S(2)}, u32[]{:S(2)}) collective-permute-start(bf16[4,2,128,128]{3,2,1,0:T(8,128)(2,1)S(1)} %slice.50), channel_id=1, source_target_pairs={{0,4},{4,8},{8,12},{12,16},{16,20},{20,24},{24,28},{28,0},{1,5},{5... | collective-permute-start | bytes 786440 | tf_op jit(solution)/shard_map/ppermute | solution.py:22
  201.6 15.2 %collective-permute-start.38 = (bf16[8,2,128,128]{3,2,1,0:T(8,128)(2,1)S(1)}, bf16[8,2,128,128]{3,2,1,0:T(8,128)(2,1)S(1)}, u32[]{:S(2)}, u32[]{:S(2)}) collective-permute-start(bf16[8,2,128,128]{3,2,1,0:T(8,128)(2,1)S(1)} %get-tuple-element.48.rest_0_), channel_id=1, source_target_pairs={{0,4},{4,8},{8,12},{12,16},{16,20},{20,24},{24,28},{28,0},{1,5},{5... | collective-permute-start | bytes 1572872 | tf_op jit(solution)/shard_map/ppermute | solution.py:22
  201.7 15.2 %collective-permute-start.39 = (bf16[8,2,128,128]{3,2,1,0:T(8,128)(2,1)S(1)}, bf16[8,2,128,128]{3,2,1,0:T(8,128)(2,1)S(1)}, u32[]{:S(2)}, u32[]{:S(2)}) collective-permute-start(bf16[8,2,128,128]{3,2,1,0:T(8,128)(2,1)S(1)} %get-tuple-element.48.rest_0_), channel_id=1, source_target_pairs={{0,28},{4,0},{8,4},{12,8},{16,12},{20,16},{24,20},{28,24},{1,29},{... | collective-permute-start | bytes 1572872 | tf_op jit(solution)/shard_map/ppermute | solution.py:22
  204.3 18.1 %collective-permute-start.30 = (bf16[4,2,128,128]{3,2,1,0:T(8,128)(2,1)S(1)}, bf16[4,2,128,128]{3,2,1,0:T(8,128)(2,1)S(1)}, u32[]{:S(2)}, u32[]{:S(2)}) collective-permute-start(bf16[4,2,128,128]{3,2,1,0:T(8,128)(2,1)S(1)} %slice.62), channel_id=1, source_target_pairs={{0,4},{4,8},{8,12},{12,16},{16,20},{20,24},{24,28},{28,0},{1,5},{5... | collective-permute-start | bytes 786440 | tf_op jit(solution)/shard_map/ppermute | solution.py:22
  204.4 18.0 %collective-permute-start.31 = (bf16[4,2,128,128]{3,2,1,0:T(8,128)(2,1)S(1)}, bf16[4,2,128,128]{3,2,1,0:T(8,128)(2,1)S(1)}, u32[]{:S(2)}, u32[]{:S(2)}) collective-permute-start(bf16[4,2,128,128]{3,2,1,0:T(8,128)(2,1)S(1)} %slice.63), channel_id=1, source_target_pairs={{0,28},{4,0},{8,4},{12,8},{16,12},{20,16},{24,20},{28,24},{1,29},{... | collective-permute-start | bytes 786440 | tf_op jit(solution)/shard_map/ppermute | solution.py:22
  216.8 10.9 %collective-permute-start.40 = (bf16[4,2,128,128]{3,2,1,0:T(8,128)(2,1)S(1)}, bf16[4,2,128,128]{3,2,1,0:T(8,128)(2,1)S(1)}, u32[]{:S(2)}, u32[]{:S(2)}) collective-permute-start(bf16[4,2,128,128]{3,2,1,0:T(8,128)(2,1)S(1)} %slice.64), channel_id=1, source_target_pairs={{0,4},{4,8},{8,12},{12,16},{16,20},{20,24},{24,28},{28,0},{1,5},{5... | collective-permute-start | bytes 786440 | tf_op jit(solution)/shard_map/ppermute | solution.py:22
  216.9 10.8 %collective-permute-start.41 = (bf16[4,2,128,128]{3,2,1,0:T(8,128)(2,1)S(1)}, bf16[4,2,128,128]{3,2,1,0:T(8,128)(2,1)S(1)}, u32[]{:S(2)}, u32[]{:S(2)}) collective-permute-start(bf16[4,2,128,128]{3,2,1,0:T(8,128)(2,1)S(1)} %slice.65), channel_id=1, source_target_pairs={{0,28},{4,0},{8,4},{12,8},{16,12},{20,16},{24,20},{28,24},{1,29},{... | collective-permute-start | bytes 786440 | tf_op jit(solution)/shard_map/ppermute | solution.py:22
  219.6 14.0 %collective-permute-start.32 = (bf16[1024,128]{1,0:T(8,128)(2,1)S(1)}, bf16[1024,128]{1,0:T(8,128)(2,1)S(1)}, u32[]{:S(2)}, u32[]{:S(2)}) collective-permute-start(bf16[1024,128]{1,0:T(8,128)(2,1)S(1)} %shard_map.110.rest_0_), channel_id=1, source_target_pairs={{0,2},{2,3},{3,1},{1,0},{4,6},{6,7},{7,5},{5,4},{8,10},{10,11},{11... | collective-permute-start | bytes 786440 | tf_op jit(solution)/shard_map/ppermute | solution.py:35
  225.7 11.0 %collective-permute-start.33 = (bf16[1024,128]{1,0:T(8,128)(2,1)S(1)}, bf16[1024,128]{1,0:T(8,128)(2,1)S(1)}, u32[]{:S(2)}, u32[]{:S(2)}) collective-permute-start(bf16[1024,128]{1,0:T(8,128)(2,1)S(1)} %shard_map.111.rest_1_), channel_id=1, source_target_pairs={{0,2},{2,3},{3,1},{1,0},{4,6},{6,7},{7,5},{5,4},{8,10},{10,11},{11... | collective-permute-start | bytes 786440 | tf_op jit(solution)/shard_map/ppermute | solution.py:35
  227.4 21.4 %collective-permute-start.34 = (bf16[1024,128]{1,0:T(8,128)(2,1)S(1)}, bf16[1024,128]{1,0:T(8,128)(2,1)S(1)}, u32[]{:S(2)}, u32[]{:S(2)}) collective-permute-start(bf16[1024,128]{1,0:T(8,128)(2,1)S(1)} %shard_map.110.rest_0_), channel_id=1, source_target_pairs={{2,0},{3,2},{1,3},{0,1},{6,4},{7,6},{5,7},{4,5},{10,8},{11,10},{9,... | collective-permute-start | bytes 786440 | tf_op jit(solution)/shard_map/ppermute | solution.py:38
  231.0 17.9 %collective-permute-start.42 = (bf16[1024,128]{1,0:T(8,128)(2,1)S(1)}, bf16[1024,128]{1,0:T(8,128)(2,1)S(1)}, u32[]{:S(2)}, u32[]{:S(2)}) collective-permute-start(bf16[1024,128]{1,0:T(8,128)(2,1)S(1)} %shard_map.113.rest_0_), channel_id=1, source_target_pairs={{0,2},{2,3},{3,1},{1,0},{4,6},{6,7},{7,5},{5,4},{8,10},{10,11},{11... | collective-permute-start | bytes 786440 | tf_op jit(solution)/shard_map/ppermute | solution.py:35
  233.7 19.9 %collective-permute-start.36 = (bf16[1024,128]{1,0:T(8,128)(2,1)S(1)}, bf16[1024,128]{1,0:T(8,128)(2,1)S(1)}, u32[]{:S(2)}, u32[]{:S(2)}) collective-permute-start(bf16[1024,128]{1,0:T(8,128)(2,1)S(1)} %collective-permute-done.32.rest_2_), channel_id=1, source_target_pairs={{0,2},{2,3},{3,1},{1,0},{4,6},{6,7},{7,5},{5,4},{8,10},{10,11},{11... | collective-permute-start | bytes 786440 | tf_op jit(solution)/shard_map/ppermute | solution.py:35
  234.1 26.0 %collective-permute-start.35 = (bf16[1024,128]{1,0:T(8,128)(2,1)S(1)}, bf16[1024,128]{1,0:T(8,128)(2,1)S(1)}, u32[]{:S(2)}, u32[]{:S(2)}) collective-permute-start(bf16[1024,128]{1,0:T(8,128)(2,1)S(1)} %shard_map.111.rest_1_), channel_id=1, source_target_pairs={{2,0},{3,2},{1,3},{0,1},{6,4},{7,6},{5,7},{4,5},{10,8},{11,10},{9,... | collective-permute-start | bytes 786440 | tf_op jit(solution)/shard_map/ppermute | solution.py:38
  236.7 28.1 %collective-permute-start.37 = (bf16[1024,128]{1,0:T(8,128)(2,1)S(1)}, bf16[1024,128]{1,0:T(8,128)(2,1)S(1)}, u32[]{:S(2)}, u32[]{:S(2)}) collective-permute-start(bf16[1024,128]{1,0:T(8,128)(2,1)S(1)} %collective-permute-done.33.rest_3_), channel_id=1, source_target_pairs={{0,2},{2,3},{3,1},{1,0},{4,6},{6,7},{7,5},{5,4},{8,10},{10,11},{11... | collective-permute-start | bytes 786440 | tf_op jit(solution)/shard_map/ppermute | solution.py:35
  248.9 20.4 %collective-permute-start.43 = (bf16[1024,128]{1,0:T(8,128)(2,1)S(1)}, bf16[1024,128]{1,0:T(8,128)(2,1)S(1)}, u32[]{:S(2)}, u32[]{:S(2)}) collective-permute-start(bf16[1024,128]{1,0:T(8,128)(2,1)S(1)} %shard_map.113.rest_0_), channel_id=1, source_target_pairs={{2,0},{3,2},{1,3},{0,1},{6,4},{7,6},{5,7},{4,5},{10,8},{11,10},{9,... | collective-permute-start | bytes 786440 | tf_op jit(solution)/shard_map/ppermute | solution.py:38
  248.9 22.5 %collective-permute-start.44 = (bf16[1024,128]{1,0:T(8,128)(2,1)S(1)}, bf16[1024,128]{1,0:T(8,128)(2,1)S(1)}, u32[]{:S(2)}, u32[]{:S(2)}) collective-permute-start(bf16[1024,128]{1,0:T(8,128)(2,1)S(1)} %collective-permute-done.42.rest_1_), channel_id=1, source_target_pairs={{0,2},{2,3},{3,1},{1,0},{4,6},{6,7},{7,5},{5,4},{8,10},{10,11},{11... | collective-permute-start | bytes 786440 | tf_op jit(solution)/shard_map/ppermute | solution.py:35
  (9 other events, 12.6 us)
Sparse Core Ops, SparseCore 0:
  54.6 40.8 all-gather.2

commit v4 on v3

v4 whole, which is shorter than its diff:
```python
import functools
import math

import jax
import jax.numpy as jnp
from jax import lax
from jax.experimental import pallas as pl
from jax.experimental.pallas import tpu as pltpu
from jax.sharding import PartitionSpec as P

HD = 128
BLK = 128
STEPS = 2
TILE = 256
COST = 3.0
R1PIN = 3
ATT_COST = 0.0
PART_COST = 0.0
PAST_VMEM = 52
REST_VMEM = (62, 16)
CHUNKS = ((0,), (1,), (2,))
MIB = 1024 * 1024
SCALE = math.log2(math.e) / math.sqrt(HD)


def sent(value, to):
    count = lax.axis_size("space")
    return lax.ppermute(value, "space", [(i, to(i, count) % count) for i in range(count)])


def across(i, count):
    return i + 1 if i % 2 else i - 1


def beyond(i, count):
    return i - 2 if i % 2 else i + 2


def beside(i, count):
    return i ^ 1


def opposite(i, count):
    return i + count // 2


def turned(value, axis, hops):
    count = lax.axis_size(axis)
    order = list(range(0, count, 2)) + list(range(1, count, 2))[::-1]
    return lax.ppermute(value, axis, [(order[i], order[(i + hops) % count]) for i in range(count)])


def around(value, axis, then=()):
    came = [value]
    for hop in range(1, lax.axis_size(axis)):
        sign = 1 if hop % 2 == 1 else -1
        came.append(turned(came[0] if hop <= 2 else after(came[hop - 2], *then), axis, sign))
    return came


def after(value, *others):
    return lax.optimization_barrier((value,) + others)[0]


def call(body, grid, in_specs, out_specs, out_shape, vmem, scratch=(), prefetch=0, micros=0.0):
    return pl.pallas_call(
        body,
        grid_spec=pltpu.PrefetchScalarGridSpec(
            num_scalar_prefetch=prefetch,
            grid=grid,
            in_specs=in_specs,
            out_specs=out_specs,
            scratch_shapes=list(scratch),
        ),
        out_shape=out_shape,
        compiler_params=pltpu.CompilerParams(
            dimension_semantics=("arbitrary",) * len(grid), vmem_limit_bytes=vmem * MIB
        ),
        cost_estimate=pl.CostEstimate(flops=int(COST * micros * 1.15e9), bytes_accessed=0, transcendentals=0),
    )


def dot(a, b):
    return jnp.dot(a, b, preferred_element_type=jnp.float32)


def normalize(state, gain):
    meansq = jnp.mean(state * state, axis=-1, keepdims=True)
    return (state * lax.rsqrt(meansq + 1e-05) * gain).astype(jnp.bfloat16)


def store_blocks(kv_ref, at, key, value):
    for block in range(key.shape[0] // BLK):
        rows = slice(block * BLK, (block + 1) * BLK)
        kv_ref[block, at, 0] = key[rows].astype(jnp.bfloat16)
        kv_ref[block, at, 1] = value[rows].T.astype(jnp.bfloat16)


def first_body(state_ref, gain_ref, wk_ref, wv_ref, kv_ref, w_scr):
    @pl.when(pl.program_id(0) == 0)
    def _():
        w_scr[:, :HD] = wk_ref[...]
        w_scr[:, HD:] = wv_ref[...]

    both = dot(normalize(state_ref[...].astype(jnp.float32), gain_ref[...]), w_scr[...])
    store_blocks(kv_ref, 0, both[:, :HD], both[:, HD:])


def first_projection(state, gain, w_key, w_value):
    rows, width = state.shape
    per_tile = TILE // BLK
    return call(
        first_body,
        (rows // TILE,),
        [
            pl.BlockSpec((TILE, width), lambda i: (i, 0)),
            pl.BlockSpec((width,), lambda i: (0,)),
            pl.BlockSpec((width, HD), lambda i: (0, 0)),
            pl.BlockSpec((width, HD), lambda i: (0, 0)),
        ],
        pl.BlockSpec((per_tile, 1, 2, BLK, HD), lambda i: (i, 0, 0, 0, 0)),
        jax.ShapeDtypeStruct((rows // BLK, 1, 2, BLK, HD), jnp.bfloat16),
        60,
        scratch=[pltpu.VMEM((width, 2 * HD), jnp.bfloat16)],
        micros=5.0,
    )(state, gain, w_key, w_value)


def rest_body(heads, state_ref, gain_ref, wq_ref, wk_ref, wv_ref, *outs):
    normed = normalize(state_ref[...].astype(jnp.float32), gain_ref[...])
    key = dot(normed, wk_ref[:, HD:])
    value = dot(normed, wv_ref[:, HD:])
    for chunk, kv_ref in zip(CHUNKS[1:], outs, strict=False):
        for at, head in enumerate(chunk):
            cols = slice((head - 1) * HD, head * HD)
            store_blocks(kv_ref, at, key[:, cols], value[:, cols])
    query = dot(normed, wq_ref[...])
    for block in range(TILE // BLK):
        for head in range(heads):
            part = query[block * BLK : (block + 1) * BLK, head * HD : (head + 1) * HD]
            outs[-1][block, head] = part.T.astype(jnp.bfloat16)


def rest_projection(state, gain, w_query, w_key, w_value, vmem):
    rows, width = state.shape
    local = w_query.shape[1]
    heads = local // HD
    per_tile = TILE // BLK
    full = pl.BlockSpec((width, local), lambda i: (0, 0))
    return call(
        functools.partial(rest_body, heads),
        (rows // TILE,),
        [
            pl.BlockSpec((TILE, width), lambda i: (i, 0)),
            pl.BlockSpec((width,), lambda i: (0,)),
            full,
            full,
            full,
        ],
        [pl.BlockSpec((per_tile, len(c), 2, BLK, HD), lambda i: (i, 0, 0, 0, 0)) for c in CHUNKS[1:]]
        + [pl.BlockSpec((per_tile, heads, HD, BLK), lambda i: (i, 0, 0, 0))],
        [jax.ShapeDtypeStruct((rows // BLK, len(c), 2, BLK, HD), jnp.bfloat16) for c in CHUNKS[1:]]
        + [jax.ShapeDtypeStruct((rows // BLK, heads, HD, BLK), jnp.bfloat16)],
        vmem,
        micros=5.0,
    )(state, gain, w_query, w_key, w_value)


def same_token():
    return lax.broadcasted_iota(jnp.int32, (BLK, BLK), 0) == lax.broadcasted_iota(jnp.int32, (BLK, BLK), 1)


def past_body(frames, heads, newer, qt_ref, ck_hbm, cv_hbm, *rest):
    last, (acc_ref, stat_ref, slots, sems) = rest[:-4], rest[-4:]
    place = {head: (c, at) for c, chunk in enumerate(CHUNKS) for at, head in enumerate(chunk)}
    tile = pl.program_id(0)

    def copies(tile):
        rows = pl.ds(pl.multiple_of(tile * TILE, TILE), TILE)
        return [
            pltpu.make_async_copy(cache.at[:, rows], slots.at[tile, which], sems.at[tile, which])
            for which, cache in enumerate((ck_hbm, cv_hbm))
        ]

    @pl.when(tile == 0)
    def _():
        for ahead in range(slots.shape[0]):
            for copy in copies(ahead):
                copy.start()

    for copy in copies(tile):
        copy.wait()
    ck_ref, cv_ref = (slots.at[tile, which] for which in range(2))
    eye = same_token()
    none = jnp.zeros((BLK, BLK), jnp.bfloat16)
    for block in range(qt_ref.shape[0]):
        rows = slice(block * BLK, (block + 1) * BLK)
        for head in range(heads):
            cols = slice(head * HD, (head + 1) * HD)
            keys = [ck_ref[frame, rows, cols] for frame in range(frames)]
            if newer:
                keys[0] = last[place[head][0]][block, place[head][1], 0]
            pairs = dot(jnp.concatenate(keys, axis=0), qt_ref[block, head])
            scores = [
                jnp.sum(jnp.where(eye, pairs[frame * BLK : (frame + 1) * BLK], 0.0), axis=0, keepdims=True)
                for frame in range(frames)
            ]
            top = functools.reduce(jnp.maximum, scores)
            weights = [jnp.exp2((score - top) * SCALE) for score in scores]
            stat_ref[block, head, 0:1] = top
            stat_ref[block, head, 1:2] = functools.reduce(jnp.add, weights)
            spread = [jnp.where(eye, weight, 0.0).astype(jnp.bfloat16) for weight in weights]
            if newer:
                spread[0] = none
            values = jnp.concatenate([cv_ref[frame, rows, cols] for frame in range(frames)], axis=0)
            mixed = dot(jnp.concatenate(spread, axis=1), values).T
            if newer:
                mixed = mixed + last[place[head][0]][block, place[head][1], 1].astype(jnp.float32) * weights[0]
            acc_ref[block, head] = mixed


def attend_past(queries, cache_key, cache_value, last):
    blocks, heads = queries.shape[:2]
    frames, rows, local = cache_key.shape
    per_tile = TILE // BLK
    cached = pl.BlockSpec(memory_space=pltpu.HBM)
    return call(
        functools.partial(past_body, frames, heads, len(last) > 0),
        (blocks // per_tile,),
        [pl.BlockSpec((per_tile, heads, HD, BLK), lambda i: (i, 0, 0, 0)), cached, cached]
        + [pl.BlockSpec((per_tile, *piece.shape[1:]), lambda i: (i, 0, 0, 0, 0)) for piece in last],
        [
            pl.BlockSpec((per_tile, heads, HD, BLK), lambda i: (i, 0, 0, 0)),
            pl.BlockSpec((per_tile, heads, 2, BLK), lambda i: (i, 0, 0, 0)),
        ],
        [
            jax.ShapeDtypeStruct((blocks, heads, HD, BLK), jnp.float32),
            jax.ShapeDtypeStruct((blocks, heads, 2, BLK), jnp.float32),
        ],
        PAST_VMEM,
        scratch=[
            pltpu.VMEM((blocks // per_tile, 2, frames, TILE, local), jnp.bfloat16),
            pltpu.SemaphoreType.DMA((blocks // per_tile, 2)),
        ],
        micros=6.0,
    )(queries, cache_key, cache_value, *last)


def attend_body(blocks, slots, inner, where_ref, counts_ref, qt_ref, acc_ref, stat_ref, *rest):
    pieces, (out_ref, window, sem) = rest[:-3], rest[-3:]
    place = 0
    copies = []
    for piece in pieces:
        copies.append(pltpu.make_async_copy(piece, window.at[pl.ds(place, piece.shape[0])], sem.at[len(copies)]))
        place += piece.shape[0]
    for copy in copies:
        copy.start()
    for copy in copies:
        copy.wait()
    for block in range(blocks):
        live = counts_ref[block]
        places = [where_ref[block * slots + slot] for slot in range(slots)]
        for at in range(inner):
            pairs = dot(jnp.concatenate([window[p, at, 0] for p in places], axis=0), qt_ref[block, at])
            scores = [pairs[:BLK]]
            for slot in range(1, slots):
                score = pairs[slot * BLK : (slot + 1) * BLK]
                scores.append(jnp.where(slot < live, score, jnp.float32(-1e30)))
            past_top = stat_ref[block, at, 0:1]
            top = jnp.maximum(functools.reduce(jnp.maximum, scores).max(axis=0, keepdims=True), past_top)
            weights = [jnp.exp2((score - top) * SCALE) for score in scores]
            fade = jnp.exp2((past_top - top) * SCALE)
            total = functools.reduce(jnp.add, weights).sum(axis=0, keepdims=True) + stat_ref[block, at, 1:2] * fade
            share = 1.0 / total
            values = jnp.concatenate([window[p, at, 1] for p in places], axis=1)
            mixed = dot(values, jnp.concatenate([weight.astype(jnp.bfloat16) for weight in weights], axis=0))
            mixed = mixed * share + acc_ref[block, at] * (fade * share)
            rows = slice(block * BLK, (block + 1) * BLK)
            out_ref[rows, at * HD : (at + 1) * HD] = mixed.T.astype(jnp.bfloat16)


def attend(heads, where_block, counts, queries, past, stats, pieces):
    blocks = queries.shape[0]
    rows = blocks * BLK
    slots = where_block.shape[0] // blocks
    inner = len(heads)
    total_blocks = sum(piece.shape[0] for piece in pieces)

    def of_heads(*shape):
        whole = (pl.Element(blocks), pl.Element(inner), pl.Element(shape[0]), pl.Element(shape[1]))
        return pl.BlockSpec(whole, lambda i, *_: (0, heads[0], 0, 0))

    return call(
        functools.partial(attend_body, blocks, slots, inner),
        (1,),
        [of_heads(HD, BLK), of_heads(HD, BLK), of_heads(2, BLK)]
        + [pl.BlockSpec(memory_space=pl.ANY)] * len(pieces),
        pl.BlockSpec((rows, inner * HD), lambda i, *_: (0, 0)),
        jax.ShapeDtypeStruct((rows, inner * HD), jnp.bfloat16),
        12,
        scratch=[
            pltpu.VMEM((total_blocks, inner, 2, BLK, HD), jnp.bfloat16),
            pltpu.SemaphoreType.DMA((len(pieces),)),
        ],
        prefetch=2,
        micros=ATT_COST,
    )(where_block, counts, queries, past, stats, *pieces)


def part_body(count, state_ref, w_ref, *rest):
    pieces, out_ref = rest[:count], rest[count]
    attended = jnp.concatenate([piece[...] for piece in pieces], axis=1)
    out_ref[...] = (state_ref[...].astype(jnp.float32) + dot(attended, w_ref[...])).astype(out_ref.dtype)


def add_heads(state, w_rows, pieces, out_dtype):
    rows, width = state.shape
    return call(
        functools.partial(part_body, len(pieces)),
        (rows // TILE,),
        [pl.BlockSpec((TILE, width), lambda i: (i, 0)), pl.BlockSpec(w_rows.shape, lambda i: (0, 0))]
        + [pl.BlockSpec((TILE, piece.shape[1]), lambda i: (i, 0)) for piece in pieces],
        pl.BlockSpec((TILE, width), lambda i: (i, 0)),
        jax.ShapeDtypeStruct((rows, width), out_dtype),
        18,
        micros=PART_COST,
    )(state, w_rows, *pieces)


def turn_body(count, part_ref, w_ref, gain_ref, wk_ref, wv_ref, *rest):
    pieces, (state_ref, kv_ref, kv_scr) = rest[:count], rest[count:]

    @pl.when(pl.program_id(0) == 0)
    def _():
        kv_scr[:, :HD] = wk_ref[...]
        kv_scr[:, HD:] = wv_ref[...]

    attended = jnp.concatenate([piece[...] for piece in pieces], axis=1)
    state = (part_ref[...] + dot(attended, w_ref[...])).astype(jnp.bfloat16)
    state_ref[...] = state
    both = dot(normalize(state.astype(jnp.float32), gain_ref[...]), kv_scr[...])
    store_blocks(kv_ref, 0, both[:, :HD], both[:, HD:])


def turn(part, w_rows, pieces, gain, w_key, w_value):
    rows, width = part.shape
    per_tile = TILE // BLK
    tile = pl.BlockSpec((TILE, width), lambda i: (i, 0))
    return call(
        functools.partial(turn_body, len(pieces)),
        (rows // TILE,),
        [
            tile,
            pl.BlockSpec(w_rows.shape, lambda i: (0, 0)),
            pl.BlockSpec((width,), lambda i: (0,)),
            pl.BlockSpec((width, HD), lambda i: (0, 0)),
            pl.BlockSpec((width, HD), lambda i: (0, 0)),
        ]
        + [pl.BlockSpec((TILE, piece.shape[1]), lambda i: (i, 0)) for piece in pieces],
        [tile, pl.BlockSpec((per_tile, 1, 2, BLK, HD), lambda i: (i, 0, 0, 0, 0))],
        [
            jax.ShapeDtypeStruct((rows, width), jnp.bfloat16),
            jax.ShapeDtypeStruct((rows // BLK, 1, 2, BLK, HD), jnp.bfloat16),
        ],
        18,
        scratch=[pltpu.VMEM((width, 2 * HD), jnp.bfloat16)],
        micros=7.0,
    )(part, w_rows, gain, w_key, w_value, *pieces)


def facing(kv):
    half = kv.shape[0] // 2
    return lax.dynamic_slice_in_dim(kv, half * (1 - lax.axis_index("space") % 2), half, 0)


def halo(kv):
    return sent(kv, across), sent(facing(kv), beyond), sent(kv, beside)


def fetch_rows(w_out):
    half = lax.axis_size("space") // 2
    local, width = w_out.shape
    me = lax.axis_index("space")
    quarters = w_out.reshape(local // HD, 4, HD // 4, width)
    mine = lax.dynamic_index_in_dim(quarters, me % 2 + 2 * (me // half), 1, keepdims=False)
    return around(mine, "head")[1:]


def share_rows(w_out, fetched, then):
    fetched = jnp.stack(fetched)
    count = lax.axis_size("space")
    half = count // 2
    local, width = w_out.shape
    heads = local // HD
    me = lax.axis_index("space")
    second = sent(fetched, beside)
    third = sent(fetched, opposite)
    fourth = sent(after(third, then), beside)
    odd, upper = me % 2 == 1, me >= half
    near = (jnp.where(odd, second, fetched), jnp.where(odd, fetched, second))
    far = (jnp.where(odd, fourth, third), jnp.where(odd, third, fourth))
    four = [jnp.where(upper, b, a) for a, b in zip(near + far, far + near, strict=True)]
    others = jnp.stack(four, axis=2).reshape(-1, heads, HD, width)
    return jnp.concatenate([w_out.reshape(1, heads, HD, width), others])


def on_device(snapshot, norm_gain, w_query, w_key, w_value, w_out, cache_key, cache_value, pattern, counts):
    tok_rows, width = snapshot.shape
    blocks = tok_rows // BLK
    half = blocks // 2
    count = blocks * lax.axis_size("space")
    me = lax.axis_index("space")
    own_block = jnp.arange(blocks, dtype=jnp.int32)[:, None]
    relative = (pattern - own_block - me * blocks + count // 2) % count - count // 2
    place = own_block + blocks + half + relative
    turn_by = jnp.where(place < half + blocks, 2 * blocks, jnp.where(place < half + 2 * blocks, 0, -2 * blocks))
    end = 3 * blocks + half
    turn_by = jnp.where(place < half, end, jnp.where(place >= end, -end, turn_by))
    where_block = jnp.where(me % 2 == 1, place + turn_by, place).reshape(-1)
    state = snapshot
    kv_first = first_projection(state, norm_gain, w_key, w_value)
    last = []
    for rollout in range(STEPS):
        near = [halo(kv_first)]
        *kv_rest, queries = rest_projection(state, norm_gain, w_query, w_key, w_value, REST_VMEM[rollout])
        kv = [kv_first] + list(kv_rest)
        near += [halo(piece) for piece in kv_rest]
        if rollout == 0:
            fetched = fetch_rows(w_out)
            queries = after(queries, *fetched[:2])
        past, stats = attend_past(queries, cache_key, cache_value, last)
        came = []
        attended = past
        for chunk, of_chunk in enumerate(CHUNKS):
            next_pair, further, other = near[chunk]
            shared = sent(facing(after(next_pair, attended)), beside)
            own = kv[chunk]
            if chunk == 0 and rollout == 0:
                own = after(own, *fetched)
            if chunk >= 1:
                own = after(own, *came[-1][1:R1PIN])
            if chunk >= 2:
                own = after(own, *came[-2][2:])
            pieces = (further, next_pair, own, other, shared)
            attended = attend(of_chunk, where_block, counts, queries, past, stats, pieces)
            if rollout == 0 and chunk == 0:
                fetched = [after(piece, attended) for piece in fetched]
            came.append(around(attended, "head", came[-1][2:] if came else ()))
        if rollout == 0:
            rows_of = share_rows(w_out, fetched, came[-1][1])
        if rollout == 0:
            w_early = rows_of[:, : CHUNKS[-1][0]].reshape(-1, width)
            w_last = rows_of[:, CHUNKS[-1][0] :].reshape(-1, width)
        early = [piece for group in zip(*came[:-1], strict=True) for piece in group]
        part = add_heads(state, w_early, early, jnp.float32)
        if rollout + 1 < STEPS:
            state, kv_first = turn(part, w_last, came[-1], norm_gain, w_key, w_value)
            last = kv
        else:
            state = add_heads(part, w_last, came[-1], jnp.bfloat16)
    return state


def solution(mesh):
    placed = (
        P("space", None),
        P(),
        P(None, "head"),
        P(None, "head"),
        P(None, "head"),
        P("head", None),
        P(None, "space", "head"),
        P(None, "space", "head"),
        P("space", None),
        P("space"),
    )
    return jax.shard_map(
        on_device, mesh=mesh, in_specs=placed, out_specs=P("space", None), check_vma=False
    )
```

time: 282 us -> 232 us (0.82)
  starting transfers between devices: 66.1 us -> 41.4 us
  between operations: 13.9 us -> 0.52 us
  waiting for transfers between devices: 105 us -> 92.3 us
  local copies, waits for them, and re-layouts: 23.3 us -> 15.6 us
  other arithmetic: 1.55 us -> 5.49 us
  Pallas kernels: 72 us -> 75.6 us
    ppermute x45 -> x48, starting transfers between devices: 66.1 us -> 41.4 us  [the longest x21 25.8 us: turned(): lax.ppermute(value, axis, [(order[i], order[(i + hops) % count]) for i in...]
    ppermute x45 -> x48, waiting for transfers between devices: 105 us -> 92.3 us  [the longest x21 78.6 us: turned(): lax.ppermute(value, axis, [(order[i], order[(i + hops) % count]) for i in...]
    slice x12 -> x1, local copies, waits for them, and re-layouts: 5.42 us -> 0.2 us  [on_device(): w_early = rows_of[:, :CHUNKS[-1][0]].reshape(-1, width)]
    pallas_call x2, Pallas kernels: 13.1 us -> 17.5 us  [attend_past(): call(functools.partial(past_body, frames, heads, len(last) > 0), (blocks...]
    another operation x1 -> x3, other arithmetic: 1.01 us -> 4.98 us  [the longest x2 2.73 us: share_rows(): others = jnp.stack(four, axis=2).reshape(-1, heads, HD, width)]
    dynamic_slice x0 -> x12, local copies, waits for them, and re-layouts: none -> 3.65 us  [facing(): lax.dynamic_slice_in_dim(kv, half * (1 - lax.axis_index('space') % 2), ha...]
    unnamed x54 -> x56, local copies, waits for them, and re-layouts: 13.1 us -> 10.7 us
  transfers between devices with their start and end apart: 46 -> 48, of which waited for: 19 -> 18; matrix products, arithmetic and copies ran while one was open for 3% -> 4% of each run, Pallas kernels for 20% -> 27%
where the time goes in v4:
time: 232 us; the launch traced here: 231 us
  waiting for transfers between devices  92.3 us (40%)
  Pallas kernels  75.6 us (33%)
  starting transfers between devices  41.4 us (18%)
  local copies, waits for them, and re-layouts  15.6 us (7%)
  other arithmetic  5.49 us (2%)
    ppermute x21, waiting for transfers between devices, turned(): lax.ppermute(value, axis, [(order[i], order[(i + hops) % count]) for i in...  78.6 us
    ppermute x21, starting transfers between devices, turned(): lax.ppermute(value, axis, [(order[i], order[(i + hops) % count]) for i in...  25.8 us
    pallas_call x6, Pallas kernels, attend(): call(functools.partial(attend_body, blocks, slots, inner), (1,), [of_head...  21.6 us
    pallas_call x2, Pallas kernels, attend_past(): call(functools.partial(past_body, frames, heads, len(last) > 0), (blocks...  17.5 us
    ppermute x27, starting transfers between devices, sent(): lax.ppermute(value, 'space', [(i, to(i, count) % count) for i in range(co...  15.6 us
    ppermute x27, waiting for transfers between devices, sent(): lax.ppermute(value, 'space', [(i, to(i, count) % count) for i in range(co...  13.7 us
    pallas_call x2, Pallas kernels, rest_projection(): call(functools.partial(rest_body, heads), (rows // TILE,), [pl.BlockSpec(...  12.9 us
    pallas_call x3, Pallas kernels, add_heads(): call(functools.partial(part_body, len(pieces)), (rows // TILE,), [pl.Bloc...  11.4 us
  transfers between devices with their start and end apart: 48, of which 18 were waited for; matrix products, arithmetic and copies ran while one was open for 4% of the time, Pallas kernels for 27%

profile of v4, /device:TPU:0, one launch (start us, length us, event | category | flops | bytes accessed | tf_op | source)
XLA Modules:
  0.0 230.9 jit_solution(10294900811903832672)
XLA Ops:
  0.0 1.0 dynamic-slice_bitcast_fusion
  1.0 4.1 %collective-permute-start = (bf16[3,32,1536]{2,1,0:T(8,128)(2,1)S(1)}, bf16[3,32,1536]{2,1,0:T(8,128)(2,1)}, u32[]{:S(2)}, u32[]{:S(2)}) collective-permute-start(bf16[3,32,1536]{2,1,0:T(8,128)(2,1)S(1)} %dynamic-slice_bitcast_fusion), channel_id=1, source_target_pairs={{0,2},{2,3},{3,1},{1,0},{4,6},{6,7},{7,5},{5,4},{8,10},{10,11},{11... | collective-permute-start | bytes 884744 | tf_op jit(solution)/shard_map/ppermute | solution.py:50
  5.1 5.2 %shard_map.102.rest_2_.rest_0_ = bf16[8,1,2,128,128]{4,3,2,1,0:T(8,128)(2,1)} custom-call(bf16[1024,1536]{1,0:T(8,128)(2,1)} %state_ref.5, f32[1536]{0:T(1024)} %gain_ref.7, bf16[1536,384]{1,0:T(8,128)(2,1)} %wk_ref.7, bf16[1536,384]{1,0:T(8,128)(2,1)} %wv_ref.7), custom_call_target="tpu_custom_call" | custom-call | flops 17250000896 | tf_op jit(solution)/shard_map/pallas_call | solution.py:112
  10.3 1.6 collective-permute-start.3
  11.9 1.7 constant_dynamic-slice_fusion.11
  13.6 1.5 collective-permute-start.2
  15.1 7.9 %shard_map.100 = (bf16[8,1,2,128,128]{4,3,2,1,0:T(8,128)(2,1)}, bf16[8,1,2,128,128]{4,3,2,1,0:T(8,128)(2,1)}, bf16[8,3,128,128]{3,2,1,0:T(8,128)(2,1)}) custom-call(bf16[1024,1536]{1,0:T(8,128)(2,1)} %state_ref.5, f32[1536]{0:T(1024)} %gain_ref.7, bf16[1536,384]{1,0:T(8,128)(2,1)} %wq_ref.3, bf16[1536,384]{1,0:T(8,128)(2,1)} %wk_ref.7, bf16[1536,384]{1,0:T(8,128)(2,1)} %wv_ref.7), custom_call_target="tpu_custom_call" | custom-call | flops 17250000896 | tf_op jit(solution)/shard_map/pallas_call | solution.py:150
  23.0 0.9 collective-permute-start.11
  23.9 2.9 %collective-permute-start.4 = (bf16[3,32,1536]{2,1,0:T(8,128)(2,1)}, bf16[3,32,1536]{2,1,0:T(8,128)(2,1)}, u32[]{:S(2)}, u32[]{:S(2)}) collective-permute-start(bf16[3,32,1536]{2,1,0:T(8,128)(2,1)} %collective-permute-done), channel_id=1, source_target_pairs={{0,2},{2,3},{3,1},{1,0},{4,6},{6,7},{7,5},{5,4},{8,10},{10,11},{11... | collective-permute-start | bytes 884744 | tf_op jit(solution)/shard_map/ppermute | solution.py:50
  26.8 1.1 copy-done.3
  28.0 8.1 %shard_map.101 = (f32[8,3,128,128]{3,2,1,0:T(8,128)}, f32[8,3,2,128]{3,2,1,0:T(2,128)S(1)}) custom-call(bf16[8,3,128,128]{3,2,1,0:T(8,128)(2,1)S(1)} %copy-done.3, bf16[8,1024,384]{2,1,0:T(8,128)(2,1)} %ck_hbm.3, bf16[8,1024,384]{2,1,0:T(8,128)(2,1)} %cv_hbm.3), custom_call_target="tpu_custom_call" | custom-call | flops 20700000256 | tf_op jit(solution)/shard_map/pallas_call | solution.py:227
  36.1 1.7 constant_dynamic-slice_fusion.10
  38.5 1.2 collective-permute-done.6.rest_4_
  40.4 1.4 copy-done
  41.8 0.9 copy-done.20
  42.8 4.2 %shard_map.103.rest_0_ = bf16[1024,128]{1,0:T(8,128)(2,1)S(1)} custom-call(s32[64]{0:T(128)S(1)} %reshape.25.where_ref, s32[8]{0:T(128)S(1)} %copy-done.21, bf16[8,3,128,128]{3,2,1,0:T(8,128)(2,1)S(1)} %copy-done.4, f32[8,3,128,128]{3,2,1,0:T(8,128)S(1)} %copy-done, f32[8,3,2,128]{3,2,1,0:T(2,128)S(1)} %get-tuple-element.42.stat_ref, ...), custom_call_target="tpu_custom_call" | custom-call | tf_op jit(solution)/shard_map/pallas_call | solution.py:293
  48.4 1.3 collective-permute-start.9
  49.7 1.4 collective-permute-start.13
  51.1 10.2 %collective-permute-done.12.rest_2_ = bf16[1024,128]{1,0:T(8,128)(2,1)S(1)} collective-permute-done((bf16[1024,128]{1,0:T(8,128)(2,1)S(1)}, bf16[1024,128]{1,0:T(8,128)(2,1)S(1)}, u32[]{:S(2)}, u32[]{:S(2)}) %collective-permute-start.12) | collective-permute-done | bytes 262176 | tf_op jit(solution)/shard_map/ppermute | solution.py:50
  61.2 2.3 pad_maximum_fusion.2
  64.0 3.1 %shard_map.104.rest_1_ = bf16[1024,128]{1,0:T(8,128)(2,1)S(1)} custom-call(s32[64]{0:T(128)S(1)} %reshape.25.where_ref, s32[8]{0:T(128)S(1)} %copy-done.21, bf16[8,3,128,128]{3,2,1,0:T(8,128)(2,1)S(1)} %copy-done.4, f32[8,3,128,128]{3,2,1,0:T(8,128)S(1)} %copy-done.1, f32[8,3,2,128]{3,2,1,0:T(2,128)S(1)} %get-tuple-element.42.stat_ref, ...), custom_call_target="tpu_custom_call" | custom-call | tf_op jit(solution)/shard_map/pallas_call | solution.py:293
  67.5 1.8 collective-permute-start.17
  69.3 1.2 collective-permute-start.18
  70.5 11.5 %collective-permute-done.16.rest_3_ = bf16[1024,128]{1,0:T(8,128)(2,1)S(1)} collective-permute-done((bf16[1024,128]{1,0:T(8,128)(2,1)S(1)}, bf16[1024,128]{1,0:T(8,128)(2,1)S(1)}, u32[]{:S(2)}, u32[]{:S(2)}) %collective-permute-start.16) | collective-permute-done | bytes 262176 | tf_op jit(solution)/shard_map/ppermute | solution.py:50
  82.0 1.5 collective-permute-start.8
  83.5 3.3 %collective-permute-done.18.rest_6_ = bf16[1024,128]{1,0:T(8,128)(2,1)S(1)} collective-permute-done((bf16[1024,128]{1,0:T(8,128)(2,1)S(1)}, bf16[1024,128]{1,0:T(8,128)(2,1)S(1)}, u32[]{:S(2)}, u32[]{:S(2)}) %collective-permute-start.18) | collective-permute-done | bytes 262176 | tf_op jit(solution)/shard_map/ppermute | solution.py:50
  86.8 2.4 %collective-permute-done.8.rest_0_ = bf16[4,1,2,128,128]{4,3,2,1,0:T(8,128)(2,1)S(1)} collective-permute-done((bf16[4,1,2,128,128]{4,3,2,1,0:T(8,128)(2,1)S(1)}, bf16[4,1,2,128,128]{4,3,2,1,0:T(8,128)(2,1)S(1)}, u32[]{:S(2)}, u32[]{:S(2)}) %collective-permute-start.8) | collective-permute-done | bytes 262176 | tf_op jit(solution)/shard_map/ppermute | solution.py:28
  89.3 3.8 %shard_map.105.rest_0_ = bf16[1024,128]{1,0:T(8,128)(2,1)} custom-call(s32[64]{0:T(128)S(1)} %reshape.25.where_ref, s32[8]{0:T(128)S(1)} %copy-done.21, bf16[8,3,128,128]{3,2,1,0:T(8,128)(2,1)S(1)} %copy-done.4, f32[8,3,128,128]{3,2,1,0:T(8,128)S(1)} %copy-done.1, f32[8,3,2,128]{3,2,1,0:T(2,128)S(1)} %get-tuple-element.42.stat_ref, ...), custom_call_target="tpu_custom_call" | custom-call | tf_op jit(solution)/shard_map/pallas_call | solution.py:293
  93.3 6.5 %collective-permute-done.21.rest_1_ = bf16[1024,128]{1,0:T(8,128)(2,1)S(1)} collective-permute-done((bf16[1024,128]{1,0:T(8,128)(2,1)}, bf16[1024,128]{1,0:T(8,128)(2,1)S(1)}, u32[]{:S(2)}, u32[]{:S(2)}) %collective-permute-start.21) | collective-permute-done | bytes 262176 | tf_op jit(solution)/shard_map/ppermute | solution.py:50
  99.8 1.2 collective-permute-start.24
  101.9 6.7 %collective-permute-done.24.rest_7_ = bf16[1024,128]{1,0:T(8,128)(2,1)S(1)} collective-permute-done((bf16[1024,128]{1,0:T(8,128)(2,1)S(1)}, bf16[1024,128]{1,0:T(8,128)(2,1)S(1)}, u32[]{:S(2)}, u32[]{:S(2)}) %collective-permute-start.24) | collective-permute-done | bytes 262176 | tf_op jit(solution)/shard_map/ppermute | solution.py:50
  108.6 2.5 %collective-permute-start.26 = (bf16[1024,128]{1,0:T(8,128)(2,1)S(1)}, bf16[1024,128]{1,0:T(8,128)(2,1)S(1)}, u32[]{:S(2)}, u32[]{:S(2)}) collective-permute-start(bf16[1024,128]{1,0:T(8,128)(2,1)S(1)} %collective-permute-done.21.rest_1_), channel_id=1, source_target_pairs={{0,2},{2,3},{3,1},{1,0},{4,6},{6,7},{7,5},{5,4},{8,10},{10,11},{11... | collective-permute-start | bytes 786440 | tf_op jit(solution)/shard_map/ppermute | solution.py:50
  111.1 2.2 select_bitcast_fusion.3
  115.2 1.6 copy-done.7
  117.0 3.9 %shard_map.106.part_ref = f32[1024,1536]{1,0:T(8,128)S(1)} custom-call(bf16[1024,1536]{1,0:T(8,128)(2,1)S(1)} %copy-done.7, bf16[1024,1536]{1,0:T(8,128)(2,1)S(1)} %bitcast.30, bf16[1024,128]{1,0:T(8,128)(2,1)S(1)} %shard_map.103.rest_0_, bf16[1024,128]{1,0:T(8,128)(2,1)S(1)} %copy-done.12, bf16[1024,128]{1,0:T(8,128)(2,1)S(1)} %copy-done.14, ...), custom_call_target="tpu_custom_call" | custom-call | tf_op jit(solution)/shard_map/pallas_call | solution.py:318
  121.2 1.1 copy-done.23
  122.6 7.1 %shard_map.107 = (bf16[1024,1536]{1,0:T(8,128)(2,1)S(1)}, bf16[8,1,2,128,128]{4,3,2,1,0:T(8,128)(2,1)S(1)}) custom-call(f32[1024,1536]{1,0:T(8,128)S(1)} %shard_map.106.part_ref, bf16[512,1536]{1,0:T(8,128)(2,1)S(1)} %bitcast.32, f32[1536]{0:T(1024)S(1)} %copy-done.25, bf16[1536,384]{1,0:T(8,128)(2,1)S(1)} %copy-done.23, bf16[1536,384]{1,0:T(8,128)(2,1)S(1)} %copy-done.24, ...), custom_call_target="tpu_custom_call" | custom-call | flops 24149999616 | tf_op jit(solution)/shard_map/pallas_call | solution.py:349
  129.8 1.6 collective-permute-start.29
  131.4 4.9 %shard_map.108 = (bf16[8,1,2,128,128]{4,3,2,1,0:T(8,128)(2,1)S(1)}, bf16[8,1,2,128,128]{4,3,2,1,0:T(8,128)(2,1)S(1)}, bf16[8,3,128,128]{3,2,1,0:T(8,128)(2,1)S(1)}) custom-call(bf16[1024,1536]{1,0:T(8,128)(2,1)S(1)} %get-tuple-element.58.state_ref, f32[1536]{0:T(1024)S(1)} %copy-done.25, bf16[1536,384]{1,0:T(8,128)(2,1)S(1)} %copy-done.22, ...), custom_call_target="tpu_custom_call" | custom-call | flops 17250000896 | tf_op jit(solution)/shard_map/pallas_call | solution.py:150
  136.3 0.9 copy-done.5
  137.3 9.4 %shard_map.109 = (f32[8,3,128,128]{3,2,1,0:T(8,128)}, f32[8,3,2,128]{3,2,1,0:T(2,128)S(1)}) custom-call(bf16[8,3,128,128]{3,2,1,0:T(8,128)(2,1)} %copy-done.5, bf16[8,1024,384]{2,1,0:T(8,128)(2,1)} %ck_hbm.3, bf16[8,1024,384]{2,1,0:T(8,128)(2,1)} %cv_hbm.3, bf16[8,1,2,128,128]{4,3,2,1,0:T(8,128)(2,1)S(1)} %copy-done.8, ...), custom_call_target="tpu_custom_call" | custom-call | flops 20700000256 | tf_op jit(solution)/shard_map/pallas_call | solution.py:227
  146.7 1.5 collective-permute-start.27
  148.9 8.0 %collective-permute-done.27.rest_0_ = bf16[4,1,2,128,128]{4,3,2,1,0:T(8,128)(2,1)S(1)} collective-permute-done((bf16[4,1,2,128,128]{4,3,2,1,0:T(8,128)(2,1)S(1)}, bf16[4,1,2,128,128]{4,3,2,1,0:T(8,128)(2,1)S(1)}, u32[]{:S(2)}, u32[]{:S(2)}) %collective-permute-start.27) | collective-permute-done | bytes 262176 | tf_op jit(solution)/shard_map/ppermute | solution.py:28
  156.9 1.4 copy-done.2
  158.3 4.1 %shard_map.110.rest_0_ = bf16[1024,128]{1,0:T(8,128)(2,1)S(1)} custom-call(s32[64]{0:T(128)S(1)} %reshape.25.where_ref, s32[8]{0:T(128)S(1)} %copy-done.21, bf16[8,3,128,128]{3,2,1,0:T(8,128)(2,1)S(1)} %copy-done.6, f32[8,3,128,128]{3,2,1,0:T(8,128)S(1)} %copy-done.2, f32[8,3,2,128]{3,2,1,0:T(2,128)S(1)} %get-tuple-element.61.stat_ref, ...), custom_call_target="tpu_custom_call" | custom-call | tf_op jit(solution)/shard_map/pallas_call | solution.py:293
  163.2 1.1 collective-permute-start.42
  164.3 1.8 collective-permute-done.32.rest_1_
  166.3 2.5 %collective-permute-done.33.rest_2_ = bf16[1024,128]{1,0:T(8,128)(2,1)S(1)} collective-permute-done((bf16[1024,128]{1,0:T(8,128)(2,1)S(1)}, bf16[1024,128]{1,0:T(8,128)(2,1)S(1)}, u32[]{:S(2)}, u32[]{:S(2)}) %collective-permute-start.33) | collective-permute-done | bytes 262176 | tf_op jit(solution)/shard_map/ppermute | solution.py:50
  168.9 6.9 %collective-permute-done.34.rest_4_ = bf16[1024,128]{1,0:T(8,128)(2,1)S(1)} collective-permute-done((bf16[1024,128]{1,0:T(8,128)(2,1)S(1)}, bf16[1024,128]{1,0:T(8,128)(2,1)S(1)}, u32[]{:S(2)}, u32[]{:S(2)}) %collective-permute-start.34) | collective-permute-done | bytes 262176 | tf_op jit(solution)/shard_map/ppermute | solution.py:50
  175.8 3.1 %shard_map.111.rest_1_ = bf16[1024,128]{1,0:T(8,128)(2,1)S(1)} custom-call(s32[64]{0:T(128)S(1)} %reshape.25.where_ref, s32[8]{0:T(128)S(1)} %copy-done.21, bf16[8,3,128,128]{3,2,1,0:T(8,128)(2,1)S(1)} %copy-done.6, f32[8,3,128,128]{3,2,1,0:T(8,128)S(1)} %copy-done.2, f32[8,3,2,128]{3,2,1,0:T(2,128)S(1)} %get-tuple-element.61.stat_ref, ...), custom_call_target="tpu_custom_call" | custom-call | tf_op jit(solution)/shard_map/pallas_call | solution.py:293
  179.1 1.3 collective-permute-start.41
  180.4 1.4 collective-permute-start.38
  182.0 1.3 collective-permute-start.39
  183.3 10.4 %collective-permute-done.37.rest_3_ = bf16[1024,128]{1,0:T(8,128)(2,1)S(1)} collective-permute-done((bf16[1024,128]{1,0:T(8,128)(2,1)S(1)}, bf16[1024,128]{1,0:T(8,128)(2,1)S(1)}, u32[]{:S(2)}, u32[]{:S(2)}) %collective-permute-start.37) | collective-permute-done | bytes 262176 | tf_op jit(solution)/shard_map/ppermute | solution.py:50
  193.8 5.2 %collective-permute-done.39.rest_6_ = bf16[1024,128]{1,0:T(8,128)(2,1)S(1)} collective-permute-done((bf16[1024,128]{1,0:T(8,128)(2,1)S(1)}, bf16[1024,128]{1,0:T(8,128)(2,1)S(1)}, u32[]{:S(2)}, u32[]{:S(2)}) %collective-permute-start.39) | collective-permute-done | bytes 262176 | tf_op jit(solution)/shard_map/ppermute | solution.py:50
  199.0 3.1 %shard_map.113.rest_0_ = bf16[1024,128]{1,0:T(8,128)(2,1)S(1)} custom-call(s32[64]{0:T(128)S(1)} %reshape.25.where_ref, s32[8]{0:T(128)S(1)} %copy-done.21, bf16[8,3,128,128]{3,2,1,0:T(8,128)(2,1)S(1)} %copy-done.6, f32[8,3,128,128]{3,2,1,0:T(8,128)S(1)} %copy-done.2, f32[8,3,2,128]{3,2,1,0:T(2,128)S(1)} %get-tuple-element.61.stat_ref, ...), custom_call_target="tpu_custom_call" | custom-call | tf_op jit(solution)/shard_map/pallas_call | solution.py:293
  202.1 1.3 collective-permute-start.45
  204.1 1.3 collective-permute-start.46
  205.4 6.1 %collective-permute-done.45.rest_1_ = bf16[1024,128]{1,0:T(8,128)(2,1)S(1)} collective-permute-done((bf16[1024,128]{1,0:T(8,128)(2,1)S(1)}, bf16[1024,128]{1,0:T(8,128)(2,1)S(1)}, u32[]{:S(2)}, u32[]{:S(2)}) %collective-permute-start.45) | collective-permute-done | bytes 262176 | tf_op jit(solution)/shard_map/ppermute | solution.py:50
  211.5 4.9 %collective-permute-done.40.rest_7_ = bf16[1024,128]{1,0:T(8,128)(2,1)S(1)} collective-permute-done((bf16[1024,128]{1,0:T(8,128)(2,1)S(1)}, bf16[1024,128]{1,0:T(8,128)(2,1)S(1)}, u32[]{:S(2)}, u32[]{:S(2)}) %collective-permute-start.40) | collective-permute-done | bytes 262176 | tf_op jit(solution)/shard_map/ppermute | solution.py:50
  216.4 2.7 %collective-permute-start.47 = (bf16[1024,128]{1,0:T(8,128)(2,1)S(1)}, bf16[1024,128]{1,0:T(8,128)(2,1)S(1)}, u32[]{:S(2)}, u32[]{:S(2)}) collective-permute-start(bf16[1024,128]{1,0:T(8,128)(2,1)S(1)} %collective-permute-done.45.rest_1_), channel_id=1, source_target_pairs={{0,2},{2,3},{3,1},{1,0},{4,6},{6,7},{7,5},{5,4},{8,10},{10,11},{11... | collective-permute-start | bytes 786440 | tf_op jit(solution)/shard_map/ppermute | solution.py:50
  219.2 3.9 %shard_map.112.state_ref = f32[1024,1536]{1,0:T(8,128)S(1)} custom-call(bf16[1024,1536]{1,0:T(8,128)(2,1)S(1)} %get-tuple-element.58.state_ref, bf16[1024,1536]{1,0:T(8,128)(2,1)S(1)} %bitcast.31, bf16[1024,128]{1,0:T(8,128)(2,1)S(1)} %shard_map.110.rest_0_, bf16[1024,128]{1,0:T(8,128)(2,1)S(1)} %shard_map.111.rest_1_, ...), custom_call_target="tpu_custom_call" | custom-call | tf_op jit(solution)/shard_map/pallas_call | solution.py:318
  223.3 4.0 %collective-permute-done.47.rest_3_ = bf16[1024,128]{1,0:T(8,128)(2,1)S(1)} collective-permute-done((bf16[1024,128]{1,0:T(8,128)(2,1)S(1)}, bf16[1024,128]{1,0:T(8,128)(2,1)S(1)}, u32[]{:S(2)}, u32[]{:S(2)}) %collective-permute-start.47) | collective-permute-done | bytes 262176 | tf_op jit(solution)/shard_map/ppermute | solution.py:50
  227.4 3.5 %shard_map.114 = bf16[1024,1536]{1,0:T(8,128)(2,1)} custom-call(f32[1024,1536]{1,0:T(8,128)S(1)} %shard_map.112.state_ref, bf16[512,1536]{1,0:T(8,128)(2,1)S(1)} %bitcast.33, bf16[1024,128]{1,0:T(8,128)(2,1)S(1)} %shard_map.113.rest_0_, bf16[1024,128]{1,0:T(8,128)(2,1)S(1)} %collective-permute-done.45.rest_1_, ...), custom_call_target="tpu_custom_call" | custom-call | tf_op jit(solution)/shard_map/pallas_call | solution.py:318
  (125 shorter events, 10.1 us)
Async XLA Ops:
  1.0 22.0 %collective-permute-start = (bf16[3,32,1536]{2,1,0:T(8,128)(2,1)S(1)}, bf16[3,32,1536]{2,1,0:T(8,128)(2,1)}, u32[]{:S(2)}, u32[]{:S(2)}) collective-permute-start(bf16[3,32,1536]{2,1,0:T(8,128)(2,1)S(1)} %dynamic-slice_bitcast_fusion), channel_id=1, source_target_pairs={{0,2},{2,3},{3,1},{1,0},{4,6},{6,7},{7,5},{5,4},{8,10},{10,11},{11... | collective-permute-start | bytes 884744 | tf_op jit(solution)/shard_map/ppermute | solution.py:50
  5.1 18.8 %collective-permute-start.1 = (bf16[3,32,1536]{2,1,0:T(8,128)(2,1)S(1)}, bf16[3,32,1536]{2,1,0:T(8,128)(2,1)}, u32[]{:S(2)}, u32[]{:S(2)}) collective-permute-start(bf16[3,32,1536]{2,1,0:T(8,128)(2,1)S(1)} %dynamic-slice_bitcast_fusion), channel_id=1, source_target_pairs={{0,1},{2,0},{3,2},{1,3},{4,5},{6,4},{7,6},{5,7},{8,9},{10,8},{11,1... | collective-permute-start | bytes 884744 | tf_op jit(solution)/shard_map/ppermute | solution.py:50
  10.3 25.8 %collective-permute-start.3 = (bf16[8,1,2,128,128]{4,3,2,1,0:T(8,128)(2,1)}, bf16[8,1,2,128,128]{4,3,2,1,0:T(8,128)(2,1)}, u32[]{:S(2)}, u32[]{:S(2)}) collective-permute-start(bf16[8,1,2,128,128]{4,3,2,1,0:T(8,128)(2,1)} %shard_map.102.rest_2_.rest_0_), channel_id=1, source_target_pairs={{0,28},{4,8},{8,4},{12,16},{16,12},{20,24},{24,20},{28,0},{1,29},{... | collective-permute-start | bytes 1572872 | tf_op jit(solution)/shard_map/ppermute | solution.py:28
  11.9 26.6 %collective-permute-start.5 = (bf16[8,1,2,128,128]{4,3,2,1,0:T(8,128)(2,1)}, bf16[8,1,2,128,128]{4,3,2,1,0:T(8,128)(2,1)}, u32[]{:S(2)}, u32[]{:S(2)}) collective-permute-start(bf16[8,1,2,128,128]{4,3,2,1,0:T(8,128)(2,1)} %shard_map.102.rest_2_.rest_0_), channel_id=1, source_target_pairs={{0,4},{4,0},{8,12},{12,8},{16,20},{20,16},{24,28},{28,24},{1,5},{5... | collective-permute-start | bytes 1572872 | tf_op jit(solution)/shard_map/ppermute | solution.py:28
  13.6 24.9 %collective-permute-start.2 = (bf16[4,1,2,128,128]{4,3,2,1,0:T(8,128)(2,1)}, bf16[4,1,2,128,128]{4,3,2,1,0:T(8,128)(2,1)}, u32[]{:S(2)}, u32[]{:S(2)}) collective-permute-start(bf16[4,1,2,128,128]{4,3,2,1,0:T(8,128)(2,1)} %constant_dynamic-slice_fusion.11), channel_id=1, source_target_pairs={{0,8},{4,28},{8,16},{12,4},{16,24},{20,12},{24,0},{28,20},{1,9},{5... | collective-permute-start | bytes 786440 | tf_op jit(solution)/shard_map/ppermute | solution.py:28
  23.0 26.7 %collective-permute-start.11 = (bf16[8,1,2,128,128]{4,3,2,1,0:T(8,128)(2,1)}, bf16[8,1,2,128,128]{4,3,2,1,0:T(8,128)(2,1)S(1)}, u32[]{:S(2)}, u32[]{:S(2)}) collective-permute-start(bf16[8,1,2,128,128]{4,3,2,1,0:T(8,128)(2,1)} %get-tuple-element.50.rest_2_.rest_1_), channel_id=1, source_target_pairs={{0,28},{4,8},{8,4},{12,16},{16,12},{20,24},{24,20},{28,0},{1,29},{... | collective-permute-start | bytes 1572872 | tf_op jit(solution)/shard_map/ppermute | solution.py:28
  23.9 14.6 %collective-permute-start.4 = (bf16[3,32,1536]{2,1,0:T(8,128)(2,1)}, bf16[3,32,1536]{2,1,0:T(8,128)(2,1)}, u32[]{:S(2)}, u32[]{:S(2)}) collective-permute-start(bf16[3,32,1536]{2,1,0:T(8,128)(2,1)} %collective-permute-done), channel_id=1, source_target_pairs={{0,2},{2,3},{3,1},{1,0},{4,6},{6,7},{7,5},{5,4},{8,10},{10,11},{11... | collective-permute-start | bytes 884744 | tf_op jit(solution)/shard_map/ppermute | solution.py:50
  27.9 10.4 %copy-start.27 = (s32[8,8]{1,0:T(8,128)S(1)}, s32[8,8]{1,0:T(8,128)}, u32[]{:S(2)}) copy-start(s32[8,8]{1,0:T(8,128)} %param.18) | copy-start | bytes 772
  28.0 12.4 %copy-start.4 = (bf16[8,3,128,128]{3,2,1,0:T(8,128)(2,1)S(1)}, bf16[8,3,128,128]{3,2,1,0:T(8,128)(2,1)}, u32[]{:S(2)}) copy-start(bf16[8,3,128,128]{3,2,1,0:T(8,128)(2,1)} %get-tuple-element.40.qt_ref) | copy-start | bytes 2359300
  28.0 12.4 %copy-start.8 = (bf16[8,1,2,128,128]{4,3,2,1,0:T(8,128)(2,1)S(1)}, bf16[8,1,2,128,128]{4,3,2,1,0:T(8,128)(2,1)}, u32[]{:S(2)}) copy-start(bf16[8,1,2,128,128]{4,3,2,1,0:T(8,128)(2,1)} %shard_map.102.rest_2_.rest_0_) | copy-start | bytes 1572868
  28.0 12.4 %copy-start.21 = (s32[8]{0:T(128)S(1)}, s32[8]{0:T(128)}, u32[]{:S(2)}) copy-start(s32[8]{0:T(128)} %counts_ref.11) | copy-start | bytes 100
  28.0 20.5 %copy-start.10 = (bf16[8,1,2,128,128]{4,3,2,1,0:T(8,128)(2,1)S(1)}, bf16[8,1,2,128,128]{4,3,2,1,0:T(8,128)(2,1)}, u32[]{:S(2)}) copy-start(bf16[8,1,2,128,128]{4,3,2,1,0:T(8,128)(2,1)} %get-tuple-element.53.rest_2_) | copy-start | bytes 1572868
  36.1 11.7 %copy-start.9 = (bf16[8,1,2,128,128]{4,3,2,1,0:T(8,128)(2,1)S(1)}, bf16[8,1,2,128,128]{4,3,2,1,0:T(8,128)(2,1)}, u32[]{:S(2)}) copy-start(bf16[8,1,2,128,128]{4,3,2,1,0:T(8,128)(2,1)} %get-tuple-element.50.rest_2_.rest_1_) | copy-start | bytes 1572868
  37.8 1.8 collective-permute-start.6
  42.8 21.3 %copy-start.1 = (f32[8,3,128,128]{3,2,1,0:T(8,128)S(1)}, f32[8,3,128,128]{3,2,1,0:T(8,128)}, u32[]{:S(2)}) copy-start(f32[8,3,128,128]{3,2,1,0:T(8,128)} %get-tuple-element.41.acc_ref) | copy-start | bytes 4718596
  47.0 14.3 %collective-permute-start.12 = (bf16[1024,128]{1,0:T(8,128)(2,1)S(1)}, bf16[1024,128]{1,0:T(8,128)(2,1)S(1)}, u32[]{:S(2)}, u32[]{:S(2)}) collective-permute-start(bf16[1024,128]{1,0:T(8,128)(2,1)S(1)} %shard_map.103.rest_0_), channel_id=1, source_target_pairs={{0,2},{2,3},{3,1},{1,0},{4,6},{6,7},{7,5},{5,4},{8,10},{10,11},{11... | collective-permute-start | bytes 786440 | tf_op jit(solution)/shard_map/ppermute | solution.py:50
  47.7 16.3 %collective-permute-start.14 = (bf16[8,1,2,128,128]{4,3,2,1,0:T(8,128)(2,1)S(1)}, bf16[8,1,2,128,128]{4,3,2,1,0:T(8,128)(2,1)S(1)}, u32[]{:S(2)}, u32[]{:S(2)}) collective-permute-start(bf16[8,1,2,128,128]{4,3,2,1,0:T(8,128)(2,1)S(1)} %copy-done.9), channel_id=1, source_target_pairs={{0,4},{4,0},{8,12},{12,8},{16,20},{20,16},{24,28},{28,24},{1,5},{5... | collective-permute-start | bytes 1572872 | tf_op jit(solution)/shard_map/ppermute | solution.py:28
  47.8 16.2 %collective-permute-start.10 = (bf16[4,1,2,128,128]{4,3,2,1,0:T(8,128)(2,1)S(1)}, bf16[4,1,2,128,128]{4,3,2,1,0:T(8,128)(2,1)S(1)}, u32[]{:S(2)}, u32[]{:S(2)}) collective-permute-start(bf16[4,1,2,128,128]{4,3,2,1,0:T(8,128)(2,1)S(1)} %constant_dynamic-slice_fusion.8), channel_id=1, source_target_pairs={{0,8},{4,28},{8,16},{12,4},{16,24},{20,12},{24,0},{28,20},{1,9},{5... | collective-permute-start | bytes 786440 | tf_op jit(solution)/shard_map/ppermute | solution.py:28
  48.4 20.9 %collective-permute-start.9 = (bf16[8,1,2,128,128]{4,3,2,1,0:T(8,128)(2,1)S(1)}, bf16[8,1,2,128,128]{4,3,2,1,0:T(8,128)(2,1)S(1)}, u32[]{:S(2)}, u32[]{:S(2)}) collective-permute-start(bf16[8,1,2,128,128]{4,3,2,1,0:T(8,128)(2,1)S(1)} %copy-done.10), channel_id=1, source_target_pairs={{0,28},{4,8},{8,4},{12,16},{16,12},{20,24},{24,20},{28,0},{1,29},{... | collective-permute-start | bytes 1572872 | tf_op jit(solution)/shard_map/ppermute | solution.py:28
  49.7 13.8 %collective-permute-start.13 = (bf16[1024,128]{1,0:T(8,128)(2,1)S(1)}, bf16[1024,128]{1,0:T(8,128)(2,1)S(1)}, u32[]{:S(2)}, u32[]{:S(2)}) collective-permute-start(bf16[1024,128]{1,0:T(8,128)(2,1)S(1)} %shard_map.103.rest_0_), channel_id=1, source_target_pairs={{0,1},{2,0},{3,2},{1,3},{4,5},{6,4},{7,6},{5,7},{8,9},{10,8},{11,1... | collective-permute-start | bytes 786440 | tf_op jit(solution)/shard_map/ppermute | solution.py:50
  61.2 8.1 %copy-start.13 = (bf16[1024,128]{1,0:T(8,128)(2,1)}, bf16[1024,128]{1,0:T(8,128)(2,1)S(1)}, u32[]{:S(2)}) copy-start(bf16[1024,128]{1,0:T(8,128)(2,1)S(1)} %collective-permute-done.12.rest_2_) | copy-start | bytes 786436
  61.2 2.8 %collective-permute-start.15 = (bf16[4,1,2,128,128]{4,3,2,1,0:T(8,128)(2,1)S(1)}, bf16[4,1,2,128,128]{4,3,2,1,0:T(8,128)(2,1)S(1)}, u32[]{:S(2)}, u32[]{:S(2)}) collective-permute-start(bf16[4,1,2,128,128]{4,3,2,1,0:T(8,128)(2,1)S(1)} %constant_dynamic-slice_fusion.7), channel_id=1, source_target_pairs={{0,4},{4,0},{8,12},{12,8},{16,20},{20,16},{24,28},{28,24},{1,5},{5... | collective-permute-start | bytes 786440 | tf_op jit(solution)/shard_map/ppermute | solution.py:28
  63.5 29.6 %copy-start.15 = (bf16[1024,128]{1,0:T(8,128)(2,1)}, bf16[1024,128]{1,0:T(8,128)(2,1)S(1)}, u32[]{:S(2)}) copy-start(bf16[1024,128]{1,0:T(8,128)(2,1)S(1)} %collective-permute-done.13.rest_4_) | copy-start | bytes 786436
  63.5 36.3 %collective-permute-start.7 = (bf16[3,3,32,1536]{3,2,0,1:T(8,128)(2,1)}, bf16[3,3,32,1536]{3,2,0,1:T(8,128)(2,1)}, u32[]{:S(2)}, u32[]{:S(2)}) collective-permute-start(bf16[3,3,32,1536]{3,2,0,1:T(8,128)(2,1)} %pad_maximum_fusion.2), channel_id=1, source_target_pairs={{0,16},{4,20},{8,24},{12,28},{16,0},{20,4},{24,8},{28,12},{1,17},{... | collective-permute-start | bytes 2654216 | tf_op jit(solution)/shard_map/ppermute | solution.py:28
  67.2 22.1 %copy-start.11 = (bf16[1024,128]{1,0:T(8,128)(2,1)}, bf16[1024,128]{1,0:T(8,128)(2,1)S(1)}, u32[]{:S(2)}) copy-start(bf16[1024,128]{1,0:T(8,128)(2,1)S(1)} %shard_map.104.rest_1_) | copy-start | bytes 786436
  67.2 14.8 %collective-permute-start.16 = (bf16[1024,128]{1,0:T(8,128)(2,1)S(1)}, bf16[1024,128]{1,0:T(8,128)(2,1)S(1)}, u32[]{:S(2)}, u32[]{:S(2)}) collective-permute-start(bf16[1024,128]{1,0:T(8,128)(2,1)S(1)} %shard_map.104.rest_1_), channel_id=1, source_target_pairs={{0,2},{2,3},{3,1},{1,0},{4,6},{6,7},{7,5},{5,4},{8,10},{10,11},{11... | collective-permute-start | bytes 786440 | tf_op jit(solution)/shard_map/ppermute | solution.py:50
  67.3 22.0 %collective-permute-start.19 = (bf16[8,1,2,128,128]{4,3,2,1,0:T(8,128)(2,1)S(1)}, bf16[8,1,2,128,128]{4,3,2,1,0:T(8,128)(2,1)S(1)}, u32[]{:S(2)}, u32[]{:S(2)}) collective-permute-start(bf16[8,1,2,128,128]{4,3,2,1,0:T(8,128)(2,1)S(1)} %copy-done.10), channel_id=1, source_target_pairs={{0,4},{4,0},{8,12},{12,8},{16,20},{20,16},{24,28},{28,24},{1,5},{5... | collective-permute-start | bytes 1572872 | tf_op jit(solution)/shard_map/ppermute | solution.py:28
  67.5 16.0 %collective-permute-start.17 = (bf16[1024,128]{1,0:T(8,128)(2,1)S(1)}, bf16[1024,128]{1,0:T(8,128)(2,1)S(1)}, u32[]{:S(2)}, u32[]{:S(2)}) collective-permute-start(bf16[1024,128]{1,0:T(8,128)(2,1)S(1)} %shard_map.104.rest_1_), channel_id=1, source_target_pairs={{0,1},{2,0},{3,2},{1,3},{4,5},{6,4},{7,6},{5,7},{8,9},{10,8},{11,1... | collective-permute-start | bytes 786440 | tf_op jit(solution)/shard_map/ppermute | solution.py:50
  69.3 17.5 %collective-permute-start.18 = (bf16[1024,128]{1,0:T(8,128)(2,1)S(1)}, bf16[1024,128]{1,0:T(8,128)(2,1)S(1)}, u32[]{:S(2)}, u32[]{:S(2)}) collective-permute-start(bf16[1024,128]{1,0:T(8,128)(2,1)S(1)} %collective-permute-done.12.rest_2_), channel_id=1, source_target_pairs={{0,2},{2,3},{3,1},{1,0},{4,6},{6,7},{7,5},{5,4},{8,10},{10,11},{11... | collective-permute-start | bytes 786440 | tf_op jit(solution)/shard_map/ppermute | solution.py:50
  82.0 7.3 %collective-permute-start.8 = (bf16[4,1,2,128,128]{4,3,2,1,0:T(8,128)(2,1)S(1)}, bf16[4,1,2,128,128]{4,3,2,1,0:T(8,128)(2,1)S(1)}, u32[]{:S(2)}, u32[]{:S(2)}) collective-permute-start(bf16[4,1,2,128,128]{4,3,2,1,0:T(8,128)(2,1)S(1)} %constant_dynamic-slice_fusion.9), channel_id=1, source_target_pairs={{0,8},{4,28},{8,16},{12,4},{16,24},{20,12},{24,0},{28,20},{1,9},{5... | collective-permute-start | bytes 786440 | tf_op jit(solution)/shard_map/ppermute | solution.py:28
  83.5 5.8 %collective-permute-start.20 = (bf16[4,1,2,128,128]{4,3,2,1,0:T(8,128)(2,1)S(1)}, bf16[4,1,2,128,128]{4,3,2,1,0:T(8,128)(2,1)S(1)}, u32[]{:S(2)}, u32[]{:S(2)}) collective-permute-start(bf16[4,1,2,128,128]{4,3,2,1,0:T(8,128)(2,1)S(1)} %constant_dynamic-slice_fusion.6), channel_id=1, source_target_pairs={{0,4},{4,0},{8,12},{12,8},{16,20},{20,16},{24,28},{28,24},{1,5},{5... | collective-permute-start | bytes 786440 | tf_op jit(solution)/shard_map/ppermute | solution.py:28
  86.8 12.9 %copy-start.17 = (bf16[1024,128]{1,0:T(8,128)(2,1)}, bf16[1024,128]{1,0:T(8,128)(2,1)S(1)}, u32[]{:S(2)}) copy-start(bf16[1024,128]{1,0:T(8,128)(2,1)S(1)} %collective-permute-done.18.rest_6_) | copy-start | bytes 786436
  93.1 6.6 %collective-permute-start.21 = (bf16[1024,128]{1,0:T(8,128)(2,1)}, bf16[1024,128]{1,0:T(8,128)(2,1)S(1)}, u32[]{:S(2)}, u32[]{:S(2)}) collective-permute-start(bf16[1024,128]{1,0:T(8,128)(2,1)} %shard_map.105.rest_0_), channel_id=1, source_target_pairs={{0,2},{2,3},{3,1},{1,0},{4,6},{6,7},{7,5},{5,4},{8,10},{10,11},{11... | collective-permute-start | bytes 786440 | tf_op jit(solution)/shard_map/ppermute | solution.py:50
  93.2 17.9 %collective-permute-start.23 = (bf16[3,3,32,1536]{3,2,0,1:T(8,128)(2,1)}, bf16[3,3,32,1536]{3,2,0,1:T(8,128)(2,1)}, u32[]{:S(2)}, u32[]{:S(2)}) collective-permute-start(bf16[3,3,32,1536]{3,2,0,1:T(8,128)(2,1)} %pad_maximum_fusion.2), channel_id=1, source_target_pairs={{0,4},{4,0},{8,12},{12,8},{16,20},{20,16},{24,28},{28,24},{1,5},{5... | collective-permute-start | bytes 2654216 | tf_op jit(solution)/shard_map/ppermute | solution.py:28
  99.8 11.3 %collective-permute-start.22 = (bf16[3,3,32,1536]{3,2,0,1:T(8,128)(2,1)}, bf16[3,3,32,1536]{3,2,0,1:T(8,128)(2,1)}, u32[]{:S(2)}, u32[]{:S(2)}) collective-permute-start(bf16[3,3,32,1536]{3,2,0,1:T(8,128)(2,1)} %collective-permute-done.7), channel_id=1, source_target_pairs={{0,4},{4,0},{8,12},{12,8},{16,20},{20,16},{24,28},{28,24},{1,5},{5... | collective-permute-start | bytes 2654216 | tf_op jit(solution)/shard_map/ppermute | solution.py:28
  99.8 8.8 %collective-permute-start.24 = (bf16[1024,128]{1,0:T(8,128)(2,1)S(1)}, bf16[1024,128]{1,0:T(8,128)(2,1)S(1)}, u32[]{:S(2)}, u32[]{:S(2)}) collective-permute-start(bf16[1024,128]{1,0:T(8,128)(2,1)S(1)} %collective-permute-done.16.rest_3_), channel_id=1, source_target_pairs={{0,2},{2,3},{3,1},{1,0},{4,6},{6,7},{7,5},{5,4},{8,10},{10,11},{11... | collective-permute-start | bytes 786440 | tf_op jit(solution)/shard_map/ppermute | solution.py:50
  101.0 20.1 %collective-permute-start.25 = (bf16[1024,128]{1,0:T(8,128)(2,1)}, bf16[1024,128]{1,0:T(8,128)(2,1)S(1)}, u32[]{:S(2)}, u32[]{:S(2)}) collective-permute-start(bf16[1024,128]{1,0:T(8,128)(2,1)} %shard_map.105.rest_0_), channel_id=1, source_target_pairs={{0,1},{2,0},{3,2},{1,3},{4,5},{6,4},{7,6},{5,7},{8,9},{10,8},{11,1... | collective-permute-start | bytes 786440 | tf_op jit(solution)/shard_map/ppermute | solution.py:50
  108.6 12.6 %collective-permute-start.26 = (bf16[1024,128]{1,0:T(8,128)(2,1)S(1)}, bf16[1024,128]{1,0:T(8,128)(2,1)S(1)}, u32[]{:S(2)}, u32[]{:S(2)}) collective-permute-start(bf16[1024,128]{1,0:T(8,128)(2,1)S(1)} %collective-permute-done.21.rest_1_), channel_id=1, source_target_pairs={{0,2},{2,3},{3,1},{1,0},{4,6},{6,7},{7,5},{5,4},{8,10},{10,11},{11... | collective-permute-start | bytes 786440 | tf_op jit(solution)/shard_map/ppermute | solution.py:50
  114.9 2.0 copy-start.14
  114.9 2.0 copy-start.16
  115.0 2.1 copy-start.18
  122.6 8.8 %copy-start.22 = (bf16[1536,384]{1,0:T(8,128)(2,1)S(1)}, bf16[1536,384]{1,0:T(8,128)(2,1)}, u32[]{:S(2)}) copy-start(bf16[1536,384]{1,0:T(8,128)(2,1)} %wq_ref.3) | copy-start | bytes 3538948
  129.7 18.5 %collective-permute-start.28 = (bf16[8,1,2,128,128]{4,3,2,1,0:T(8,128)(2,1)S(1)}, bf16[8,1,2,128,128]{4,3,2,1,0:T(8,128)(2,1)S(1)}, u32[]{:S(2)}, u32[]{:S(2)}) collective-permute-start(bf16[8,1,2,128,128]{4,3,2,1,0:T(8,128)(2,1)S(1)} %get-tuple-element.62.rest_2_), channel_id=1, source_target_pairs={{0,28},{4,8},{8,4},{12,16},{16,12},{20,24},{24,20},{28,0},{1,29},{... | collective-permute-start | bytes 1572872 | tf_op jit(solution)/shard_map/ppermute | solution.py:28
  129.8 27.1 %collective-permute-start.29 = (bf16[8,1,2,128,128]{4,3,2,1,0:T(8,128)(2,1)S(1)}, bf16[8,1,2,128,128]{4,3,2,1,0:T(8,128)(2,1)}, u32[]{:S(2)}, u32[]{:S(2)}) collective-permute-start(bf16[8,1,2,128,128]{4,3,2,1,0:T(8,128)(2,1)S(1)} %get-tuple-element.62.rest_2_), channel_id=1, source_target_pairs={{0,4},{4,0},{8,12},{12,8},{16,20},{20,16},{24,28},{28,24},{1,5},{5... | collective-permute-start | bytes 1572872 | tf_op jit(solution)/shard_map/ppermute | solution.py:28
  137.3 19.6 %copy-start.6 = (bf16[8,3,128,128]{3,2,1,0:T(8,128)(2,1)S(1)}, bf16[8,3,128,128]{3,2,1,0:T(8,128)(2,1)}, u32[]{:S(2)}) copy-start(bf16[8,3,128,128]{3,2,1,0:T(8,128)(2,1)} %copy-done.5) | copy-start | bytes 2359300
  146.7 10.2 %collective-permute-start.27 = (bf16[4,1,2,128,128]{4,3,2,1,0:T(8,128)(2,1)S(1)}, bf16[4,1,2,128,128]{4,3,2,1,0:T(8,128)(2,1)S(1)}, u32[]{:S(2)}, u32[]{:S(2)}) collective-permute-start(bf16[4,1,2,128,128]{4,3,2,1,0:T(8,128)(2,1)S(1)} %constant_dynamic-slice_fusion.5), channel_id=1, source_target_pairs={{0,8},{4,28},{8,16},{12,4},{16,24},{20,12},{24,0},{28,20},{1,9},{5... | collective-permute-start | bytes 786440 | tf_op jit(solution)/shard_map/ppermute | solution.py:28
  148.2 17.9 %collective-permute-start.32 = (bf16[8,1,2,128,128]{4,3,2,1,0:T(8,128)(2,1)S(1)}, bf16[8,1,2,128,128]{4,3,2,1,0:T(8,128)(2,1)S(1)}, u32[]{:S(2)}, u32[]{:S(2)}) collective-permute-start(bf16[8,1,2,128,128]{4,3,2,1,0:T(8,128)(2,1)S(1)} %get-tuple-element.65.rest_2_), channel_id=1, source_target_pairs={{0,28},{4,8},{8,4},{12,16},{16,12},{20,24},{24,20},{28,0},{1,29},{... | collective-permute-start | bytes 1572872 | tf_op jit(solution)/shard_map/ppermute | solution.py:28
  148.3 8.6 %collective-permute-start.30 = (bf16[4,1,2,128,128]{4,3,2,1,0:T(8,128)(2,1)S(1)}, bf16[4,1,2,128,128]{4,3,2,1,0:T(8,128)(2,1)S(1)}, u32[]{:S(2)}, u32[]{:S(2)}) collective-permute-start(bf16[4,1,2,128,128]{4,3,2,1,0:T(8,128)(2,1)S(1)} %constant_dynamic-slice_fusion.4), channel_id=1, source_target_pairs={{0,4},{4,0},{8,12},{12,8},{16,20},{20,16},{24,28},{28,24},{1,5},{5... | collective-permute-start | bytes 786440 | tf_op jit(solution)/shard_map/ppermute | solution.py:28
  162.4 6.4 %collective-permute-start.33 = (bf16[1024,128]{1,0:T(8,128)(2,1)S(1)}, bf16[1024,128]{1,0:T(8,128)(2,1)S(1)}, u32[]{:S(2)}, u32[]{:S(2)}) collective-permute-start(bf16[1024,128]{1,0:T(8,128)(2,1)S(1)} %shard_map.110.rest_0_), channel_id=1, source_target_pairs={{0,2},{2,3},{3,1},{1,0},{4,6},{6,7},{7,5},{5,4},{8,10},{10,11},{11... | collective-permute-start | bytes 786440 | tf_op jit(solution)/shard_map/ppermute | solution.py:50
  162.5 13.3 %collective-permute-start.35 = (bf16[8,1,2,128,128]{4,3,2,1,0:T(8,128)(2,1)S(1)}, bf16[8,1,2,128,128]{4,3,2,1,0:T(8,128)(2,1)S(1)}, u32[]{:S(2)}, u32[]{:S(2)}) collective-permute-start(bf16[8,1,2,128,128]{4,3,2,1,0:T(8,128)(2,1)S(1)} %get-tuple-element.65.rest_2_), channel_id=1, source_target_pairs={{0,4},{4,0},{8,12},{12,8},{16,20},{20,16},{24,28},{28,24},{1,5},{5... | collective-permute-start | bytes 1572872 | tf_op jit(solution)/shard_map/ppermute | solution.py:28
  162.6 13.2 %collective-permute-start.31 = (bf16[4,1,2,128,128]{4,3,2,1,0:T(8,128)(2,1)S(1)}, bf16[4,1,2,128,128]{4,3,2,1,0:T(8,128)(2,1)S(1)}, u32[]{:S(2)}, u32[]{:S(2)}) collective-permute-start(bf16[4,1,2,128,128]{4,3,2,1,0:T(8,128)(2,1)S(1)} %constant_dynamic-slice_fusion.3), channel_id=1, source_target_pairs={{0,8},{4,28},{8,16},{12,4},{16,24},{20,12},{24,0},{28,20},{1,9},{5... | collective-permute-start | bytes 786440 | tf_op jit(solution)/shard_map/ppermute | solution.py:28
  163.2 18.8 %collective-permute-start.42 = (bf16[8,1,2,128,128]{4,3,2,1,0:T(8,128)(2,1)S(1)}, bf16[8,1,2,128,128]{4,3,2,1,0:T(8,128)(2,1)S(1)}, u32[]{:S(2)}, u32[]{:S(2)}) collective-permute-start(bf16[8,1,2,128,128]{4,3,2,1,0:T(8,128)(2,1)S(1)} %get-tuple-element.70.rest_2_), channel_id=1, source_target_pairs={{0,28},{4,8},{8,4},{12,16},{16,12},{20,24},{24,20},{28,0},{1,29},{... | collective-permute-start | bytes 1572872 | tf_op jit(solution)/shard_map/ppermute | solution.py:28
  166.2 9.6 %collective-permute-start.34 = (bf16[1024,128]{1,0:T(8,128)(2,1)S(1)}, bf16[1024,128]{1,0:T(8,128)(2,1)S(1)}, u32[]{:S(2)}, u32[]{:S(2)}) collective-permute-start(bf16[1024,128]{1,0:T(8,128)(2,1)S(1)} %shard_map.110.rest_0_), channel_id=1, source_target_pairs={{0,1},{2,0},{3,2},{1,3},{4,5},{6,4},{7,6},{5,7},{8,9},{10,8},{11,1... | collective-permute-start | bytes 786440 | tf_op jit(solution)/shard_map/ppermute | solution.py:50
  168.9 7.0 %collective-permute-start.36 = (bf16[4,1,2,128,128]{4,3,2,1,0:T(8,128)(2,1)S(1)}, bf16[4,1,2,128,128]{4,3,2,1,0:T(8,128)(2,1)S(1)}, u32[]{:S(2)}, u32[]{:S(2)}) collective-permute-start(bf16[4,1,2,128,128]{4,3,2,1,0:T(8,128)(2,1)S(1)} %constant_dynamic-slice_fusion.2), channel_id=1, source_target_pairs={{0,4},{4,0},{8,12},{12,8},{16,20},{20,16},{24,28},{28,24},{1,5},{5... | collective-permute-start | bytes 786440 | tf_op jit(solution)/shard_map/ppermute | solution.py:28
  175.8 23.2 %collective-permute-start.43 = (bf16[8,1,2,128,128]{4,3,2,1,0:T(8,128)(2,1)S(1)}, bf16[8,1,2,128,128]{4,3,2,1,0:T(8,128)(2,1)S(1)}, u32[]{:S(2)}, u32[]{:S(2)}) collective-permute-start(bf16[8,1,2,128,128]{4,3,2,1,0:T(8,128)(2,1)S(1)} %get-tuple-element.70.rest_2_), channel_id=1, source_target_pairs={{0,4},{4,0},{8,12},{12,8},{16,20},{20,16},{24,28},{28,24},{1,5},{5... | collective-permute-start | bytes 1572872 | tf_op jit(solution)/shard_map/ppermute | solution.py:28
  179.0 14.8 %collective-permute-start.37 = (bf16[1024,128]{1,0:T(8,128)(2,1)S(1)}, bf16[1024,128]{1,0:T(8,128)(2,1)S(1)}, u32[]{:S(2)}, u32[]{:S(2)}) collective-permute-start(bf16[1024,128]{1,0:T(8,128)(2,1)S(1)} %shard_map.111.rest_1_), channel_id=1, source_target_pairs={{0,2},{2,3},{3,1},{1,0},{4,6},{6,7},{7,5},{5,4},{8,10},{10,11},{11... | collective-permute-start | bytes 786440 | tf_op jit(solution)/shard_map/ppermute | solution.py:50
  179.1 19.9 %collective-permute-start.41 = (bf16[4,1,2,128,128]{4,3,2,1,0:T(8,128)(2,1)S(1)}, bf16[4,1,2,128,128]{4,3,2,1,0:T(8,128)(2,1)S(1)}, u32[]{:S(2)}, u32[]{:S(2)}) collective-permute-start(bf16[4,1,2,128,128]{4,3,2,1,0:T(8,128)(2,1)S(1)} %constant_dynamic-slice_fusion.1), channel_id=1, source_target_pairs={{0,8},{4,28},{8,16},{12,4},{16,24},{20,12},{24,0},{28,20},{1,9},{5... | collective-permute-start | bytes 786440 | tf_op jit(solution)/shard_map/ppermute | solution.py:28
  180.4 13.4 %collective-permute-start.38 = (bf16[1024,128]{1,0:T(8,128)(2,1)S(1)}, bf16[1024,128]{1,0:T(8,128)(2,1)S(1)}, u32[]{:S(2)}, u32[]{:S(2)}) collective-permute-start(bf16[1024,128]{1,0:T(8,128)(2,1)S(1)} %shard_map.111.rest_1_), channel_id=1, source_target_pairs={{0,1},{2,0},{3,2},{1,3},{4,5},{6,4},{7,6},{5,7},{8,9},{10,8},{11,1... | collective-permute-start | bytes 786440 | tf_op jit(solution)/shard_map/ppermute | solution.py:50
  182.0 17.0 %collective-permute-start.39 = (bf16[1024,128]{1,0:T(8,128)(2,1)S(1)}, bf16[1024,128]{1,0:T(8,128)(2,1)S(1)}, u32[]{:S(2)}, u32[]{:S(2)}) collective-permute-start(bf16[1024,128]{1,0:T(8,128)(2,1)S(1)} %collective-permute-done.33.rest_2_), channel_id=1, source_target_pairs={{0,2},{2,3},{3,1},{1,0},{4,6},{6,7},{7,5},{5,4},{8,10},{10,11},{11... | collective-permute-start | bytes 786440 | tf_op jit(solution)/shard_map/ppermute | solution.py:50
  193.7 5.2 %collective-permute-start.44 = (bf16[4,1,2,128,128]{4,3,2,1,0:T(8,128)(2,1)S(1)}, bf16[4,1,2,128,128]{4,3,2,1,0:T(8,128)(2,1)S(1)}, u32[]{:S(2)}, u32[]{:S(2)}) collective-permute-start(bf16[4,1,2,128,128]{4,3,2,1,0:T(8,128)(2,1)S(1)} %constant_dynamic-slice_fusion), channel_id=1, source_target_pairs={{0,4},{4,0},{8,12},{12,8},{16,20},{20,16},{24,28},{28,24},{1,5},{5... | collective-permute-start | bytes 786440 | tf_op jit(solution)/shard_map/ppermute | solution.py:28
  202.1 9.4 %collective-permute-start.45 = (bf16[1024,128]{1,0:T(8,128)(2,1)S(1)}, bf16[1024,128]{1,0:T(8,128)(2,1)S(1)}, u32[]{:S(2)}, u32[]{:S(2)}) collective-permute-start(bf16[1024,128]{1,0:T(8,128)(2,1)S(1)} %shard_map.113.rest_0_), channel_id=1, source_target_pairs={{0,2},{2,3},{3,1},{1,0},{4,6},{6,7},{7,5},{5,4},{8,10},{10,11},{11... | collective-permute-start | bytes 786440 | tf_op jit(solution)/shard_map/ppermute | solution.py:50
  203.4 13.0 %collective-permute-start.40 = (bf16[1024,128]{1,0:T(8,128)(2,1)S(1)}, bf16[1024,128]{1,0:T(8,128)(2,1)S(1)}, u32[]{:S(2)}, u32[]{:S(2)}) collective-permute-start(bf16[1024,128]{1,0:T(8,128)(2,1)S(1)} %collective-permute-done.37.rest_3_), channel_id=1, source_target_pairs={{0,2},{2,3},{3,1},{1,0},{4,6},{6,7},{7,5},{5,4},{8,10},{10,11},{11... | collective-permute-start | bytes 786440 | tf_op jit(solution)/shard_map/ppermute | solution.py:50
  204.1 19.2 %collective-permute-start.46 = (bf16[1024,128]{1,0:T(8,128)(2,1)S(1)}, bf16[1024,128]{1,0:T(8,128)(2,1)S(1)}, u32[]{:S(2)}, u32[]{:S(2)}) collective-permute-start(bf16[1024,128]{1,0:T(8,128)(2,1)S(1)} %shard_map.113.rest_0_), channel_id=1, source_target_pairs={{0,1},{2,0},{3,2},{1,3},{4,5},{6,4},{7,6},{5,7},{8,9},{10,8},{11,1... | collective-permute-start | bytes 786440 | tf_op jit(solution)/shard_map/ppermute | solution.py:50
  216.4 11.0 %collective-permute-start.47 = (bf16[1024,128]{1,0:T(8,128)(2,1)S(1)}, bf16[1024,128]{1,0:T(8,128)(2,1)S(1)}, u32[]{:S(2)}, u32[]{:S(2)}) collective-permute-start(bf16[1024,128]{1,0:T(8,128)(2,1)S(1)} %collective-permute-done.45.rest_1_), channel_id=1, source_target_pairs={{0,2},{2,3},{3,1},{1,0},{4,6},{6,7},{7,5},{5,4},{8,10},{10,11},{11... | collective-permute-start | bytes 786440 | tf_op jit(solution)/shard_map/ppermute | solution.py:50
  (12 other events, 16.1 us)

commit v5 on v4

--- a/solution.py
+++ b/solution.py
@@ -13,10 +13,13 @@
 STEPS = 2
 TILE = 256
 COST = 3.0
-R1PIN = 3
+AHEAD = 2
+C2PIN = 1
+ATT_PINS = (3, 2)
+SEND_PIN = 2
 ATT_COST = 0.0
 PART_COST = 0.0
-PAST_VMEM = 52
+PAST_VMEM = 49
 REST_VMEM = (62, 16)
 CHUNKS = ((0,), (1,), (2,))
 MIB = 1024 * 1024
@@ -184,9 +187,14 @@
 
     @pl.when(tile == 0)
     def _():
-        for ahead in range(slots.shape[0]):
+        for ahead in range(AHEAD):
             for copy in copies(ahead):
                 copy.start()
+
+    @pl.when(tile + AHEAD < pl.num_programs(0))
+    def _():
+        for copy in copies(tile + AHEAD):
+            copy.start()
 
     for copy in copies(tile):
         copy.wait()
@@ -377,13 +385,13 @@
     return sent(kv, across), sent(facing(kv), beyond), sent(kv, beside)
 
 
-def fetch_rows(w_out):
+def fetch_rows(w_out, then):
     half = lax.axis_size("space") // 2
     local, width = w_out.shape
     me = lax.axis_index("space")
     quarters = w_out.reshape(local // HD, 4, HD // 4, width)
     mine = lax.dynamic_index_in_dim(quarters, me % 2 + 2 * (me // half), 1, keepdims=False)
-    return around(mine, "head")[1:]
+    return around(after(mine, then), "head")[1:]
 
 
 def share_rows(w_out, fetched, then):
@@ -426,25 +434,26 @@
         kv = [kv_first] + list(kv_rest)
         near += [halo(piece) for piece in kv_rest]
         if rollout == 0:
-            fetched = fetch_rows(w_out)
+            fetched = fetch_rows(w_out, kv_first)
             queries = after(queries, *fetched[:2])
         past, stats = attend_past(queries, cache_key, cache_value, last)
         came = []
         attended = past
         for chunk, of_chunk in enumerate(CHUNKS):
             next_pair, further, other = near[chunk]
-            shared = sent(facing(after(next_pair, attended)), beside)
+            held = (attended, further) if chunk == 0 and rollout >= C2PIN else (attended,)
+            shared = sent(facing(after(next_pair, *held)), beside)
             own = kv[chunk]
             if chunk == 0 and rollout == 0:
                 own = after(own, *fetched)
             if chunk >= 1:
-                own = after(own, *came[-1][1:R1PIN])
-            if chunk >= 2:
-                own = after(own, *came[-2][2:])
+                own = after(own, *came[-1][1 : ATT_PINS[chunk - 1]])
             pieces = (further, next_pair, own, other, shared)
             attended = attend(of_chunk, where_block, counts, queries, past, stats, pieces)
             if rollout == 0 and chunk == 0:
                 fetched = [after(piece, attended) for piece in fetched]
+            if 1 <= chunk <= SEND_PIN:
+                attended = after(attended, came[-1][-1])
             came.append(around(attended, "head", came[-1][2:] if came else ()))
         if rollout == 0:
             rows_of = share_rows(w_out, fetched, came[-1][1])

time: 232 us -> 210 us (0.905)
  waiting for transfers between devices: 92.3 us -> 71.1 us
  starting transfers between devices: 41.4 us -> 46 us
    ppermute x21, waiting for transfers between devices: 78.6 us -> 59.6 us  [turned(): lax.ppermute(value, axis, [(order[i], order[(i + hops) % count]) for i in...]
    unnamed x56 -> x60, local copies, waits for them, and re-layouts: 10.7 us -> 7.62 us
    pallas_call x2, Pallas kernels: 17.5 us -> 14.5 us  [attend_past(): call(functools.partial(past_body, frames, heads, len(last) > 0), (blocks...]
    ppermute x21, starting transfers between devices: 25.8 us -> 28.7 us  [turned(): lax.ppermute(value, axis, [(order[i], order[(i + hops) % count]) for i in...]
  transfers between devices with their start and end apart: 48 -> 48, of which waited for: 18 -> 21; matrix products, arithmetic and copies ran while one was open for 4% -> 5% of each run, Pallas kernels for 27% -> 28%
where the time goes in v5:
time: 210 us; the launch traced here: 209 us
  Pallas kernels  73.3 us (35%)
  waiting for transfers between devices  71.1 us (34%)
  starting transfers between devices  46 us (22%)
  local copies, waits for them, and re-layouts  13.4 us (6%)
  other arithmetic  4.87 us (2%)
    ppermute x21, waiting for transfers between devices, turned(): lax.ppermute(value, axis, [(order[i], order[(i + hops) % count]) for i in...  59.6 us
    ppermute x21, starting transfers between devices, turned(): lax.ppermute(value, axis, [(order[i], order[(i + hops) % count]) for i in...  28.7 us
    pallas_call x6, Pallas kernels, attend(): call(functools.partial(attend_body, blocks, slots, inner), (1,), [of_head...  22.2 us
    ppermute x27, starting transfers between devices, sent(): lax.ppermute(value, 'space', [(i, to(i, count) % count) for i in range(co...  17.3 us
    pallas_call x2, Pallas kernels, attend_past(): call(functools.partial(past_body, frames, heads, len(last) > 0), (blocks...  14.5 us
    pallas_call x2, Pallas kernels, rest_projection(): call(functools.partial(rest_body, heads), (rows // TILE,), [pl.BlockSpec(...  12.9 us
    pallas_call x3, Pallas kernels, add_heads(): call(functools.partial(part_body, len(pieces)), (rows // TILE,), [pl.Bloc...  12.2 us
    ppermute x27, waiting for transfers between devices, sent(): lax.ppermute(value, 'space', [(i, to(i, count) % count) for i in range(co...  11.5 us
  transfers between devices with their start and end apart: 48, of which 21 were waited for; matrix products, arithmetic and copies ran while one was open for 5% of the time, Pallas kernels for 28%

profile of v5, /device:TPU:0, one launch (start us, length us, event | category | flops | bytes accessed | tf_op | source)
XLA Modules:
  0.0 209.2 jit_solution(9897012477356945685)
XLA Ops:
  0.0 1.0 dynamic-slice_bitcast_fusion
  1.0 5.2 %shard_map.100.rest_2_.rest_0_ = bf16[8,1,2,128,128]{4,3,2,1,0:T(8,128)(2,1)} custom-call(bf16[1024,1536]{1,0:T(8,128)(2,1)} %state_ref.5, f32[1536]{0:T(1024)} %gain_ref.7, bf16[1536,384]{1,0:T(8,128)(2,1)} %wk_ref.7, bf16[1536,384]{1,0:T(8,128)(2,1)} %wv_ref.7), custom_call_target="tpu_custom_call" | custom-call | flops 17250000896 | tf_op jit(solution)/shard_map/pallas_call | solution.py:115
  6.2 4.0 %collective-permute-start = (bf16[3,32,1536]{2,1,0:T(8,128)(2,1)S(1)}, bf16[3,32,1536]{2,1,0:T(8,128)(2,1)}, u32[]{:S(2)}, u32[]{:S(2)}) collective-permute-start(bf16[3,32,1536]{2,1,0:T(8,128)(2,1)S(1)} %dynamic-slice_bitcast_fusion), channel_id=1, source_target_pairs={{0,2},{2,3},{3,1},{1,0},{4,6},{6,7},{7,5},{5,4},{8,10},{10,11},{11... | collective-permute-start | bytes 884744 | tf_op jit(solution)/shard_map/ppermute | solution.py:53
  10.3 1.6 collective-permute-start.3
  11.9 1.7 constant_dynamic-slice_fusion.11
  13.6 1.5 collective-permute-start.2
  15.0 7.9 %shard_map.101 = (bf16[8,1,2,128,128]{4,3,2,1,0:T(8,128)(2,1)}, bf16[8,1,2,128,128]{4,3,2,1,0:T(8,128)(2,1)}, bf16[8,3,128,128]{3,2,1,0:T(8,128)(2,1)}) custom-call(bf16[1024,1536]{1,0:T(8,128)(2,1)} %state_ref.5, f32[1536]{0:T(1024)} %gain_ref.7, bf16[1536,384]{1,0:T(8,128)(2,1)} %wq_ref.3, bf16[1536,384]{1,0:T(8,128)(2,1)} %wk_ref.7, bf16[1536,384]{1,0:T(8,128)(2,1)} %wv_ref.7), custom_call_target="tpu_custom_call" | custom-call | flops 17250000896 | tf_op jit(solution)/shard_map/pallas_call | solution.py:153
  25.4 2.1 %collective-permute-start.4 = (bf16[3,32,1536]{2,1,0:T(8,128)(2,1)}, bf16[3,32,1536]{2,1,0:T(8,128)(2,1)}, u32[]{:S(2)}, u32[]{:S(2)}) collective-permute-start(bf16[3,32,1536]{2,1,0:T(8,128)(2,1)} %collective-permute-done), channel_id=1, source_target_pairs={{0,2},{2,3},{3,1},{1,0},{4,6},{6,7},{7,5},{5,4},{8,10},{10,11},{11... | collective-permute-start | bytes 884744 | tf_op jit(solution)/shard_map/ppermute | solution.py:53
  27.5 1.1 copy-done
  28.6 7.3 %shard_map.102 = (f32[8,3,128,128]{3,2,1,0:T(8,128)S(1)}, f32[8,3,2,128]{3,2,1,0:T(2,128)S(1)}) custom-call(bf16[8,3,128,128]{3,2,1,0:T(8,128)(2,1)S(1)} %copy-done, bf16[8,1024,384]{2,1,0:T(8,128)(2,1)} %ck_hbm.3, bf16[8,1024,384]{2,1,0:T(8,128)(2,1)} %cv_hbm.3), custom_call_target="tpu_custom_call" | custom-call | flops 20700000256 | tf_op jit(solution)/shard_map/pallas_call | solution.py:235
  35.9 1.7 constant_dynamic-slice_fusion.10
  38.3 1.3 collective-permute-done.6.rest_4_
  39.6 4.4 %shard_map.103.rest_0_ = bf16[1024,128]{1,0:T(8,128)(2,1)S(1)} custom-call(s32[64]{0:T(128)S(1)} %reshape.25.where_ref, s32[8]{0:T(128)S(1)} %copy-done.21, bf16[8,3,128,128]{3,2,1,0:T(8,128)(2,1)S(1)} %copy-done.1, f32[8,3,128,128]{3,2,1,0:T(8,128)S(1)} %get-tuple-element.45.acc_ref, f32[8,3,2,128]{3,2,1,0:T(2,128)S(1)} %get-tuple-element.46.stat_ref, ...), custom_call_target="tpu_custom_call" | custom-call | tf_op jit(solution)/shard_map/pallas_call | solution.py:301
  45.0 1.5 collective-permute-start.10
  47.0 1.0 collective-permute-start.9
  48.1 1.2 collective-permute-start.13
  49.3 1.0 constant_dynamic-slice_fusion.7
  50.3 3.3 %collective-permute-done.12.rest_2_ = bf16[1024,128]{1,0:T(8,128)(2,1)S(1)} collective-permute-done((bf16[1024,128]{1,0:T(8,128)(2,1)S(1)}, bf16[1024,128]{1,0:T(8,128)(2,1)S(1)}, u32[]{:S(2)}, u32[]{:S(2)}) %collective-permute-start.12) | collective-permute-done | bytes 262176 | tf_op jit(solution)/shard_map/ppermute | solution.py:53
  53.5 1.6 collective-permute-done.10.rest_0_
  55.1 1.2 collective-permute-start.16
  56.3 2.1 pad_maximum_fusion.2
  59.7 1.5 collective-permute-start.7
  61.2 4.9 %shard_map.104.rest_1_ = bf16[1024,128]{1,0:T(8,128)(2,1)} custom-call(s32[64]{0:T(128)S(1)} %reshape.25.where_ref, s32[8]{0:T(128)S(1)} %copy-done.21, bf16[8,3,128,128]{3,2,1,0:T(8,128)(2,1)S(1)} %copy-done.1, f32[8,3,128,128]{3,2,1,0:T(8,128)S(1)} %get-tuple-element.45.acc_ref, f32[8,3,2,128]{3,2,1,0:T(2,128)S(1)} %get-tuple-element.46.stat_ref, ...), custom_call_target="tpu_custom_call" | custom-call | tf_op jit(solution)/shard_map/pallas_call | solution.py:301
  66.7 1.5 collective-permute-start.8
  68.4 6.7 %collective-permute-done.17.rest_3_ = bf16[1024,128]{1,0:T(8,128)(2,1)S(1)} collective-permute-done((bf16[1024,128]{1,0:T(8,128)(2,1)}, bf16[1024,128]{1,0:T(8,128)(2,1)S(1)}, u32[]{:S(2)}, u32[]{:S(2)}) %collective-permute-start.17) | collective-permute-done | bytes 262176 | tf_op jit(solution)/shard_map/ppermute | solution.py:53
  75.1 1.4 collective-permute-start.20
  76.5 3.2 %shard_map.105.rest_0_ = bf16[1024,128]{1,0:T(8,128)(2,1)S(1)} custom-call(s32[64]{0:T(128)S(1)} %reshape.25.where_ref, s32[8]{0:T(128)S(1)} %copy-done.21, bf16[8,3,128,128]{3,2,1,0:T(8,128)(2,1)S(1)} %copy-done.1, f32[8,3,128,128]{3,2,1,0:T(8,128)S(1)} %get-tuple-element.45.acc_ref, f32[8,3,2,128]{3,2,1,0:T(2,128)S(1)} %get-tuple-element.46.stat_ref, ...), custom_call_target="tpu_custom_call" | custom-call | tf_op jit(solution)/shard_map/pallas_call | solution.py:301
  79.8 3.3 %collective-permute-done.20.rest_7_ = bf16[1024,128]{1,0:T(8,128)(2,1)S(1)} collective-permute-done((bf16[1024,128]{1,0:T(8,128)(2,1)S(1)}, bf16[1024,128]{1,0:T(8,128)(2,1)S(1)}, u32[]{:S(2)}, u32[]{:S(2)}) %collective-permute-start.20) | collective-permute-done | bytes 262176 | tf_op jit(solution)/shard_map/ppermute | solution.py:53
  83.9 2.2 %collective-permute-start.21 = (bf16[1024,128]{1,0:T(8,128)(2,1)S(1)}, bf16[1024,128]{1,0:T(8,128)(2,1)S(1)}, u32[]{:S(2)}, u32[]{:S(2)}) collective-permute-start(bf16[1024,128]{1,0:T(8,128)(2,1)S(1)} %shard_map.105.rest_0_), channel_id=1, source_target_pairs={{0,2},{2,3},{3,1},{1,0},{4,6},{6,7},{7,5},{5,4},{8,10},{10,11},{11... | collective-permute-start | bytes 786440 | tf_op jit(solution)/shard_map/ppermute | solution.py:53
  86.1 5.5 %collective-permute-done.21.rest_1_ = bf16[1024,128]{1,0:T(8,128)(2,1)S(1)} collective-permute-done((bf16[1024,128]{1,0:T(8,128)(2,1)S(1)}, bf16[1024,128]{1,0:T(8,128)(2,1)S(1)}, u32[]{:S(2)}, u32[]{:S(2)}) %collective-permute-start.21) | collective-permute-done | bytes 262176 | tf_op jit(solution)/shard_map/ppermute | solution.py:53
  91.5 2.6 %collective-permute-start.24 = (bf16[1024,128]{1,0:T(8,128)(2,1)}, bf16[1024,128]{1,0:T(8,128)(2,1)S(1)}, u32[]{:S(2)}, u32[]{:S(2)}) collective-permute-start(bf16[1024,128]{1,0:T(8,128)(2,1)} %shard_map.104.rest_1_), channel_id=1, source_target_pairs={{0,1},{2,0},{3,2},{1,3},{4,5},{6,4},{7,6},{5,7},{8,9},{10,8},{11,1... | collective-permute-start | bytes 786440 | tf_op jit(solution)/shard_map/ppermute | solution.py:53
  94.2 7.5 %collective-permute-done.24.rest_5_ = bf16[1024,128]{1,0:T(8,128)(2,1)S(1)} collective-permute-done((bf16[1024,128]{1,0:T(8,128)(2,1)}, bf16[1024,128]{1,0:T(8,128)(2,1)S(1)}, u32[]{:S(2)}, u32[]{:S(2)}) %collective-permute-start.24) | collective-permute-done | bytes 262176 | tf_op jit(solution)/shard_map/ppermute | solution.py:53
  101.7 1.6 collective-permute-start.26
  103.3 1.8 select_bitcast_fusion.3
  107.0 1.6 copy-done.2
  109.0 4.8 %shard_map.106.part_ref = f32[1024,1536]{1,0:T(8,128)S(1)} custom-call(bf16[1024,1536]{1,0:T(8,128)(2,1)S(1)} %copy-done.2, bf16[1024,1536]{1,0:T(8,128)(2,1)S(1)} %bitcast.30, bf16[1024,128]{1,0:T(8,128)(2,1)S(1)} %copy-done.8, bf16[1024,128]{1,0:T(8,128)(2,1)} %shard_map.104.rest_1_, bf16[1024,128]{1,0:T(8,128)(2,1)S(1)} %copy-done.10, ...), custom_call_target="tpu_custom_call" | custom-call | tf_op jit(solution)/shard_map/pallas_call | solution.py:326
  115.6 6.2 %shard_map.107 = (bf16[1024,1536]{1,0:T(8,128)(2,1)S(1)}, bf16[8,1,2,128,128]{4,3,2,1,0:T(8,128)(2,1)S(1)}) custom-call(f32[1024,1536]{1,0:T(8,128)S(1)} %shard_map.106.part_ref, bf16[512,1536]{1,0:T(8,128)(2,1)S(1)} %bitcast.32, f32[1536]{0:T(1024)S(1)} %copy-done.25, bf16[1536,384]{1,0:T(8,128)(2,1)S(1)} %copy-done.23, bf16[1536,384]{1,0:T(8,128)(2,1)S(1)} %copy-done.24, ...), custom_call_target="tpu_custom_call" | custom-call | flops 24149999616 | tf_op jit(solution)/shard_map/pallas_call | solution.py:357
  122.0 1.5 collective-permute-start.29
  123.5 5.0 %shard_map.108 = (bf16[8,1,2,128,128]{4,3,2,1,0:T(8,128)(2,1)S(1)}, bf16[8,1,2,128,128]{4,3,2,1,0:T(8,128)(2,1)S(1)}, bf16[8,3,128,128]{3,2,1,0:T(8,128)(2,1)S(1)}) custom-call(bf16[1024,1536]{1,0:T(8,128)(2,1)S(1)} %get-tuple-element.63.state_ref, f32[1536]{0:T(1024)S(1)} %copy-done.25, bf16[1536,384]{1,0:T(8,128)(2,1)S(1)} %copy-done.22, ...), custom_call_target="tpu_custom_call" | custom-call | flops 17250000896 | tf_op jit(solution)/shard_map/pallas_call | solution.py:153
  129.0 7.2 %shard_map.109 = (f32[8,3,128,128]{3,2,1,0:T(8,128)S(1)}, f32[8,3,2,128]{3,2,1,0:T(2,128)S(1)}) custom-call(bf16[8,3,128,128]{3,2,1,0:T(8,128)(2,1)S(1)} %get-tuple-element.64.qt_ref, bf16[8,1024,384]{2,1,0:T(8,128)(2,1)} %ck_hbm.3, bf16[8,1024,384]{2,1,0:T(8,128)(2,1)} %cv_hbm.3, bf16[8,1,2,128,128]{4,3,2,1,0:T(8,128)(2,1)S(1)} %copy-done.3, ...), custom_call_target="tpu_custom_call" | custom-call | flops 20700000256 | tf_op jit(solution)/shard_map/pallas_call | solution.py:235
  136.3 0.9 collective-permute-start.32
  137.2 3.7 %collective-permute-done.27.rest_0_ = bf16[4,1,2,128,128]{4,3,2,1,0:T(8,128)(2,1)S(1)} collective-permute-done((bf16[4,1,2,128,128]{4,3,2,1,0:T(8,128)(2,1)S(1)}, bf16[4,1,2,128,128]{4,3,2,1,0:T(8,128)(2,1)S(1)}, u32[]{:S(2)}, u32[]{:S(2)}) %collective-permute-start.27) | collective-permute-done | bytes 262176 | tf_op jit(solution)/shard_map/ppermute | solution.py:31
  141.5 1.2 collective-permute-done.30.rest_4_
  142.6 3.2 %shard_map.110.rest_0_ = bf16[1024,128]{1,0:T(8,128)(2,1)S(1)} custom-call(s32[64]{0:T(128)S(1)} %reshape.25.where_ref, s32[8]{0:T(128)S(1)} %copy-done.21, bf16[8,3,128,128]{3,2,1,0:T(8,128)(2,1)S(1)} %get-tuple-element.64.qt_ref, f32[8,3,128,128]{3,2,1,0:T(8,128)S(1)} %get-tuple-element.65.acc_ref, f32[8,3,2,128]{3,2,1,0:T(2,128)S(1)} %get-tuple-element.66.stat_ref, ...), custom_call_target="tpu_custom_call" | custom-call | tf_op jit(solution)/shard_map/pallas_call | solution.py:301
  145.9 1.3 collective-permute-start.33
  148.1 1.4 collective-permute-start.31
  149.5 3.7 %collective-permute-done.32.rest_1_ = bf16[8,1,2,128,128]{4,3,2,1,0:T(8,128)(2,1)S(1)} collective-permute-done((bf16[8,1,2,128,128]{4,3,2,1,0:T(8,128)(2,1)S(1)}, bf16[8,1,2,128,128]{4,3,2,1,0:T(8,128)(2,1)S(1)}, u32[]{:S(2)}, u32[]{:S(2)}) %collective-permute-start.32) | collective-permute-done | bytes 524320 | tf_op jit(solution)/shard_map/ppermute | solution.py:31
  153.3 1.4 collective-permute-done.33.rest_2_
  154.6 6.4 %collective-permute-done.34.rest_4_ = bf16[1024,128]{1,0:T(8,128)(2,1)S(1)} collective-permute-done((bf16[1024,128]{1,0:T(8,128)(2,1)S(1)}, bf16[1024,128]{1,0:T(8,128)(2,1)S(1)}, u32[]{:S(2)}, u32[]{:S(2)}) %collective-permute-start.34) | collective-permute-done | bytes 262176 | tf_op jit(solution)/shard_map/ppermute | solution.py:53
  161.6 3.2 %shard_map.111.rest_1_ = bf16[1024,128]{1,0:T(8,128)(2,1)S(1)} custom-call(s32[64]{0:T(128)S(1)} %reshape.25.where_ref, s32[8]{0:T(128)S(1)} %copy-done.21, bf16[8,3,128,128]{3,2,1,0:T(8,128)(2,1)S(1)} %get-tuple-element.64.qt_ref, f32[8,3,128,128]{3,2,1,0:T(8,128)S(1)} %get-tuple-element.65.acc_ref, f32[8,3,2,128]{3,2,1,0:T(2,128)S(1)} %get-tuple-element.66.stat_ref, ...), custom_call_target="tpu_custom_call" | custom-call | tf_op jit(solution)/shard_map/pallas_call | solution.py:301
  164.9 4.4 %collective-permute-done.37.rest_6_ = bf16[1024,128]{1,0:T(8,128)(2,1)S(1)} collective-permute-done((bf16[1024,128]{1,0:T(8,128)(2,1)S(1)}, bf16[1024,128]{1,0:T(8,128)(2,1)S(1)}, u32[]{:S(2)}, u32[]{:S(2)}) %collective-permute-start.37) | collective-permute-done | bytes 262176 | tf_op jit(solution)/shard_map/ppermute | solution.py:53
  169.3 1.2 collective-permute-start.38
  170.5 1.3 collective-permute-start.41
  171.9 4.8 %collective-permute-done.38.rest_3_ = bf16[1024,128]{1,0:T(8,128)(2,1)S(1)} collective-permute-done((bf16[1024,128]{1,0:T(8,128)(2,1)S(1)}, bf16[1024,128]{1,0:T(8,128)(2,1)S(1)}, u32[]{:S(2)}, u32[]{:S(2)}) %collective-permute-start.38) | collective-permute-done | bytes 262176 | tf_op jit(solution)/shard_map/ppermute | solution.py:53
  176.7 1.7 collective-permute-start.40
  178.7 3.2 %shard_map.113.rest_0_ = bf16[1024,128]{1,0:T(8,128)(2,1)S(1)} custom-call(s32[64]{0:T(128)S(1)} %reshape.25.where_ref, s32[8]{0:T(128)S(1)} %copy-done.21, bf16[8,3,128,128]{3,2,1,0:T(8,128)(2,1)S(1)} %get-tuple-element.64.qt_ref, f32[8,3,128,128]{3,2,1,0:T(8,128)S(1)} %get-tuple-element.65.acc_ref, f32[8,3,2,128]{3,2,1,0:T(2,128)S(1)} %get-tuple-element.66.stat_ref, ...), custom_call_target="tpu_custom_call" | custom-call | tf_op jit(solution)/shard_map/pallas_call | solution.py:301
  182.0 4.2 %collective-permute-done.40.rest_7_ = bf16[1024,128]{1,0:T(8,128)(2,1)S(1)} collective-permute-done((bf16[1024,128]{1,0:T(8,128)(2,1)S(1)}, bf16[1024,128]{1,0:T(8,128)(2,1)S(1)}, u32[]{:S(2)}, u32[]{:S(2)}) %collective-permute-start.40) | collective-permute-done | bytes 262176 | tf_op jit(solution)/shard_map/ppermute | solution.py:53
  186.2 2.4 %collective-permute-start.45 = (bf16[1024,128]{1,0:T(8,128)(2,1)S(1)}, bf16[1024,128]{1,0:T(8,128)(2,1)S(1)}, u32[]{:S(2)}, u32[]{:S(2)}) collective-permute-start(bf16[1024,128]{1,0:T(8,128)(2,1)S(1)} %shard_map.113.rest_0_), channel_id=1, source_target_pairs={{0,2},{2,3},{3,1},{1,0},{4,6},{6,7},{7,5},{5,4},{8,10},{10,11},{11... | collective-permute-start | bytes 786440 | tf_op jit(solution)/shard_map/ppermute | solution.py:53
  188.6 5.7 %collective-permute-done.39.rest_5_ = bf16[1024,128]{1,0:T(8,128)(2,1)S(1)} collective-permute-done((bf16[1024,128]{1,0:T(8,128)(2,1)S(1)}, bf16[1024,128]{1,0:T(8,128)(2,1)S(1)}, u32[]{:S(2)}, u32[]{:S(2)}) %collective-permute-start.39) | collective-permute-done | bytes 262176 | tf_op jit(solution)/shard_map/ppermute | solution.py:53
  194.2 3.1 %collective-permute-done.45.rest_1_ = bf16[1024,128]{1,0:T(8,128)(2,1)S(1)} collective-permute-done((bf16[1024,128]{1,0:T(8,128)(2,1)S(1)}, bf16[1024,128]{1,0:T(8,128)(2,1)S(1)}, u32[]{:S(2)}, u32[]{:S(2)}) %collective-permute-start.45) | collective-permute-done | bytes 262176 | tf_op jit(solution)/shard_map/ppermute | solution.py:53
  197.4 2.5 %collective-permute-start.47 = (bf16[1024,128]{1,0:T(8,128)(2,1)S(1)}, bf16[1024,128]{1,0:T(8,128)(2,1)S(1)}, u32[]{:S(2)}, u32[]{:S(2)}) collective-permute-start(bf16[1024,128]{1,0:T(8,128)(2,1)S(1)} %collective-permute-done.45.rest_1_), channel_id=1, source_target_pairs={{0,2},{2,3},{3,1},{1,0},{4,6},{6,7},{7,5},{5,4},{8,10},{10,11},{11... | collective-permute-start | bytes 786440 | tf_op jit(solution)/shard_map/ppermute | solution.py:53
  199.9 3.9 %shard_map.112.state_ref = f32[1024,1536]{1,0:T(8,128)S(1)} custom-call(bf16[1024,1536]{1,0:T(8,128)(2,1)S(1)} %get-tuple-element.63.state_ref, bf16[1024,1536]{1,0:T(8,128)(2,1)S(1)} %bitcast.31, bf16[1024,128]{1,0:T(8,128)(2,1)S(1)} %shard_map.110.rest_0_, bf16[1024,128]{1,0:T(8,128)(2,1)S(1)} %shard_map.111.rest_1_, ...), custom_call_target="tpu_custom_call" | custom-call | tf_op jit(solution)/shard_map/pallas_call | solution.py:326
  204.5 1.3 collective-permute-done.47.rest_3_
  205.7 3.5 %shard_map.114 = bf16[1024,1536]{1,0:T(8,128)(2,1)} custom-call(f32[1024,1536]{1,0:T(8,128)S(1)} %shard_map.112.state_ref, bf16[512,1536]{1,0:T(8,128)(2,1)S(1)} %bitcast.33, bf16[1024,128]{1,0:T(8,128)(2,1)S(1)} %shard_map.113.rest_0_, bf16[1024,128]{1,0:T(8,128)(2,1)S(1)} %collective-permute-done.45.rest_1_, ...), custom_call_target="tpu_custom_call" | custom-call | tf_op jit(solution)/shard_map/pallas_call | solution.py:326
  (129 shorter events, 15.2 us)
Async XLA Ops:
  6.2 16.7 %collective-permute-start = (bf16[3,32,1536]{2,1,0:T(8,128)(2,1)S(1)}, bf16[3,32,1536]{2,1,0:T(8,128)(2,1)}, u32[]{:S(2)}, u32[]{:S(2)}) collective-permute-start(bf16[3,32,1536]{2,1,0:T(8,128)(2,1)S(1)} %dynamic-slice_bitcast_fusion), channel_id=1, source_target_pairs={{0,2},{2,3},{3,1},{1,0},{4,6},{6,7},{7,5},{5,4},{8,10},{10,11},{11... | collective-permute-start | bytes 884744 | tf_op jit(solution)/shard_map/ppermute | solution.py:53
  10.3 14.4 %collective-permute-start.1 = (bf16[3,32,1536]{2,1,0:T(8,128)(2,1)S(1)}, bf16[3,32,1536]{2,1,0:T(8,128)(2,1)S(1)}, u32[]{:S(2)}, u32[]{:S(2)}) collective-permute-start(bf16[3,32,1536]{2,1,0:T(8,128)(2,1)S(1)} %dynamic-slice_bitcast_fusion), channel_id=1, source_target_pairs={{0,1},{2,0},{3,2},{1,3},{4,5},{6,4},{7,6},{5,7},{8,9},{10,8},{11,1... | collective-permute-start | bytes 884744 | tf_op jit(solution)/shard_map/ppermute | solution.py:53
  10.3 25.7 %collective-permute-start.3 = (bf16[8,1,2,128,128]{4,3,2,1,0:T(8,128)(2,1)}, bf16[8,1,2,128,128]{4,3,2,1,0:T(8,128)(2,1)}, u32[]{:S(2)}, u32[]{:S(2)}) collective-permute-start(bf16[8,1,2,128,128]{4,3,2,1,0:T(8,128)(2,1)} %shard_map.100.rest_2_.rest_0_), channel_id=1, source_target_pairs={{0,28},{4,8},{8,4},{12,16},{16,12},{20,24},{24,20},{28,0},{1,29},{... | collective-permute-start | bytes 1572872 | tf_op jit(solution)/shard_map/ppermute | solution.py:31
  11.9 26.5 %collective-permute-start.5 = (bf16[8,1,2,128,128]{4,3,2,1,0:T(8,128)(2,1)}, bf16[8,1,2,128,128]{4,3,2,1,0:T(8,128)(2,1)}, u32[]{:S(2)}, u32[]{:S(2)}) collective-permute-start(bf16[8,1,2,128,128]{4,3,2,1,0:T(8,128)(2,1)} %shard_map.100.rest_2_.rest_0_), channel_id=1, source_target_pairs={{0,4},{4,0},{8,12},{12,8},{16,20},{20,16},{24,28},{28,24},{1,5},{5... | collective-permute-start | bytes 1572872 | tf_op jit(solution)/shard_map/ppermute | solution.py:31
  13.6 24.7 %collective-permute-start.2 = (bf16[4,1,2,128,128]{4,3,2,1,0:T(8,128)(2,1)}, bf16[4,1,2,128,128]{4,3,2,1,0:T(8,128)(2,1)}, u32[]{:S(2)}, u32[]{:S(2)}) collective-permute-start(bf16[4,1,2,128,128]{4,3,2,1,0:T(8,128)(2,1)} %constant_dynamic-slice_fusion.11), channel_id=1, source_target_pairs={{0,8},{4,28},{8,16},{12,4},{16,24},{20,12},{24,0},{28,20},{1,9},{5... | collective-permute-start | bytes 786440 | tf_op jit(solution)/shard_map/ppermute | solution.py:31
  23.0 25.1 %collective-permute-start.11 = (bf16[8,1,2,128,128]{4,3,2,1,0:T(8,128)(2,1)}, bf16[8,1,2,128,128]{4,3,2,1,0:T(8,128)(2,1)}, u32[]{:S(2)}, u32[]{:S(2)}) collective-permute-start(bf16[8,1,2,128,128]{4,3,2,1,0:T(8,128)(2,1)} %get-tuple-element.54.rest_2_.rest_1_), channel_id=1, source_target_pairs={{0,28},{4,8},{8,4},{12,16},{16,12},{20,24},{24,20},{28,0},{1,29},{... | collective-permute-start | bytes 1572872 | tf_op jit(solution)/shard_map/ppermute | solution.py:31
  25.4 13.0 %collective-permute-start.4 = (bf16[3,32,1536]{2,1,0:T(8,128)(2,1)}, bf16[3,32,1536]{2,1,0:T(8,128)(2,1)}, u32[]{:S(2)}, u32[]{:S(2)}) collective-permute-start(bf16[3,32,1536]{2,1,0:T(8,128)(2,1)} %collective-permute-done), channel_id=1, source_target_pairs={{0,2},{2,3},{3,1},{1,0},{4,6},{6,7},{7,5},{5,4},{8,10},{10,11},{11... | collective-permute-start | bytes 884744 | tf_op jit(solution)/shard_map/ppermute | solution.py:53
  28.6 9.5 %copy-start.29 = (s32[8,8]{1,0:T(8,128)S(1)}, s32[8,8]{1,0:T(8,128)}, u32[]{:S(2)}) copy-start(s32[8,8]{1,0:T(8,128)} %param.18) | copy-start | bytes 772
  28.6 11.0 %copy-start.1 = (bf16[8,3,128,128]{3,2,1,0:T(8,128)(2,1)S(1)}, bf16[8,3,128,128]{3,2,1,0:T(8,128)(2,1)}, u32[]{:S(2)}) copy-start(bf16[8,3,128,128]{3,2,1,0:T(8,128)(2,1)} %get-tuple-element.44.qt_ref) | copy-start | bytes 2359300
  28.6 11.0 %copy-start.3 = (bf16[8,1,2,128,128]{4,3,2,1,0:T(8,128)(2,1)S(1)}, bf16[8,1,2,128,128]{4,3,2,1,0:T(8,128)(2,1)}, u32[]{:S(2)}) copy-start(bf16[8,1,2,128,128]{4,3,2,1,0:T(8,128)(2,1)} %shard_map.100.rest_2_.rest_0_) | copy-start | bytes 1572868
  28.6 11.0 %copy-start.21 = (s32[8]{0:T(128)S(1)}, s32[8]{0:T(128)}, u32[]{:S(2)}) copy-start(s32[8]{0:T(128)} %counts_ref.11) | copy-start | bytes 100
  35.9 9.0 %copy-start.4 = (bf16[8,1,2,128,128]{4,3,2,1,0:T(8,128)(2,1)S(1)}, bf16[8,1,2,128,128]{4,3,2,1,0:T(8,128)(2,1)}, u32[]{:S(2)}) copy-start(bf16[8,1,2,128,128]{4,3,2,1,0:T(8,128)(2,1)} %get-tuple-element.54.rest_2_.rest_1_) | copy-start | bytes 1572868
  37.7 2.0 collective-permute-start.6
  38.3 8.7 %copy-start.5 = (bf16[8,1,2,128,128]{4,3,2,1,0:T(8,128)(2,1)S(1)}, bf16[8,1,2,128,128]{4,3,2,1,0:T(8,128)(2,1)}, u32[]{:S(2)}) copy-start(bf16[8,1,2,128,128]{4,3,2,1,0:T(8,128)(2,1)} %get-tuple-element.57.rest_2_) | copy-start | bytes 1572868
  38.3 18.0 %copy-start.28 = (bf16[3,32,1536]{2,1,0:T(8,128)(2,1)S(1)}, bf16[3,32,1536]{2,1,0:T(8,128)(2,1)}, u32[]{:S(2)}) copy-start(bf16[3,32,1536]{2,1,0:T(8,128)(2,1)} %copy-done.27) | copy-start | bytes 884740
  44.0 17.2 %copy-start.7 = (bf16[1024,128]{1,0:T(8,128)(2,1)}, bf16[1024,128]{1,0:T(8,128)(2,1)S(1)}, u32[]{:S(2)}) copy-start(bf16[1024,128]{1,0:T(8,128)(2,1)S(1)} %shard_map.103.rest_0_) | copy-start | bytes 786436
  44.1 9.5 %collective-permute-start.12 = (bf16[1024,128]{1,0:T(8,128)(2,1)S(1)}, bf16[1024,128]{1,0:T(8,128)(2,1)S(1)}, u32[]{:S(2)}, u32[]{:S(2)}) collective-permute-start(bf16[1024,128]{1,0:T(8,128)(2,1)S(1)} %shard_map.103.rest_0_), channel_id=1, source_target_pairs={{0,2},{2,3},{3,1},{1,0},{4,6},{6,7},{7,5},{5,4},{8,10},{10,11},{11... | collective-permute-start | bytes 786440 | tf_op jit(solution)/shard_map/ppermute | solution.py:53
  45.0 10.1 %collective-permute-start.10 = (bf16[4,1,2,128,128]{4,3,2,1,0:T(8,128)(2,1)S(1)}, bf16[4,1,2,128,128]{4,3,2,1,0:T(8,128)(2,1)S(1)}, u32[]{:S(2)}, u32[]{:S(2)}) collective-permute-start(bf16[4,1,2,128,128]{4,3,2,1,0:T(8,128)(2,1)S(1)} %constant_dynamic-slice_fusion.8), channel_id=1, source_target_pairs={{0,8},{4,28},{8,16},{12,4},{16,24},{20,12},{24,0},{28,20},{1,9},{5... | collective-permute-start | bytes 786440 | tf_op jit(solution)/shard_map/ppermute | solution.py:31
  46.5 14.7 %collective-permute-start.14 = (bf16[8,1,2,128,128]{4,3,2,1,0:T(8,128)(2,1)S(1)}, bf16[8,1,2,128,128]{4,3,2,1,0:T(8,128)(2,1)S(1)}, u32[]{:S(2)}, u32[]{:S(2)}) collective-permute-start(bf16[8,1,2,128,128]{4,3,2,1,0:T(8,128)(2,1)S(1)} %copy-done.4), channel_id=1, source_target_pairs={{0,4},{4,0},{8,12},{12,8},{16,20},{20,16},{24,28},{28,24},{1,5},{5... | collective-permute-start | bytes 1572872 | tf_op jit(solution)/shard_map/ppermute | solution.py:31
  47.0 21.2 %collective-permute-start.9 = (bf16[8,1,2,128,128]{4,3,2,1,0:T(8,128)(2,1)S(1)}, bf16[8,1,2,128,128]{4,3,2,1,0:T(8,128)(2,1)S(1)}, u32[]{:S(2)}, u32[]{:S(2)}) collective-permute-start(bf16[8,1,2,128,128]{4,3,2,1,0:T(8,128)(2,1)S(1)} %copy-done.5), channel_id=1, source_target_pairs={{0,28},{4,8},{8,4},{12,16},{16,12},{20,24},{24,20},{28,0},{1,29},{... | collective-permute-start | bytes 1572872 | tf_op jit(solution)/shard_map/ppermute | solution.py:31
  48.1 10.9 %collective-permute-start.13 = (bf16[1024,128]{1,0:T(8,128)(2,1)S(1)}, bf16[1024,128]{1,0:T(8,128)(2,1)S(1)}, u32[]{:S(2)}, u32[]{:S(2)}) collective-permute-start(bf16[1024,128]{1,0:T(8,128)(2,1)S(1)} %shard_map.103.rest_0_), channel_id=1, source_target_pairs={{0,1},{2,0},{3,2},{1,3},{4,5},{6,4},{7,6},{5,7},{8,9},{10,8},{11,1... | collective-permute-start | bytes 786440 | tf_op jit(solution)/shard_map/ppermute | solution.py:53
  53.5 12.6 %copy-start.9 = (bf16[1024,128]{1,0:T(8,128)(2,1)}, bf16[1024,128]{1,0:T(8,128)(2,1)S(1)}, u32[]{:S(2)}) copy-start(bf16[1024,128]{1,0:T(8,128)(2,1)S(1)} %collective-permute-done.12.rest_2_) | copy-start | bytes 786436
  53.5 7.7 %collective-permute-start.15 = (bf16[4,1,2,128,128]{4,3,2,1,0:T(8,128)(2,1)S(1)}, bf16[4,1,2,128,128]{4,3,2,1,0:T(8,128)(2,1)S(1)}, u32[]{:S(2)}, u32[]{:S(2)}) collective-permute-start(bf16[4,1,2,128,128]{4,3,2,1,0:T(8,128)(2,1)S(1)} %constant_dynamic-slice_fusion.7), channel_id=1, source_target_pairs={{0,4},{4,0},{8,12},{12,8},{16,20},{20,16},{24,28},{28,24},{1,5},{5... | collective-permute-start | bytes 786440 | tf_op jit(solution)/shard_map/ppermute | solution.py:31
  55.1 11.0 %collective-permute-start.16 = (bf16[1024,128]{1,0:T(8,128)(2,1)S(1)}, bf16[1024,128]{1,0:T(8,128)(2,1)S(1)}, u32[]{:S(2)}, u32[]{:S(2)}) collective-permute-start(bf16[1024,128]{1,0:T(8,128)(2,1)S(1)} %collective-permute-done.12.rest_2_), channel_id=1, source_target_pairs={{0,2},{2,3},{3,1},{1,0},{4,6},{6,7},{7,5},{5,4},{8,10},{10,11},{11... | collective-permute-start | bytes 786440 | tf_op jit(solution)/shard_map/ppermute | solution.py:53
  59.7 26.4 %collective-permute-start.7 = (bf16[3,3,32,1536]{3,2,0,1:T(8,128)(2,1)}, bf16[3,3,32,1536]{3,2,0,1:T(8,128)(2,1)}, u32[]{:S(2)}, u32[]{:S(2)}) collective-permute-start(bf16[3,3,32,1536]{3,2,0,1:T(8,128)(2,1)} %pad_maximum_fusion.2), channel_id=1, source_target_pairs={{0,16},{4,20},{8,24},{12,28},{16,0},{20,4},{24,8},{28,12},{1,17},{... | collective-permute-start | bytes 2654216 | tf_op jit(solution)/shard_map/ppermute | solution.py:31
  61.2 15.3 %collective-permute-start.18 = (bf16[8,1,2,128,128]{4,3,2,1,0:T(8,128)(2,1)S(1)}, bf16[8,1,2,128,128]{4,3,2,1,0:T(8,128)(2,1)S(1)}, u32[]{:S(2)}, u32[]{:S(2)}) collective-permute-start(bf16[8,1,2,128,128]{4,3,2,1,0:T(8,128)(2,1)S(1)} %copy-done.5), channel_id=1, source_target_pairs={{0,4},{4,0},{8,12},{12,8},{16,20},{20,16},{24,28},{28,24},{1,5},{5... | collective-permute-start | bytes 1572872 | tf_op jit(solution)/shard_map/ppermute | solution.py:31
  66.1 13.6 %copy-start.13 = (bf16[1024,128]{1,0:T(8,128)(2,1)}, bf16[1024,128]{1,0:T(8,128)(2,1)S(1)}, u32[]{:S(2)}) copy-start(bf16[1024,128]{1,0:T(8,128)(2,1)S(1)} %collective-permute-done.16.rest_6_) | copy-start | bytes 786436
  66.1 9.0 %collective-permute-start.17 = (bf16[1024,128]{1,0:T(8,128)(2,1)}, bf16[1024,128]{1,0:T(8,128)(2,1)S(1)}, u32[]{:S(2)}, u32[]{:S(2)}) collective-permute-start(bf16[1024,128]{1,0:T(8,128)(2,1)} %shard_map.104.rest_1_), channel_id=1, source_target_pairs={{0,2},{2,3},{3,1},{1,0},{4,6},{6,7},{7,5},{5,4},{8,10},{10,11},{11... | collective-permute-start | bytes 786440 | tf_op jit(solution)/shard_map/ppermute | solution.py:53
  66.7 9.8 %collective-permute-start.8 = (bf16[4,1,2,128,128]{4,3,2,1,0:T(8,128)(2,1)S(1)}, bf16[4,1,2,128,128]{4,3,2,1,0:T(8,128)(2,1)S(1)}, u32[]{:S(2)}, u32[]{:S(2)}) collective-permute-start(bf16[4,1,2,128,128]{4,3,2,1,0:T(8,128)(2,1)S(1)} %constant_dynamic-slice_fusion.9), channel_id=1, source_target_pairs={{0,8},{4,28},{8,16},{12,4},{16,24},{20,12},{24,0},{28,20},{1,9},{5... | collective-permute-start | bytes 786440 | tf_op jit(solution)/shard_map/ppermute | solution.py:31
  68.3 8.2 %collective-permute-start.19 = (bf16[4,1,2,128,128]{4,3,2,1,0:T(8,128)(2,1)S(1)}, bf16[4,1,2,128,128]{4,3,2,1,0:T(8,128)(2,1)S(1)}, u32[]{:S(2)}, u32[]{:S(2)}) collective-permute-start(bf16[4,1,2,128,128]{4,3,2,1,0:T(8,128)(2,1)S(1)} %constant_dynamic-slice_fusion.6), channel_id=1, source_target_pairs={{0,4},{4,0},{8,12},{12,8},{16,20},{20,16},{24,28},{28,24},{1,5},{5... | collective-permute-start | bytes 786440 | tf_op jit(solution)/shard_map/ppermute | solution.py:31
  75.1 8.0 %copy-start.15 = (bf16[1024,128]{1,0:T(8,128)(2,1)}, bf16[1024,128]{1,0:T(8,128)(2,1)S(1)}, u32[]{:S(2)}) copy-start(bf16[1024,128]{1,0:T(8,128)(2,1)S(1)} %collective-permute-done.17.rest_3_) | copy-start | bytes 786436
  75.1 8.0 %collective-permute-start.20 = (bf16[1024,128]{1,0:T(8,128)(2,1)S(1)}, bf16[1024,128]{1,0:T(8,128)(2,1)S(1)}, u32[]{:S(2)}, u32[]{:S(2)}) collective-permute-start(bf16[1024,128]{1,0:T(8,128)(2,1)S(1)} %collective-permute-done.17.rest_3_), channel_id=1, source_target_pairs={{0,2},{2,3},{3,1},{1,0},{4,6},{6,7},{7,5},{5,4},{8,10},{10,11},{11... | collective-permute-start | bytes 786440 | tf_op jit(solution)/shard_map/ppermute | solution.py:53
  79.8 11.7 %copy-start.19 = (bf16[1024,128]{1,0:T(8,128)(2,1)}, bf16[1024,128]{1,0:T(8,128)(2,1)S(1)}, u32[]{:S(2)}) copy-start(bf16[1024,128]{1,0:T(8,128)(2,1)S(1)} %shard_map.105.rest_0_) | copy-start | bytes 786436
  83.9 7.7 %collective-permute-start.21 = (bf16[1024,128]{1,0:T(8,128)(2,1)S(1)}, bf16[1024,128]{1,0:T(8,128)(2,1)S(1)}, u32[]{:S(2)}, u32[]{:S(2)}) collective-permute-start(bf16[1024,128]{1,0:T(8,128)(2,1)S(1)} %shard_map.105.rest_0_), channel_id=1, source_target_pairs={{0,2},{2,3},{3,1},{1,0},{4,6},{6,7},{7,5},{5,4},{8,10},{10,11},{11... | collective-permute-start | bytes 786440 | tf_op jit(solution)/shard_map/ppermute | solution.py:53
  86.1 17.3 %collective-permute-start.23 = (bf16[3,3,32,1536]{3,2,0,1:T(8,128)(2,1)}, bf16[3,3,32,1536]{3,2,0,1:T(8,128)(2,1)S(1)}, u32[]{:S(2)}, u32[]{:S(2)}) collective-permute-start(bf16[3,3,32,1536]{3,2,0,1:T(8,128)(2,1)} %pad_maximum_fusion.2), channel_id=1, source_target_pairs={{0,4},{4,0},{8,12},{12,8},{16,20},{20,16},{24,28},{28,24},{1,5},{5... | collective-permute-start | bytes 2654216 | tf_op jit(solution)/shard_map/ppermute | solution.py:31
  91.5 11.8 %collective-permute-start.22 = (bf16[3,3,32,1536]{3,2,0,1:T(8,128)(2,1)}, bf16[3,3,32,1536]{3,2,0,1:T(8,128)(2,1)S(1)}, u32[]{:S(2)}, u32[]{:S(2)}) collective-permute-start(bf16[3,3,32,1536]{3,2,0,1:T(8,128)(2,1)} %collective-permute-done.7), channel_id=1, source_target_pairs={{0,4},{4,0},{8,12},{12,8},{16,20},{20,16},{24,28},{28,24},{1,5},{5... | collective-permute-start | bytes 2654216 | tf_op jit(solution)/shard_map/ppermute | solution.py:31
  91.5 10.2 %collective-permute-start.24 = (bf16[1024,128]{1,0:T(8,128)(2,1)}, bf16[1024,128]{1,0:T(8,128)(2,1)S(1)}, u32[]{:S(2)}, u32[]{:S(2)}) collective-permute-start(bf16[1024,128]{1,0:T(8,128)(2,1)} %shard_map.104.rest_1_), channel_id=1, source_target_pairs={{0,1},{2,0},{3,2},{1,3},{4,5},{6,4},{7,6},{5,7},{8,9},{10,8},{11,1... | collective-permute-start | bytes 786440 | tf_op jit(solution)/shard_map/ppermute | solution.py:53
  94.2 19.9 %collective-permute-start.25 = (bf16[1024,128]{1,0:T(8,128)(2,1)}, bf16[1024,128]{1,0:T(8,128)(2,1)S(1)}, u32[]{:S(2)}, u32[]{:S(2)}) collective-permute-start(bf16[1024,128]{1,0:T(8,128)(2,1)} %copy-done.19), channel_id=1, source_target_pairs={{0,1},{2,0},{3,2},{1,3},{4,5},{6,4},{7,6},{5,7},{8,9},{10,8},{11,1... | collective-permute-start | bytes 786440 | tf_op jit(solution)/shard_map/ppermute | solution.py:53
  101.7 12.3 %collective-permute-start.26 = (bf16[1024,128]{1,0:T(8,128)(2,1)S(1)}, bf16[1024,128]{1,0:T(8,128)(2,1)S(1)}, u32[]{:S(2)}, u32[]{:S(2)}) collective-permute-start(bf16[1024,128]{1,0:T(8,128)(2,1)S(1)} %collective-permute-done.21.rest_1_), channel_id=1, source_target_pairs={{0,2},{2,3},{3,1},{1,0},{4,6},{6,7},{7,5},{5,4},{8,10},{10,11},{11... | collective-permute-start | bytes 786440 | tf_op jit(solution)/shard_map/ppermute | solution.py:53
  106.8 2.2 %copy-start.16 = (bf16[1024,128]{1,0:T(8,128)(2,1)S(1)}, bf16[1024,128]{1,0:T(8,128)(2,1)}, u32[]{:S(2)}) copy-start(bf16[1024,128]{1,0:T(8,128)(2,1)} %copy-done.15) | copy-start | bytes 786436
  106.8 2.2 %copy-start.18 = (bf16[1024,128]{1,0:T(8,128)(2,1)S(1)}, bf16[1024,128]{1,0:T(8,128)(2,1)}, u32[]{:S(2)}) copy-start(bf16[1024,128]{1,0:T(8,128)(2,1)} %copy-done.17) | copy-start | bytes 786436
  115.5 7.9 %copy-start.22 = (bf16[1536,384]{1,0:T(8,128)(2,1)S(1)}, bf16[1536,384]{1,0:T(8,128)(2,1)}, u32[]{:S(2)}) copy-start(bf16[1536,384]{1,0:T(8,128)(2,1)} %wq_ref.3) | copy-start | bytes 3538948
  121.8 19.0 %collective-permute-start.28 = (bf16[8,1,2,128,128]{4,3,2,1,0:T(8,128)(2,1)S(1)}, bf16[8,1,2,128,128]{4,3,2,1,0:T(8,128)(2,1)S(1)}, u32[]{:S(2)}, u32[]{:S(2)}) collective-permute-start(bf16[8,1,2,128,128]{4,3,2,1,0:T(8,128)(2,1)S(1)} %get-tuple-element.67.rest_2_), channel_id=1, source_target_pairs={{0,28},{4,8},{8,4},{12,16},{16,12},{20,24},{24,20},{28,0},{1,29},{... | collective-permute-start | bytes 1572872 | tf_op jit(solution)/shard_map/ppermute | solution.py:31
  122.0 19.5 %collective-permute-start.29 = (bf16[8,1,2,128,128]{4,3,2,1,0:T(8,128)(2,1)S(1)}, bf16[8,1,2,128,128]{4,3,2,1,0:T(8,128)(2,1)S(1)}, u32[]{:S(2)}, u32[]{:S(2)}) collective-permute-start(bf16[8,1,2,128,128]{4,3,2,1,0:T(8,128)(2,1)S(1)} %get-tuple-element.67.rest_2_), channel_id=1, source_target_pairs={{0,4},{4,0},{8,12},{12,8},{16,20},{20,16},{24,28},{28,24},{1,5},{5... | collective-permute-start | bytes 1572872 | tf_op jit(solution)/shard_map/ppermute | solution.py:31
  123.5 5.5 %copy-start.6 = (bf16[8,1,2,128,128]{4,3,2,1,0:T(8,128)(2,1)S(1)}, bf16[8,1,2,128,128]{4,3,2,1,0:T(8,128)(2,1)}, u32[]{:S(2)}) copy-start(bf16[8,1,2,128,128]{4,3,2,1,0:T(8,128)(2,1)} %get-tuple-element.57.rest_2_) | copy-start | bytes 1572868
  128.5 12.3 %collective-permute-start.27 = (bf16[4,1,2,128,128]{4,3,2,1,0:T(8,128)(2,1)S(1)}, bf16[4,1,2,128,128]{4,3,2,1,0:T(8,128)(2,1)S(1)}, u32[]{:S(2)}, u32[]{:S(2)}) collective-permute-start(bf16[4,1,2,128,128]{4,3,2,1,0:T(8,128)(2,1)S(1)} %constant_dynamic-slice_fusion.5), channel_id=1, source_target_pairs={{0,8},{4,28},{8,16},{12,4},{16,24},{20,12},{24,0},{28,20},{1,9},{5... | collective-permute-start | bytes 786440 | tf_op jit(solution)/shard_map/ppermute | solution.py:31
  136.3 17.0 %collective-permute-start.32 = (bf16[8,1,2,128,128]{4,3,2,1,0:T(8,128)(2,1)S(1)}, bf16[8,1,2,128,128]{4,3,2,1,0:T(8,128)(2,1)S(1)}, u32[]{:S(2)}, u32[]{:S(2)}) collective-permute-start(bf16[8,1,2,128,128]{4,3,2,1,0:T(8,128)(2,1)S(1)} %get-tuple-element.70.rest_2_), channel_id=1, source_target_pairs={{0,28},{4,8},{8,4},{12,16},{16,12},{20,24},{24,20},{28,0},{1,29},{... | collective-permute-start | bytes 1572872 | tf_op jit(solution)/shard_map/ppermute | solution.py:31
  140.9 1.8 collective-permute-start.30
  145.9 8.7 %collective-permute-start.33 = (bf16[1024,128]{1,0:T(8,128)(2,1)S(1)}, bf16[1024,128]{1,0:T(8,128)(2,1)S(1)}, u32[]{:S(2)}, u32[]{:S(2)}) collective-permute-start(bf16[1024,128]{1,0:T(8,128)(2,1)S(1)} %shard_map.110.rest_0_), channel_id=1, source_target_pairs={{0,2},{2,3},{3,1},{1,0},{4,6},{6,7},{7,5},{5,4},{8,10},{10,11},{11... | collective-permute-start | bytes 786440 | tf_op jit(solution)/shard_map/ppermute | solution.py:53
  147.2 14.4 %collective-permute-start.35 = (bf16[8,1,2,128,128]{4,3,2,1,0:T(8,128)(2,1)S(1)}, bf16[8,1,2,128,128]{4,3,2,1,0:T(8,128)(2,1)S(1)}, u32[]{:S(2)}, u32[]{:S(2)}) collective-permute-start(bf16[8,1,2,128,128]{4,3,2,1,0:T(8,128)(2,1)S(1)} %get-tuple-element.70.rest_2_), channel_id=1, source_target_pairs={{0,4},{4,0},{8,12},{12,8},{16,20},{20,16},{24,28},{28,24},{1,5},{5... | collective-permute-start | bytes 1572872 | tf_op jit(solution)/shard_map/ppermute | solution.py:31
  147.3 13.7 %collective-permute-start.34 = (bf16[1024,128]{1,0:T(8,128)(2,1)S(1)}, bf16[1024,128]{1,0:T(8,128)(2,1)S(1)}, u32[]{:S(2)}, u32[]{:S(2)}) collective-permute-start(bf16[1024,128]{1,0:T(8,128)(2,1)S(1)} %shard_map.110.rest_0_), channel_id=1, source_target_pairs={{0,1},{2,0},{3,2},{1,3},{4,5},{6,4},{7,6},{5,7},{8,9},{10,8},{11,1... | collective-permute-start | bytes 786440 | tf_op jit(solution)/shard_map/ppermute | solution.py:53
  148.1 13.5 %collective-permute-start.31 = (bf16[4,1,2,128,128]{4,3,2,1,0:T(8,128)(2,1)S(1)}, bf16[4,1,2,128,128]{4,3,2,1,0:T(8,128)(2,1)S(1)}, u32[]{:S(2)}, u32[]{:S(2)}) collective-permute-start(bf16[4,1,2,128,128]{4,3,2,1,0:T(8,128)(2,1)S(1)} %constant_dynamic-slice_fusion.3), channel_id=1, source_target_pairs={{0,8},{4,28},{8,16},{12,4},{16,24},{20,12},{24,0},{28,20},{1,9},{5... | collective-permute-start | bytes 786440 | tf_op jit(solution)/shard_map/ppermute | solution.py:31
  153.2 18.5 %collective-permute-start.42 = (bf16[8,1,2,128,128]{4,3,2,1,0:T(8,128)(2,1)S(1)}, bf16[8,1,2,128,128]{4,3,2,1,0:T(8,128)(2,1)S(1)}, u32[]{:S(2)}, u32[]{:S(2)}) collective-permute-start(bf16[8,1,2,128,128]{4,3,2,1,0:T(8,128)(2,1)S(1)} %get-tuple-element.75.rest_2_), channel_id=1, source_target_pairs={{0,28},{4,8},{8,4},{12,16},{16,12},{20,24},{24,20},{28,0},{1,29},{... | collective-permute-start | bytes 1572872 | tf_op jit(solution)/shard_map/ppermute | solution.py:31
  154.6 7.0 %collective-permute-start.36 = (bf16[4,1,2,128,128]{4,3,2,1,0:T(8,128)(2,1)S(1)}, bf16[4,1,2,128,128]{4,3,2,1,0:T(8,128)(2,1)S(1)}, u32[]{:S(2)}, u32[]{:S(2)}) collective-permute-start(bf16[4,1,2,128,128]{4,3,2,1,0:T(8,128)(2,1)S(1)} %constant_dynamic-slice_fusion.2), channel_id=1, source_target_pairs={{0,4},{4,0},{8,12},{12,8},{16,20},{20,16},{24,28},{28,24},{1,5},{5... | collective-permute-start | bytes 786440 | tf_op jit(solution)/shard_map/ppermute | solution.py:31
  161.0 8.3 %collective-permute-start.37 = (bf16[1024,128]{1,0:T(8,128)(2,1)S(1)}, bf16[1024,128]{1,0:T(8,128)(2,1)S(1)}, u32[]{:S(2)}, u32[]{:S(2)}) collective-permute-start(bf16[1024,128]{1,0:T(8,128)(2,1)S(1)} %collective-permute-done.33.rest_2_), channel_id=1, source_target_pairs={{0,2},{2,3},{3,1},{1,0},{4,6},{6,7},{7,5},{5,4},{8,10},{10,11},{11... | collective-permute-start | bytes 786440 | tf_op jit(solution)/shard_map/ppermute | solution.py:53
  161.6 17.1 %collective-permute-start.43 = (bf16[8,1,2,128,128]{4,3,2,1,0:T(8,128)(2,1)S(1)}, bf16[8,1,2,128,128]{4,3,2,1,0:T(8,128)(2,1)S(1)}, u32[]{:S(2)}, u32[]{:S(2)}) collective-permute-start(bf16[8,1,2,128,128]{4,3,2,1,0:T(8,128)(2,1)S(1)} %get-tuple-element.75.rest_2_), channel_id=1, source_target_pairs={{0,4},{4,0},{8,12},{12,8},{16,20},{20,16},{24,28},{28,24},{1,5},{5... | collective-permute-start | bytes 1572872 | tf_op jit(solution)/shard_map/ppermute | solution.py:31
  169.3 7.4 %collective-permute-start.38 = (bf16[1024,128]{1,0:T(8,128)(2,1)S(1)}, bf16[1024,128]{1,0:T(8,128)(2,1)S(1)}, u32[]{:S(2)}, u32[]{:S(2)}) collective-permute-start(bf16[1024,128]{1,0:T(8,128)(2,1)S(1)} %shard_map.111.rest_1_), channel_id=1, source_target_pairs={{0,2},{2,3},{3,1},{1,0},{4,6},{6,7},{7,5},{5,4},{8,10},{10,11},{11... | collective-permute-start | bytes 786440 | tf_op jit(solution)/shard_map/ppermute | solution.py:53
  170.5 8.3 %collective-permute-start.41 = (bf16[4,1,2,128,128]{4,3,2,1,0:T(8,128)(2,1)S(1)}, bf16[4,1,2,128,128]{4,3,2,1,0:T(8,128)(2,1)S(1)}, u32[]{:S(2)}, u32[]{:S(2)}) collective-permute-start(bf16[4,1,2,128,128]{4,3,2,1,0:T(8,128)(2,1)S(1)} %constant_dynamic-slice_fusion.1), channel_id=1, source_target_pairs={{0,8},{4,28},{8,16},{12,4},{16,24},{20,12},{24,0},{28,20},{1,9},{5... | collective-permute-start | bytes 786440 | tf_op jit(solution)/shard_map/ppermute | solution.py:31
  171.8 6.9 %collective-permute-start.44 = (bf16[4,1,2,128,128]{4,3,2,1,0:T(8,128)(2,1)S(1)}, bf16[4,1,2,128,128]{4,3,2,1,0:T(8,128)(2,1)S(1)}, u32[]{:S(2)}, u32[]{:S(2)}) collective-permute-start(bf16[4,1,2,128,128]{4,3,2,1,0:T(8,128)(2,1)S(1)} %constant_dynamic-slice_fusion), channel_id=1, source_target_pairs={{0,4},{4,0},{8,12},{12,8},{16,20},{20,16},{24,28},{28,24},{1,5},{5... | collective-permute-start | bytes 786440 | tf_op jit(solution)/shard_map/ppermute | solution.py:31
  176.7 9.5 %collective-permute-start.40 = (bf16[1024,128]{1,0:T(8,128)(2,1)S(1)}, bf16[1024,128]{1,0:T(8,128)(2,1)S(1)}, u32[]{:S(2)}, u32[]{:S(2)}) collective-permute-start(bf16[1024,128]{1,0:T(8,128)(2,1)S(1)} %collective-permute-done.38.rest_3_), channel_id=1, source_target_pairs={{0,2},{2,3},{3,1},{1,0},{4,6},{6,7},{7,5},{5,4},{8,10},{10,11},{11... | collective-permute-start | bytes 786440 | tf_op jit(solution)/shard_map/ppermute | solution.py:53
  178.4 15.8 %collective-permute-start.39 = (bf16[1024,128]{1,0:T(8,128)(2,1)S(1)}, bf16[1024,128]{1,0:T(8,128)(2,1)S(1)}, u32[]{:S(2)}, u32[]{:S(2)}) collective-permute-start(bf16[1024,128]{1,0:T(8,128)(2,1)S(1)} %shard_map.111.rest_1_), channel_id=1, source_target_pairs={{0,1},{2,0},{3,2},{1,3},{4,5},{6,4},{7,6},{5,7},{8,9},{10,8},{11,1... | collective-permute-start | bytes 786440 | tf_op jit(solution)/shard_map/ppermute | solution.py:53
  186.2 11.2 %collective-permute-start.45 = (bf16[1024,128]{1,0:T(8,128)(2,1)S(1)}, bf16[1024,128]{1,0:T(8,128)(2,1)S(1)}, u32[]{:S(2)}, u32[]{:S(2)}) collective-permute-start(bf16[1024,128]{1,0:T(8,128)(2,1)S(1)} %shard_map.113.rest_0_), channel_id=1, source_target_pairs={{0,2},{2,3},{3,1},{1,0},{4,6},{6,7},{7,5},{5,4},{8,10},{10,11},{11... | collective-permute-start | bytes 786440 | tf_op jit(solution)/shard_map/ppermute | solution.py:53
  188.6 15.9 %collective-permute-start.46 = (bf16[1024,128]{1,0:T(8,128)(2,1)S(1)}, bf16[1024,128]{1,0:T(8,128)(2,1)S(1)}, u32[]{:S(2)}, u32[]{:S(2)}) collective-permute-start(bf16[1024,128]{1,0:T(8,128)(2,1)S(1)} %shard_map.113.rest_0_), channel_id=1, source_target_pairs={{0,1},{2,0},{3,2},{1,3},{4,5},{6,4},{7,6},{5,7},{8,9},{10,8},{11,1... | collective-permute-start | bytes 786440 | tf_op jit(solution)/shard_map/ppermute | solution.py:53
  197.4 8.4 %collective-permute-start.47 = (bf16[1024,128]{1,0:T(8,128)(2,1)S(1)}, bf16[1024,128]{1,0:T(8,128)(2,1)S(1)}, u32[]{:S(2)}, u32[]{:S(2)}) collective-permute-start(bf16[1024,128]{1,0:T(8,128)(2,1)S(1)} %collective-permute-done.45.rest_1_), channel_id=1, source_target_pairs={{0,2},{2,3},{3,1},{1,0},{4,6},{6,7},{7,5},{5,4},{8,10},{10,11},{11... | collective-permute-start | bytes 786440 | tf_op jit(solution)/shard_map/ppermute | solution.py:53
  (14 other events, 20.1 us)

commit v6 on v5

--- a/solution.py
+++ b/solution.py
@@ -12,9 +12,15 @@
 BLK = 128
 STEPS = 2
 TILE = 256
+REST_TILE = 512
+ADD_TILE = 512
 COST = 3.0
 AHEAD = 2
 C2PIN = 1
+WPAST = 0
+WPINS = (2, 3)
+SENDALL = 2
+SHARE = 0
 ATT_PINS = (3, 2)
 SEND_PIN = 2
 ATT_COST = 0.0
@@ -99,34 +105,69 @@
         kv_ref[block, at, 1] = value[rows].T.astype(jnp.bfloat16)
 
 
-def first_body(state_ref, gain_ref, wk_ref, wv_ref, kv_ref, w_scr):
+def position():
+    me, count = lax.axis_index("space"), lax.axis_size("space")
+    return lax.rem(me, 2), lax.rem(me, 2) + 2 * lax.div(me, count // 2)
+
+
+def store_first(kv_ref, facing_ref, both):
+    store_blocks(kv_ref, 0, both[:, :HD], both[:, HD:])
+
+    @pl.when(pl.program_id(0) == 1 - position()[0])
+    def _():
+        store_blocks(facing_ref, 0, both[:, :HD], both[:, HD:])
+
+
+def first_body(state_ref, gain_ref, wk_ref, wv_ref, w_out_hbm, kv_ref, facing_ref, mine_ref, w_scr, sems):
+    heads, slice_rows, _ = mine_ref.shape
+    copies = []
+    for head in range(heads):
+        rows = pl.ds(pl.multiple_of(head * HD + position()[1] * slice_rows, slice_rows), slice_rows)
+        copies.append(pltpu.make_async_copy(w_out_hbm.at[rows], mine_ref.at[head], sems.at[head]))
+
     @pl.when(pl.program_id(0) == 0)
     def _():
+        for copy in copies:
+            copy.start()
         w_scr[:, :HD] = wk_ref[...]
         w_scr[:, HD:] = wv_ref[...]
 
-    both = dot(normalize(state_ref[...].astype(jnp.float32), gain_ref[...]), w_scr[...])
-    store_blocks(kv_ref, 0, both[:, :HD], both[:, HD:])
-
-
-def first_projection(state, gain, w_key, w_value):
+    store_first(kv_ref, facing_ref, dot(normalize(state_ref[...].astype(jnp.float32), gain_ref[...]), w_scr[...]))
+
+    @pl.when(pl.program_id(0) == pl.num_programs(0) - 1)
+    def _():
+        for copy in copies:
+            copy.wait()
+
+
+def first_projection(state, gain, w_key, w_value, w_out):
     rows, width = state.shape
-    per_tile = TILE // BLK
+    half = rows // 2
+    heads = w_out.shape[0] // HD
     return call(
         first_body,
-        (rows // TILE,),
-        [
-            pl.BlockSpec((TILE, width), lambda i: (i, 0)),
+        (2,),
+        [
+            pl.BlockSpec((half, width), lambda i: (i, 0)),
             pl.BlockSpec((width,), lambda i: (0,)),
             pl.BlockSpec((width, HD), lambda i: (0, 0)),
             pl.BlockSpec((width, HD), lambda i: (0, 0)),
-        ],
-        pl.BlockSpec((per_tile, 1, 2, BLK, HD), lambda i: (i, 0, 0, 0, 0)),
-        jax.ShapeDtypeStruct((rows // BLK, 1, 2, BLK, HD), jnp.bfloat16),
+            pl.BlockSpec(memory_space=pltpu.HBM),
+        ],
+        [
+            pl.BlockSpec((half // BLK, 1, 2, BLK, HD), lambda i: (i, 0, 0, 0, 0)),
+            pl.BlockSpec((half // BLK, 1, 2, BLK, HD), lambda i: (0, 0, 0, 0, 0)),
+            pl.BlockSpec((heads, HD // 4, width), lambda i: (0, 0, 0)),
+        ],
+        [
+            jax.ShapeDtypeStruct((rows // BLK, 1, 2, BLK, HD), jnp.bfloat16),
+            jax.ShapeDtypeStruct((half // BLK, 1, 2, BLK, HD), jnp.bfloat16),
+            jax.ShapeDtypeStruct((heads, HD // 4, width), jnp.bfloat16),
+        ],
         60,
-        scratch=[pltpu.VMEM((width, 2 * HD), jnp.bfloat16)],
+        scratch=[pltpu.VMEM((width, 2 * HD), jnp.bfloat16), pltpu.SemaphoreType.DMA((heads,))],
         micros=5.0,
-    )(state, gain, w_key, w_value)
+    )(state, gain, w_key, w_value, w_out)
 
 
 def rest_body(heads, state_ref, gain_ref, wq_ref, wk_ref, wv_ref, *outs):
@@ -138,7 +179,7 @@
             cols = slice((head - 1) * HD, head * HD)
             store_blocks(kv_ref, at, key[:, cols], value[:, cols])
     query = dot(normed, wq_ref[...])
-    for block in range(TILE // BLK):
+    for block in range(REST_TILE // BLK):
         for head in range(heads):
             part = query[block * BLK : (block + 1) * BLK, head * HD : (head + 1) * HD]
             outs[-1][block, head] = part.T.astype(jnp.bfloat16)
@@ -148,13 +189,13 @@
     rows, width = state.shape
     local = w_query.shape[1]
     heads = local // HD
-    per_tile = TILE // BLK
+    per_tile = REST_TILE // BLK
     full = pl.BlockSpec((width, local), lambda i: (0, 0))
     return call(
         functools.partial(rest_body, heads),
-        (rows // TILE,),
-        [
-            pl.BlockSpec((TILE, width), lambda i: (i, 0)),
+        (rows // REST_TILE,),
+        [
+            pl.BlockSpec((REST_TILE, width), lambda i: (i, 0)),
             pl.BlockSpec((width,), lambda i: (0,)),
             full,
             full,
@@ -325,10 +366,10 @@
     rows, width = state.shape
     return call(
         functools.partial(part_body, len(pieces)),
-        (rows // TILE,),
-        [pl.BlockSpec((TILE, width), lambda i: (i, 0)), pl.BlockSpec(w_rows.shape, lambda i: (0, 0))]
-        + [pl.BlockSpec((TILE, piece.shape[1]), lambda i: (i, 0)) for piece in pieces],
-        pl.BlockSpec((TILE, width), lambda i: (i, 0)),
+        (rows // ADD_TILE,),
+        [pl.BlockSpec((ADD_TILE, width), lambda i: (i, 0)), pl.BlockSpec(w_rows.shape, lambda i: (0, 0))]
+        + [pl.BlockSpec((ADD_TILE, piece.shape[1]), lambda i: (i, 0)) for piece in pieces],
+        pl.BlockSpec((ADD_TILE, width), lambda i: (i, 0)),
         jax.ShapeDtypeStruct((rows, width), out_dtype),
         18,
         micros=PART_COST,
@@ -336,7 +377,7 @@
 
 
 def turn_body(count, part_ref, w_ref, gain_ref, wk_ref, wv_ref, *rest):
-    pieces, (state_ref, kv_ref, kv_scr) = rest[:count], rest[count:]
+    pieces, (state_ref, kv_ref, facing_ref, kv_scr) = rest[:count], rest[count:]
 
     @pl.when(pl.program_id(0) == 0)
     def _():
@@ -346,17 +387,16 @@
     attended = jnp.concatenate([piece[...] for piece in pieces], axis=1)
     state = (part_ref[...] + dot(attended, w_ref[...])).astype(jnp.bfloat16)
     state_ref[...] = state
-    both = dot(normalize(state.astype(jnp.float32), gain_ref[...]), kv_scr[...])
-    store_blocks(kv_ref, 0, both[:, :HD], both[:, HD:])
+    store_first(kv_ref, facing_ref, dot(normalize(state.astype(jnp.float32), gain_ref[...]), kv_scr[...]))
 
 
 def turn(part, w_rows, pieces, gain, w_key, w_value):
     rows, width = part.shape
-    per_tile = TILE // BLK
-    tile = pl.BlockSpec((TILE, width), lambda i: (i, 0))
+    half = rows // 2
+    tile = pl.BlockSpec((half, width), lambda i: (i, 0))
     return call(
         functools.partial(turn_body, len(pieces)),
-        (rows // TILE,),
+        (2,),
         [
             tile,
             pl.BlockSpec(w_rows.shape, lambda i: (0, 0)),
@@ -364,11 +404,16 @@
             pl.BlockSpec((width, HD), lambda i: (0, 0)),
             pl.BlockSpec((width, HD), lambda i: (0, 0)),
         ]
-        + [pl.BlockSpec((TILE, piece.shape[1]), lambda i: (i, 0)) for piece in pieces],
-        [tile, pl.BlockSpec((per_tile, 1, 2, BLK, HD), lambda i: (i, 0, 0, 0, 0))],
+        + [pl.BlockSpec((half, piece.shape[1]), lambda i: (i, 0)) for piece in pieces],
+        [
+            tile,
+            pl.BlockSpec((half // BLK, 1, 2, BLK, HD), lambda i: (i, 0, 0, 0, 0)),
+            pl.BlockSpec((half // BLK, 1, 2, BLK, HD), lambda i: (0, 0, 0, 0, 0)),
+        ],
         [
             jax.ShapeDtypeStruct((rows, width), jnp.bfloat16),
             jax.ShapeDtypeStruct((rows // BLK, 1, 2, BLK, HD), jnp.bfloat16),
+            jax.ShapeDtypeStruct((half // BLK, 1, 2, BLK, HD), jnp.bfloat16),
         ],
         18,
         scratch=[pltpu.VMEM((width, 2 * HD), jnp.bfloat16)],
@@ -381,17 +426,9 @@
     return lax.dynamic_slice_in_dim(kv, half * (1 - lax.axis_index("space") % 2), half, 0)
 
 
-def halo(kv):
-    return sent(kv, across), sent(facing(kv), beyond), sent(kv, beside)
-
-
-def fetch_rows(w_out, then):
-    half = lax.axis_size("space") // 2
-    local, width = w_out.shape
-    me = lax.axis_index("space")
-    quarters = w_out.reshape(local // HD, 4, HD // 4, width)
-    mine = lax.dynamic_index_in_dim(quarters, me % 2 + 2 * (me // half), 1, keepdims=False)
-    return around(after(mine, then), "head")[1:]
+def halo(kv, faces=None):
+    faces = facing(kv) if faces is None else faces
+    return sent(kv, across), sent(faces, beyond), sent(kv, beside)
 
 
 def share_rows(w_out, fetched, then):
@@ -426,16 +463,16 @@
     turn_by = jnp.where(place < half, end, jnp.where(place >= end, -end, turn_by))
     where_block = jnp.where(me % 2 == 1, place + turn_by, place).reshape(-1)
     state = snapshot
-    kv_first = first_projection(state, norm_gain, w_key, w_value)
+    kv_first, faces, mine = first_projection(state, norm_gain, w_key, w_value, w_out)
     last = []
     for rollout in range(STEPS):
-        near = [halo(kv_first)]
+        near = [halo(kv_first, faces)]
         *kv_rest, queries = rest_projection(state, norm_gain, w_query, w_key, w_value, REST_VMEM[rollout])
         kv = [kv_first] + list(kv_rest)
         near += [halo(piece) for piece in kv_rest]
         if rollout == 0:
-            fetched = fetch_rows(w_out, kv_first)
-            queries = after(queries, *fetched[:2])
+            fetched = around(mine, "head")[1:]
+            queries = after(queries, *fetched[:WPAST])
         past, stats = attend_past(queries, cache_key, cache_value, last)
         came = []
         attended = past
@@ -444,16 +481,16 @@
             held = (attended, further) if chunk == 0 and rollout >= C2PIN else (attended,)
             shared = sent(facing(after(next_pair, *held)), beside)
             own = kv[chunk]
-            if chunk == 0 and rollout == 0:
-                own = after(own, *fetched)
+            if chunk < 2 and rollout == 0:
+                own = after(own, *fetched[: WPINS[chunk]])
             if chunk >= 1:
                 own = after(own, *came[-1][1 : ATT_PINS[chunk - 1]])
             pieces = (further, next_pair, own, other, shared)
             attended = attend(of_chunk, where_block, counts, queries, past, stats, pieces)
-            if rollout == 0 and chunk == 0:
+            if rollout == 0 and chunk == SHARE:
                 fetched = [after(piece, attended) for piece in fetched]
             if 1 <= chunk <= SEND_PIN:
-                attended = after(attended, came[-1][-1])
+                attended = after(attended, *came[-1][SENDALL:])
             came.append(around(attended, "head", came[-1][2:] if came else ()))
         if rollout == 0:
             rows_of = share_rows(w_out, fetched, came[-1][1])
@@ -463,7 +500,7 @@
         early = [piece for group in zip(*came[:-1], strict=True) for piece in group]
         part = add_heads(state, w_early, early, jnp.float32)
         if rollout + 1 < STEPS:
-            state, kv_first = turn(part, w_last, came[-1], norm_gain, w_key, w_value)
+            state, kv_first, faces = turn(part, w_last, came[-1], norm_gain, w_key, w_value)
             last = kv
         else:
             state = add_heads(part, w_last, came[-1], jnp.bfloat16)

time: 210 us -> 204 us (0.971)
  waiting for transfers between devices: 71.1 us -> 76.2 us
  Pallas kernels: 73.3 us -> 68.3 us
  starting transfers between devices: 46 us -> 42.8 us
  local copies, waits for them, and re-layouts: 13.4 us -> 10.7 us
    pallas_call x7, Pallas kernels: 36.6 us -> 32.3 us  [the longest x2 11.9 us: rest_projection(): call(functools.partial(rest_body, heads), (rows // REST_TILE,), [pl.Block...]
    ppermute x21, waiting for transfers between devices: 59.6 us -> 62.7 us  [turned(): lax.ppermute(value, axis, [(order[i], order[(i + hops) % count]) for i in...]
    dynamic_slice x12 -> x10, local copies, waits for them, and re-layouts: 4.56 us -> 2.86 us  [facing(): lax.dynamic_slice_in_dim(kv, half * (1 - lax.axis_index('space') % 2), ha...]
    unnamed x60 -> x64, local copies, waits for them, and re-layouts: 7.62 us -> 7.38 us
  transfers between devices with their start and end apart: 48 -> 48, of which waited for: 21 -> 21; matrix products, arithmetic and copies ran while one was open for 5% -> 4% of each run, Pallas kernels for 28% -> 27%
where the time goes in v6:
time: 204 us
  waiting for transfers between devices  76.2 us (37%)
  Pallas kernels  68.3 us (33%)
  starting transfers between devices  42.8 us (21%)
  local copies, waits for them, and re-layouts  10.7 us (5%)
  other arithmetic  5.01 us (2%)
    ppermute x21, waiting for transfers between devices, turned(): lax.ppermute(value, axis, [(order[i], order[(i + hops) % count]) for i in...  62.7 us
    ppermute x21, starting transfers between devices, turned(): lax.ppermute(value, axis, [(order[i], order[(i + hops) % count]) for i in...  27.4 us
    pallas_call x6, Pallas kernels, attend(): call(functools.partial(attend_body, blocks, slots, inner), (1,), [of_head...  21.5 us
    ppermute x27, starting transfers between devices, sent(): lax.ppermute(value, 'space', [(i, to(i, count) % count) for i in range(co...  15.4 us
    pallas_call x2, Pallas kernels, attend_past(): call(functools.partial(past_body, frames, heads, len(last) > 0), (blocks...  14.5 us
    ppermute x27, waiting for transfers between devices, sent(): lax.ppermute(value, 'space', [(i, to(i, count) % count) for i in range(co...  13.4 us
    pallas_call x2, Pallas kernels, rest_projection(): call(functools.partial(rest_body, heads), (rows // REST_TILE,), [pl.Block...  11.9 us
    pallas_call x3, Pallas kernels, add_heads(): call(functools.partial(part_body, len(pieces)), (rows // ADD_TILE,), [pl....  10.3 us
  transfers between devices with their start and end apart: 48, of which 21 were waited for; matrix products, arithmetic and copies ran while one was open for 4% of the time, Pallas kernels for 27%

profile of v6, /device:TPU:0, one launch (start us, length us, event | category | flops | bytes accessed | tf_op | source)
XLA Modules:
  0.0 203.5 jit_solution(7350895406864351693)
XLA Ops:
  0.0 4.6 %shard_map.100 = (bf16[8,1,2,128,128]{4,3,2,1,0:T(8,128)(2,1)}, bf16[4,1,2,128,128]{4,3,2,1,0:T(8,128)(2,1)}, bf16[3,32,1536]{2,1,0:T(8,128)(2,1)}) custom-call(bf16[1024,1536]{1,0:T(8,128)(2,1)} %state_ref.5, f32[1536]{0:T(1024)} %gain_ref.7, bf16[1536,384]{1,0:T(8,128)(2,1)} %wk_ref.7, bf16[1536,384]{1,0:T(8,128)(2,1)} %wv_ref.7, bf16[384,1536]{1,0:T(8,128)(2,1)} %w_out_hbm.1), custom_call_target="tpu_custom_call" | custom-call | flops 17250000896 | tf_op jit(solution)/shard_map/pallas_call | solution.py:147
  4.7 4.1 %collective-permute-start = (bf16[3,32,1536]{2,1,0:T(8,128)(2,1)}, bf16[3,32,1536]{2,1,0:T(8,128)(2,1)}, u32[]{:S(2)}, u32[]{:S(2)}) collective-permute-start(bf16[3,32,1536]{2,1,0:T(8,128)(2,1)} %get-tuple-element.45), channel_id=1, source_target_pairs={{0,2},{2,3},{3,1},{1,0},{4,6},{6,7},{7,5},{5,4},{8,10},{10,11},{11... | collective-permute-start | bytes 884744 | tf_op jit(solution)/shard_map/ppermute | solution.py:59
  8.7 1.6 collective-permute-start.2
  10.4 1.5 collective-permute-start.1
  11.8 7.5 %shard_map.101 = (bf16[8,1,2,128,128]{4,3,2,1,0:T(8,128)(2,1)}, bf16[8,1,2,128,128]{4,3,2,1,0:T(8,128)(2,1)}, bf16[8,3,128,128]{3,2,1,0:T(8,128)(2,1)}) custom-call(bf16[1024,1536]{1,0:T(8,128)(2,1)} %state_ref.5, f32[1536]{0:T(1024)} %gain_ref.7, bf16[1536,384]{1,0:T(8,128)(2,1)} %wq_ref.3, bf16[1536,384]{1,0:T(8,128)(2,1)} %wk_ref.7, bf16[1536,384]{1,0:T(8,128)(2,1)} %wv_ref.7), custom_call_target="tpu_custom_call" | custom-call | flops 17250000896 | tf_op jit(solution)/shard_map/pallas_call | solution.py:194
  19.4 1.1 copy-done
  20.5 7.3 %shard_map.102 = (f32[8,3,128,128]{3,2,1,0:T(8,128)S(1)}, f32[8,3,2,128]{3,2,1,0:T(2,128)S(1)}) custom-call(bf16[8,3,128,128]{3,2,1,0:T(8,128)(2,1)S(1)} %copy-done, bf16[8,1024,384]{2,1,0:T(8,128)(2,1)} %ck_hbm.3, bf16[8,1024,384]{2,1,0:T(8,128)(2,1)} %cv_hbm.3), custom_call_target="tpu_custom_call" | custom-call | flops 20700000256 | tf_op jit(solution)/shard_map/pallas_call | solution.py:276
  27.9 0.9 collective-permute-start.11
  28.7 1.8 constant_dynamic-slice_fusion.9
  31.3 2.9 %collective-permute-start.6 = (bf16[3,32,1536]{2,1,0:T(8,128)(2,1)}, bf16[3,32,1536]{2,1,0:T(8,128)(2,1)}, u32[]{:S(2)}, u32[]{:S(2)}) collective-permute-start(bf16[3,32,1536]{2,1,0:T(8,128)(2,1)} %collective-permute-done), channel_id=1, source_target_pairs={{0,2},{2,3},{3,1},{1,0},{4,6},{6,7},{7,5},{5,4},{8,10},{10,11},{11... | collective-permute-start | bytes 884744 | tf_op jit(solution)/shard_map/ppermute | solution.py:59
  34.5 1.0 copy-done.9
  35.6 4.4 %shard_map.103.rest_0_ = bf16[1024,128]{1,0:T(8,128)(2,1)S(1)} custom-call(s32[64]{0:T(128)S(1)} %reshape.21.where_ref, s32[8]{0:T(128)S(1)} %copy-done.25, bf16[8,3,128,128]{3,2,1,0:T(8,128)(2,1)S(1)} %copy-done.1, f32[8,3,128,128]{3,2,1,0:T(8,128)S(1)} %get-tuple-element.47.acc_ref, f32[8,3,2,128]{3,2,1,0:T(2,128)S(1)} %get-tuple-element.48.stat_ref, ...), custom_call_target="tpu_custom_call" | custom-call | tf_op jit(solution)/shard_map/pallas_call | solution.py:342
  40.0 1.3 collective-permute-start.12
  42.1 1.0 collective-permute-done.11.rest_1_
  43.6 1.0 constant_dynamic-slice_fusion.6
  45.5 3.4 %collective-permute-done.12.rest_2_ = bf16[1024,128]{1,0:T(8,128)(2,1)S(1)} collective-permute-done((bf16[1024,128]{1,0:T(8,128)(2,1)S(1)}, bf16[1024,128]{1,0:T(8,128)(2,1)S(1)}, u32[]{:S(2)}, u32[]{:S(2)}) %collective-permute-start.12) | collective-permute-done | bytes 262176 | tf_op jit(solution)/shard_map/ppermute | solution.py:59
  48.9 5.9 %collective-permute-done.13.rest_4_ = bf16[1024,128]{1,0:T(8,128)(2,1)S(1)} collective-permute-done((bf16[1024,128]{1,0:T(8,128)(2,1)S(1)}, bf16[1024,128]{1,0:T(8,128)(2,1)S(1)}, u32[]{:S(2)}, u32[]{:S(2)}) %collective-permute-start.13) | collective-permute-done | bytes 262176 | tf_op jit(solution)/shard_map/ppermute | solution.py:59
  56.1 2.1 %pad_maximum_fusion.2 = bf16[3,3,32,1536]{3,2,1,0:T(8,128)(2,1)} fusion(bf16[1,3,32,1536]{3,2,1,0:T(8,128)(2,1)} %bitcast.3, bf16[1,3,32,1536]{3,2,1,0:T(8,128)(2,1)} %bitcast.2, bf16[1,3,32,1536]{3,2,1,0:T(8,128)(2,1)} %bitcast.1), kind=kLoop, calls=%fused_computation.5 | loop fusion | flops 884736 | bytes 1769472 | tf_op jit(solution)/shard_map/stack | solution.py:435
  58.8 4.1 %shard_map.104.rest_1_ = bf16[1024,128]{1,0:T(8,128)(2,1)S(1)} custom-call(s32[64]{0:T(128)S(1)} %reshape.21.where_ref, s32[8]{0:T(128)S(1)} %copy-done.25, bf16[8,3,128,128]{3,2,1,0:T(8,128)(2,1)S(1)} %copy-done.1, f32[8,3,128,128]{3,2,1,0:T(8,128)S(1)} %get-tuple-element.47.acc_ref, f32[8,3,2,128]{3,2,1,0:T(2,128)S(1)} %get-tuple-element.48.stat_ref, ...), custom_call_target="tpu_custom_call" | custom-call | tf_op jit(solution)/shard_map/pallas_call | solution.py:342
  63.7 1.8 collective-permute-start.17
  65.5 1.5 collective-permute-start.8
  67.1 5.1 %collective-permute-done.17.rest_3_ = bf16[1024,128]{1,0:T(8,128)(2,1)S(1)} collective-permute-done((bf16[1024,128]{1,0:T(8,128)(2,1)S(1)}, bf16[1024,128]{1,0:T(8,128)(2,1)S(1)}, u32[]{:S(2)}, u32[]{:S(2)}) %collective-permute-start.17) | collective-permute-done | bytes 262176 | tf_op jit(solution)/shard_map/ppermute | solution.py:59
  72.2 2.5 %collective-permute-done.8.rest_0_ = bf16[4,1,2,128,128]{4,3,2,1,0:T(8,128)(2,1)S(1)} collective-permute-done((bf16[4,1,2,128,128]{4,3,2,1,0:T(8,128)(2,1)S(1)}, bf16[4,1,2,128,128]{4,3,2,1,0:T(8,128)(2,1)S(1)}, u32[]{:S(2)}, u32[]{:S(2)}) %collective-permute-start.8) | collective-permute-done | bytes 262176 | tf_op jit(solution)/shard_map/ppermute | solution.py:37
  74.7 1.1 collective-permute-start.21
  75.9 3.2 %shard_map.105.rest_0_ = bf16[1024,128]{1,0:T(8,128)(2,1)S(1)} custom-call(s32[64]{0:T(128)S(1)} %reshape.21.where_ref, s32[8]{0:T(128)S(1)} %copy-done.25, bf16[8,3,128,128]{3,2,1,0:T(8,128)(2,1)S(1)} %copy-done.1, f32[8,3,128,128]{3,2,1,0:T(8,128)S(1)} %get-tuple-element.47.acc_ref, f32[8,3,2,128]{3,2,1,0:T(2,128)S(1)} %get-tuple-element.48.stat_ref, ...), custom_call_target="tpu_custom_call" | custom-call | tf_op jit(solution)/shard_map/pallas_call | solution.py:342
  79.9 4.5 %collective-permute-done.21.rest_7_ = bf16[1024,128]{1,0:T(8,128)(2,1)S(1)} collective-permute-done((bf16[1024,128]{1,0:T(8,128)(2,1)S(1)}, bf16[1024,128]{1,0:T(8,128)(2,1)S(1)}, u32[]{:S(2)}, u32[]{:S(2)}) %collective-permute-start.21) | collective-permute-done | bytes 262176 | tf_op jit(solution)/shard_map/ppermute | solution.py:59
  85.1 1.6 collective-permute-start.22
  86.8 6.6 %collective-permute-done.22.rest_1_ = bf16[1024,128]{1,0:T(8,128)(2,1)S(1)} collective-permute-done((bf16[1024,128]{1,0:T(8,128)(2,1)S(1)}, bf16[1024,128]{1,0:T(8,128)(2,1)S(1)}, u32[]{:S(2)}, u32[]{:S(2)}) %collective-permute-start.22) | collective-permute-done | bytes 262176 | tf_op jit(solution)/shard_map/ppermute | solution.py:59
  93.4 1.3 collective-permute-start.25
  94.7 1.6 collective-permute-start.26
  96.3 1.8 select_bitcast_fusion.3
  99.0 0.9 copy-done.30
  100.3 1.5 copy-done.2
  102.4 3.6 %shard_map.106.part_ref = f32[1024,1536]{1,0:T(8,128)S(1)} custom-call(bf16[1024,1536]{1,0:T(8,128)(2,1)S(1)} %copy-done.2, bf16[1024,1536]{1,0:T(8,128)(2,1)S(1)} %bitcast.15, bf16[1024,128]{1,0:T(8,128)(2,1)S(1)} %copy-done.6, bf16[1024,128]{1,0:T(8,128)(2,1)S(1)} %copy-done.8, bf16[1024,128]{1,0:T(8,128)(2,1)S(1)} %copy-done.12, ...), custom_call_target="tpu_custom_call" | custom-call | tf_op jit(solution)/shard_map/pallas_call | solution.py:367
  106.2 2.6 %collective-permute-done.26.rest_3_ = bf16[1024,128]{1,0:T(8,128)(2,1)S(1)} collective-permute-done((bf16[1024,128]{1,0:T(8,128)(2,1)S(1)}, bf16[1024,128]{1,0:T(8,128)(2,1)S(1)}, u32[]{:S(2)}, u32[]{:S(2)}) %collective-permute-start.26) | collective-permute-done | bytes 262176 | tf_op jit(solution)/shard_map/ppermute | solution.py:59
  108.8 5.4 %shard_map.107 = (bf16[1024,1536]{1,0:T(8,128)(2,1)S(1)}, bf16[8,1,2,128,128]{4,3,2,1,0:T(8,128)(2,1)S(1)}, bf16[4,1,2,128,128]{4,3,2,1,0:T(8,128)(2,1)S(1)}) custom-call(f32[1024,1536]{1,0:T(8,128)S(1)} %shard_map.106.part_ref, bf16[512,1536]{1,0:T(8,128)(2,1)S(1)} %bitcast.17, f32[1536]{0:T(1024)S(1)} %copy-done.29, bf16[1536,384]{1,0:T(8,128)(2,1)S(1)} %copy-done.26, ...), custom_call_target="tpu_custom_call" | custom-call | flops 24149999616 | tf_op jit(solution)/shard_map/pallas_call | solution.py:397
  114.2 1.2 collective-permute-start.28
  115.9 4.4 %shard_map.108 = (bf16[8,1,2,128,128]{4,3,2,1,0:T(8,128)(2,1)S(1)}, bf16[8,1,2,128,128]{4,3,2,1,0:T(8,128)(2,1)S(1)}, bf16[8,3,128,128]{3,2,1,0:T(8,128)(2,1)S(1)}) custom-call(bf16[1024,1536]{1,0:T(8,128)(2,1)S(1)} %get-tuple-element.68.state_ref, f32[1536]{0:T(1024)S(1)} %copy-done.29, bf16[1536,384]{1,0:T(8,128)(2,1)S(1)} %copy-done.28, ...), custom_call_target="tpu_custom_call" | custom-call | flops 17250000896 | tf_op jit(solution)/shard_map/pallas_call | solution.py:194
  120.3 1.8 collective-permute-start.27
  122.1 7.2 %shard_map.109 = (f32[8,3,128,128]{3,2,1,0:T(8,128)S(1)}, f32[8,3,2,128]{3,2,1,0:T(2,128)S(1)}) custom-call(bf16[8,3,128,128]{3,2,1,0:T(8,128)(2,1)S(1)} %get-tuple-element.69.qt_ref, bf16[8,1024,384]{2,1,0:T(8,128)(2,1)} %ck_hbm.3, bf16[8,1024,384]{2,1,0:T(8,128)(2,1)} %cv_hbm.3, bf16[8,1,2,128,128]{4,3,2,1,0:T(8,128)(2,1)S(1)} %copy-done.10, ...), custom_call_target="tpu_custom_call" | custom-call | flops 20700000256 | tf_op jit(solution)/shard_map/pallas_call | solution.py:276
  130.0 5.3 %collective-permute-done.27.rest_0_ = bf16[4,1,2,128,128]{4,3,2,1,0:T(8,128)(2,1)S(1)} collective-permute-done((bf16[4,1,2,128,128]{4,3,2,1,0:T(8,128)(2,1)S(1)}, bf16[4,1,2,128,128]{4,3,2,1,0:T(8,128)(2,1)S(1)}, u32[]{:S(2)}, u32[]{:S(2)}) %collective-permute-start.27) | collective-permute-done | bytes 262176 | tf_op jit(solution)/shard_map/ppermute | solution.py:37
  135.4 1.5 collective-permute-done.30.rest_4_
  136.9 3.2 %shard_map.110.rest_0_ = bf16[1024,128]{1,0:T(8,128)(2,1)S(1)} custom-call(s32[64]{0:T(128)S(1)} %reshape.21.where_ref, s32[8]{0:T(128)S(1)} %copy-done.25, bf16[8,3,128,128]{3,2,1,0:T(8,128)(2,1)S(1)} %get-tuple-element.69.qt_ref, f32[8,3,128,128]{3,2,1,0:T(8,128)S(1)} %get-tuple-element.70.acc_ref, f32[8,3,2,128]{3,2,1,0:T(2,128)S(1)} %get-tuple-element.71.stat_ref, ...), custom_call_target="tpu_custom_call" | custom-call | tf_op jit(solution)/shard_map/pallas_call | solution.py:342
  140.1 1.2 collective-permute-start.33
  141.3 0.9 collective-permute-start.34
  142.8 3.1 %collective-permute-done.32.rest_1_ = bf16[8,1,2,128,128]{4,3,2,1,0:T(8,128)(2,1)S(1)} collective-permute-done((bf16[8,1,2,128,128]{4,3,2,1,0:T(8,128)(2,1)S(1)}, bf16[8,1,2,128,128]{4,3,2,1,0:T(8,128)(2,1)S(1)}, u32[]{:S(2)}, u32[]{:S(2)}) %collective-permute-start.32) | collective-permute-done | bytes 524320 | tf_op jit(solution)/shard_map/ppermute | solution.py:37
  146.0 1.7 collective-permute-start.42
  147.7 1.0 collective-permute-done.33.rest_2_
  148.6 6.6 %collective-permute-done.34.rest_4_ = bf16[1024,128]{1,0:T(8,128)(2,1)S(1)} collective-permute-done((bf16[1024,128]{1,0:T(8,128)(2,1)S(1)}, bf16[1024,128]{1,0:T(8,128)(2,1)S(1)}, u32[]{:S(2)}, u32[]{:S(2)}) %collective-permute-start.34) | collective-permute-done | bytes 262176 | tf_op jit(solution)/shard_map/ppermute | solution.py:59
  155.9 3.2 %shard_map.111.rest_1_ = bf16[1024,128]{1,0:T(8,128)(2,1)S(1)} custom-call(s32[64]{0:T(128)S(1)} %reshape.21.where_ref, s32[8]{0:T(128)S(1)} %copy-done.25, bf16[8,3,128,128]{3,2,1,0:T(8,128)(2,1)S(1)} %get-tuple-element.69.qt_ref, f32[8,3,128,128]{3,2,1,0:T(8,128)S(1)} %get-tuple-element.70.acc_ref, f32[8,3,2,128]{3,2,1,0:T(2,128)S(1)} %get-tuple-element.71.stat_ref, ...), custom_call_target="tpu_custom_call" | custom-call | tf_op jit(solution)/shard_map/pallas_call | solution.py:342
  159.2 4.4 %collective-permute-done.37.rest_6_ = bf16[1024,128]{1,0:T(8,128)(2,1)S(1)} collective-permute-done((bf16[1024,128]{1,0:T(8,128)(2,1)S(1)}, bf16[1024,128]{1,0:T(8,128)(2,1)S(1)}, u32[]{:S(2)}, u32[]{:S(2)}) %collective-permute-start.37) | collective-permute-done | bytes 262176 | tf_op jit(solution)/shard_map/ppermute | solution.py:59
  163.6 1.2 collective-permute-start.38
  166.0 6.7 %collective-permute-done.38.rest_3_ = bf16[1024,128]{1,0:T(8,128)(2,1)S(1)} collective-permute-done((bf16[1024,128]{1,0:T(8,128)(2,1)S(1)}, bf16[1024,128]{1,0:T(8,128)(2,1)S(1)}, u32[]{:S(2)}, u32[]{:S(2)}) %collective-permute-start.38) | collective-permute-done | bytes 262176 | tf_op jit(solution)/shard_map/ppermute | solution.py:59
  172.7 2.2 %collective-permute-start.40 = (bf16[1024,128]{1,0:T(8,128)(2,1)S(1)}, bf16[1024,128]{1,0:T(8,128)(2,1)S(1)}, u32[]{:S(2)}, u32[]{:S(2)}) collective-permute-start(bf16[1024,128]{1,0:T(8,128)(2,1)S(1)} %collective-permute-done.38.rest_3_), channel_id=1, source_target_pairs={{0,2},{2,3},{3,1},{1,0},{4,6},{6,7},{7,5},{5,4},{8,10},{10,11},{11... | collective-permute-start | bytes 786440 | tf_op jit(solution)/shard_map/ppermute | solution.py:59
  174.9 3.2 %shard_map.113.rest_0_ = bf16[1024,128]{1,0:T(8,128)(2,1)S(1)} custom-call(s32[64]{0:T(128)S(1)} %reshape.21.where_ref, s32[8]{0:T(128)S(1)} %copy-done.25, bf16[8,3,128,128]{3,2,1,0:T(8,128)(2,1)S(1)} %get-tuple-element.69.qt_ref, f32[8,3,128,128]{3,2,1,0:T(8,128)S(1)} %get-tuple-element.70.acc_ref, f32[8,3,2,128]{3,2,1,0:T(2,128)S(1)} %get-tuple-element.71.stat_ref, ...), custom_call_target="tpu_custom_call" | custom-call | tf_op jit(solution)/shard_map/pallas_call | solution.py:342
  178.2 1.5 collective-permute-done.39.rest_5_
  179.6 2.6 %collective-permute-done.40.rest_7_ = bf16[1024,128]{1,0:T(8,128)(2,1)S(1)} collective-permute-done((bf16[1024,128]{1,0:T(8,128)(2,1)S(1)}, bf16[1024,128]{1,0:T(8,128)(2,1)S(1)}, u32[]{:S(2)}, u32[]{:S(2)}) %collective-permute-start.40) | collective-permute-done | bytes 262176 | tf_op jit(solution)/shard_map/ppermute | solution.py:59
  182.2 1.8 collective-permute-start.45
  184.3 8.5 %collective-permute-done.45.rest_1_ = bf16[1024,128]{1,0:T(8,128)(2,1)S(1)} collective-permute-done((bf16[1024,128]{1,0:T(8,128)(2,1)S(1)}, bf16[1024,128]{1,0:T(8,128)(2,1)S(1)}, u32[]{:S(2)}, u32[]{:S(2)}) %collective-permute-start.45) | collective-permute-done | bytes 262176 | tf_op jit(solution)/shard_map/ppermute | solution.py:59
  192.8 1.4 collective-permute-start.47
  194.1 3.6 %shard_map.112.state_ref = f32[1024,1536]{1,0:T(8,128)S(1)} custom-call(bf16[1024,1536]{1,0:T(8,128)(2,1)S(1)} %get-tuple-element.68.state_ref, bf16[1024,1536]{1,0:T(8,128)(2,1)S(1)} %bitcast.16, bf16[1024,128]{1,0:T(8,128)(2,1)S(1)} %shard_map.110.rest_0_, bf16[1024,128]{1,0:T(8,128)(2,1)S(1)} %shard_map.111.rest_1_, ...), custom_call_target="tpu_custom_call" | custom-call | tf_op jit(solution)/shard_map/pallas_call | solution.py:367
  197.7 0.9 collective-permute-done.46.rest_2_
  198.6 1.8 collective-permute-done.47.rest_3_
  200.4 3.1 %shard_map.114 = bf16[1024,1536]{1,0:T(8,128)(2,1)} custom-call(f32[1024,1536]{1,0:T(8,128)S(1)} %shard_map.112.state_ref, bf16[512,1536]{1,0:T(8,128)(2,1)S(1)} %bitcast.18, bf16[1024,128]{1,0:T(8,128)(2,1)S(1)} %shard_map.113.rest_0_, bf16[1024,128]{1,0:T(8,128)(2,1)S(1)} %collective-permute-done.45.rest_1_, ...), custom_call_target="tpu_custom_call" | custom-call | tf_op jit(solution)/shard_map/pallas_call | solution.py:367
  (130 shorter events, 13.6 us)
Async XLA Ops:
  4.7 25.8 %collective-permute-start = (bf16[3,32,1536]{2,1,0:T(8,128)(2,1)}, bf16[3,32,1536]{2,1,0:T(8,128)(2,1)}, u32[]{:S(2)}, u32[]{:S(2)}) collective-permute-start(bf16[3,32,1536]{2,1,0:T(8,128)(2,1)} %get-tuple-element.45), channel_id=1, source_target_pairs={{0,2},{2,3},{3,1},{1,0},{4,6},{6,7},{7,5},{5,4},{8,10},{10,11},{11... | collective-permute-start | bytes 884744 | tf_op jit(solution)/shard_map/ppermute | solution.py:59
  8.7 22.5 %collective-permute-start.3 = (bf16[3,32,1536]{2,1,0:T(8,128)(2,1)}, bf16[3,32,1536]{2,1,0:T(8,128)(2,1)}, u32[]{:S(2)}, u32[]{:S(2)}) collective-permute-start(bf16[3,32,1536]{2,1,0:T(8,128)(2,1)} %get-tuple-element.45), channel_id=1, source_target_pairs={{0,1},{2,0},{3,2},{1,3},{4,5},{6,4},{7,6},{5,7},{8,9},{10,8},{11,1... | collective-permute-start | bytes 884744 | tf_op jit(solution)/shard_map/ppermute | solution.py:59
  8.7 19.1 %collective-permute-start.2 = (bf16[8,1,2,128,128]{4,3,2,1,0:T(8,128)(2,1)}, bf16[8,1,2,128,128]{4,3,2,1,0:T(8,128)(2,1)}, u32[]{:S(2)}, u32[]{:S(2)}) collective-permute-start(bf16[8,1,2,128,128]{4,3,2,1,0:T(8,128)(2,1)} %get-tuple-element.51.rest_2_.rest_0_), channel_id=1, source_target_pairs={{0,28},{4,8},{8,4},{12,16},{16,12},{20,24},{24,20},{28,0},{1,29},{... | collective-permute-start | bytes 1572872 | tf_op jit(solution)/shard_map/ppermute | solution.py:37
  10.4 24.1 %collective-permute-start.4 = (bf16[8,1,2,128,128]{4,3,2,1,0:T(8,128)(2,1)}, bf16[8,1,2,128,128]{4,3,2,1,0:T(8,128)(2,1)}, u32[]{:S(2)}, u32[]{:S(2)}) collective-permute-start(bf16[8,1,2,128,128]{4,3,2,1,0:T(8,128)(2,1)} %get-tuple-element.51.rest_2_.rest_0_), channel_id=1, source_target_pairs={{0,4},{4,0},{8,12},{12,8},{16,20},{20,16},{24,28},{28,24},{1,5},{5... | collective-permute-start | bytes 1572872 | tf_op jit(solution)/shard_map/ppermute | solution.py:37
  10.4 24.0 %collective-permute-start.1 = (bf16[4,1,2,128,128]{4,3,2,1,0:T(8,128)(2,1)}, bf16[4,1,2,128,128]{4,3,2,1,0:T(8,128)(2,1)}, u32[]{:S(2)}, u32[]{:S(2)}) collective-permute-start(bf16[4,1,2,128,128]{4,3,2,1,0:T(8,128)(2,1)} %get-tuple-element.49), channel_id=1, source_target_pairs={{0,8},{4,28},{8,16},{12,4},{16,24},{20,12},{24,0},{28,20},{1,9},{5... | collective-permute-start | bytes 786440 | tf_op jit(solution)/shard_map/ppermute | solution.py:37
  20.5 7.3 %copy-start.3 = (bf16[8,1,2,128,128]{4,3,2,1,0:T(8,128)(2,1)S(1)}, bf16[8,1,2,128,128]{4,3,2,1,0:T(8,128)(2,1)}, u32[]{:S(2)}) copy-start(bf16[8,1,2,128,128]{4,3,2,1,0:T(8,128)(2,1)} %get-tuple-element.59.rest_2_.rest_1_) | copy-start | bytes 1572868
  20.5 13.7 %copy-start.31 = (s32[8,8]{1,0:T(8,128)S(1)}, s32[8,8]{1,0:T(8,128)}, u32[]{:S(2)}) copy-start(s32[8,8]{1,0:T(8,128)} %param.18) | copy-start | bytes 772
  20.5 14.0 %copy-start.1 = (bf16[8,3,128,128]{3,2,1,0:T(8,128)(2,1)S(1)}, bf16[8,3,128,128]{3,2,1,0:T(8,128)(2,1)}, u32[]{:S(2)}) copy-start(bf16[8,3,128,128]{3,2,1,0:T(8,128)(2,1)} %get-tuple-element.46.qt_ref) | copy-start | bytes 2359300
  20.5 14.0 %copy-start.25 = (s32[8]{0:T(128)S(1)}, s32[8]{0:T(128)}, u32[]{:S(2)}) copy-start(s32[8]{0:T(128)} %counts_ref.11) | copy-start | bytes 100
  27.9 15.2 %collective-permute-start.11 = (bf16[8,1,2,128,128]{4,3,2,1,0:T(8,128)(2,1)S(1)}, bf16[8,1,2,128,128]{4,3,2,1,0:T(8,128)(2,1)}, u32[]{:S(2)}, u32[]{:S(2)}) collective-permute-start(bf16[8,1,2,128,128]{4,3,2,1,0:T(8,128)(2,1)S(1)} %copy-done.3), channel_id=1, source_target_pairs={{0,28},{4,8},{8,4},{12,16},{16,12},{20,24},{24,20},{28,0},{1,29},{... | collective-permute-start | bytes 1572872 | tf_op jit(solution)/shard_map/ppermute | solution.py:37
  28.7 15.9 %copy-start.4 = (bf16[8,1,2,128,128]{4,3,2,1,0:T(8,128)(2,1)S(1)}, bf16[8,1,2,128,128]{4,3,2,1,0:T(8,128)(2,1)}, u32[]{:S(2)}) copy-start(bf16[8,1,2,128,128]{4,3,2,1,0:T(8,128)(2,1)} %get-tuple-element.62.rest_2_) | copy-start | bytes 1572868
  30.5 4.0 %collective-permute-start.5 = (bf16[4,1,2,128,128]{4,3,2,1,0:T(8,128)(2,1)}, bf16[4,1,2,128,128]{4,3,2,1,0:T(8,128)(2,1)}, u32[]{:S(2)}, u32[]{:S(2)}) collective-permute-start(bf16[4,1,2,128,128]{4,3,2,1,0:T(8,128)(2,1)} %constant_dynamic-slice_fusion.9), channel_id=1, source_target_pairs={{0,4},{4,0},{8,12},{12,8},{16,20},{20,16},{24,28},{28,24},{1,5},{5... | collective-permute-start | bytes 786440 | tf_op jit(solution)/shard_map/ppermute | solution.py:37
  31.3 13.3 %collective-permute-start.6 = (bf16[3,32,1536]{2,1,0:T(8,128)(2,1)}, bf16[3,32,1536]{2,1,0:T(8,128)(2,1)}, u32[]{:S(2)}, u32[]{:S(2)}) collective-permute-start(bf16[3,32,1536]{2,1,0:T(8,128)(2,1)} %collective-permute-done), channel_id=1, source_target_pairs={{0,2},{2,3},{3,1},{1,0},{4,6},{6,7},{7,5},{5,4},{8,10},{10,11},{11... | collective-permute-start | bytes 884744 | tf_op jit(solution)/shard_map/ppermute | solution.py:59
  34.4 23.9 %collective-permute-start.14 = (bf16[8,1,2,128,128]{4,3,2,1,0:T(8,128)(2,1)S(1)}, bf16[8,1,2,128,128]{4,3,2,1,0:T(8,128)(2,1)S(1)}, u32[]{:S(2)}, u32[]{:S(2)}) collective-permute-start(bf16[8,1,2,128,128]{4,3,2,1,0:T(8,128)(2,1)S(1)} %copy-done.3), channel_id=1, source_target_pairs={{0,4},{4,0},{8,12},{12,8},{16,20},{20,16},{24,28},{28,24},{1,5},{5... | collective-permute-start | bytes 1572872 | tf_op jit(solution)/shard_map/ppermute | solution.py:37
  40.0 4.7 %copy-start.5 = (bf16[1024,128]{1,0:T(8,128)(2,1)}, bf16[1024,128]{1,0:T(8,128)(2,1)S(1)}, u32[]{:S(2)}) copy-start(bf16[1024,128]{1,0:T(8,128)(2,1)S(1)} %shard_map.103.rest_0_) | copy-start | bytes 786436
  40.0 8.9 %collective-permute-start.12 = (bf16[1024,128]{1,0:T(8,128)(2,1)S(1)}, bf16[1024,128]{1,0:T(8,128)(2,1)S(1)}, u32[]{:S(2)}, u32[]{:S(2)}) collective-permute-start(bf16[1024,128]{1,0:T(8,128)(2,1)S(1)} %shard_map.103.rest_0_), channel_id=1, source_target_pairs={{0,2},{2,3},{3,1},{1,0},{4,6},{6,7},{7,5},{5,4},{8,10},{10,11},{11... | collective-permute-start | bytes 786440 | tf_op jit(solution)/shard_map/ppermute | solution.py:59
  41.2 13.5 %collective-permute-start.13 = (bf16[1024,128]{1,0:T(8,128)(2,1)S(1)}, bf16[1024,128]{1,0:T(8,128)(2,1)S(1)}, u32[]{:S(2)}, u32[]{:S(2)}) collective-permute-start(bf16[1024,128]{1,0:T(8,128)(2,1)S(1)} %shard_map.103.rest_0_), channel_id=1, source_target_pairs={{0,1},{2,0},{3,2},{1,3},{4,5},{6,4},{7,6},{5,7},{8,9},{10,8},{11,1... | collective-permute-start | bytes 786440 | tf_op jit(solution)/shard_map/ppermute | solution.py:59
  43.1 15.2 %collective-permute-start.10 = (bf16[4,1,2,128,128]{4,3,2,1,0:T(8,128)(2,1)S(1)}, bf16[4,1,2,128,128]{4,3,2,1,0:T(8,128)(2,1)S(1)}, u32[]{:S(2)}, u32[]{:S(2)}) collective-permute-start(bf16[4,1,2,128,128]{4,3,2,1,0:T(8,128)(2,1)S(1)} %constant_dynamic-slice_fusion.7), channel_id=1, source_target_pairs={{0,8},{4,28},{8,16},{12,4},{16,24},{20,12},{24,0},{28,20},{1,9},{5... | collective-permute-start | bytes 786440 | tf_op jit(solution)/shard_map/ppermute | solution.py:37
  44.6 22.4 %collective-permute-start.9 = (bf16[8,1,2,128,128]{4,3,2,1,0:T(8,128)(2,1)S(1)}, bf16[8,1,2,128,128]{4,3,2,1,0:T(8,128)(2,1)S(1)}, u32[]{:S(2)}, u32[]{:S(2)}) collective-permute-start(bf16[8,1,2,128,128]{4,3,2,1,0:T(8,128)(2,1)S(1)} %copy-done.4), channel_id=1, source_target_pairs={{0,28},{4,8},{8,4},{12,16},{16,12},{20,24},{24,20},{28,0},{1,29},{... | collective-permute-start | bytes 1572872 | tf_op jit(solution)/shard_map/ppermute | solution.py:37
  48.9 14.1 %copy-start.11 = (bf16[1024,128]{1,0:T(8,128)(2,1)}, bf16[1024,128]{1,0:T(8,128)(2,1)S(1)}, u32[]{:S(2)}) copy-start(bf16[1024,128]{1,0:T(8,128)(2,1)S(1)} %collective-permute-done.12.rest_2_) | copy-start | bytes 786436
  48.9 10.0 %collective-permute-start.15 = (bf16[4,1,2,128,128]{4,3,2,1,0:T(8,128)(2,1)S(1)}, bf16[4,1,2,128,128]{4,3,2,1,0:T(8,128)(2,1)S(1)}, u32[]{:S(2)}, u32[]{:S(2)}) collective-permute-start(bf16[4,1,2,128,128]{4,3,2,1,0:T(8,128)(2,1)S(1)} %constant_dynamic-slice_fusion.6), channel_id=1, source_target_pairs={{0,4},{4,0},{8,12},{12,8},{16,20},{20,16},{24,28},{28,24},{1,5},{5... | collective-permute-start | bytes 786440 | tf_op jit(solution)/shard_map/ppermute | solution.py:37
  55.5 8.2 %collective-permute-start.16 = (bf16[1024,128]{1,0:T(8,128)(2,1)S(1)}, bf16[1024,128]{1,0:T(8,128)(2,1)S(1)}, u32[]{:S(2)}, u32[]{:S(2)}) collective-permute-start(bf16[1024,128]{1,0:T(8,128)(2,1)S(1)} %collective-permute-done.12.rest_2_), channel_id=1, source_target_pairs={{0,2},{2,3},{3,1},{1,0},{4,6},{6,7},{7,5},{5,4},{8,10},{10,11},{11... | collective-permute-start | bytes 786440 | tf_op jit(solution)/shard_map/ppermute | solution.py:59
  58.2 17.6 %collective-permute-start.18 = (bf16[8,1,2,128,128]{4,3,2,1,0:T(8,128)(2,1)S(1)}, bf16[8,1,2,128,128]{4,3,2,1,0:T(8,128)(2,1)S(1)}, u32[]{:S(2)}, u32[]{:S(2)}) collective-permute-start(bf16[8,1,2,128,128]{4,3,2,1,0:T(8,128)(2,1)S(1)} %copy-done.4), channel_id=1, source_target_pairs={{0,4},{4,0},{8,12},{12,8},{16,20},{20,16},{24,28},{28,24},{1,5},{5... | collective-permute-start | bytes 1572872 | tf_op jit(solution)/shard_map/ppermute | solution.py:37
  58.3 28.5 %collective-permute-start.7 = (bf16[3,3,32,1536]{3,2,1,0:T(8,128)(2,1)}, bf16[3,3,32,1536]{3,2,1,0:T(8,128)(2,1)}, u32[]{:S(2)}, u32[]{:S(2)}) collective-permute-start(bf16[3,3,32,1536]{3,2,1,0:T(8,128)(2,1)} %pad_maximum_fusion.2), channel_id=1, source_target_pairs={{0,16},{4,20},{8,24},{12,28},{16,0},{20,4},{24,8},{28,12},{1,17},{... | collective-permute-start | bytes 2654216 | tf_op jit(solution)/shard_map/ppermute | solution.py:37
  63.0 16.1 %copy-start.7 = (bf16[1024,128]{1,0:T(8,128)(2,1)}, bf16[1024,128]{1,0:T(8,128)(2,1)S(1)}, u32[]{:S(2)}) copy-start(bf16[1024,128]{1,0:T(8,128)(2,1)S(1)} %shard_map.104.rest_1_) | copy-start | bytes 786436
  63.7 15.4 %copy-start.15 = (bf16[1024,128]{1,0:T(8,128)(2,1)}, bf16[1024,128]{1,0:T(8,128)(2,1)S(1)}, u32[]{:S(2)}) copy-start(bf16[1024,128]{1,0:T(8,128)(2,1)S(1)} %collective-permute-done.16.rest_6_) | copy-start | bytes 786436
  63.7 8.5 %collective-permute-start.17 = (bf16[1024,128]{1,0:T(8,128)(2,1)S(1)}, bf16[1024,128]{1,0:T(8,128)(2,1)S(1)}, u32[]{:S(2)}, u32[]{:S(2)}) collective-permute-start(bf16[1024,128]{1,0:T(8,128)(2,1)S(1)} %shard_map.104.rest_1_), channel_id=1, source_target_pairs={{0,2},{2,3},{3,1},{1,0},{4,6},{6,7},{7,5},{5,4},{8,10},{10,11},{11... | collective-permute-start | bytes 786440 | tf_op jit(solution)/shard_map/ppermute | solution.py:59
  65.5 9.2 %collective-permute-start.8 = (bf16[4,1,2,128,128]{4,3,2,1,0:T(8,128)(2,1)S(1)}, bf16[4,1,2,128,128]{4,3,2,1,0:T(8,128)(2,1)S(1)}, u32[]{:S(2)}, u32[]{:S(2)}) collective-permute-start(bf16[4,1,2,128,128]{4,3,2,1,0:T(8,128)(2,1)S(1)} %constant_dynamic-slice_fusion.8), channel_id=1, source_target_pairs={{0,8},{4,28},{8,16},{12,4},{16,24},{20,12},{24,0},{28,20},{1,9},{5... | collective-permute-start | bytes 786440 | tf_op jit(solution)/shard_map/ppermute | solution.py:37
  67.1 12.1 %collective-permute-start.20 = (bf16[1024,128]{1,0:T(8,128)(2,1)S(1)}, bf16[1024,128]{1,0:T(8,128)(2,1)S(1)}, u32[]{:S(2)}, u32[]{:S(2)}) collective-permute-start(bf16[1024,128]{1,0:T(8,128)(2,1)S(1)} %shard_map.104.rest_1_), channel_id=1, source_target_pairs={{0,1},{2,0},{3,2},{1,3},{4,5},{6,4},{7,6},{5,7},{8,9},{10,8},{11,1... | collective-permute-start | bytes 786440 | tf_op jit(solution)/shard_map/ppermute | solution.py:59
  72.2 12.2 %copy-start.17 = (bf16[1024,128]{1,0:T(8,128)(2,1)}, bf16[1024,128]{1,0:T(8,128)(2,1)S(1)}, u32[]{:S(2)}) copy-start(bf16[1024,128]{1,0:T(8,128)(2,1)S(1)} %collective-permute-done.17.rest_3_) | copy-start | bytes 786436
  72.2 3.6 %collective-permute-start.19 = (bf16[4,1,2,128,128]{4,3,2,1,0:T(8,128)(2,1)S(1)}, bf16[4,1,2,128,128]{4,3,2,1,0:T(8,128)(2,1)S(1)}, u32[]{:S(2)}, u32[]{:S(2)}) collective-permute-start(bf16[4,1,2,128,128]{4,3,2,1,0:T(8,128)(2,1)S(1)} %constant_dynamic-slice_fusion.5), channel_id=1, source_target_pairs={{0,4},{4,0},{8,12},{12,8},{16,20},{20,16},{24,28},{28,24},{1,5},{5... | collective-permute-start | bytes 786440 | tf_op jit(solution)/shard_map/ppermute | solution.py:37
  74.7 9.7 %collective-permute-start.21 = (bf16[1024,128]{1,0:T(8,128)(2,1)S(1)}, bf16[1024,128]{1,0:T(8,128)(2,1)S(1)}, u32[]{:S(2)}, u32[]{:S(2)}) collective-permute-start(bf16[1024,128]{1,0:T(8,128)(2,1)S(1)} %collective-permute-done.17.rest_3_), channel_id=1, source_target_pairs={{0,2},{2,3},{3,1},{1,0},{4,6},{6,7},{7,5},{5,4},{8,10},{10,11},{11... | collective-permute-start | bytes 786440 | tf_op jit(solution)/shard_map/ppermute | solution.py:59
  79.1 7.7 %copy-start.23 = (bf16[1024,128]{1,0:T(8,128)(2,1)}, bf16[1024,128]{1,0:T(8,128)(2,1)S(1)}, u32[]{:S(2)}) copy-start(bf16[1024,128]{1,0:T(8,128)(2,1)S(1)} %shard_map.105.rest_0_) | copy-start | bytes 786436
  85.1 8.2 %collective-permute-start.22 = (bf16[1024,128]{1,0:T(8,128)(2,1)S(1)}, bf16[1024,128]{1,0:T(8,128)(2,1)S(1)}, u32[]{:S(2)}, u32[]{:S(2)}) collective-permute-start(bf16[1024,128]{1,0:T(8,128)(2,1)S(1)} %shard_map.105.rest_0_), channel_id=1, source_target_pairs={{0,2},{2,3},{3,1},{1,0},{4,6},{6,7},{7,5},{5,4},{8,10},{10,11},{11... | collective-permute-start | bytes 786440 | tf_op jit(solution)/shard_map/ppermute | solution.py:59
  86.8 9.5 %collective-permute-start.24 = (bf16[3,3,32,1536]{3,2,1,0:T(8,128)(2,1)}, bf16[3,3,32,1536]{3,2,1,0:T(8,128)(2,1)S(1)}, u32[]{:S(2)}, u32[]{:S(2)}) collective-permute-start(bf16[3,3,32,1536]{3,2,1,0:T(8,128)(2,1)} %pad_maximum_fusion.2), channel_id=1, source_target_pairs={{0,4},{4,0},{8,12},{12,8},{16,20},{20,16},{24,28},{28,24},{1,5},{5... | collective-permute-start | bytes 2654216 | tf_op jit(solution)/shard_map/ppermute | solution.py:37
  93.4 2.9 %collective-permute-start.23 = (bf16[3,3,32,1536]{3,2,1,0:T(8,128)(2,1)}, bf16[3,3,32,1536]{3,2,1,0:T(8,128)(2,1)S(1)}, u32[]{:S(2)}, u32[]{:S(2)}) collective-permute-start(bf16[3,3,32,1536]{3,2,1,0:T(8,128)(2,1)} %collective-permute-done.7), channel_id=1, source_target_pairs={{0,4},{4,0},{8,12},{12,8},{16,20},{20,16},{24,28},{28,24},{1,5},{5... | collective-permute-start | bytes 2654216 | tf_op jit(solution)/shard_map/ppermute | solution.py:37
  93.4 12.8 %collective-permute-start.25 = (bf16[1024,128]{1,0:T(8,128)(2,1)}, bf16[1024,128]{1,0:T(8,128)(2,1)S(1)}, u32[]{:S(2)}, u32[]{:S(2)}) collective-permute-start(bf16[1024,128]{1,0:T(8,128)(2,1)} %copy-done.23), channel_id=1, source_target_pairs={{0,1},{2,0},{3,2},{1,3},{4,5},{6,4},{7,6},{5,7},{8,9},{10,8},{11,1... | collective-permute-start | bytes 786440 | tf_op jit(solution)/shard_map/ppermute | solution.py:59
  94.7 14.1 %collective-permute-start.26 = (bf16[1024,128]{1,0:T(8,128)(2,1)S(1)}, bf16[1024,128]{1,0:T(8,128)(2,1)S(1)}, u32[]{:S(2)}, u32[]{:S(2)}) collective-permute-start(bf16[1024,128]{1,0:T(8,128)(2,1)S(1)} %collective-permute-done.22.rest_1_), channel_id=1, source_target_pairs={{0,2},{2,3},{3,1},{1,0},{4,6},{6,7},{7,5},{5,4},{8,10},{10,11},{11... | collective-permute-start | bytes 786440 | tf_op jit(solution)/shard_map/ppermute | solution.py:59
  106.0 2.8 %copy-start.24 = (bf16[1024,128]{1,0:T(8,128)(2,1)S(1)}, bf16[1024,128]{1,0:T(8,128)(2,1)}, u32[]{:S(2)}) copy-start(bf16[1024,128]{1,0:T(8,128)(2,1)} %copy-done.23) | copy-start | bytes 786436
  106.0 2.8 %copy-start.26 = (bf16[1536,384]{1,0:T(8,128)(2,1)S(1)}, bf16[1536,384]{1,0:T(8,128)(2,1)}, u32[]{:S(2)}) copy-start(bf16[1536,384]{1,0:T(8,128)(2,1)} %wk_ref.7) | copy-start | bytes 3538948
  106.0 2.7 %copy-start.27 = (bf16[1536,384]{1,0:T(8,128)(2,1)S(1)}, bf16[1536,384]{1,0:T(8,128)(2,1)}, u32[]{:S(2)}) copy-start(bf16[1536,384]{1,0:T(8,128)(2,1)} %wv_ref.7) | copy-start | bytes 3538948
  108.8 7.2 %copy-start.28 = (bf16[1536,384]{1,0:T(8,128)(2,1)S(1)}, bf16[1536,384]{1,0:T(8,128)(2,1)}, u32[]{:S(2)}) copy-start(bf16[1536,384]{1,0:T(8,128)(2,1)} %wq_ref.3) | copy-start | bytes 3538948
  114.2 21.1 %collective-permute-start.28 = (bf16[8,1,2,128,128]{4,3,2,1,0:T(8,128)(2,1)S(1)}, bf16[8,1,2,128,128]{4,3,2,1,0:T(8,128)(2,1)S(1)}, u32[]{:S(2)}, u32[]{:S(2)}) collective-permute-start(bf16[8,1,2,128,128]{4,3,2,1,0:T(8,128)(2,1)S(1)} %get-tuple-element.73.rest_2_), channel_id=1, source_target_pairs={{0,28},{4,8},{8,4},{12,16},{16,12},{20,24},{24,20},{28,0},{1,29},{... | collective-permute-start | bytes 1572872 | tf_op jit(solution)/shard_map/ppermute | solution.py:37
  115.4 20.0 %collective-permute-start.29 = (bf16[8,1,2,128,128]{4,3,2,1,0:T(8,128)(2,1)S(1)}, bf16[8,1,2,128,128]{4,3,2,1,0:T(8,128)(2,1)S(1)}, u32[]{:S(2)}, u32[]{:S(2)}) collective-permute-start(bf16[8,1,2,128,128]{4,3,2,1,0:T(8,128)(2,1)S(1)} %get-tuple-element.73.rest_2_), channel_id=1, source_target_pairs={{0,4},{4,0},{8,12},{12,8},{16,20},{20,16},{24,28},{28,24},{1,5},{5... | collective-permute-start | bytes 1572872 | tf_op jit(solution)/shard_map/ppermute | solution.py:37
  115.9 6.2 %copy-start.10 = (bf16[8,1,2,128,128]{4,3,2,1,0:T(8,128)(2,1)S(1)}, bf16[8,1,2,128,128]{4,3,2,1,0:T(8,128)(2,1)}, u32[]{:S(2)}) copy-start(bf16[8,1,2,128,128]{4,3,2,1,0:T(8,128)(2,1)} %get-tuple-element.51.rest_2_.rest_0_) | copy-start | bytes 1572868
  120.3 15.0 %collective-permute-start.27 = (bf16[4,1,2,128,128]{4,3,2,1,0:T(8,128)(2,1)S(1)}, bf16[4,1,2,128,128]{4,3,2,1,0:T(8,128)(2,1)S(1)}, u32[]{:S(2)}, u32[]{:S(2)}) collective-permute-start(bf16[4,1,2,128,128]{4,3,2,1,0:T(8,128)(2,1)S(1)} %get-tuple-element.72), channel_id=1, source_target_pairs={{0,8},{4,28},{8,16},{12,4},{16,24},{20,12},{24,0},{28,20},{1,9},{5... | collective-permute-start | bytes 786440 | tf_op jit(solution)/shard_map/ppermute | solution.py:37
  129.3 16.7 %collective-permute-start.32 = (bf16[8,1,2,128,128]{4,3,2,1,0:T(8,128)(2,1)S(1)}, bf16[8,1,2,128,128]{4,3,2,1,0:T(8,128)(2,1)S(1)}, u32[]{:S(2)}, u32[]{:S(2)}) collective-permute-start(bf16[8,1,2,128,128]{4,3,2,1,0:T(8,128)(2,1)S(1)} %get-tuple-element.76.rest_2_), channel_id=1, source_target_pairs={{0,28},{4,8},{8,4},{12,16},{16,12},{20,24},{24,20},{28,0},{1,29},{... | collective-permute-start | bytes 1572872 | tf_op jit(solution)/shard_map/ppermute | solution.py:37
  135.3 1.6 collective-permute-start.30
  140.1 8.5 %collective-permute-start.33 = (bf16[1024,128]{1,0:T(8,128)(2,1)S(1)}, bf16[1024,128]{1,0:T(8,128)(2,1)S(1)}, u32[]{:S(2)}, u32[]{:S(2)}) collective-permute-start(bf16[1024,128]{1,0:T(8,128)(2,1)S(1)} %shard_map.110.rest_0_), channel_id=1, source_target_pairs={{0,2},{2,3},{3,1},{1,0},{4,6},{6,7},{7,5},{5,4},{8,10},{10,11},{11... | collective-permute-start | bytes 786440 | tf_op jit(solution)/shard_map/ppermute | solution.py:59
  141.3 14.6 %collective-permute-start.35 = (bf16[8,1,2,128,128]{4,3,2,1,0:T(8,128)(2,1)S(1)}, bf16[8,1,2,128,128]{4,3,2,1,0:T(8,128)(2,1)S(1)}, u32[]{:S(2)}, u32[]{:S(2)}) collective-permute-start(bf16[8,1,2,128,128]{4,3,2,1,0:T(8,128)(2,1)S(1)} %get-tuple-element.76.rest_2_), channel_id=1, source_target_pairs={{0,4},{4,0},{8,12},{12,8},{16,20},{20,16},{24,28},{28,24},{1,5},{5... | collective-permute-start | bytes 1572872 | tf_op jit(solution)/shard_map/ppermute | solution.py:37
  141.3 13.9 %collective-permute-start.34 = (bf16[1024,128]{1,0:T(8,128)(2,1)S(1)}, bf16[1024,128]{1,0:T(8,128)(2,1)S(1)}, u32[]{:S(2)}, u32[]{:S(2)}) collective-permute-start(bf16[1024,128]{1,0:T(8,128)(2,1)S(1)} %shard_map.110.rest_0_), channel_id=1, source_target_pairs={{0,1},{2,0},{3,2},{1,3},{4,5},{6,4},{7,6},{5,7},{8,9},{10,8},{11,1... | collective-permute-start | bytes 786440 | tf_op jit(solution)/shard_map/ppermute | solution.py:59
  142.2 13.6 %collective-permute-start.31 = (bf16[4,1,2,128,128]{4,3,2,1,0:T(8,128)(2,1)S(1)}, bf16[4,1,2,128,128]{4,3,2,1,0:T(8,128)(2,1)S(1)}, u32[]{:S(2)}, u32[]{:S(2)}) collective-permute-start(bf16[4,1,2,128,128]{4,3,2,1,0:T(8,128)(2,1)S(1)} %constant_dynamic-slice_fusion.3), channel_id=1, source_target_pairs={{0,8},{4,28},{8,16},{12,4},{16,24},{20,12},{24,0},{28,20},{1,9},{5... | collective-permute-start | bytes 786440 | tf_op jit(solution)/shard_map/ppermute | solution.py:37
  146.0 20.0 %collective-permute-start.42 = (bf16[8,1,2,128,128]{4,3,2,1,0:T(8,128)(2,1)S(1)}, bf16[8,1,2,128,128]{4,3,2,1,0:T(8,128)(2,1)S(1)}, u32[]{:S(2)}, u32[]{:S(2)}) collective-permute-start(bf16[8,1,2,128,128]{4,3,2,1,0:T(8,128)(2,1)S(1)} %get-tuple-element.81.rest_2_), channel_id=1, source_target_pairs={{0,28},{4,8},{8,4},{12,16},{16,12},{20,24},{24,20},{28,0},{1,29},{... | collective-permute-start | bytes 1572872 | tf_op jit(solution)/shard_map/ppermute | solution.py:37
  148.6 7.3 %collective-permute-start.36 = (bf16[4,1,2,128,128]{4,3,2,1,0:T(8,128)(2,1)S(1)}, bf16[4,1,2,128,128]{4,3,2,1,0:T(8,128)(2,1)S(1)}, u32[]{:S(2)}, u32[]{:S(2)}) collective-permute-start(bf16[4,1,2,128,128]{4,3,2,1,0:T(8,128)(2,1)S(1)} %constant_dynamic-slice_fusion.2), channel_id=1, source_target_pairs={{0,4},{4,0},{8,12},{12,8},{16,20},{20,16},{24,28},{28,24},{1,5},{5... | collective-permute-start | bytes 786440 | tf_op jit(solution)/shard_map/ppermute | solution.py:37
  155.3 8.3 %collective-permute-start.37 = (bf16[1024,128]{1,0:T(8,128)(2,1)S(1)}, bf16[1024,128]{1,0:T(8,128)(2,1)S(1)}, u32[]{:S(2)}, u32[]{:S(2)}) collective-permute-start(bf16[1024,128]{1,0:T(8,128)(2,1)S(1)} %collective-permute-done.33.rest_2_), channel_id=1, source_target_pairs={{0,2},{2,3},{3,1},{1,0},{4,6},{6,7},{7,5},{5,4},{8,10},{10,11},{11... | collective-permute-start | bytes 786440 | tf_op jit(solution)/shard_map/ppermute | solution.py:59
  155.9 19.0 %collective-permute-start.43 = (bf16[8,1,2,128,128]{4,3,2,1,0:T(8,128)(2,1)S(1)}, bf16[8,1,2,128,128]{4,3,2,1,0:T(8,128)(2,1)S(1)}, u32[]{:S(2)}, u32[]{:S(2)}) collective-permute-start(bf16[8,1,2,128,128]{4,3,2,1,0:T(8,128)(2,1)S(1)} %get-tuple-element.81.rest_2_), channel_id=1, source_target_pairs={{0,4},{4,0},{8,12},{12,8},{16,20},{20,16},{24,28},{28,24},{1,5},{5... | collective-permute-start | bytes 1572872 | tf_op jit(solution)/shard_map/ppermute | solution.py:37
  163.6 9.1 %collective-permute-start.38 = (bf16[1024,128]{1,0:T(8,128)(2,1)S(1)}, bf16[1024,128]{1,0:T(8,128)(2,1)S(1)}, u32[]{:S(2)}, u32[]{:S(2)}) collective-permute-start(bf16[1024,128]{1,0:T(8,128)(2,1)S(1)} %shard_map.111.rest_1_), channel_id=1, source_target_pairs={{0,2},{2,3},{3,1},{1,0},{4,6},{6,7},{7,5},{5,4},{8,10},{10,11},{11... | collective-permute-start | bytes 786440 | tf_op jit(solution)/shard_map/ppermute | solution.py:59
  164.8 10.1 %collective-permute-start.41 = (bf16[4,1,2,128,128]{4,3,2,1,0:T(8,128)(2,1)S(1)}, bf16[4,1,2,128,128]{4,3,2,1,0:T(8,128)(2,1)S(1)}, u32[]{:S(2)}, u32[]{:S(2)}) collective-permute-start(bf16[4,1,2,128,128]{4,3,2,1,0:T(8,128)(2,1)S(1)} %constant_dynamic-slice_fusion.1), channel_id=1, source_target_pairs={{0,8},{4,28},{8,16},{12,4},{16,24},{20,12},{24,0},{28,20},{1,9},{5... | collective-permute-start | bytes 786440 | tf_op jit(solution)/shard_map/ppermute | solution.py:37
  165.1 14.5 %collective-permute-start.39 = (bf16[1024,128]{1,0:T(8,128)(2,1)S(1)}, bf16[1024,128]{1,0:T(8,128)(2,1)S(1)}, u32[]{:S(2)}, u32[]{:S(2)}) collective-permute-start(bf16[1024,128]{1,0:T(8,128)(2,1)S(1)} %shard_map.111.rest_1_), channel_id=1, source_target_pairs={{0,1},{2,0},{3,2},{1,3},{4,5},{6,4},{7,6},{5,7},{8,9},{10,8},{11,1... | collective-permute-start | bytes 786440 | tf_op jit(solution)/shard_map/ppermute | solution.py:59
  166.0 8.9 %collective-permute-start.44 = (bf16[4,1,2,128,128]{4,3,2,1,0:T(8,128)(2,1)S(1)}, bf16[4,1,2,128,128]{4,3,2,1,0:T(8,128)(2,1)S(1)}, u32[]{:S(2)}, u32[]{:S(2)}) collective-permute-start(bf16[4,1,2,128,128]{4,3,2,1,0:T(8,128)(2,1)S(1)} %constant_dynamic-slice_fusion), channel_id=1, source_target_pairs={{0,4},{4,0},{8,12},{12,8},{16,20},{20,16},{24,28},{28,24},{1,5},{5... | collective-permute-start | bytes 786440 | tf_op jit(solution)/shard_map/ppermute | solution.py:37
  172.7 9.5 %collective-permute-start.40 = (bf16[1024,128]{1,0:T(8,128)(2,1)S(1)}, bf16[1024,128]{1,0:T(8,128)(2,1)S(1)}, u32[]{:S(2)}, u32[]{:S(2)}) collective-permute-start(bf16[1024,128]{1,0:T(8,128)(2,1)S(1)} %collective-permute-done.38.rest_3_), channel_id=1, source_target_pairs={{0,2},{2,3},{3,1},{1,0},{4,6},{6,7},{7,5},{5,4},{8,10},{10,11},{11... | collective-permute-start | bytes 786440 | tf_op jit(solution)/shard_map/ppermute | solution.py:59
  182.2 10.5 %collective-permute-start.45 = (bf16[1024,128]{1,0:T(8,128)(2,1)S(1)}, bf16[1024,128]{1,0:T(8,128)(2,1)S(1)}, u32[]{:S(2)}, u32[]{:S(2)}) collective-permute-start(bf16[1024,128]{1,0:T(8,128)(2,1)S(1)} %shard_map.113.rest_0_), channel_id=1, source_target_pairs={{0,2},{2,3},{3,1},{1,0},{4,6},{6,7},{7,5},{5,4},{8,10},{10,11},{11... | collective-permute-start | bytes 786440 | tf_op jit(solution)/shard_map/ppermute | solution.py:59
  184.0 14.6 %collective-permute-start.46 = (bf16[1024,128]{1,0:T(8,128)(2,1)S(1)}, bf16[1024,128]{1,0:T(8,128)(2,1)S(1)}, u32[]{:S(2)}, u32[]{:S(2)}) collective-permute-start(bf16[1024,128]{1,0:T(8,128)(2,1)S(1)} %shard_map.113.rest_0_), channel_id=1, source_target_pairs={{0,1},{2,0},{3,2},{1,3},{4,5},{6,4},{7,6},{5,7},{8,9},{10,8},{11,1... | collective-permute-start | bytes 786440 | tf_op jit(solution)/shard_map/ppermute | solution.py:59
  192.8 7.6 %collective-permute-start.47 = (bf16[1024,128]{1,0:T(8,128)(2,1)S(1)}, bf16[1024,128]{1,0:T(8,128)(2,1)S(1)}, u32[]{:S(2)}, u32[]{:S(2)}) collective-permute-start(bf16[1024,128]{1,0:T(8,128)(2,1)S(1)} %collective-permute-done.45.rest_1_), channel_id=1, source_target_pairs={{0,2},{2,3},{3,1},{1,0},{4,6},{6,7},{7,5},{5,4},{8,10},{10,11},{11... | collective-permute-start | bytes 786440 | tf_op jit(solution)/shard_map/ppermute | solution.py:59
  (16 other events, 27.5 us)

commit v7 on v6

--- a/solution.py
+++ b/solution.py
@@ -21,7 +21,7 @@
 WPINS = (2, 3)
 SENDALL = 2
 SHARE = 0
-ATT_PINS = (3, 2)
+ATT_PINS = (3, 1)
 SEND_PIN = 2
 ATT_COST = 0.0
 PART_COST = 0.0
@@ -491,7 +491,7 @@
                 fetched = [after(piece, attended) for piece in fetched]
             if 1 <= chunk <= SEND_PIN:
                 attended = after(attended, *came[-1][SENDALL:])
-            came.append(around(attended, "head", came[-1][2:] if came else ()))
+            came.append(around(attended, "head", came[-1][3:] if came else ()))
         if rollout == 0:
             rows_of = share_rows(w_out, fetched, came[-1][1])
         if rollout == 0:

time: 204 us -> 204 us (level)
  no operation moved by 1% of the time
where the time goes in v7:
time: 204 us
  waiting for transfers between devices  76.2 us (37%)
  Pallas kernels  68.3 us (33%)
  starting transfers between devices  42.8 us (21%)
  local copies, waits for them, and re-layouts  10.7 us (5%)
  other arithmetic  5.01 us (2%)
    ppermute x21, waiting for transfers between devices, turned(): lax.ppermute(value, axis, [(order[i], order[(i + hops) % count]) for i in...  62.7 us
    ppermute x21, starting transfers between devices, turned(): lax.ppermute(value, axis, [(order[i], order[(i + hops) % count]) for i in...  27.4 us
    pallas_call x6, Pallas kernels, attend(): call(functools.partial(attend_body, blocks, slots, inner), (1,), [of_head...  21.5 us
    ppermute x27, starting transfers between devices, sent(): lax.ppermute(value, 'space', [(i, to(i, count) % count) for i in range(co...  15.4 us
    pallas_call x2, Pallas kernels, attend_past(): call(functools.partial(past_body, frames, heads, len(last) > 0), (blocks...  14.5 us
    ppermute x27, waiting for transfers between devices, sent(): lax.ppermute(value, 'space', [(i, to(i, count) % count) for i in range(co...  13.4 us
    pallas_call x2, Pallas kernels, rest_projection(): call(functools.partial(rest_body, heads), (rows // REST_TILE,), [pl.Block...  11.9 us
    pallas_call x3, Pallas kernels, add_heads(): call(functools.partial(part_body, len(pieces)), (rows // ADD_TILE,), [pl....  10.3 us
  transfers between devices with their start and end apart: 48, of which 21 were waited for; matrix products, arithmetic and copies ran while one was open for 4% of the time, Pallas kernels for 27%

profile of v7, /device:TPU:0, one launch (start us, length us, event | category | flops | bytes accessed | tf_op | source)
XLA Modules:
  0.0 203.5 jit_solution(15947745539026385450)
XLA Ops:
  0.0 4.6 %shard_map.100 = (bf16[8,1,2,128,128]{4,3,2,1,0:T(8,128)(2,1)}, bf16[4,1,2,128,128]{4,3,2,1,0:T(8,128)(2,1)}, bf16[3,32,1536]{2,1,0:T(8,128)(2,1)}) custom-call(bf16[1024,1536]{1,0:T(8,128)(2,1)} %state_ref.5, f32[1536]{0:T(1024)} %gain_ref.7, bf16[1536,384]{1,0:T(8,128)(2,1)} %wk_ref.7, bf16[1536,384]{1,0:T(8,128)(2,1)} %wv_ref.7, bf16[384,1536]{1,0:T(8,128)(2,1)} %w_out_hbm.1), custom_call_target="tpu_custom_call" | custom-call | flops 17250000896 | tf_op jit(solution)/shard_map/pallas_call | solution.py:147
  4.7 4.1 %collective-permute-start = (bf16[3,32,1536]{2,1,0:T(8,128)(2,1)}, bf16[3,32,1536]{2,1,0:T(8,128)(2,1)}, u32[]{:S(2)}, u32[]{:S(2)}) collective-permute-start(bf16[3,32,1536]{2,1,0:T(8,128)(2,1)} %get-tuple-element.43), channel_id=1, source_target_pairs={{0,2},{2,3},{3,1},{1,0},{4,6},{6,7},{7,5},{5,4},{8,10},{10,11},{11... | collective-permute-start | bytes 884744 | tf_op jit(solution)/shard_map/ppermute | solution.py:59
  8.7 1.6 collective-permute-start.2
  10.4 1.5 collective-permute-start.1
  11.8 7.5 %shard_map.101 = (bf16[8,1,2,128,128]{4,3,2,1,0:T(8,128)(2,1)}, bf16[8,1,2,128,128]{4,3,2,1,0:T(8,128)(2,1)}, bf16[8,3,128,128]{3,2,1,0:T(8,128)(2,1)}) custom-call(bf16[1024,1536]{1,0:T(8,128)(2,1)} %state_ref.5, f32[1536]{0:T(1024)} %gain_ref.7, bf16[1536,384]{1,0:T(8,128)(2,1)} %wq_ref.3, bf16[1536,384]{1,0:T(8,128)(2,1)} %wk_ref.7, bf16[1536,384]{1,0:T(8,128)(2,1)} %wv_ref.7), custom_call_target="tpu_custom_call" | custom-call | flops 17250000896 | tf_op jit(solution)/shard_map/pallas_call | solution.py:194
  19.4 1.1 copy-done
  20.5 7.3 %shard_map.102 = (f32[8,3,128,128]{3,2,1,0:T(8,128)S(1)}, f32[8,3,2,128]{3,2,1,0:T(2,128)S(1)}) custom-call(bf16[8,3,128,128]{3,2,1,0:T(8,128)(2,1)S(1)} %copy-done, bf16[8,1024,384]{2,1,0:T(8,128)(2,1)} %ck_hbm.3, bf16[8,1024,384]{2,1,0:T(8,128)(2,1)} %cv_hbm.3), custom_call_target="tpu_custom_call" | custom-call | flops 20700000256 | tf_op jit(solution)/shard_map/pallas_call | solution.py:276
  27.9 0.9 collective-permute-start.12
  28.7 1.8 constant_dynamic-slice_fusion.9
  31.3 2.9 %collective-permute-start.6 = (bf16[3,32,1536]{2,1,0:T(8,128)(2,1)}, bf16[3,32,1536]{2,1,0:T(8,128)(2,1)}, u32[]{:S(2)}, u32[]{:S(2)}) collective-permute-start(bf16[3,32,1536]{2,1,0:T(8,128)(2,1)} %collective-permute-done), channel_id=1, source_target_pairs={{0,2},{2,3},{3,1},{1,0},{4,6},{6,7},{7,5},{5,4},{8,10},{10,11},{11... | collective-permute-start | bytes 884744 | tf_op jit(solution)/shard_map/ppermute | solution.py:59
  34.5 1.0 copy-done.9
  35.6 4.4 %shard_map.103.rest_0_ = bf16[1024,128]{1,0:T(8,128)(2,1)S(1)} custom-call(s32[64]{0:T(128)S(1)} %reshape.21.where_ref, s32[8]{0:T(128)S(1)} %copy-done.25, bf16[8,3,128,128]{3,2,1,0:T(8,128)(2,1)S(1)} %copy-done.1, f32[8,3,128,128]{3,2,1,0:T(8,128)S(1)} %get-tuple-element.45.acc_ref, f32[8,3,2,128]{3,2,1,0:T(2,128)S(1)} %get-tuple-element.46.stat_ref, ...), custom_call_target="tpu_custom_call" | custom-call | tf_op jit(solution)/shard_map/pallas_call | solution.py:342
  40.0 1.3 collective-permute-start.13
  42.1 1.0 collective-permute-done.12.rest_1_
  43.6 1.0 constant_dynamic-slice_fusion.6
  45.5 3.4 %collective-permute-done.13.rest_2_ = bf16[1024,128]{1,0:T(8,128)(2,1)S(1)} collective-permute-done((bf16[1024,128]{1,0:T(8,128)(2,1)S(1)}, bf16[1024,128]{1,0:T(8,128)(2,1)S(1)}, u32[]{:S(2)}, u32[]{:S(2)}) %collective-permute-start.13) | collective-permute-done | bytes 262176 | tf_op jit(solution)/shard_map/ppermute | solution.py:59
  48.9 5.9 %collective-permute-done.14.rest_4_ = bf16[1024,128]{1,0:T(8,128)(2,1)S(1)} collective-permute-done((bf16[1024,128]{1,0:T(8,128)(2,1)S(1)}, bf16[1024,128]{1,0:T(8,128)(2,1)S(1)}, u32[]{:S(2)}, u32[]{:S(2)}) %collective-permute-start.14) | collective-permute-done | bytes 262176 | tf_op jit(solution)/shard_map/ppermute | solution.py:59
  56.1 2.1 %pad_maximum_fusion.2 = bf16[3,3,32,1536]{3,2,1,0:T(8,128)(2,1)} fusion(bf16[1,3,32,1536]{3,2,1,0:T(8,128)(2,1)} %bitcast.3, bf16[1,3,32,1536]{3,2,1,0:T(8,128)(2,1)} %bitcast.2, bf16[1,3,32,1536]{3,2,1,0:T(8,128)(2,1)} %bitcast.1), kind=kLoop, calls=%fused_computation.5 | loop fusion | flops 884736 | bytes 1769472 | tf_op jit(solution)/shard_map/stack | solution.py:435
  58.8 4.1 %shard_map.104.rest_1_ = bf16[1024,128]{1,0:T(8,128)(2,1)S(1)} custom-call(s32[64]{0:T(128)S(1)} %reshape.21.where_ref, s32[8]{0:T(128)S(1)} %copy-done.25, bf16[8,3,128,128]{3,2,1,0:T(8,128)(2,1)S(1)} %copy-done.1, f32[8,3,128,128]{3,2,1,0:T(8,128)S(1)} %get-tuple-element.45.acc_ref, f32[8,3,2,128]{3,2,1,0:T(2,128)S(1)} %get-tuple-element.46.stat_ref, ...), custom_call_target="tpu_custom_call" | custom-call | tf_op jit(solution)/shard_map/pallas_call | solution.py:342
  63.7 1.8 collective-permute-start.20
  65.5 1.5 collective-permute-start.8
  67.1 5.1 %collective-permute-done.20.rest_3_ = bf16[1024,128]{1,0:T(8,128)(2,1)S(1)} collective-permute-done((bf16[1024,128]{1,0:T(8,128)(2,1)S(1)}, bf16[1024,128]{1,0:T(8,128)(2,1)S(1)}, u32[]{:S(2)}, u32[]{:S(2)}) %collective-permute-start.20) | collective-permute-done | bytes 262176 | tf_op jit(solution)/shard_map/ppermute | solution.py:59
  72.2 2.5 %collective-permute-done.8.rest_0_ = bf16[4,1,2,128,128]{4,3,2,1,0:T(8,128)(2,1)S(1)} collective-permute-done((bf16[4,1,2,128,128]{4,3,2,1,0:T(8,128)(2,1)S(1)}, bf16[4,1,2,128,128]{4,3,2,1,0:T(8,128)(2,1)S(1)}, u32[]{:S(2)}, u32[]{:S(2)}) %collective-permute-start.8) | collective-permute-done | bytes 262176 | tf_op jit(solution)/shard_map/ppermute | solution.py:37
  74.7 1.1 collective-permute-start.21
  75.9 3.2 %shard_map.105.rest_0_ = bf16[1024,128]{1,0:T(8,128)(2,1)S(1)} custom-call(s32[64]{0:T(128)S(1)} %reshape.21.where_ref, s32[8]{0:T(128)S(1)} %copy-done.25, bf16[8,3,128,128]{3,2,1,0:T(8,128)(2,1)S(1)} %copy-done.1, f32[8,3,128,128]{3,2,1,0:T(8,128)S(1)} %get-tuple-element.45.acc_ref, f32[8,3,2,128]{3,2,1,0:T(2,128)S(1)} %get-tuple-element.46.stat_ref, ...), custom_call_target="tpu_custom_call" | custom-call | tf_op jit(solution)/shard_map/pallas_call | solution.py:342
  79.9 4.5 %collective-permute-done.21.rest_7_ = bf16[1024,128]{1,0:T(8,128)(2,1)S(1)} collective-permute-done((bf16[1024,128]{1,0:T(8,128)(2,1)S(1)}, bf16[1024,128]{1,0:T(8,128)(2,1)S(1)}, u32[]{:S(2)}, u32[]{:S(2)}) %collective-permute-start.21) | collective-permute-done | bytes 262176 | tf_op jit(solution)/shard_map/ppermute | solution.py:59
  85.1 1.6 collective-permute-start.22
  86.8 6.6 %collective-permute-done.22.rest_1_ = bf16[1024,128]{1,0:T(8,128)(2,1)S(1)} collective-permute-done((bf16[1024,128]{1,0:T(8,128)(2,1)S(1)}, bf16[1024,128]{1,0:T(8,128)(2,1)S(1)}, u32[]{:S(2)}, u32[]{:S(2)}) %collective-permute-start.22) | collective-permute-done | bytes 262176 | tf_op jit(solution)/shard_map/ppermute | solution.py:59
  93.4 1.3 collective-permute-start.25
  94.7 1.6 collective-permute-start.26
  96.3 1.8 select_bitcast_fusion.3
  99.0 0.9 copy-done.30
  100.3 1.5 copy-done.2
  102.4 3.6 %shard_map.106.part_ref = f32[1024,1536]{1,0:T(8,128)S(1)} custom-call(bf16[1024,1536]{1,0:T(8,128)(2,1)S(1)} %copy-done.2, bf16[1024,1536]{1,0:T(8,128)(2,1)S(1)} %bitcast.15, bf16[1024,128]{1,0:T(8,128)(2,1)S(1)} %copy-done.6, bf16[1024,128]{1,0:T(8,128)(2,1)S(1)} %copy-done.8, bf16[1024,128]{1,0:T(8,128)(2,1)S(1)} %copy-done.12, ...), custom_call_target="tpu_custom_call" | custom-call | tf_op jit(solution)/shard_map/pallas_call | solution.py:367
  106.2 2.6 %collective-permute-done.26.rest_3_ = bf16[1024,128]{1,0:T(8,128)(2,1)S(1)} collective-permute-done((bf16[1024,128]{1,0:T(8,128)(2,1)S(1)}, bf16[1024,128]{1,0:T(8,128)(2,1)S(1)}, u32[]{:S(2)}, u32[]{:S(2)}) %collective-permute-start.26) | collective-permute-done | bytes 262176 | tf_op jit(solution)/shard_map/ppermute | solution.py:59
  108.8 5.4 %shard_map.107 = (bf16[1024,1536]{1,0:T(8,128)(2,1)S(1)}, bf16[8,1,2,128,128]{4,3,2,1,0:T(8,128)(2,1)S(1)}, bf16[4,1,2,128,128]{4,3,2,1,0:T(8,128)(2,1)S(1)}) custom-call(f32[1024,1536]{1,0:T(8,128)S(1)} %shard_map.106.part_ref, bf16[512,1536]{1,0:T(8,128)(2,1)S(1)} %bitcast.17, f32[1536]{0:T(1024)S(1)} %copy-done.29, bf16[1536,384]{1,0:T(8,128)(2,1)S(1)} %copy-done.26, ...), custom_call_target="tpu_custom_call" | custom-call | flops 24149999616 | tf_op jit(solution)/shard_map/pallas_call | solution.py:397
  114.2 1.2 collective-permute-start.28
  115.9 4.4 %shard_map.108 = (bf16[8,1,2,128,128]{4,3,2,1,0:T(8,128)(2,1)S(1)}, bf16[8,1,2,128,128]{4,3,2,1,0:T(8,128)(2,1)S(1)}, bf16[8,3,128,128]{3,2,1,0:T(8,128)(2,1)S(1)}) custom-call(bf16[1024,1536]{1,0:T(8,128)(2,1)S(1)} %get-tuple-element.65.state_ref, f32[1536]{0:T(1024)S(1)} %copy-done.29, bf16[1536,384]{1,0:T(8,128)(2,1)S(1)} %copy-done.28, ...), custom_call_target="tpu_custom_call" | custom-call | flops 17250000896 | tf_op jit(solution)/shard_map/pallas_call | solution.py:194
  120.3 1.8 collective-permute-start.27
  122.1 7.2 %shard_map.109 = (f32[8,3,128,128]{3,2,1,0:T(8,128)S(1)}, f32[8,3,2,128]{3,2,1,0:T(2,128)S(1)}) custom-call(bf16[8,3,128,128]{3,2,1,0:T(8,128)(2,1)S(1)} %get-tuple-element.66.qt_ref, bf16[8,1024,384]{2,1,0:T(8,128)(2,1)} %ck_hbm.3, bf16[8,1024,384]{2,1,0:T(8,128)(2,1)} %cv_hbm.3, bf16[8,1,2,128,128]{4,3,2,1,0:T(8,128)(2,1)S(1)} %copy-done.10, ...), custom_call_target="tpu_custom_call" | custom-call | flops 20700000256 | tf_op jit(solution)/shard_map/pallas_call | solution.py:276
  130.0 5.3 %collective-permute-done.27.rest_0_ = bf16[4,1,2,128,128]{4,3,2,1,0:T(8,128)(2,1)S(1)} collective-permute-done((bf16[4,1,2,128,128]{4,3,2,1,0:T(8,128)(2,1)S(1)}, bf16[4,1,2,128,128]{4,3,2,1,0:T(8,128)(2,1)S(1)}, u32[]{:S(2)}, u32[]{:S(2)}) %collective-permute-start.27) | collective-permute-done | bytes 262176 | tf_op jit(solution)/shard_map/ppermute | solution.py:37
  135.4 1.5 collective-permute-done.30.rest_4_
  136.9 3.2 %shard_map.110.rest_0_ = bf16[1024,128]{1,0:T(8,128)(2,1)S(1)} custom-call(s32[64]{0:T(128)S(1)} %reshape.21.where_ref, s32[8]{0:T(128)S(1)} %copy-done.25, bf16[8,3,128,128]{3,2,1,0:T(8,128)(2,1)S(1)} %get-tuple-element.66.qt_ref, f32[8,3,128,128]{3,2,1,0:T(8,128)S(1)} %get-tuple-element.67.acc_ref, f32[8,3,2,128]{3,2,1,0:T(2,128)S(1)} %get-tuple-element.68.stat_ref, ...), custom_call_target="tpu_custom_call" | custom-call | tf_op jit(solution)/shard_map/pallas_call | solution.py:342
  140.1 1.2 collective-permute-start.33
  141.3 0.9 collective-permute-start.34
  142.8 3.1 %collective-permute-done.32.rest_1_ = bf16[8,1,2,128,128]{4,3,2,1,0:T(8,128)(2,1)S(1)} collective-permute-done((bf16[8,1,2,128,128]{4,3,2,1,0:T(8,128)(2,1)S(1)}, bf16[8,1,2,128,128]{4,3,2,1,0:T(8,128)(2,1)S(1)}, u32[]{:S(2)}, u32[]{:S(2)}) %collective-permute-start.32) | collective-permute-done | bytes 524320 | tf_op jit(solution)/shard_map/ppermute | solution.py:37
  146.0 1.7 collective-permute-start.42
  147.7 1.0 collective-permute-done.33.rest_2_
  148.6 6.6 %collective-permute-done.34.rest_4_ = bf16[1024,128]{1,0:T(8,128)(2,1)S(1)} collective-permute-done((bf16[1024,128]{1,0:T(8,128)(2,1)S(1)}, bf16[1024,128]{1,0:T(8,128)(2,1)S(1)}, u32[]{:S(2)}, u32[]{:S(2)}) %collective-permute-start.34) | collective-permute-done | bytes 262176 | tf_op jit(solution)/shard_map/ppermute | solution.py:59
  155.9 3.2 %shard_map.111.rest_1_ = bf16[1024,128]{1,0:T(8,128)(2,1)S(1)} custom-call(s32[64]{0:T(128)S(1)} %reshape.21.where_ref, s32[8]{0:T(128)S(1)} %copy-done.25, bf16[8,3,128,128]{3,2,1,0:T(8,128)(2,1)S(1)} %get-tuple-element.66.qt_ref, f32[8,3,128,128]{3,2,1,0:T(8,128)S(1)} %get-tuple-element.67.acc_ref, f32[8,3,2,128]{3,2,1,0:T(2,128)S(1)} %get-tuple-element.68.stat_ref, ...), custom_call_target="tpu_custom_call" | custom-call | tf_op jit(solution)/shard_map/pallas_call | solution.py:342
  159.2 4.4 %collective-permute-done.37.rest_6_ = bf16[1024,128]{1,0:T(8,128)(2,1)S(1)} collective-permute-done((bf16[1024,128]{1,0:T(8,128)(2,1)S(1)}, bf16[1024,128]{1,0:T(8,128)(2,1)S(1)}, u32[]{:S(2)}, u32[]{:S(2)}) %collective-permute-start.37) | collective-permute-done | bytes 262176 | tf_op jit(solution)/shard_map/ppermute | solution.py:59
  163.6 1.2 collective-permute-start.38
  166.0 6.7 %collective-permute-done.38.rest_3_ = bf16[1024,128]{1,0:T(8,128)(2,1)S(1)} collective-permute-done((bf16[1024,128]{1,0:T(8,128)(2,1)S(1)}, bf16[1024,128]{1,0:T(8,128)(2,1)S(1)}, u32[]{:S(2)}, u32[]{:S(2)}) %collective-permute-start.38) | collective-permute-done | bytes 262176 | tf_op jit(solution)/shard_map/ppermute | solution.py:59
  172.7 2.2 %collective-permute-start.40 = (bf16[1024,128]{1,0:T(8,128)(2,1)S(1)}, bf16[1024,128]{1,0:T(8,128)(2,1)S(1)}, u32[]{:S(2)}, u32[]{:S(2)}) collective-permute-start(bf16[1024,128]{1,0:T(8,128)(2,1)S(1)} %collective-permute-done.38.rest_3_), channel_id=1, source_target_pairs={{0,2},{2,3},{3,1},{1,0},{4,6},{6,7},{7,5},{5,4},{8,10},{10,11},{11... | collective-permute-start | bytes 786440 | tf_op jit(solution)/shard_map/ppermute | solution.py:59
  174.9 3.2 %shard_map.113.rest_0_ = bf16[1024,128]{1,0:T(8,128)(2,1)S(1)} custom-call(s32[64]{0:T(128)S(1)} %reshape.21.where_ref, s32[8]{0:T(128)S(1)} %copy-done.25, bf16[8,3,128,128]{3,2,1,0:T(8,128)(2,1)S(1)} %get-tuple-element.66.qt_ref, f32[8,3,128,128]{3,2,1,0:T(8,128)S(1)} %get-tuple-element.67.acc_ref, f32[8,3,2,128]{3,2,1,0:T(2,128)S(1)} %get-tuple-element.68.stat_ref, ...), custom_call_target="tpu_custom_call" | custom-call | tf_op jit(solution)/shard_map/pallas_call | solution.py:342
  178.2 1.5 collective-permute-done.39.rest_5_
  179.6 2.6 %collective-permute-done.40.rest_7_ = bf16[1024,128]{1,0:T(8,128)(2,1)S(1)} collective-permute-done((bf16[1024,128]{1,0:T(8,128)(2,1)S(1)}, bf16[1024,128]{1,0:T(8,128)(2,1)S(1)}, u32[]{:S(2)}, u32[]{:S(2)}) %collective-permute-start.40) | collective-permute-done | bytes 262176 | tf_op jit(solution)/shard_map/ppermute | solution.py:59
  182.2 1.8 collective-permute-start.45
  184.3 8.5 %collective-permute-done.45.rest_1_ = bf16[1024,128]{1,0:T(8,128)(2,1)S(1)} collective-permute-done((bf16[1024,128]{1,0:T(8,128)(2,1)S(1)}, bf16[1024,128]{1,0:T(8,128)(2,1)S(1)}, u32[]{:S(2)}, u32[]{:S(2)}) %collective-permute-start.45) | collective-permute-done | bytes 262176 | tf_op jit(solution)/shard_map/ppermute | solution.py:59
  192.8 1.4 collective-permute-start.47
  194.1 3.6 %shard_map.112.state_ref = f32[1024,1536]{1,0:T(8,128)S(1)} custom-call(bf16[1024,1536]{1,0:T(8,128)(2,1)S(1)} %get-tuple-element.65.state_ref, bf16[1024,1536]{1,0:T(8,128)(2,1)S(1)} %bitcast.16, bf16[1024,128]{1,0:T(8,128)(2,1)S(1)} %shard_map.110.rest_0_, bf16[1024,128]{1,0:T(8,128)(2,1)S(1)} %shard_map.111.rest_1_, ...), custom_call_target="tpu_custom_call" | custom-call | tf_op jit(solution)/shard_map/pallas_call | solution.py:367
  197.7 0.9 collective-permute-done.46.rest_2_
  198.6 1.8 collective-permute-done.47.rest_3_
  200.4 3.1 %shard_map.114 = bf16[1024,1536]{1,0:T(8,128)(2,1)} custom-call(f32[1024,1536]{1,0:T(8,128)S(1)} %shard_map.112.state_ref, bf16[512,1536]{1,0:T(8,128)(2,1)S(1)} %bitcast.18, bf16[1024,128]{1,0:T(8,128)(2,1)S(1)} %shard_map.113.rest_0_, bf16[1024,128]{1,0:T(8,128)(2,1)S(1)} %collective-permute-done.45.rest_1_, ...), custom_call_target="tpu_custom_call" | custom-call | tf_op jit(solution)/shard_map/pallas_call | solution.py:367
  (130 shorter events, 13.6 us)
Async XLA Ops:
  4.7 25.8 %collective-permute-start = (bf16[3,32,1536]{2,1,0:T(8,128)(2,1)}, bf16[3,32,1536]{2,1,0:T(8,128)(2,1)}, u32[]{:S(2)}, u32[]{:S(2)}) collective-permute-start(bf16[3,32,1536]{2,1,0:T(8,128)(2,1)} %get-tuple-element.43), channel_id=1, source_target_pairs={{0,2},{2,3},{3,1},{1,0},{4,6},{6,7},{7,5},{5,4},{8,10},{10,11},{11... | collective-permute-start | bytes 884744 | tf_op jit(solution)/shard_map/ppermute | solution.py:59
  8.7 22.5 %collective-permute-start.3 = (bf16[3,32,1536]{2,1,0:T(8,128)(2,1)}, bf16[3,32,1536]{2,1,0:T(8,128)(2,1)}, u32[]{:S(2)}, u32[]{:S(2)}) collective-permute-start(bf16[3,32,1536]{2,1,0:T(8,128)(2,1)} %get-tuple-element.43), channel_id=1, source_target_pairs={{0,1},{2,0},{3,2},{1,3},{4,5},{6,4},{7,6},{5,7},{8,9},{10,8},{11,1... | collective-permute-start | bytes 884744 | tf_op jit(solution)/shard_map/ppermute | solution.py:59
  8.7 19.1 %collective-permute-start.2 = (bf16[8,1,2,128,128]{4,3,2,1,0:T(8,128)(2,1)}, bf16[8,1,2,128,128]{4,3,2,1,0:T(8,128)(2,1)}, u32[]{:S(2)}, u32[]{:S(2)}) collective-permute-start(bf16[8,1,2,128,128]{4,3,2,1,0:T(8,128)(2,1)} %get-tuple-element.49.rest_2_.rest_0_), channel_id=1, source_target_pairs={{0,28},{4,8},{8,4},{12,16},{16,12},{20,24},{24,20},{28,0},{1,29},{... | collective-permute-start | bytes 1572872 | tf_op jit(solution)/shard_map/ppermute | solution.py:37
  10.4 24.1 %collective-permute-start.4 = (bf16[8,1,2,128,128]{4,3,2,1,0:T(8,128)(2,1)}, bf16[8,1,2,128,128]{4,3,2,1,0:T(8,128)(2,1)}, u32[]{:S(2)}, u32[]{:S(2)}) collective-permute-start(bf16[8,1,2,128,128]{4,3,2,1,0:T(8,128)(2,1)} %get-tuple-element.49.rest_2_.rest_0_), channel_id=1, source_target_pairs={{0,4},{4,0},{8,12},{12,8},{16,20},{20,16},{24,28},{28,24},{1,5},{5... | collective-permute-start | bytes 1572872 | tf_op jit(solution)/shard_map/ppermute | solution.py:37
  10.4 24.0 %collective-permute-start.1 = (bf16[4,1,2,128,128]{4,3,2,1,0:T(8,128)(2,1)}, bf16[4,1,2,128,128]{4,3,2,1,0:T(8,128)(2,1)}, u32[]{:S(2)}, u32[]{:S(2)}) collective-permute-start(bf16[4,1,2,128,128]{4,3,2,1,0:T(8,128)(2,1)} %get-tuple-element.47), channel_id=1, source_target_pairs={{0,8},{4,28},{8,16},{12,4},{16,24},{20,12},{24,0},{28,20},{1,9},{5... | collective-permute-start | bytes 786440 | tf_op jit(solution)/shard_map/ppermute | solution.py:37
  20.5 7.3 %copy-start.3 = (bf16[8,1,2,128,128]{4,3,2,1,0:T(8,128)(2,1)S(1)}, bf16[8,1,2,128,128]{4,3,2,1,0:T(8,128)(2,1)}, u32[]{:S(2)}) copy-start(bf16[8,1,2,128,128]{4,3,2,1,0:T(8,128)(2,1)} %get-tuple-element.57.rest_2_.rest_1_) | copy-start | bytes 1572868
  20.5 13.7 %copy-start.31 = (s32[8,8]{1,0:T(8,128)S(1)}, s32[8,8]{1,0:T(8,128)}, u32[]{:S(2)}) copy-start(s32[8,8]{1,0:T(8,128)} %param.18) | copy-start | bytes 772
  20.5 14.0 %copy-start.1 = (bf16[8,3,128,128]{3,2,1,0:T(8,128)(2,1)S(1)}, bf16[8,3,128,128]{3,2,1,0:T(8,128)(2,1)}, u32[]{:S(2)}) copy-start(bf16[8,3,128,128]{3,2,1,0:T(8,128)(2,1)} %get-tuple-element.44.qt_ref) | copy-start | bytes 2359300
  20.5 14.0 %copy-start.25 = (s32[8]{0:T(128)S(1)}, s32[8]{0:T(128)}, u32[]{:S(2)}) copy-start(s32[8]{0:T(128)} %counts_ref.11) | copy-start | bytes 100
  27.9 15.2 %collective-permute-start.12 = (bf16[8,1,2,128,128]{4,3,2,1,0:T(8,128)(2,1)S(1)}, bf16[8,1,2,128,128]{4,3,2,1,0:T(8,128)(2,1)}, u32[]{:S(2)}, u32[]{:S(2)}) collective-permute-start(bf16[8,1,2,128,128]{4,3,2,1,0:T(8,128)(2,1)S(1)} %copy-done.3), channel_id=1, source_target_pairs={{0,28},{4,8},{8,4},{12,16},{16,12},{20,24},{24,20},{28,0},{1,29},{... | collective-permute-start | bytes 1572872 | tf_op jit(solution)/shard_map/ppermute | solution.py:37
  28.7 15.9 %copy-start.4 = (bf16[8,1,2,128,128]{4,3,2,1,0:T(8,128)(2,1)S(1)}, bf16[8,1,2,128,128]{4,3,2,1,0:T(8,128)(2,1)}, u32[]{:S(2)}) copy-start(bf16[8,1,2,128,128]{4,3,2,1,0:T(8,128)(2,1)} %get-tuple-element.54.rest_2_) | copy-start | bytes 1572868
  30.5 4.0 %collective-permute-start.5 = (bf16[4,1,2,128,128]{4,3,2,1,0:T(8,128)(2,1)}, bf16[4,1,2,128,128]{4,3,2,1,0:T(8,128)(2,1)}, u32[]{:S(2)}, u32[]{:S(2)}) collective-permute-start(bf16[4,1,2,128,128]{4,3,2,1,0:T(8,128)(2,1)} %constant_dynamic-slice_fusion.9), channel_id=1, source_target_pairs={{0,4},{4,0},{8,12},{12,8},{16,20},{20,16},{24,28},{28,24},{1,5},{5... | collective-permute-start | bytes 786440 | tf_op jit(solution)/shard_map/ppermute | solution.py:37
  31.3 13.3 %collective-permute-start.6 = (bf16[3,32,1536]{2,1,0:T(8,128)(2,1)}, bf16[3,32,1536]{2,1,0:T(8,128)(2,1)}, u32[]{:S(2)}, u32[]{:S(2)}) collective-permute-start(bf16[3,32,1536]{2,1,0:T(8,128)(2,1)} %collective-permute-done), channel_id=1, source_target_pairs={{0,2},{2,3},{3,1},{1,0},{4,6},{6,7},{7,5},{5,4},{8,10},{10,11},{11... | collective-permute-start | bytes 884744 | tf_op jit(solution)/shard_map/ppermute | solution.py:59
  34.4 23.9 %collective-permute-start.15 = (bf16[8,1,2,128,128]{4,3,2,1,0:T(8,128)(2,1)S(1)}, bf16[8,1,2,128,128]{4,3,2,1,0:T(8,128)(2,1)S(1)}, u32[]{:S(2)}, u32[]{:S(2)}) collective-permute-start(bf16[8,1,2,128,128]{4,3,2,1,0:T(8,128)(2,1)S(1)} %copy-done.3), channel_id=1, source_target_pairs={{0,4},{4,0},{8,12},{12,8},{16,20},{20,16},{24,28},{28,24},{1,5},{5... | collective-permute-start | bytes 1572872 | tf_op jit(solution)/shard_map/ppermute | solution.py:37
  40.0 4.7 %copy-start.5 = (bf16[1024,128]{1,0:T(8,128)(2,1)}, bf16[1024,128]{1,0:T(8,128)(2,1)S(1)}, u32[]{:S(2)}) copy-start(bf16[1024,128]{1,0:T(8,128)(2,1)S(1)} %shard_map.103.rest_0_) | copy-start | bytes 786436
  40.0 8.9 %collective-permute-start.13 = (bf16[1024,128]{1,0:T(8,128)(2,1)S(1)}, bf16[1024,128]{1,0:T(8,128)(2,1)S(1)}, u32[]{:S(2)}, u32[]{:S(2)}) collective-permute-start(bf16[1024,128]{1,0:T(8,128)(2,1)S(1)} %shard_map.103.rest_0_), channel_id=1, source_target_pairs={{0,2},{2,3},{3,1},{1,0},{4,6},{6,7},{7,5},{5,4},{8,10},{10,11},{11... | collective-permute-start | bytes 786440 | tf_op jit(solution)/shard_map/ppermute | solution.py:59
  41.2 13.5 %collective-permute-start.14 = (bf16[1024,128]{1,0:T(8,128)(2,1)S(1)}, bf16[1024,128]{1,0:T(8,128)(2,1)S(1)}, u32[]{:S(2)}, u32[]{:S(2)}) collective-permute-start(bf16[1024,128]{1,0:T(8,128)(2,1)S(1)} %shard_map.103.rest_0_), channel_id=1, source_target_pairs={{0,1},{2,0},{3,2},{1,3},{4,5},{6,4},{7,6},{5,7},{8,9},{10,8},{11,1... | collective-permute-start | bytes 786440 | tf_op jit(solution)/shard_map/ppermute | solution.py:59
  43.1 15.2 %collective-permute-start.11 = (bf16[4,1,2,128,128]{4,3,2,1,0:T(8,128)(2,1)S(1)}, bf16[4,1,2,128,128]{4,3,2,1,0:T(8,128)(2,1)S(1)}, u32[]{:S(2)}, u32[]{:S(2)}) collective-permute-start(bf16[4,1,2,128,128]{4,3,2,1,0:T(8,128)(2,1)S(1)} %constant_dynamic-slice_fusion.7), channel_id=1, source_target_pairs={{0,8},{4,28},{8,16},{12,4},{16,24},{20,12},{24,0},{28,20},{1,9},{5... | collective-permute-start | bytes 786440 | tf_op jit(solution)/shard_map/ppermute | solution.py:37
  44.6 22.4 %collective-permute-start.9 = (bf16[8,1,2,128,128]{4,3,2,1,0:T(8,128)(2,1)S(1)}, bf16[8,1,2,128,128]{4,3,2,1,0:T(8,128)(2,1)S(1)}, u32[]{:S(2)}, u32[]{:S(2)}) collective-permute-start(bf16[8,1,2,128,128]{4,3,2,1,0:T(8,128)(2,1)S(1)} %copy-done.4), channel_id=1, source_target_pairs={{0,28},{4,8},{8,4},{12,16},{16,12},{20,24},{24,20},{28,0},{1,29},{... | collective-permute-start | bytes 1572872 | tf_op jit(solution)/shard_map/ppermute | solution.py:37
  48.9 14.1 %copy-start.11 = (bf16[1024,128]{1,0:T(8,128)(2,1)}, bf16[1024,128]{1,0:T(8,128)(2,1)S(1)}, u32[]{:S(2)}) copy-start(bf16[1024,128]{1,0:T(8,128)(2,1)S(1)} %collective-permute-done.13.rest_2_) | copy-start | bytes 786436
  48.9 10.0 %collective-permute-start.16 = (bf16[4,1,2,128,128]{4,3,2,1,0:T(8,128)(2,1)S(1)}, bf16[4,1,2,128,128]{4,3,2,1,0:T(8,128)(2,1)S(1)}, u32[]{:S(2)}, u32[]{:S(2)}) collective-permute-start(bf16[4,1,2,128,128]{4,3,2,1,0:T(8,128)(2,1)S(1)} %constant_dynamic-slice_fusion.6), channel_id=1, source_target_pairs={{0,4},{4,0},{8,12},{12,8},{16,20},{20,16},{24,28},{28,24},{1,5},{5... | collective-permute-start | bytes 786440 | tf_op jit(solution)/shard_map/ppermute | solution.py:37
  55.5 8.2 %collective-permute-start.17 = (bf16[1024,128]{1,0:T(8,128)(2,1)S(1)}, bf16[1024,128]{1,0:T(8,128)(2,1)S(1)}, u32[]{:S(2)}, u32[]{:S(2)}) collective-permute-start(bf16[1024,128]{1,0:T(8,128)(2,1)S(1)} %collective-permute-done.13.rest_2_), channel_id=1, source_target_pairs={{0,2},{2,3},{3,1},{1,0},{4,6},{6,7},{7,5},{5,4},{8,10},{10,11},{11... | collective-permute-start | bytes 786440 | tf_op jit(solution)/shard_map/ppermute | solution.py:59
  58.2 17.6 %collective-permute-start.10 = (bf16[8,1,2,128,128]{4,3,2,1,0:T(8,128)(2,1)S(1)}, bf16[8,1,2,128,128]{4,3,2,1,0:T(8,128)(2,1)S(1)}, u32[]{:S(2)}, u32[]{:S(2)}) collective-permute-start(bf16[8,1,2,128,128]{4,3,2,1,0:T(8,128)(2,1)S(1)} %copy-done.4), channel_id=1, source_target_pairs={{0,4},{4,0},{8,12},{12,8},{16,20},{20,16},{24,28},{28,24},{1,5},{5... | collective-permute-start | bytes 1572872 | tf_op jit(solution)/shard_map/ppermute | solution.py:37
  58.3 28.5 %collective-permute-start.7 = (bf16[3,3,32,1536]{3,2,1,0:T(8,128)(2,1)}, bf16[3,3,32,1536]{3,2,1,0:T(8,128)(2,1)}, u32[]{:S(2)}, u32[]{:S(2)}) collective-permute-start(bf16[3,3,32,1536]{3,2,1,0:T(8,128)(2,1)} %pad_maximum_fusion.2), channel_id=1, source_target_pairs={{0,16},{4,20},{8,24},{12,28},{16,0},{20,4},{24,8},{28,12},{1,17},{... | collective-permute-start | bytes 2654216 | tf_op jit(solution)/shard_map/ppermute | solution.py:37
  63.0 16.1 %copy-start.7 = (bf16[1024,128]{1,0:T(8,128)(2,1)}, bf16[1024,128]{1,0:T(8,128)(2,1)S(1)}, u32[]{:S(2)}) copy-start(bf16[1024,128]{1,0:T(8,128)(2,1)S(1)} %shard_map.104.rest_1_) | copy-start | bytes 786436
  63.7 15.4 %copy-start.15 = (bf16[1024,128]{1,0:T(8,128)(2,1)}, bf16[1024,128]{1,0:T(8,128)(2,1)S(1)}, u32[]{:S(2)}) copy-start(bf16[1024,128]{1,0:T(8,128)(2,1)S(1)} %collective-permute-done.17.rest_6_) | copy-start | bytes 786436
  63.7 8.5 %collective-permute-start.20 = (bf16[1024,128]{1,0:T(8,128)(2,1)S(1)}, bf16[1024,128]{1,0:T(8,128)(2,1)S(1)}, u32[]{:S(2)}, u32[]{:S(2)}) collective-permute-start(bf16[1024,128]{1,0:T(8,128)(2,1)S(1)} %shard_map.104.rest_1_), channel_id=1, source_target_pairs={{0,2},{2,3},{3,1},{1,0},{4,6},{6,7},{7,5},{5,4},{8,10},{10,11},{11... | collective-permute-start | bytes 786440 | tf_op jit(solution)/shard_map/ppermute | solution.py:59
  65.5 9.2 %collective-permute-start.8 = (bf16[4,1,2,128,128]{4,3,2,1,0:T(8,128)(2,1)S(1)}, bf16[4,1,2,128,128]{4,3,2,1,0:T(8,128)(2,1)S(1)}, u32[]{:S(2)}, u32[]{:S(2)}) collective-permute-start(bf16[4,1,2,128,128]{4,3,2,1,0:T(8,128)(2,1)S(1)} %constant_dynamic-slice_fusion.8), channel_id=1, source_target_pairs={{0,8},{4,28},{8,16},{12,4},{16,24},{20,12},{24,0},{28,20},{1,9},{5... | collective-permute-start | bytes 786440 | tf_op jit(solution)/shard_map/ppermute | solution.py:37
  67.1 12.1 %collective-permute-start.19 = (bf16[1024,128]{1,0:T(8,128)(2,1)S(1)}, bf16[1024,128]{1,0:T(8,128)(2,1)S(1)}, u32[]{:S(2)}, u32[]{:S(2)}) collective-permute-start(bf16[1024,128]{1,0:T(8,128)(2,1)S(1)} %shard_map.104.rest_1_), channel_id=1, source_target_pairs={{0,1},{2,0},{3,2},{1,3},{4,5},{6,4},{7,6},{5,7},{8,9},{10,8},{11,1... | collective-permute-start | bytes 786440 | tf_op jit(solution)/shard_map/ppermute | solution.py:59
  72.2 12.2 %copy-start.17 = (bf16[1024,128]{1,0:T(8,128)(2,1)}, bf16[1024,128]{1,0:T(8,128)(2,1)S(1)}, u32[]{:S(2)}) copy-start(bf16[1024,128]{1,0:T(8,128)(2,1)S(1)} %collective-permute-done.20.rest_3_) | copy-start | bytes 786436
  72.2 3.6 %collective-permute-start.18 = (bf16[4,1,2,128,128]{4,3,2,1,0:T(8,128)(2,1)S(1)}, bf16[4,1,2,128,128]{4,3,2,1,0:T(8,128)(2,1)S(1)}, u32[]{:S(2)}, u32[]{:S(2)}) collective-permute-start(bf16[4,1,2,128,128]{4,3,2,1,0:T(8,128)(2,1)S(1)} %constant_dynamic-slice_fusion.5), channel_id=1, source_target_pairs={{0,4},{4,0},{8,12},{12,8},{16,20},{20,16},{24,28},{28,24},{1,5},{5... | collective-permute-start | bytes 786440 | tf_op jit(solution)/shard_map/ppermute | solution.py:37
  74.7 9.7 %collective-permute-start.21 = (bf16[1024,128]{1,0:T(8,128)(2,1)S(1)}, bf16[1024,128]{1,0:T(8,128)(2,1)S(1)}, u32[]{:S(2)}, u32[]{:S(2)}) collective-permute-start(bf16[1024,128]{1,0:T(8,128)(2,1)S(1)} %collective-permute-done.20.rest_3_), channel_id=1, source_target_pairs={{0,2},{2,3},{3,1},{1,0},{4,6},{6,7},{7,5},{5,4},{8,10},{10,11},{11... | collective-permute-start | bytes 786440 | tf_op jit(solution)/shard_map/ppermute | solution.py:59
  79.1 7.7 %copy-start.23 = (bf16[1024,128]{1,0:T(8,128)(2,1)}, bf16[1024,128]{1,0:T(8,128)(2,1)S(1)}, u32[]{:S(2)}) copy-start(bf16[1024,128]{1,0:T(8,128)(2,1)S(1)} %shard_map.105.rest_0_) | copy-start | bytes 786436
  85.1 8.2 %collective-permute-start.22 = (bf16[1024,128]{1,0:T(8,128)(2,1)S(1)}, bf16[1024,128]{1,0:T(8,128)(2,1)S(1)}, u32[]{:S(2)}, u32[]{:S(2)}) collective-permute-start(bf16[1024,128]{1,0:T(8,128)(2,1)S(1)} %shard_map.105.rest_0_), channel_id=1, source_target_pairs={{0,2},{2,3},{3,1},{1,0},{4,6},{6,7},{7,5},{5,4},{8,10},{10,11},{11... | collective-permute-start | bytes 786440 | tf_op jit(solution)/shard_map/ppermute | solution.py:59
  86.8 9.5 %collective-permute-start.24 = (bf16[3,3,32,1536]{3,2,1,0:T(8,128)(2,1)}, bf16[3,3,32,1536]{3,2,1,0:T(8,128)(2,1)S(1)}, u32[]{:S(2)}, u32[]{:S(2)}) collective-permute-start(bf16[3,3,32,1536]{3,2,1,0:T(8,128)(2,1)} %pad_maximum_fusion.2), channel_id=1, source_target_pairs={{0,4},{4,0},{8,12},{12,8},{16,20},{20,16},{24,28},{28,24},{1,5},{5... | collective-permute-start | bytes 2654216 | tf_op jit(solution)/shard_map/ppermute | solution.py:37
  93.4 2.9 %collective-permute-start.23 = (bf16[3,3,32,1536]{3,2,1,0:T(8,128)(2,1)}, bf16[3,3,32,1536]{3,2,1,0:T(8,128)(2,1)S(1)}, u32[]{:S(2)}, u32[]{:S(2)}) collective-permute-start(bf16[3,3,32,1536]{3,2,1,0:T(8,128)(2,1)} %collective-permute-done.7), channel_id=1, source_target_pairs={{0,4},{4,0},{8,12},{12,8},{16,20},{20,16},{24,28},{28,24},{1,5},{5... | collective-permute-start | bytes 2654216 | tf_op jit(solution)/shard_map/ppermute | solution.py:37
  93.4 12.8 %collective-permute-start.25 = (bf16[1024,128]{1,0:T(8,128)(2,1)}, bf16[1024,128]{1,0:T(8,128)(2,1)S(1)}, u32[]{:S(2)}, u32[]{:S(2)}) collective-permute-start(bf16[1024,128]{1,0:T(8,128)(2,1)} %copy-done.23), channel_id=1, source_target_pairs={{0,1},{2,0},{3,2},{1,3},{4,5},{6,4},{7,6},{5,7},{8,9},{10,8},{11,1... | collective-permute-start | bytes 786440 | tf_op jit(solution)/shard_map/ppermute | solution.py:59
  94.7 14.1 %collective-permute-start.26 = (bf16[1024,128]{1,0:T(8,128)(2,1)S(1)}, bf16[1024,128]{1,0:T(8,128)(2,1)S(1)}, u32[]{:S(2)}, u32[]{:S(2)}) collective-permute-start(bf16[1024,128]{1,0:T(8,128)(2,1)S(1)} %collective-permute-done.22.rest_1_), channel_id=1, source_target_pairs={{0,2},{2,3},{3,1},{1,0},{4,6},{6,7},{7,5},{5,4},{8,10},{10,11},{11... | collective-permute-start | bytes 786440 | tf_op jit(solution)/shard_map/ppermute | solution.py:59
  106.0 2.8 %copy-start.24 = (bf16[1024,128]{1,0:T(8,128)(2,1)S(1)}, bf16[1024,128]{1,0:T(8,128)(2,1)}, u32[]{:S(2)}) copy-start(bf16[1024,128]{1,0:T(8,128)(2,1)} %copy-done.23) | copy-start | bytes 786436
  106.0 2.8 %copy-start.26 = (bf16[1536,384]{1,0:T(8,128)(2,1)S(1)}, bf16[1536,384]{1,0:T(8,128)(2,1)}, u32[]{:S(2)}) copy-start(bf16[1536,384]{1,0:T(8,128)(2,1)} %wk_ref.7) | copy-start | bytes 3538948
  106.0 2.7 %copy-start.27 = (bf16[1536,384]{1,0:T(8,128)(2,1)S(1)}, bf16[1536,384]{1,0:T(8,128)(2,1)}, u32[]{:S(2)}) copy-start(bf16[1536,384]{1,0:T(8,128)(2,1)} %wv_ref.7) | copy-start | bytes 3538948
  108.8 7.2 %copy-start.28 = (bf16[1536,384]{1,0:T(8,128)(2,1)S(1)}, bf16[1536,384]{1,0:T(8,128)(2,1)}, u32[]{:S(2)}) copy-start(bf16[1536,384]{1,0:T(8,128)(2,1)} %wq_ref.3) | copy-start | bytes 3538948
  114.2 21.1 %collective-permute-start.28 = (bf16[8,1,2,128,128]{4,3,2,1,0:T(8,128)(2,1)S(1)}, bf16[8,1,2,128,128]{4,3,2,1,0:T(8,128)(2,1)S(1)}, u32[]{:S(2)}, u32[]{:S(2)}) collective-permute-start(bf16[8,1,2,128,128]{4,3,2,1,0:T(8,128)(2,1)S(1)} %get-tuple-element.70.rest_2_), channel_id=1, source_target_pairs={{0,28},{4,8},{8,4},{12,16},{16,12},{20,24},{24,20},{28,0},{1,29},{... | collective-permute-start | bytes 1572872 | tf_op jit(solution)/shard_map/ppermute | solution.py:37
  115.4 20.0 %collective-permute-start.29 = (bf16[8,1,2,128,128]{4,3,2,1,0:T(8,128)(2,1)S(1)}, bf16[8,1,2,128,128]{4,3,2,1,0:T(8,128)(2,1)S(1)}, u32[]{:S(2)}, u32[]{:S(2)}) collective-permute-start(bf16[8,1,2,128,128]{4,3,2,1,0:T(8,128)(2,1)S(1)} %get-tuple-element.70.rest_2_), channel_id=1, source_target_pairs={{0,4},{4,0},{8,12},{12,8},{16,20},{20,16},{24,28},{28,24},{1,5},{5... | collective-permute-start | bytes 1572872 | tf_op jit(solution)/shard_map/ppermute | solution.py:37
  115.9 6.2 %copy-start.10 = (bf16[8,1,2,128,128]{4,3,2,1,0:T(8,128)(2,1)S(1)}, bf16[8,1,2,128,128]{4,3,2,1,0:T(8,128)(2,1)}, u32[]{:S(2)}) copy-start(bf16[8,1,2,128,128]{4,3,2,1,0:T(8,128)(2,1)} %get-tuple-element.49.rest_2_.rest_0_) | copy-start | bytes 1572868
  120.3 15.0 %collective-permute-start.27 = (bf16[4,1,2,128,128]{4,3,2,1,0:T(8,128)(2,1)S(1)}, bf16[4,1,2,128,128]{4,3,2,1,0:T(8,128)(2,1)S(1)}, u32[]{:S(2)}, u32[]{:S(2)}) collective-permute-start(bf16[4,1,2,128,128]{4,3,2,1,0:T(8,128)(2,1)S(1)} %get-tuple-element.69), channel_id=1, source_target_pairs={{0,8},{4,28},{8,16},{12,4},{16,24},{20,12},{24,0},{28,20},{1,9},{5... | collective-permute-start | bytes 786440 | tf_op jit(solution)/shard_map/ppermute | solution.py:37
  129.3 16.7 %collective-permute-start.32 = (bf16[8,1,2,128,128]{4,3,2,1,0:T(8,128)(2,1)S(1)}, bf16[8,1,2,128,128]{4,3,2,1,0:T(8,128)(2,1)S(1)}, u32[]{:S(2)}, u32[]{:S(2)}) collective-permute-start(bf16[8,1,2,128,128]{4,3,2,1,0:T(8,128)(2,1)S(1)} %get-tuple-element.73.rest_2_), channel_id=1, source_target_pairs={{0,28},{4,8},{8,4},{12,16},{16,12},{20,24},{24,20},{28,0},{1,29},{... | collective-permute-start | bytes 1572872 | tf_op jit(solution)/shard_map/ppermute | solution.py:37
  135.3 1.6 collective-permute-start.30
  140.1 8.5 %collective-permute-start.33 = (bf16[1024,128]{1,0:T(8,128)(2,1)S(1)}, bf16[1024,128]{1,0:T(8,128)(2,1)S(1)}, u32[]{:S(2)}, u32[]{:S(2)}) collective-permute-start(bf16[1024,128]{1,0:T(8,128)(2,1)S(1)} %shard_map.110.rest_0_), channel_id=1, source_target_pairs={{0,2},{2,3},{3,1},{1,0},{4,6},{6,7},{7,5},{5,4},{8,10},{10,11},{11... | collective-permute-start | bytes 786440 | tf_op jit(solution)/shard_map/ppermute | solution.py:59
  141.3 14.6 %collective-permute-start.35 = (bf16[8,1,2,128,128]{4,3,2,1,0:T(8,128)(2,1)S(1)}, bf16[8,1,2,128,128]{4,3,2,1,0:T(8,128)(2,1)S(1)}, u32[]{:S(2)}, u32[]{:S(2)}) collective-permute-start(bf16[8,1,2,128,128]{4,3,2,1,0:T(8,128)(2,1)S(1)} %get-tuple-element.73.rest_2_), channel_id=1, source_target_pairs={{0,4},{4,0},{8,12},{12,8},{16,20},{20,16},{24,28},{28,24},{1,5},{5... | collective-permute-start | bytes 1572872 | tf_op jit(solution)/shard_map/ppermute | solution.py:37
  141.3 13.9 %collective-permute-start.34 = (bf16[1024,128]{1,0:T(8,128)(2,1)S(1)}, bf16[1024,128]{1,0:T(8,128)(2,1)S(1)}, u32[]{:S(2)}, u32[]{:S(2)}) collective-permute-start(bf16[1024,128]{1,0:T(8,128)(2,1)S(1)} %shard_map.110.rest_0_), channel_id=1, source_target_pairs={{0,1},{2,0},{3,2},{1,3},{4,5},{6,4},{7,6},{5,7},{8,9},{10,8},{11,1... | collective-permute-start | bytes 786440 | tf_op jit(solution)/shard_map/ppermute | solution.py:59
  142.2 13.6 %collective-permute-start.31 = (bf16[4,1,2,128,128]{4,3,2,1,0:T(8,128)(2,1)S(1)}, bf16[4,1,2,128,128]{4,3,2,1,0:T(8,128)(2,1)S(1)}, u32[]{:S(2)}, u32[]{:S(2)}) collective-permute-start(bf16[4,1,2,128,128]{4,3,2,1,0:T(8,128)(2,1)S(1)} %constant_dynamic-slice_fusion.3), channel_id=1, source_target_pairs={{0,8},{4,28},{8,16},{12,4},{16,24},{20,12},{24,0},{28,20},{1,9},{5... | collective-permute-start | bytes 786440 | tf_op jit(solution)/shard_map/ppermute | solution.py:37
  146.0 20.0 %collective-permute-start.42 = (bf16[8,1,2,128,128]{4,3,2,1,0:T(8,128)(2,1)S(1)}, bf16[8,1,2,128,128]{4,3,2,1,0:T(8,128)(2,1)S(1)}, u32[]{:S(2)}, u32[]{:S(2)}) collective-permute-start(bf16[8,1,2,128,128]{4,3,2,1,0:T(8,128)(2,1)S(1)} %get-tuple-element.77.rest_2_), channel_id=1, source_target_pairs={{0,28},{4,8},{8,4},{12,16},{16,12},{20,24},{24,20},{28,0},{1,29},{... | collective-permute-start | bytes 1572872 | tf_op jit(solution)/shard_map/ppermute | solution.py:37
  148.6 7.3 %collective-permute-start.36 = (bf16[4,1,2,128,128]{4,3,2,1,0:T(8,128)(2,1)S(1)}, bf16[4,1,2,128,128]{4,3,2,1,0:T(8,128)(2,1)S(1)}, u32[]{:S(2)}, u32[]{:S(2)}) collective-permute-start(bf16[4,1,2,128,128]{4,3,2,1,0:T(8,128)(2,1)S(1)} %constant_dynamic-slice_fusion.2), channel_id=1, source_target_pairs={{0,4},{4,0},{8,12},{12,8},{16,20},{20,16},{24,28},{28,24},{1,5},{5... | collective-permute-start | bytes 786440 | tf_op jit(solution)/shard_map/ppermute | solution.py:37
  155.3 8.3 %collective-permute-start.37 = (bf16[1024,128]{1,0:T(8,128)(2,1)S(1)}, bf16[1024,128]{1,0:T(8,128)(2,1)S(1)}, u32[]{:S(2)}, u32[]{:S(2)}) collective-permute-start(bf16[1024,128]{1,0:T(8,128)(2,1)S(1)} %collective-permute-done.33.rest_2_), channel_id=1, source_target_pairs={{0,2},{2,3},{3,1},{1,0},{4,6},{6,7},{7,5},{5,4},{8,10},{10,11},{11... | collective-permute-start | bytes 786440 | tf_op jit(solution)/shard_map/ppermute | solution.py:59
  155.9 19.0 %collective-permute-start.43 = (bf16[8,1,2,128,128]{4,3,2,1,0:T(8,128)(2,1)S(1)}, bf16[8,1,2,128,128]{4,3,2,1,0:T(8,128)(2,1)S(1)}, u32[]{:S(2)}, u32[]{:S(2)}) collective-permute-start(bf16[8,1,2,128,128]{4,3,2,1,0:T(8,128)(2,1)S(1)} %get-tuple-element.77.rest_2_), channel_id=1, source_target_pairs={{0,4},{4,0},{8,12},{12,8},{16,20},{20,16},{24,28},{28,24},{1,5},{5... | collective-permute-start | bytes 1572872 | tf_op jit(solution)/shard_map/ppermute | solution.py:37
  163.6 9.1 %collective-permute-start.38 = (bf16[1024,128]{1,0:T(8,128)(2,1)S(1)}, bf16[1024,128]{1,0:T(8,128)(2,1)S(1)}, u32[]{:S(2)}, u32[]{:S(2)}) collective-permute-start(bf16[1024,128]{1,0:T(8,128)(2,1)S(1)} %shard_map.111.rest_1_), channel_id=1, source_target_pairs={{0,2},{2,3},{3,1},{1,0},{4,6},{6,7},{7,5},{5,4},{8,10},{10,11},{11... | collective-permute-start | bytes 786440 | tf_op jit(solution)/shard_map/ppermute | solution.py:59
  164.8 10.1 %collective-permute-start.41 = (bf16[4,1,2,128,128]{4,3,2,1,0:T(8,128)(2,1)S(1)}, bf16[4,1,2,128,128]{4,3,2,1,0:T(8,128)(2,1)S(1)}, u32[]{:S(2)}, u32[]{:S(2)}) collective-permute-start(bf16[4,1,2,128,128]{4,3,2,1,0:T(8,128)(2,1)S(1)} %constant_dynamic-slice_fusion.1), channel_id=1, source_target_pairs={{0,8},{4,28},{8,16},{12,4},{16,24},{20,12},{24,0},{28,20},{1,9},{5... | collective-permute-start | bytes 786440 | tf_op jit(solution)/shard_map/ppermute | solution.py:37
  165.1 14.5 %collective-permute-start.39 = (bf16[1024,128]{1,0:T(8,128)(2,1)S(1)}, bf16[1024,128]{1,0:T(8,128)(2,1)S(1)}, u32[]{:S(2)}, u32[]{:S(2)}) collective-permute-start(bf16[1024,128]{1,0:T(8,128)(2,1)S(1)} %shard_map.111.rest_1_), channel_id=1, source_target_pairs={{0,1},{2,0},{3,2},{1,3},{4,5},{6,4},{7,6},{5,7},{8,9},{10,8},{11,1... | collective-permute-start | bytes 786440 | tf_op jit(solution)/shard_map/ppermute | solution.py:59
  166.0 8.9 %collective-permute-start.44 = (bf16[4,1,2,128,128]{4,3,2,1,0:T(8,128)(2,1)S(1)}, bf16[4,1,2,128,128]{4,3,2,1,0:T(8,128)(2,1)S(1)}, u32[]{:S(2)}, u32[]{:S(2)}) collective-permute-start(bf16[4,1,2,128,128]{4,3,2,1,0:T(8,128)(2,1)S(1)} %constant_dynamic-slice_fusion), channel_id=1, source_target_pairs={{0,4},{4,0},{8,12},{12,8},{16,20},{20,16},{24,28},{28,24},{1,5},{5... | collective-permute-start | bytes 786440 | tf_op jit(solution)/shard_map/ppermute | solution.py:37
  172.7 9.5 %collective-permute-start.40 = (bf16[1024,128]{1,0:T(8,128)(2,1)S(1)}, bf16[1024,128]{1,0:T(8,128)(2,1)S(1)}, u32[]{:S(2)}, u32[]{:S(2)}) collective-permute-start(bf16[1024,128]{1,0:T(8,128)(2,1)S(1)} %collective-permute-done.38.rest_3_), channel_id=1, source_target_pairs={{0,2},{2,3},{3,1},{1,0},{4,6},{6,7},{7,5},{5,4},{8,10},{10,11},{11... | collective-permute-start | bytes 786440 | tf_op jit(solution)/shard_map/ppermute | solution.py:59
  182.2 10.5 %collective-permute-start.45 = (bf16[1024,128]{1,0:T(8,128)(2,1)S(1)}, bf16[1024,128]{1,0:T(8,128)(2,1)S(1)}, u32[]{:S(2)}, u32[]{:S(2)}) collective-permute-start(bf16[1024,128]{1,0:T(8,128)(2,1)S(1)} %shard_map.113.rest_0_), channel_id=1, source_target_pairs={{0,2},{2,3},{3,1},{1,0},{4,6},{6,7},{7,5},{5,4},{8,10},{10,11},{11... | collective-permute-start | bytes 786440 | tf_op jit(solution)/shard_map/ppermute | solution.py:59
  184.0 14.6 %collective-permute-start.46 = (bf16[1024,128]{1,0:T(8,128)(2,1)S(1)}, bf16[1024,128]{1,0:T(8,128)(2,1)S(1)}, u32[]{:S(2)}, u32[]{:S(2)}) collective-permute-start(bf16[1024,128]{1,0:T(8,128)(2,1)S(1)} %shard_map.113.rest_0_), channel_id=1, source_target_pairs={{0,1},{2,0},{3,2},{1,3},{4,5},{6,4},{7,6},{5,7},{8,9},{10,8},{11,1... | collective-permute-start | bytes 786440 | tf_op jit(solution)/shard_map/ppermute | solution.py:59
  192.8 7.6 %collective-permute-start.47 = (bf16[1024,128]{1,0:T(8,128)(2,1)S(1)}, bf16[1024,128]{1,0:T(8,128)(2,1)S(1)}, u32[]{:S(2)}, u32[]{:S(2)}) collective-permute-start(bf16[1024,128]{1,0:T(8,128)(2,1)S(1)} %collective-permute-done.45.rest_1_), channel_id=1, source_target_pairs={{0,2},{2,3},{3,1},{1,0},{4,6},{6,7},{7,5},{5,4},{8,10},{10,11},{11... | collective-permute-start | bytes 786440 | tf_op jit(solution)/shard_map/ppermute | solution.py:59
  (16 other events, 27.5 us)
